TPU v7x, 32 devices: a whole 2x2x4 slice. The times are simulated.
32 devices in a mesh: group: 2 (over x), block: 16 (over z, y, core).
Axes of the slice: x: 2, y: 2, z: 4, core: 2. Of those that a mesh axis runs over, the one named last changes fastest.
Arguments:
- populations: float32 [19, 384, 8, 128], P(None, ('group', 'block')), parts along dimension 1, as said below
- design: float32 [384, 8, 128], P(('group', 'block')), parts along dimension 0, may hold values from 0.05 to 1
- fluid_mask: int32 [384, 8, 128], P(('group', 'block')), parts along dimension 0, may hold values 0 or 1
- owner_after: int32 [96], P('group'), parts along dimension 0, may hold values from 0 to 15, as said below
Outputs:
- populations_after: float32 [19, 640, 8, 128], P(None, ('group', 'block')), parts along dimension 1
- sensitivity: float32 [640, 8, 128], P(('group', 'block')), parts along dimension 0
There are 2 independent parts, one for each index of `group`. A program takes and returns all parts, laid end to end along the dimension named above; each array names one. Nothing has to cross between parts.
Inputs may be any that keep to these rules, and one draw needn't show every extreme that they name: `populations`: every population lies between 0.4 and 2.5 times its lattice weight. `owner_after`: the list never falls along the duct; every block goes to its home device (block index // 3) or a neighbour of it; every device owns from 1 to 5 blocks, and some device owns exactly 5; block 0 stays on device 0.
All inputs are finite; a program needn't handle non-finite values. No bound on the sum of `fluid_mask` on one device may be relied on, other than what follows from the above.
Results may differ from a plain program's by a relative error of at most 0.000021.
Values sent between devices are 32-bit elements; how exact they have to be, the bound alone decides.
No kernel may reach another device: no remote copies, remote signals or barrier semaphores. Data moves between devices by JAX's collectives and lax.ppermute only.
A program may use at most 64 MiB of HBM per device.

v0:
```python
import functools
import math

import jax
import jax.numpy as jnp
from jax import lax
from jax.experimental import pallas as pl
from jax.experimental.pallas import tpu as pltpu
from jax.sharding import PartitionSpec as P

BX = 4
STEPS = 3
HALO = STEPS
MIB = 2**20

VELOCITY = (
    (0, 0, 0),
    (1, 0, 0),
    (-1, 0, 0),
    (0, 1, 0),
    (0, -1, 0),
    (0, 0, 1),
    (0, 0, -1),
    (1, 1, 0),
    (-1, -1, 0),
    (1, -1, 0),
    (-1, 1, 0),
    (1, 0, 1),
    (-1, 0, -1),
    (1, 0, -1),
    (-1, 0, 1),
    (0, 1, 1),
    (0, -1, -1),
    (0, 1, -1),
    (0, -1, 1),
)
OPP = (0,) + tuple(m + 1 if m % 2 else m - 1 for m in range(1, 19))
AHEAD = tuple(m for m in range(19) if VELOCITY[m][0] == 1)
BEHIND = tuple(m for m in range(19) if VELOCITY[m][0] == -1)
FORCE = 0.02
ROOT_45 = math.sqrt(4.5)
ROOT_2 = math.sqrt(2.0)


def rolled(field, step_y, step_z):
    if step_y:
        field = pltpu.roll(field, step_y % field.shape[0], 0)
    if step_z:
        field = pltpu.roll(field, step_z % field.shape[1], 1)
    return field


def pairs(values):
    plus = [values[2 * k + 1] + values[2 * k + 2] for k in range(9)]
    minus = [values[2 * k + 1] - values[2 * k + 2] for k in range(9)]
    return plus, minus


def first_moments(minus, scale):
    along_x, along_y, along_z = minus[:3]
    if scale != 1.0:
        along_x, along_y, along_z = scale * along_x, scale * along_y, scale * along_z
    along_x = along_x + ((minus[3] + minus[4]) + (minus[5] + minus[6]))
    along_y = along_y + ((minus[3] - minus[4]) + (minus[7] + minus[8]))
    along_z = along_z + ((minus[5] - minus[6]) + (minus[7] - minus[8]))
    return along_x, along_y, along_z


def density_velocity(state):
    plus, minus = pairs(state)
    axes = (plus[0] + plus[1]) + (plus[2] + state[0])
    diagonals = (plus[3] + plus[4]) + (plus[5] + plus[6]) + (plus[7] + plus[8])
    density = axes + diagonals
    inverse = 1.0 / density
    momentum = first_moments(minus, 1.0)
    return density, [part * inverse for part in momentum]


def collide(state, density, flow, open_rate):
    rate = ROOT_45 * open_rate
    x, y, z = (flow[0] + FORCE) * rate, flow[1] * rate, flow[2] * rate
    xx, yy, zz = x * x, y * y, z * z
    base = 1.0 - (xx + yy + zz) * (1.0 / 3.0)
    axis_weight = density * (1.2 / 18.0)
    axis_slope = density * (1.2 * ROOT_2 / 18.0)
    side_weight = density * (1.2 / 36.0)
    side_slope = density * (1.2 * ROOT_2 / 36.0)
    result = [density * 0.4 * base - 0.2 * state[0]]
    for k, along in enumerate((x, y, z, x + y, x - y, x + z, x - z, y + z, y - z)):
        if k < 3:
            even = axis_weight * (base + (xx, yy, zz)[k])
            odd = axis_slope * along
        else:
            even = side_weight * (base + along * along)
            odd = side_slope * along
        result.append((even + odd) - 0.2 * state[2 * k + 1])
        result.append((even - odd) - 0.2 * state[2 * k + 2])
    return result


def spread(level, slope):
    x, y, z = slope
    result = [level]
    for along in (x, y, z, x + y, x - y, x + z, x - z, y + z, y - z):
        result.append(level + along)
        result.append(level - along)
    return result


def pull(source, plane, word):
    here = [source[m, plane] for m in range(19)]
    result = [here[0]]
    for m in range(1, 19):
        step_x, step_y, step_z = VELOCITY[m]
        moved = here[m] if step_x == 0 else source[m, plane - step_x]
        moved = rolled(moved, step_y, step_z)
        result.append(jnp.where((word & (1 << m)) != 0, moved, here[OPP[m]]))
    return result


def link_word(behind, here, ahead):
    rows = lax.broadcasted_iota(jnp.int32, here.shape, 0)
    columns = lax.broadcasted_iota(jnp.int32, here.shape, 1)
    joined = behind + 2 * here + 4 * ahead
    word = jnp.zeros_like(here)
    for step_y in (-1, 0, 1):
        for step_z in (-1, 0, 1):
            if step_y and step_z:
                inner = {0: 1}
            else:
                inner = {1: 0, 0: 1, -1: 2}
            near = rolled(joined, step_y, step_z)
            if step_y == 1:
                near = jnp.where(rows == 0, 0, near)
            if step_y == -1:
                near = jnp.where(rows == here.shape[0] - 1, 0, near)
            if step_z == 1:
                near = jnp.where(columns == 0, 0, near)
            if step_z == -1:
                near = jnp.where(columns == here.shape[1] - 1, 0, near)
            for step_x, place in inner.items():
                if (step_x, step_y, step_z) == (0, 0, 0):
                    continue
                m = VELOCITY.index((step_x, step_y, step_z))
                word = word | ((near & (1 << place)) << (m - place))
    return jnp.where(here > 0, word, 0)


def each_plane(low, high, body):
    def two(index, carry):
        body(low + 2 * index)
        body(low + 2 * index + 1)
        return carry

    lax.fori_loop(0, (high - low) // 2, two, 0)
    if (high - low) % 2:
        body(high - 1)


def is_fluid_rate(mark):
    design = jnp.maximum(mark, 0.0)
    return (mark >= 0.0).astype(jnp.int32), (1.0 + 4.0 * design) / (1.6 + 3.4 * design)


def store(target, plane, values):
    for m, part in enumerate(values):
        target[m, plane] = part


def remember(history, step, plane, density, flow):
    history[4 * step, plane] = density
    for axis in range(3):
        history[4 * step + 1 + axis, plane] = flow[axis]


def drag_terms(flow, open_rate):
    return (flow[0] * flow[0] + flow[1] * flow[1] + flow[2] * flow[2]) / open_rate


def parity(axis="block"):
    return 1 - lax.rem(lax.axis_index(axis), 2)


def pick(flag, yes, no):
    return no + flag * (yes - no)


def edge_kernel(home, pops, design, mask, near, far, design_near, mask_near, sems):
    up = parity()
    copies = []
    for side, (out, ahead) in enumerate(((near, up), (far, 1 - up))):
        first = ahead * (home - HALO)
        copies.append(
            pltpu.make_async_copy(
                pops.at[:, pl.ds(first, HALO)], out.at[pl.ds(0, 19)], sems.at[3 * side]
            )
        )
        for place, (source, kept) in enumerate(((design, design_near), (mask, mask_near))):
            copies.append(
                pltpu.make_async_copy(
                    source.at[pl.ds(first, HALO)], kept.at[side], sems.at[3 * side + 1 + place]
                )
            )
    for copy in copies:
        copy.start()
    for side, out in enumerate((near, far)):
        copies[3 * side + 1].wait()
        copies[3 * side + 2].wait()
        for plane in range(HALO):
            out[19, plane] = jnp.where(mask_near[side, plane] > 0, design_near[side, plane], -1.0)
    copies[0].wait()
    copies[3].wait()


def interior_kernel(
    home,
    owner,
    pops_far,
    design,
    mask,
    to_near,
    to_far,
    edges,
    history,
    final,
    opens,
    fluid,
    words,
    drag,
    marked,
    where,
    pops,
    even,
    odd,
    designs,
    masks,
    sems,
):
    copies = [
        pltpu.make_async_copy(source, target, sems.at[place])
        for place, (source, target) in enumerate(((pops_far, pops), (design, designs), (mask, masks)))
    ]
    for copy in copies:
        copy.start()
    up = parity()
    rank = lax.axis_index("block")
    home_blocks = home // BX

    def count(block, carry):
        below, own = carry
        holder = owner[block]
        return below + (holder < rank).astype(jnp.int32), own + (holder == rank).astype(jnp.int32)

    def stray(device, found):
        late = owner[home_blocks * device + 1] < device
        early = owner[home_blocks * device + home_blocks - 2] > device
        return found | late.astype(jnp.int32) | early.astype(jnp.int32)

    below, own = lax.fori_loop(0, owner.shape[0], count, (jnp.int32(0), jnp.int32(0)))
    where[0] = below - home_blocks * rank
    where[1] = own
    where[2] = lax.fori_loop(0, owner.shape[0] // home_blocks, stray, jnp.int32(0))
    for copy in copies:
        copy.wait()

    def start(plane):
        mark = jnp.where(masks[plane] > 0, designs[plane], -1.0)
        marked[plane] = mark
        fluid[plane], open_rate = is_fluid_rate(mark)
        opens[plane] = open_rate
        state = [pops[m, plane] for m in range(19)]
        density, flow = density_velocity(state)
        remember(history, 0, plane, density, flow)
        store(even, plane, collide(state, density, flow, open_rate))

    def link(plane):
        words[plane] = link_word(fluid[plane - 1], fluid[plane], fluid[plane + 1])

    def advance(step, source, target, plane):
        state = pull(source, plane, words[plane])
        density, flow = density_velocity(state)
        remember(history, step, plane, density, flow)
        store(target, plane, collide(state, density, flow, opens[plane]))

    def finish(plane):
        state = pull(even, plane, words[plane])
        density, flow = density_velocity(state)
        remember(history, 3, plane, density, flow)
        here = fluid[plane] > 0
        for m in range(19):
            final[m, plane - STEPS] = jnp.where(here, state[m], pops[m, plane])
        drag[...] += jnp.where(here, drag_terms(flow, opens[plane]), 0.0)

    def send(step, source):
        for out, ahead in ((to_near, up), (to_far, 1 - up)):
            plane = pick(ahead, home - 1 - STEPS, STEPS)
            for slot in range(5):
                out[5 * step + slot] = source[AHEAD[slot] + 1 - ahead, plane]
            if step == 0:
                out[15] = marked[plane]
        for m in range(19):
            for side in range(2):
                edges[m, 4 * step + side] = source[m, step + side]
                edges[m, 4 * step + 2 + side] = source[m, home - 2 - step + side]

    drag[...] = jnp.zeros_like(drag)
    each_plane(0, home, start)
    send(0, even)
    each_plane(1, home - 1, link)
    each_plane(1, home - 1, functools.partial(advance, 1, even, odd))
    send(1, odd)
    each_plane(2, home - 2, functools.partial(advance, 2, odd, even))
    send(2, even)
    each_plane(3, home - 3, finish)


def boundary_kernel(
    home,
    own_near,
    own_far,
    near,
    far,
    from_near,
    from_far,
    edges,
    inner_history,
    inner_final,
    inner_opens,
    inner_fluid,
    inner_words,
    inner_drag,
    final,
    history,
    opens,
    words,
    drag,
    even,
    odd,
    fluid,
    sems,
):
    span = home + 2 * HALO
    up = parity()
    sides = ((up, own_near, near, from_near), (1 - up, own_far, far, from_far))
    copies = [
        pltpu.make_async_copy(
            inner_history.at[pl.ds(4 * step, 4), pl.ds(step, home - 2 * step)],
            history.at[pl.ds(4 * step, 4), pl.ds(HALO + step, home - 2 * step)],
            sems.at[step],
        )
        for step in range(4)
    ]
    copies.append(
        pltpu.make_async_copy(inner_final, final.at[:, pl.ds(BX + STEPS, home - 2 * STEPS)], sems.at[4])
    )
    for copy in copies:
        copy.start()

    for plane in range(home):
        fluid[plane + HALO + 1] = inner_fluid[plane]
        opens[plane + HALO] = inner_opens[plane]
    for plane in range(1, home - 1):
        words[plane + HALO] = inner_words[plane]
    for ahead, _, _, message in sides:
        fluid[ahead * (span + 1)] = (message[15] >= 0.0).astype(jnp.int32)

    def begin(ahead, side, plane):
        index = plane + ahead * (HALO + home)
        fluid[index + 1], open_rate = is_fluid_rate(side[19, plane])
        opens[index] = open_rate
        state = [side[m, plane] for m in range(19)]
        density, flow = density_velocity(state)
        store(even, index + 1, collide(state, density, flow, open_rate))

    def start(plane, carry):
        for ahead, _, side, _ in sides:
            begin(ahead, side, plane)
        return carry

    lax.fori_loop(0, HALO, start, 0)

    def receive(step, target):
        for ahead, _, _, message in sides:
            for slot in range(5):
                target[AHEAD[slot] + ahead, ahead * (span + 1)] = message[5 * step + slot]
        for m in range(19):
            for side in range(2):
                target[m, HALO + 1 + step + side] = edges[m, 4 * step + side]
                target[m, HALO + home - 1 - step + side] = edges[m, 4 * step + 2 + side]

    def both(step, body):
        def two(place, carry):
            body(place)
            body(place + HALO + home - step)
            return carry

        lax.fori_loop(0, HALO + step, two, 0)

    def link(index):
        words[index] = link_word(fluid[index], fluid[index + 1], fluid[index + 2])

    def advance(step, source, target, index):
        state = pull(source, index + 1, words[index])
        density, flow = density_velocity(state)
        remember(history, step, index, density, flow)
        store(target, index + 1, collide(state, density, flow, opens[index]))

    both(1, link)
    receive(0, even)
    both(1, functools.partial(advance, 1, even, odd))
    receive(1, odd)
    both(2, functools.partial(advance, 2, odd, even))
    receive(2, even)
    drag[...] = inner_drag[...]

    def finish(initial, own, place, index):
        state = pull(even, index + 1, words[index])
        density, flow = density_velocity(state)
        remember(history, 3, index, density, flow)
        here = fluid[index + 1] > 0
        for m in range(19):
            final[m, index + BX - HALO] = jnp.where(here, state[m], initial[m, place])
        if own:
            drag[...] += jnp.where(here, drag_terms(flow, opens[index]), 0.0)

    def outer(place, carry):
        for ahead, _, side, _ in sides:
            finish(side, False, place, place + ahead * (HALO + home))
        return carry

    def inner(place, carry):
        for ahead, own, _, _ in sides:
            finish(own, True, place, place + HALO + ahead * (home - STEPS))
        return carry

    lax.fori_loop(0, HALO, outer, 0)
    lax.fori_loop(0, STEPS, inner, 0)
    for copy in copies:
        copy.wait()


def backward_kernel(
    home, history, opens, words, marked, inner_final, gradient, to_near, to_far, even, odd, share
):
    def recall(step, plane):
        return history[4 * step, plane], [history[4 * step + 1 + axis, plane] for axis in range(3)]

    def seed(plane):
        density, flow = recall(STEPS, plane)
        damping = 1.0 / opens[plane]
        square = flow[0] * flow[0] + flow[1] * flow[1] + flow[2] * flow[2]
        share[plane] = -square * damping
        factor = 2.0 * damping / density
        slope = [part * factor for part in flow]
        values = spread(-square * factor, slope)
        for m in range(19):
            even[OPP[m], plane] = values[m]

    each_plane(0, home + 2 * HALO, seed)

    def retreat(step, source, target, plane):
        mirrored = pull(source, plane, words[plane])
        adjoint = [mirrored[OPP[m]] for m in range(19)]
        density, flow = recall(step, plane)
        open_rate = opens[plane]
        force_flow = [flow[0] + FORCE, flow[1], flow[2]]
        x, y, z = [open_rate * part for part in force_flow]
        plus, minus = pairs(adjoint)
        mx, my, mz = [part * (1.0 / 12.0) for part in first_moments(minus, 2.0)]
        xy_plus, xz_plus, yz_plus = plus[3] + plus[4], plus[5] + plus[6], plus[7] + plus[8]
        axes = [2.0 * plus[k] for k in range(3)]
        whole = 12.0 * adjoint[0] + (axes[0] + axes[1] + axes[2]) + (xy_plus + xz_plus + yz_plus)
        third = whole * (1.0 / 3.0)
        xx = axes[0] + (xy_plus + xz_plus) - third
        yy = axes[1] + (xy_plus + yz_plus) - third
        zz = axes[2] + (xz_plus + yz_plus) - third
        xy, xz, yz = plus[3] - plus[4], plus[5] - plus[6], plus[7] - plus[8]
        hx = 0.25 * (xx * x + xy * y + xz * z)
        hy = 0.25 * (xy * x + yy * y + yz * z)
        hz = 0.25 * (xz * x + yz * y + zz * z)
        rate = 1.2 * open_rate
        slope = [rate * (mx + hx), rate * (my + hy), rate * (mz + hz)]
        pushed = slope[0] * force_flow[0] + slope[1] * force_flow[1] + slope[2] * force_flow[2]
        share[plane] += density * pushed
        if target is None:
            return
        level = whole * (1.2 / 36.0) + 1.2 * (
            x * (mx + 0.5 * hx) + y * (my + 0.5 * hy) + z * (mz + 0.5 * hz)
        )
        level = level - (slope[0] * flow[0] + slope[1] * flow[1] + slope[2] * flow[2])
        values = spread(level, slope)
        for m in range(19):
            target[OPP[m], plane] = values[m] - 0.2 * adjoint[m]

    each_plane(HALO - 2, HALO + home + 2, functools.partial(retreat, 2, even, odd))
    each_plane(HALO - 1, HALO + home + 1, functools.partial(retreat, 1, odd, even))
    each_plane(HALO, HALO + home, functools.partial(retreat, 0, even, None))

    for plane in range(home):
        design = marked[plane]
        slope = 3.0 / ((1.6 + 3.4 * design) * (1.0 + 4.0 * design))
        gradient[plane] = jnp.where(design >= 0.0, share[plane + HALO] * slope, 0.0)
    up = parity()
    for out, ahead in ((to_near, up), (to_far, 1 - up)):
        for plane in range(BX):
            out[19 + plane] = gradient[ahead * (home - BX) + plane]
        for m in range(19):
            out[m] = inner_final[m, ahead * (home - 2 * STEPS - 1)]


def scaled(home, cells, where, drag, joined, out):
    factor = cells / jnp.sum(drag[...])
    reach = (joined.shape[0] - home) // 2
    for plane in range(out.shape[0]):
        spot = jnp.clip(where[0] * BX + reach + plane, 0, joined.shape[0] - 1)
        live = plane < where[1] * BX
        out[plane] = jnp.where(live, joined[spot] * factor, 0.0)


def near_kernel(
    home, cells, where, final, drag, gradient, from_near, from_far, out, slots, joined, outer, zeros, sems
):
    up = parity()
    blocks = out.shape[1] // BX
    last = home // BX + 1
    zeros[...] = jnp.zeros_like(zeros)
    for m in range(19):
        for plane in range(BX - 1):
            outer[0, m, plane + 1] = final[m, plane + 1]
            outer[1, m, plane] = final[m, BX + home + plane]
        for ahead, message in ((up, from_near), (1 - up, from_far)):
            outer[ahead, m, ahead * (BX - 1)] = message[m]
    for slot in range(blocks):
        target = out.at[:, pl.ds(slot * BX, BX)]
        live = slot < where[1]
        block = jnp.clip(where[0] + 1 + slot, 0, last)
        inside = (block > 0) & (block < last)

        @pl.when(live & inside)
        def _():
            source = final.at[:, pl.ds(block * BX, BX)]
            pltpu.make_async_copy(source, target, sems.at[slot]).start()

        @pl.when(live & jnp.logical_not(inside))
        def _():
            source = outer.at[(block > 0).astype(jnp.int32)]
            pltpu.make_async_copy(source, target, sems.at[slot]).start()

        @pl.when(jnp.logical_not(live))
        def _():
            pltpu.make_async_copy(zeros, target, sems.at[slot]).start()

    for ahead, message in ((up, from_near), (1 - up, from_far)):
        joined[pl.ds(ahead * (BX + home), BX)] = message[pl.ds(19, BX)]
    joined[pl.ds(BX, home)] = gradient[...]
    scaled(home, cells, where, drag, joined, slots)
    for slot in range(blocks):
        pltpu.make_async_copy(zeros, out.at[:, pl.ds(slot * BX, BX)], sems.at[slot]).wait()


def far_kernel(
    home, cells, where, final, drag, gradient, from_left, from_right, out, slots, joined, zeros, sems
):
    zeros[...] = jnp.zeros_like(zeros)
    blocks = out.shape[1] // BX
    most = final.shape[1] // BX - 1
    for slot in range(blocks):
        target = out.at[:, pl.ds(slot * BX, BX)]
        live = slot < where[1]
        begin = jnp.clip(where[0] + home // BX + slot, 0, most) * BX

        @pl.when(live)
        def _():
            pltpu.make_async_copy(final.at[:, pl.ds(begin, BX)], target, sems.at[slot]).start()

        @pl.when(jnp.logical_not(live))
        def _():
            pltpu.make_async_copy(zeros, target, sems.at[slot]).start()

    joined[pl.ds(0, home)] = from_left[...]
    joined[pl.ds(home, home)] = gradient[...]
    joined[pl.ds(2 * home, home)] = from_right[...]
    scaled(home, cells, where, drag, joined, slots)
    for slot in range(blocks):
        pltpu.make_async_copy(zeros, out.at[:, pl.ds(slot * BX, BX)], sems.at[slot]).wait()


def body(populations, design, fluid_mask, owner_after):
    count = lax.axis_size("block")
    home, width_y, width_z = design.shape
    slots = home // BX + 2
    span = home + 2 * HALO
    plane = (width_y, width_z)
    vmem = pl.BlockSpec(memory_space=pltpu.VMEM)
    hbm = pl.BlockSpec(memory_space=pltpu.HBM)
    anywhere = pl.BlockSpec(memory_space=pl.ANY)
    smem = pl.BlockSpec(memory_space=pltpu.SMEM)
    cells = float(count * home * width_y * width_z)
    near_pairs = [(i, i ^ 1) for i in range(count)]
    far_pairs = [(i, (i + 1 if i % 2 else i - 1) % count) for i in range(count)]
    inner_pairs = far_pairs[1:-1]

    def planes(*lead, dtype=jnp.float32):
        return jax.ShapeDtypeStruct(lead + plane, dtype)

    def scratch(*lead, dtype=jnp.float32):
        return pltpu.VMEM(lead + plane, dtype)

    def call(kernel, name, ins, outs, scratches, limit, moved, *operands):
        return pl.pallas_call(
            kernel,
            out_shape=[shape for shape, _ in outs],
            in_specs=ins,
            out_specs=[spec for _, spec in outs],
            scratch_shapes=scratches,
            compiler_params=pltpu.CompilerParams(vmem_limit_bytes=limit * MIB),
            cost_estimate=pl.CostEstimate(flops=0, bytes_accessed=moved, transcendentals=0),
            name=name,
        )(*operands)

    populations, design, fluid_mask = [
        pltpu.with_memory_space_constraint(part, pltpu.HBM)
        for part in (populations, design, fluid_mask)
    ]
    own_near, own_far = call(
        functools.partial(edge_kernel, home),
        "edge_planes",
        [hbm] * 3,
        [(planes(20, HALO), vmem)] * 2,
        [scratch(2, HALO), scratch(2, HALO, dtype=jnp.int32), pltpu.SemaphoreType.DMA((6,))],
        4,
        1_000_000,
        populations,
        design,
        fluid_mask,
    )
    far = lax.ppermute(own_far, "block", far_pairs)
    near = lax.ppermute(own_near, "block", near_pairs)

    deep = home - 2 * STEPS
    inner_shapes = (
        planes(16),
        planes(16),
        planes(19, 12),
        planes(16, home),
        planes(19, deep),
        planes(home),
        planes(home, dtype=jnp.int32),
        planes(home, dtype=jnp.int32),
        planes(),
        planes(home),
    )
    to_near, to_far, *inner, drag, marked, where = call(
        functools.partial(interior_kernel, home),
        "interior_steps",
        [smem] + [hbm] * 3,
        [(shape, vmem) for shape in inner_shapes] + [(jax.ShapeDtypeStruct((3,), jnp.int32), smem)],
        [scratch(19, home)] * 3
        + [scratch(home), scratch(home, dtype=jnp.int32), pltpu.SemaphoreType.DMA((3,))],
        16,
        6_000_000,
        owner_after,
        populations,
        design,
        fluid_mask,
    )
    from_far = lax.ppermute(to_far, "block", far_pairs)
    from_near = lax.ppermute(to_near, "block", near_pairs)

    boundary_shapes = (
        planes(19, home + 2 * BX),
        planes(16, span),
        planes(span),
        planes(span, dtype=jnp.int32),
        planes(),
    )
    final, history, opens, words, drag = call(
        functools.partial(boundary_kernel, home),
        "boundary_steps",
        [vmem] * 7 + [anywhere] * 2 + [vmem] * 4,
        [(shape, vmem) for shape in boundary_shapes],
        [
            scratch(19, span + 2),
            scratch(19, span + 2),
            scratch(span + 2, dtype=jnp.int32),
            pltpu.SemaphoreType.DMA((5,)),
        ],
        20,
        8_000_000,
        own_near,
        own_far,
        near,
        far,
        from_near,
        from_far,
        *inner,
        drag,
    )

    distance = 1
    while distance < count:
        swap = [(i, i ^ distance) for i in range(count)]
        drag = drag + lax.ppermute(drag, "block", swap)
        distance *= 2

    gradient, to_near, to_far = call(
        functools.partial(backward_kernel, home),
        "backward_steps",
        [vmem] * 5,
        [(planes(home), vmem), (planes(19 + BX), vmem), (planes(19 + BX), vmem)],
        [scratch(19, span), scratch(19, span), scratch(span)],
        20,
        8_000_000,
        history,
        opens,
        words,
        marked,
        inner[2],
    )
    from_far = lax.ppermute(to_far, "block", inner_pairs)
    from_near = lax.ppermute(to_near, "block", near_pairs)

    def slotted(kernel, name, reach, extra, *operands):
        return call(
            functools.partial(kernel, home, cells),
            name,
            [smem, anywhere if not extra else vmem] + [vmem] * 4,
            [(planes(19, slots * BX), anywhere), (planes(slots * BX), vmem)],
            [scratch(home + 2 * reach)]
            + extra
            + [scratch(19, BX), pltpu.SemaphoreType.DMA((slots,))],
            10,
            4_000_000,
            *operands,
        )

    def near_slots(*operands):
        return slotted(near_kernel, "near_slots", BX, [scratch(2, 19, BX)], *operands)

    def far_slots(where, final, drag, gradient, *_):
        own = final[:, BX : BX + home]
        ring = [(i, i + 1) for i in range(count - 1)]
        back = [(i + 1, i) for i in range(count - 1)]
        wide = [lax.ppermute(own, "block", route) for route in (ring, back)]
        slopes = [lax.ppermute(gradient, "block", route) for route in (ring, back)]
        joined = jnp.concatenate([wide[0], own, wide[1]], axis=1)
        return slotted(far_kernel, "far_slots", home, [], where, joined, drag, gradient, *slopes)

    operands = (where, final, drag, gradient, from_near, from_far)
    return tuple(lax.cond(where[2] > 0, far_slots, near_slots, *operands))


def solution(mesh):
    placed = (
        P(None, ("group", "block"), None, None),
        P(("group", "block"), None, None),
        P(("group", "block"), None, None),
        P("group"),
    )
    return jax.shard_map(
        body,
        mesh=mesh,
        in_specs=placed,
        out_specs=(P(None, ("group", "block"), None, None), P(("group", "block"), None, None)),
        check_vma=False,
    )
```

profile of v0, /device:TPU:0, one launch (start us, length us, event | category | flops | bytes accessed | tf_op | source)
XLA Modules:
  0.0 43.0 jit_solution(11277101934222068755)
XLA Ops:
  0.6 1.2 %edge_planes.1 = (f32[20,3,8,128]{3,2,1,0:T(8,128)S(1)}, f32[20,3,8,128]{3,2,1,0:T(8,128)S(1)}) custom-call(f32[19,12,8,128]{3,2,1,0:T(8,128)} %pops.1, f32[12,8,128]{2,1,0:T(8,128)} %design.3, s32[12,8,128]{2,1,0:T(8,128)} %mask.3), custom_call_target="tpu_custom_call" | custom-call | bytes 1000000 | tf_op jit(solution)/shard_map/edge_planes/pallas_call | solution.py:610
  1.8 0.5 %collective-permute-start.4 = (f32[20,3,8,128]{3,2,1,0:T(8,128)S(1)}, f32[20,3,8,128]{3,2,1,0:T(8,128)S(1)}, u32[]{:S(2)}, u32[]{:S(2)}) collective-permute-start(f32[20,3,8,128]{3,2,1,0:T(8,128)S(1)} %get-tuple-element.54.own_near), channel_id=1, source_target_pairs={{0,1},{1,0},{2,3},{3,2},{4,5},{5,4},{6,7},{7,6},{8,9},{9,8},{10,11... | collective-permute-start | bytes 737288 | tf_op jit(solution)/shard_map/ppermute | solution.py:638
  2.3 5.7 %collective-permute-start.5 = (f32[20,3,8,128]{3,2,1,0:T(8,128)S(1)}, f32[20,3,8,128]{3,2,1,0:T(8,128)S(1)}, u32[]{:S(2)}, u32[]{:S(2)}) collective-permute-start(f32[20,3,8,128]{3,2,1,0:T(8,128)S(1)} %get-tuple-element.55.own_far), channel_id=1, source_target_pairs={{0,15},{1,2},{2,1},{3,4},{4,3},{5,6},{6,5},{7,8},{8,7},{9,10},{10,... | collective-permute-start | bytes 737288 | tf_op jit(solution)/shard_map/ppermute | solution.py:637
  8.0 0.0 copy-start
  8.0 0.7 %copy-done = s32[48]{0:T(128)S(1)} copy-done((s32[48]{0:T(128)S(1)}, s32[48]{0:T(128)}, u32[]{:S(2)}) %copy-start) | copy-done | bytes 216
  8.6 4.7 %interior_steps.1 = (f32[16,8,128]{2,1,0:T(8,128)S(1)}, f32[16,8,128]{2,1,0:T(8,128)S(1)}, f32[19,12,8,128]{3,2,1,0:T(8,128)S(1)}, f32[16,12,8,128]{3,2,1,0:T(8,...) custom-call(s32[48]{0:T(128)S(1)} %copy-done, ...), custom_call_target="tpu_custom_call" | custom-call | bytes 6000000 | tf_op jit(solution)/shard_map/interior_steps/pallas_call | solution.py:610
  13.4 0.1 collective-permute-start.6
  13.4 0.6 %collective-permute-start.7 = (f32[16,8,128]{2,1,0:T(8,128)S(1)}, f32[16,8,128]{2,1,0:T(8,128)S(1)}, u32[]{:S(2)}, u32[]{:S(2)}) collective-permute-start(f32[16,8,128]{2,1,0:T(8,128)S(1)} %get-tuple-element.57), channel_id=1, source_target_pairs={{0,15},{1,2},{2,1},{3,4},{4,3},{5,6},{6,5},{7,8},{8,7},{9,10},{10,... | collective-permute-start | bytes 196616 | tf_op jit(solution)/shard_map/ppermute | solution.py:667
  14.0 0.6 %collective-permute-done.6.from_near = f32[16,8,128]{2,1,0:T(8,128)S(1)} collective-permute-done((f32[16,8,128]{2,1,0:T(8,128)S(1)}, f32[16,8,128]{2,1,0:T(8,128)S(1)}, u32[]{:S(2)}, u32[]{:S(2)}) %collective-permute-start.6) | collective-permute-done | bytes 65568 | tf_op jit(solution)/shard_map/ppermute | solution.py:668
  14.7 5.2 %collective-permute-done.7.from_far = f32[16,8,128]{2,1,0:T(8,128)S(1)} collective-permute-done((f32[16,8,128]{2,1,0:T(8,128)S(1)}, f32[16,8,128]{2,1,0:T(8,128)S(1)}, u32[]{:S(2)}, u32[]{:S(2)}) %collective-permute-start.7) | collective-permute-done | bytes 65568 | tf_op jit(solution)/shard_map/ppermute | solution.py:667
  19.9 0.0 collective-permute-done.4.near
  19.9 0.0 collective-permute-done.5.far
  19.9 2.8 %boundary_steps.1 = (f32[19,20,8,128]{3,2,1,0:T(8,128)S(1)}, f32[16,18,8,128]{3,2,1,0:T(8,128)S(1)}, f32[18,8,128]{2,1,0:T(8,128)S(1)}, s32[18,8,128]{2,1,0:T(8,128)S(1)}, f32[8,128]{1,0:T(8,128)S(1)}) custom-call(f32[20,3,8,128]{3,2,1,0:T(8,128)S(1)} %get-tuple-element.54.own_near, f32[20,3,8,128]{3,2,1,0:T(8,128)S(1)} %get-tuple-element.55.own_far, ...), custom_call_target="tpu_custom_call" | custom-call | bytes 8000000 | tf_op jit(solution)/shard_map/boundary_steps/pallas_call | solution.py:610
  22.7 2.8 %backward_steps.1 = (f32[12,8,128]{2,1,0:T(8,128)S(1)}, f32[23,8,128]{2,1,0:T(8,128)S(1)}, f32[23,8,128]{2,1,0:T(8,128)S(1)}) custom-call(f32[16,18,8,128]{3,2,1,0:T(8,128)S(1)} %get-tuple-element.67.history, f32[18,8,128]{2,1,0:T(8,128)S(1)} %get-tuple-element.68.opens, s32[18,8,128]{2,1,0:T(8,128)S(1)} %get-tuple-element.69.words, ...), custom_call_target="tpu_custom_call" | custom-call | bytes 8000000 | tf_op jit(solution)/shard_map/backward_steps/pallas_call | solution.py:610
  25.5 0.1 collective-permute-start.12
  25.6 0.7 %collective-permute-start.13 = (f32[23,8,128]{2,1,0:T(8,128)S(1)}, f32[23,8,128]{2,1,0:T(8,128)S(1)}, u32[]{:S(2)}, u32[]{:S(2)}) collective-permute-start(f32[23,8,128]{2,1,0:T(8,128)S(1)} %get-tuple-element.73), channel_id=1, source_target_pairs={{1,2},{2,1},{3,4},{4,3},{5,6},{6,5},{7,8},{8,7},{9,10},{10,9},{11,... | collective-permute-start | bytes 282632 | tf_op jit(solution)/shard_map/ppermute | solution.py:720
  26.3 1.8 %collective-permute-start.8 = (f32[8,128]{1,0:T(8,128)S(1)}, f32[8,128]{1,0:T(8,128)S(1)}, u32[]{:S(2)}, u32[]{:S(2)}) collective-permute-start(f32[8,128]{1,0:T(8,128)S(1)} %get-tuple-element.66), channel_id=1, source_target_pairs={{0,1},{1,0},{2,3},{3,2},{4,5},{5,4},{6,7},{7,6},{8,9},{9,8},{10,11... | collective-permute-start | bytes 12296 | tf_op jit(solution)/shard_map/ppermute | solution.py:703
  28.1 0.8 %collective-permute-done.8 = f32[8,128]{1,0:T(8,128)S(1)} collective-permute-done((f32[8,128]{1,0:T(8,128)S(1)}, f32[8,128]{1,0:T(8,128)S(1)}, u32[]{:S(2)}, u32[]{:S(2)}) %collective-permute-start.8) | collective-permute-done | bytes 4128 | tf_op jit(solution)/shard_map/ppermute | solution.py:703
  28.9 2.0 %collective-permute-start.9 = (f32[8,128]{1,0:T(8,128)S(1)}, f32[8,128]{1,0:T(8,128)S(1)}, u32[]{:S(2)}, u32[]{:S(2)}) collective-permute-start(f32[8,128]{1,0:T(8,128)S(1)} %add.12), channel_id=1, source_target_pairs={{0,2},{1,3},{2,0},{3,1},{4,6},{5,7},{6,4},{7,5},{8,10},{9,11},{10,... | collective-permute-start | bytes 12296 | tf_op jit(solution)/shard_map/ppermute | solution.py:703
  30.9 1.6 %collective-permute-done.9 = f32[8,128]{1,0:T(8,128)S(1)} collective-permute-done((f32[8,128]{1,0:T(8,128)S(1)}, f32[8,128]{1,0:T(8,128)S(1)}, u32[]{:S(2)}, u32[]{:S(2)}) %collective-permute-start.9) | collective-permute-done | bytes 4128 | tf_op jit(solution)/shard_map/ppermute | solution.py:703
  32.5 0.0 collective-permute-start.10
  32.5 3.6 %collective-permute-done.10 = f32[8,128]{1,0:T(8,128)S(1)} collective-permute-done((f32[8,128]{1,0:T(8,128)S(1)}, f32[8,128]{1,0:T(8,128)S(1)}, u32[]{:S(2)}, u32[]{:S(2)}) %collective-permute-start.10) | collective-permute-done | bytes 4128 | tf_op jit(solution)/shard_map/ppermute | solution.py:703
  36.1 0.0 collective-permute-start.11
  36.1 0.6 %slice.6 = s32[1]{0:T(128)} slice(s32[3]{0:T(128)S(1)} %get-tuple-element.53), slice={[2:3]} | slice | bytes 8 | tf_op jit(solution)/shard_map/slice | solution.py:750
  37.4 3.3 %collective-permute-done.11 = f32[8,128]{1,0:T(8,128)S(1)} collective-permute-done((f32[8,128]{1,0:T(8,128)S(1)}, f32[8,128]{1,0:T(8,128)S(1)}, u32[]{:S(2)}, u32[]{:S(2)}) %collective-permute-start.11) | collective-permute-done | bytes 4128 | tf_op jit(solution)/shard_map/ppermute | solution.py:703
  40.6 0.0 collective-permute-done.12
  40.6 0.0 collective-permute-done.13
  40.6 2.4 %conditional.1 = ((f32[19,20,8,128]{3,2,1,0:T(8,128)}, f32[20,8,128]{2,1,0:T(8,128)})) conditional(s32[]{:T(128)} %bitcast, (s32[3]{0:T(128)S(1)}, f32[19,20,8,128]{3,2,1,0:T(8,128)S(1)}, f32[8,128]{1,0:T(8,128)S(1)}, f32[12,8,128]{2,1,0:T(8,128)S(1)}, f32[23,8,128]{2,1,0:T(8,128)S(1)}, /*index=5*/f32[23,8,128]{2,1,0:T(8,128)S(1)}) %tuple.13, ...), branch_computations={%region_0.0_spmd, %region_1.0_spmd} | conditional | flops 1400832 | bytes 19335592 | solution.py:750
  40.6 2.4 %near_slots.1 = (f32[19,20,8,128]{3,2,1,0:T(8,128)}, f32[20,8,128]{2,1,0:T(8,128)}) custom-call(s32[3]{0:T(128)S(1)} %get-tuple-element.20.where, f32[19,20,8,128]{3,2,1,0:T(8,128)S(1)} %get-tuple-element.21.final, f32[8,128]{1,0:T(8,128)S(1)} %get-tuple-element.22.drag, f32[12,8,128]{2,1,0:T(8,128)S(1)} %get-tuple-element.23.gradient, ...), custom_call_target="tpu_custom_call" | custom-call | bytes 4000000 | tf_op jit(solution)/shard_map/cond/branch_0_fun/near_slots/pallas_call | solution.py:610
  (4 shorter events, 0.0 us)
Async XLA Ops:
  1.8 18.1 %collective-permute-start.4 = (f32[20,3,8,128]{3,2,1,0:T(8,128)S(1)}, f32[20,3,8,128]{3,2,1,0:T(8,128)S(1)}, u32[]{:S(2)}, u32[]{:S(2)}) collective-permute-start(f32[20,3,8,128]{3,2,1,0:T(8,128)S(1)} %get-tuple-element.54.own_near), channel_id=1, source_target_pairs={{0,1},{1,0},{2,3},{3,2},{4,5},{5,4},{6,7},{7,6},{8,9},{9,8},{10,11... | collective-permute-start | bytes 737288 | tf_op jit(solution)/shard_map/ppermute | solution.py:638
  2.3 17.6 %collective-permute-start.5 = (f32[20,3,8,128]{3,2,1,0:T(8,128)S(1)}, f32[20,3,8,128]{3,2,1,0:T(8,128)S(1)}, u32[]{:S(2)}, u32[]{:S(2)}) collective-permute-start(f32[20,3,8,128]{3,2,1,0:T(8,128)S(1)} %get-tuple-element.55.own_far), channel_id=1, source_target_pairs={{0,15},{1,2},{2,1},{3,4},{4,3},{5,6},{6,5},{7,8},{8,7},{9,10},{10,... | collective-permute-start | bytes 737288 | tf_op jit(solution)/shard_map/ppermute | solution.py:637
  8.0 0.7 %copy-start = (s32[48]{0:T(128)S(1)}, s32[48]{0:T(128)}, u32[]{:S(2)}) copy-start(s32[48]{0:T(128)} %owner.1) | copy-start | bytes 580
  13.4 1.3 %collective-permute-start.6 = (f32[16,8,128]{2,1,0:T(8,128)S(1)}, f32[16,8,128]{2,1,0:T(8,128)S(1)}, u32[]{:S(2)}, u32[]{:S(2)}) collective-permute-start(f32[16,8,128]{2,1,0:T(8,128)S(1)} %get-tuple-element.56), channel_id=1, source_target_pairs={{0,1},{1,0},{2,3},{3,2},{4,5},{5,4},{6,7},{7,6},{8,9},{9,8},{10,11... | collective-permute-start | bytes 196616 | tf_op jit(solution)/shard_map/ppermute | solution.py:668
  13.4 6.5 %collective-permute-start.7 = (f32[16,8,128]{2,1,0:T(8,128)S(1)}, f32[16,8,128]{2,1,0:T(8,128)S(1)}, u32[]{:S(2)}, u32[]{:S(2)}) collective-permute-start(f32[16,8,128]{2,1,0:T(8,128)S(1)} %get-tuple-element.57), channel_id=1, source_target_pairs={{0,15},{1,2},{2,1},{3,4},{4,3},{5,6},{6,5},{7,8},{8,7},{9,10},{10,... | collective-permute-start | bytes 196616 | tf_op jit(solution)/shard_map/ppermute | solution.py:667
  25.5 15.1 %collective-permute-start.12 = (f32[23,8,128]{2,1,0:T(8,128)S(1)}, f32[23,8,128]{2,1,0:T(8,128)S(1)}, u32[]{:S(2)}, u32[]{:S(2)}) collective-permute-start(f32[23,8,128]{2,1,0:T(8,128)S(1)} %get-tuple-element.72), channel_id=1, source_target_pairs={{0,1},{1,0},{2,3},{3,2},{4,5},{5,4},{6,7},{7,6},{8,9},{9,8},{10,11... | collective-permute-start | bytes 282632 | tf_op jit(solution)/shard_map/ppermute | solution.py:721
  25.6 15.0 %collective-permute-start.13 = (f32[23,8,128]{2,1,0:T(8,128)S(1)}, f32[23,8,128]{2,1,0:T(8,128)S(1)}, u32[]{:S(2)}, u32[]{:S(2)}) collective-permute-start(f32[23,8,128]{2,1,0:T(8,128)S(1)} %get-tuple-element.73), channel_id=1, source_target_pairs={{1,2},{2,1},{3,4},{4,3},{5,6},{6,5},{7,8},{8,7},{9,10},{10,9},{11,... | collective-permute-start | bytes 282632 | tf_op jit(solution)/shard_map/ppermute | solution.py:720
  26.3 2.6 %collective-permute-start.8 = (f32[8,128]{1,0:T(8,128)S(1)}, f32[8,128]{1,0:T(8,128)S(1)}, u32[]{:S(2)}, u32[]{:S(2)}) collective-permute-start(f32[8,128]{1,0:T(8,128)S(1)} %get-tuple-element.66), channel_id=1, source_target_pairs={{0,1},{1,0},{2,3},{3,2},{4,5},{5,4},{6,7},{7,6},{8,9},{9,8},{10,11... | collective-permute-start | bytes 12296 | tf_op jit(solution)/shard_map/ppermute | solution.py:703
  28.9 3.6 %collective-permute-start.9 = (f32[8,128]{1,0:T(8,128)S(1)}, f32[8,128]{1,0:T(8,128)S(1)}, u32[]{:S(2)}, u32[]{:S(2)}) collective-permute-start(f32[8,128]{1,0:T(8,128)S(1)} %add.12), channel_id=1, source_target_pairs={{0,2},{1,3},{2,0},{3,1},{4,6},{5,7},{6,4},{7,5},{8,10},{9,11},{10,... | collective-permute-start | bytes 12296 | tf_op jit(solution)/shard_map/ppermute | solution.py:703
  32.5 3.6 %collective-permute-start.10 = (f32[8,128]{1,0:T(8,128)S(1)}, f32[8,128]{1,0:T(8,128)S(1)}, u32[]{:S(2)}, u32[]{:S(2)}) collective-permute-start(f32[8,128]{1,0:T(8,128)S(1)} %add.13), channel_id=1, source_target_pairs={{0,4},{1,5},{2,6},{3,7},{4,0},{5,1},{6,2},{7,3},{8,12},{9,13},{10,... | collective-permute-start | bytes 12296 | tf_op jit(solution)/shard_map/ppermute | solution.py:703
  36.1 4.5 %collective-permute-start.11 = (f32[8,128]{1,0:T(8,128)S(1)}, f32[8,128]{1,0:T(8,128)S(1)}, u32[]{:S(2)}, u32[]{:S(2)}) collective-permute-start(f32[8,128]{1,0:T(8,128)S(1)} %add.14), channel_id=1, source_target_pairs={{0,8},{1,9},{2,10},{3,11},{4,12},{5,13},{6,14},{7,15},{8,0},{9,1},... | collective-permute-start | bytes 12296 | tf_op jit(solution)/shard_map/ppermute | solution.py:703
where the time goes:
time: 43.3 us; the launch traced here: 43 us
  waiting for transfers between devices  15.2 us (35%)
  Pallas kernels  13.8 us (32%)
  starting transfers between devices  11.4 us (26%)
  between operations  1.35 us (3%)
  local copies, waits for them, and re-layouts  1.24 us (3%)
    pallas_call x5, Pallas kernels, call(): pl.pallas_call(kernel, out_shape=[shape for shape, _ in outs], in_specs=i...  13.8 us
    ppermute x4, waiting for transfers between devices, body(): drag = drag + lax.ppermute(drag, 'block', swap)  9.34 us
    ppermute x1, starting transfers between devices, body(): far = lax.ppermute(own_far, 'block', far_pairs)  5.67 us
    ppermute x1, waiting for transfers between devices, body(): from_far = lax.ppermute(to_far, 'block', far_pairs)  5.21 us
    ppermute x4, starting transfers between devices, body(): drag = drag + lax.ppermute(drag, 'block', swap)  3.77 us
  transfers between devices with their start and end apart: 10, of which 6 were waited for; matrix products, arithmetic and copies ran while one was open for 1% of the time, Pallas kernels for 11%

commit v1 on v0

v1 whole, which is shorter than its diff:
```python
import functools
import math

import jax
import jax.numpy as jnp
from jax import lax
from jax.experimental import pallas as pl
from jax.experimental.pallas import tpu as pltpu
from jax.sharding import PartitionSpec as P

BX = 4
STEPS = 3
HALO = STEPS
RAW = HALO - 1
MIB = 2**20

VELOCITY = (
    (0, 0, 0),
    (1, 0, 0),
    (-1, 0, 0),
    (0, 1, 0),
    (0, -1, 0),
    (0, 0, 1),
    (0, 0, -1),
    (1, 1, 0),
    (-1, -1, 0),
    (1, -1, 0),
    (-1, 1, 0),
    (1, 0, 1),
    (-1, 0, -1),
    (1, 0, -1),
    (-1, 0, 1),
    (0, 1, 1),
    (0, -1, -1),
    (0, 1, -1),
    (0, -1, 1),
)
OPP = (0,) + tuple(m + 1 if m % 2 else m - 1 for m in range(1, 19))
AHEAD = tuple(m for m in range(19) if VELOCITY[m][0] == 1)
BEHIND = tuple(m for m in range(19) if VELOCITY[m][0] == -1)
FORCE = 0.02
ROOT_45 = math.sqrt(4.5)
ROOT_2 = math.sqrt(2.0)


def rolled(field, step_y, step_z):
    if step_y:
        field = pltpu.roll(field, step_y % field.shape[0], 0)
    if step_z:
        field = pltpu.roll(field, step_z % field.shape[1], 1)
    return field


def pairs(values):
    plus = [values[2 * k + 1] + values[2 * k + 2] for k in range(9)]
    minus = [values[2 * k + 1] - values[2 * k + 2] for k in range(9)]
    return plus, minus


def first_moments(minus, scale):
    along_x, along_y, along_z = minus[:3]
    if scale != 1.0:
        along_x, along_y, along_z = scale * along_x, scale * along_y, scale * along_z
    along_x = along_x + ((minus[3] + minus[4]) + (minus[5] + minus[6]))
    along_y = along_y + ((minus[3] - minus[4]) + (minus[7] + minus[8]))
    along_z = along_z + ((minus[5] - minus[6]) + (minus[7] - minus[8]))
    return along_x, along_y, along_z


def density_velocity(state):
    plus, minus = pairs(state)
    axes = (plus[0] + plus[1]) + (plus[2] + state[0])
    diagonals = (plus[3] + plus[4]) + (plus[5] + plus[6]) + (plus[7] + plus[8])
    density = axes + diagonals
    inverse = 1.0 / density
    momentum = first_moments(minus, 1.0)
    return density, [part * inverse for part in momentum]


def collide(state, density, flow, open_rate):
    rate = ROOT_45 * open_rate
    x, y, z = (flow[0] + FORCE) * rate, flow[1] * rate, flow[2] * rate
    xx, yy, zz = x * x, y * y, z * z
    base = 1.0 - (xx + yy + zz) * (1.0 / 3.0)
    axis_weight = density * (1.2 / 18.0)
    axis_slope = density * (1.2 * ROOT_2 / 18.0)
    side_weight = density * (1.2 / 36.0)
    side_slope = density * (1.2 * ROOT_2 / 36.0)
    result = [density * 0.4 * base - 0.2 * state[0]]
    for k, along in enumerate((x, y, z, x + y, x - y, x + z, x - z, y + z, y - z)):
        if k < 3:
            even = axis_weight * (base + (xx, yy, zz)[k])
            odd = axis_slope * along
        else:
            even = side_weight * (base + along * along)
            odd = side_slope * along
        result.append((even + odd) - 0.2 * state[2 * k + 1])
        result.append((even - odd) - 0.2 * state[2 * k + 2])
    return result


def spread(level, slope):
    x, y, z = slope
    result = [level]
    for along in (x, y, z, x + y, x - y, x + z, x - z, y + z, y - z):
        result.append(level + along)
        result.append(level - along)
    return result


def pull(source, plane, word):
    here = [source[m, plane] for m in range(19)]
    result = [here[0]]
    for m in range(1, 19):
        step_x, step_y, step_z = VELOCITY[m]
        moved = here[m] if step_x == 0 else source[m, plane - step_x]
        moved = rolled(moved, step_y, step_z)
        result.append(jnp.where((word & (1 << m)) != 0, moved, here[OPP[m]]))
    return result


def link_word(behind, here, ahead):
    rows = lax.broadcasted_iota(jnp.int32, here.shape, 0)
    columns = lax.broadcasted_iota(jnp.int32, here.shape, 1)
    joined = behind + 2 * here + 4 * ahead
    word = jnp.zeros_like(here)
    for step_y in (-1, 0, 1):
        for step_z in (-1, 0, 1):
            if step_y and step_z:
                inner = {0: 1}
            else:
                inner = {1: 0, 0: 1, -1: 2}
            near = rolled(joined, step_y, step_z)
            if step_y == 1:
                near = jnp.where(rows == 0, 0, near)
            if step_y == -1:
                near = jnp.where(rows == here.shape[0] - 1, 0, near)
            if step_z == 1:
                near = jnp.where(columns == 0, 0, near)
            if step_z == -1:
                near = jnp.where(columns == here.shape[1] - 1, 0, near)
            for step_x, place in inner.items():
                if (step_x, step_y, step_z) == (0, 0, 0):
                    continue
                m = VELOCITY.index((step_x, step_y, step_z))
                word = word | ((near & (1 << place)) << (m - place))
    return jnp.where(here > 0, word, 0)


def each_plane(low, high, body):
    def two(index, carry):
        body(low + 2 * index)
        body(low + 2 * index + 1)
        return carry

    lax.fori_loop(0, (high - low) // 2, two, 0)
    if (high - low) % 2:
        body(high - 1)


def is_fluid_rate(mark):
    design = jnp.maximum(mark, 0.0)
    return (mark >= 0.0).astype(jnp.int32), (1.0 + 4.0 * design) / (1.6 + 3.4 * design)


def store(target, plane, values):
    for m, part in enumerate(values):
        target[m, plane] = part


def remember(history, step, plane, density, flow):
    history[4 * step, plane] = density
    for axis in range(3):
        history[4 * step + 1 + axis, plane] = flow[axis]


def drag_terms(flow, open_rate):
    return (flow[0] * flow[0] + flow[1] * flow[1] + flow[2] * flow[2]) / open_rate


def parity(axis="block"):
    return 1 - lax.rem(lax.axis_index(axis), 2)


def pick(flag, yes, no):
    return no + flag * (yes - no)


def edge_kernel(home, pops, design, mask, near, far, third, designs, masks, sems):
    up = parity()
    copies = []
    for side, (out, ahead) in enumerate(((near, up), (far, 1 - up))):
        first = ahead * (home - HALO)
        whole = ahead * (home - RAW)
        copies.append(
            [
                pltpu.make_async_copy(
                    pops.at[:, pl.ds(whole, RAW)], out.at[pl.ds(0, 19)], sems.at[4 * side]
                ),
                pltpu.make_async_copy(
                    pops.at[:, pl.ds(first + RAW * (1 - ahead), 1)], third.at[side], sems.at[4 * side + 1]
                ),
                pltpu.make_async_copy(
                    design.at[pl.ds(first, HALO)], designs.at[side], sems.at[4 * side + 2]
                ),
                pltpu.make_async_copy(mask.at[pl.ds(first, HALO)], masks.at[side], sems.at[4 * side + 3]),
            ]
        )
    for side in copies:
        for copy in side:
            copy.start()
    for side, (out, ahead) in enumerate(((near, up), (far, 1 - up))):
        for copy in copies[side][1:]:
            copy.wait()

        def mark(plane):
            return jnp.where(masks[side, plane] > 0, designs[side, plane], -1.0)

        for plane in range(RAW):
            out[19, plane] = mark(ahead + plane)
        last = mark(RAW * (1 - ahead))
        out[22, 1] = last
        _, open_rate = is_fluid_rate(last)
        state = [third[side, m, 0] for m in range(19)]
        density, flow = density_velocity(state)
        collided = collide(state, density, flow, open_rate)
        for slot in range(5):
            value = jnp.where(ahead > 0, collided[AHEAD[slot]], collided[BEHIND[slot]])
            out[20 + slot // 2, slot % 2] = value
    for side in copies:
        side[0].wait()


def count_kernel(home_blocks, owner, where):
    rank = lax.axis_index("block")

    def count(block, carry):
        below, own = carry
        holder = owner[block]
        return below + (holder < rank).astype(jnp.int32), own + (holder == rank).astype(jnp.int32)

    def stray(device, found):
        late = owner[home_blocks * device + 1] < device
        early = owner[home_blocks * device + home_blocks - 2] > device
        return found | late.astype(jnp.int32) | early.astype(jnp.int32)

    below, own = lax.fori_loop(0, owner.shape[0], count, (jnp.int32(0), jnp.int32(0)))
    where[0] = below - home_blocks * rank
    where[1] = own
    where[2] = lax.fori_loop(0, owner.shape[0] // home_blocks, stray, jnp.int32(0))


def interior_kernel(
    home,
    own_near,
    pops_far,
    design,
    mask,
    to_near,
    to_far,
    edges,
    history,
    final,
    opens,
    fluid,
    words,
    drag,
    marked,
    pops,
    designs,
    masks,
    even,
    odd,
    sems,
):
    del own_near
    up = parity()
    copies = [
        pltpu.make_async_copy(source, target, sems.at[place])
        for place, (source, target) in enumerate(((pops_far, pops), (design, designs), (mask, masks)))
    ]
    for copy in copies:
        copy.start()
    for copy in copies:
        copy.wait()

    def start(plane):
        mark = jnp.where(masks[plane] > 0, designs[plane], -1.0)
        marked[plane] = mark
        fluid[plane], open_rate = is_fluid_rate(mark)
        opens[plane] = open_rate
        state = [pops[m, plane] for m in range(19)]
        density, flow = density_velocity(state)
        remember(history, 0, plane, density, flow)
        store(even, plane, collide(state, density, flow, open_rate))

    def link(plane):
        words[plane] = link_word(fluid[plane - 1], fluid[plane], fluid[plane + 1])

    def advance(step, source, target, plane):
        state = pull(source, plane, words[plane])
        density, flow = density_velocity(state)
        remember(history, step, plane, density, flow)
        store(target, plane, collide(state, density, flow, opens[plane]))

    def finish(plane):
        state = pull(even, plane, words[plane])
        density, flow = density_velocity(state)
        remember(history, 3, plane, density, flow)
        here = fluid[plane] > 0
        for m in range(19):
            final[m, plane] = jnp.where(here, state[m], pops[m, plane])
        drag[...] += jnp.where(here, drag_terms(flow, opens[plane]), 0.0)

    def keep(step, source):
        for m in range(19):
            for side in range(2):
                edges[m, 4 * step + side] = source[m, step + side]
                edges[m, 4 * step + 2 + side] = source[m, home - 2 - step + side]

    def send(out, ahead, step, source):
        outer = ahead * (home - 1) + (1 - 2 * ahead) * RAW
        if step == 1:
            for slot in range(5):
                out[slot] = source[AHEAD[slot] + 1 - ahead, outer]
            return
        inner = ahead * (home - 1) + (1 - 2 * ahead) * HALO
        here = fluid[outer] > 0
        for slot in range(5):
            out[5 + slot] = source[AHEAD[slot] + 1 - ahead, inner]
        for m in range(19):
            out[10 + m] = jnp.where(here, source[m, outer], pops[m, outer])
        out[29] = marked[inner]

    drag[...] = jnp.zeros_like(drag)
    each_plane(0, home, start)
    keep(0, even)
    each_plane(1, home - 1, link)
    each_plane(1, home - 1, functools.partial(advance, 1, even, odd))
    keep(1, odd)
    each_plane(2, home - 2, functools.partial(advance, 2, odd, even))
    keep(2, even)
    for out, ahead in ((to_near, up), (to_far, 1 - up)):
        send(out, ahead, 1, odd)
        send(out, ahead, 2, even)
    each_plane(3, home - 3, finish)
    for m in range(19):
        for plane in range(STEPS):
            final[m, plane] = pops[m, plane]
            final[m, home - STEPS + plane] = pops[m, home - STEPS + plane]
        for out, ahead in ((to_near, up), (to_far, 1 - up)):
            out[30 + m] = final[m, STEPS + ahead * (home - 1 - 2 * STEPS)]


def boundary_kernel(
    home,
    near,
    far,
    edges,
    inner_history,
    inner_final,
    inner_opens,
    inner_fluid,
    inner_words,
    inner_drag,
    final,
    history,
    opens,
    fluid,
    words,
    drag,
    even,
    odd,
    sems,
):
    span = home + 2 * HALO
    up = parity()
    sides = ((up, near), (1 - up, far))
    copies = [
        pltpu.make_async_copy(
            inner_history.at[pl.ds(4 * step, 4), pl.ds(step, home - 2 * step)],
            history.at[pl.ds(4 * step, 4), pl.ds(HALO + step, home - 2 * step)],
            sems.at[step],
        )
        for step in range(4)
    ]
    copies.append(
        pltpu.make_async_copy(
            inner_final.at[:, pl.ds(STEPS, home - 2 * STEPS)],
            final.at[:, pl.ds(STEPS, home - 2 * STEPS)],
            sems.at[4],
        )
    )
    for copy in copies:
        copy.start()

    for plane in range(home):
        fluid[plane + HALO] = inner_fluid[plane]
        opens[plane + HALO] = inner_opens[plane]
    for plane in range(1, home - 1):
        words[plane + HALO] = inner_words[plane]
    for ahead, side in sides:
        fluid[ahead * (span - 1)], opens[ahead * (span - 1)] = is_fluid_rate(side[22, 1])
        for slot in range(5):
            even[AHEAD[slot] + ahead, ahead * (span - 1)] = side[20 + slot // 2, slot % 2]

    def start(plane, carry):
        for ahead, side in sides:
            index = plane + 1 + ahead * (home + RAW)
            fluid[index], open_rate = is_fluid_rate(side[19, plane])
            opens[index] = open_rate
            state = [side[m, plane] for m in range(19)]
            density, flow = density_velocity(state)
            store(even, index, collide(state, density, flow, open_rate))
        return carry

    lax.fori_loop(0, RAW, start, 0)

    def receive(step, target):
        for m in range(19):
            for side in range(2):
                target[m, HALO + step + side] = edges[m, 4 * step + side]
                target[m, HALO + home - 2 - step + side] = edges[m, 4 * step + 2 + side]

    def both(step, body):
        def two(place, carry):
            body(step + place, place, 0)
            body(span - 3 - step + place, place, 1)
            return carry

        lax.fori_loop(0, 3, two, 0)

    def link(index, place, ahead):
        words[index] = link_word(fluid[index - 1], fluid[index], fluid[index + 1])

    def advance(step, source, target, index, place, ahead):
        state = pull(source, index, words[index])
        density, flow = density_velocity(state)
        remember(history, step, index, density, flow)
        store(target, index, collide(state, density, flow, opens[index]))

    both(1, link)
    receive(0, even)
    both(1, functools.partial(advance, 1, even, odd))
    receive(1, odd)
    both(2, functools.partial(advance, 2, odd, even))
    receive(2, even)
    drag[...] = inner_drag[...]

    def finish(index, place, ahead):
        state = pull(even, index, words[index])
        density, flow = density_velocity(state)
        remember(history, 3, index, density, flow)
        here = fluid[index] > 0
        for m in range(19):
            final[m, index - HALO] = jnp.where(here, state[m], inner_final[m, index - HALO])
        drag[...] += jnp.where(here, drag_terms(flow, opens[index]), 0.0)

    both(3, finish)
    for copy in copies:
        copy.wait()


def backward_kernel(
    home,
    history,
    opens,
    fluid,
    words,
    even_state,
    odd_state,
    near,
    far,
    from_near,
    from_far,
    marked,
    summed,
    gradient,
    outer,
    to_near,
    to_far,
    even,
    odd,
    share,
    first,
    second,
    second_flow,
):
    del summed
    span = home + 2 * HALO
    up = parity()

    def recall(step, plane):
        return history[4 * step, plane], [history[4 * step + 1 + axis, plane] for axis in range(3)]

    def seed(plane, density, flow):
        damping = 1.0 / opens[plane]
        square = flow[0] * flow[0] + flow[1] * flow[1] + flow[2] * flow[2]
        share[plane] = -square * damping
        factor = 2.0 * damping / density
        slope = [part * factor for part in flow]
        values = spread(-square * factor, slope)
        for m in range(19):
            even[OPP[m], plane] = values[m]

    for ahead, raw, message in ((up, near, from_near), (1 - up, far, from_far)):
        one = first.at[ahead]
        for m in range(19):
            for place in range(HALO):
                one[m, place] = odd_state[m, ahead * (span - HALO) + place]
        for slot in range(5):
            one[AHEAD[slot] + ahead, ahead * RAW] = message[slot]
        index = 1 + ahead * (span - 3)
        state = pull(one, 1, words[index])
        density, flow = density_velocity(state)
        for place, part in enumerate([density] + flow):
            second_flow[ahead, place] = part
        two = second.at[ahead]
        store(two, 2, collide(state, density, flow, opens[index]))
        for m in range(19):
            for place in range(2):
                two[m, 3 - 3 * ahead + place] = even_state[m, 2 + ahead * (span - 6) + place]
            two[m, 1 + 2 * ahead] = message[10 + m]
        for slot in range(5):
            two[AHEAD[slot] + ahead, 4 * ahead] = message[5 + slot]
        beyond = (message[29] >= 0.0).astype(jnp.int32)
        within = fluid[1 + ahead * (span - 3)]
        edge_word = link_word(
            beyond + ahead * (within - beyond),
            fluid[ahead * (span - 1)],
            within + ahead * (beyond - within),
        )
        for place in range(HALO):
            spot = 1 + place
            index = place + ahead * (span - 3)
            word = words[index] if place == 1 else None
            if place == 0:
                word = edge_word + ahead * (words[index] - edge_word)
            if place == 2:
                word = words[index] + ahead * (edge_word - words[index])
            state = pull(two, spot, word)
            density, flow = density_velocity(state)
            seed(index, density, flow)
            here = fluid[index] > 0
            for m in range(19):
                if place == 1:
                    initial = raw[m, ahead]
                else:
                    kept = two[m, spot]
                    initial = jnp.where((ahead > 0) == (place == 2), kept, raw[m, place // 2])
                outer[ahead, m, spot - ahead] = jnp.where(here, state[m], initial)
        for m in range(19):
            outer[ahead, m, ahead * (BX - 1)] = message[30 + m]

    def seed_home(plane):
        seed(plane, *recall(STEPS, plane))

    each_plane(HALO, HALO + home, seed_home)

    def retreat(step, source, target, plane, recalled=None):
        mirrored = pull(source, plane, words[plane])
        adjoint = [mirrored[OPP[m]] for m in range(19)]
        density, flow = recalled or recall(step, plane)
        open_rate = opens[plane]
        force_flow = [flow[0] + FORCE, flow[1], flow[2]]
        x, y, z = [open_rate * part for part in force_flow]
        plus, minus = pairs(adjoint)
        mx, my, mz = [part * (1.0 / 12.0) for part in first_moments(minus, 2.0)]
        xy_plus, xz_plus, yz_plus = plus[3] + plus[4], plus[5] + plus[6], plus[7] + plus[8]
        axes = [2.0 * plus[k] for k in range(3)]
        whole = 12.0 * adjoint[0] + (axes[0] + axes[1] + axes[2]) + (xy_plus + xz_plus + yz_plus)
        third = whole * (1.0 / 3.0)
        xx = axes[0] + (xy_plus + xz_plus) - third
        yy = axes[1] + (xy_plus + yz_plus) - third
        zz = axes[2] + (xz_plus + yz_plus) - third
        xy, xz, yz = plus[3] - plus[4], plus[5] - plus[6], plus[7] - plus[8]
        hx = 0.25 * (xx * x + xy * y + xz * z)
        hy = 0.25 * (xy * x + yy * y + yz * z)
        hz = 0.25 * (xz * x + yz * y + zz * z)
        rate = 1.2 * open_rate
        slope = [rate * (mx + hx), rate * (my + hy), rate * (mz + hz)]
        pushed = slope[0] * force_flow[0] + slope[1] * force_flow[1] + slope[2] * force_flow[2]
        share[plane] += density * pushed
        if target is None:
            return
        level = whole * (1.2 / 36.0) + 1.2 * (
            x * (mx + 0.5 * hx) + y * (my + 0.5 * hy) + z * (mz + 0.5 * hz)
        )
        level = level - (slope[0] * flow[0] + slope[1] * flow[1] + slope[2] * flow[2])
        values = spread(level, slope)
        for m in range(19):
            target[OPP[m], plane] = values[m] - 0.2 * adjoint[m]

    for side in range(2):
        recalled = second_flow[side, 0], [second_flow[side, 1 + axis] for axis in range(3)]
        retreat(2, even, odd, 1 + side * (span - 3), recalled)
    each_plane(HALO - 1, HALO + home + 1, functools.partial(retreat, 2, even, odd))
    each_plane(HALO - 1, HALO + home + 1, functools.partial(retreat, 1, odd, even))
    each_plane(HALO, HALO + home, functools.partial(retreat, 0, even, None))

    for plane in range(home):
        design = marked[plane]
        slope = 3.0 / ((1.6 + 3.4 * design) * (1.0 + 4.0 * design))
        gradient[plane] = jnp.where(design >= 0.0, share[plane + HALO] * slope, 0.0)
    for out, ahead in ((to_near, up), (to_far, 1 - up)):
        for plane in range(BX):
            out[plane] = gradient[ahead * (home - BX) + plane]


def scaled(home, cells, where, drag, joined, out):
    factor = cells / jnp.sum(drag[...])
    reach = (joined.shape[0] - home) // 2
    for plane in range(out.shape[0]):
        spot = jnp.clip(where[0] * BX + reach + plane, 0, joined.shape[0] - 1)
        live = plane < where[1] * BX
        out[plane] = jnp.where(live, joined[spot] * factor, 0.0)


def near_gradient(home, cells, where, drag, gradient, from_near, from_far, out, joined):
    up = parity()
    for ahead, message in ((up, from_near), (1 - up, from_far)):
        joined[pl.ds(ahead * (BX + home), BX)] = message[...]
    joined[pl.ds(BX, home)] = gradient[...]
    scaled(home, cells, where, drag, joined, out)


def far_gradient(home, cells, where, drag, gradient, from_left, from_right, out, joined):
    joined[pl.ds(0, home)] = from_left[...]
    joined[pl.ds(home, home)] = gradient[...]
    joined[pl.ds(2 * home, home)] = from_right[...]
    scaled(home, cells, where, drag, joined, out)


def place_kernel(where, final, outer, out, zeros, sems):
    blocks = out.shape[1] // BX
    home_blocks = final.shape[1] // BX
    beyond = outer.shape[2] // BX
    zeros[...] = jnp.zeros_like(zeros)
    for slot in range(blocks):
        target = out.at[:, pl.ds(slot * BX, BX)]
        live = slot < where[1]
        block = jnp.clip(where[0] + slot, -beyond, home_blocks + beyond - 1)
        inside = (block >= 0) & (block < home_blocks)

        @pl.when(live & inside)
        def _():
            source = final.at[:, pl.ds(block * BX, BX)]
            pltpu.make_async_copy(source, target, sems.at[slot]).start()

        @pl.when(live & jnp.logical_not(inside))
        def _():
            after = (block >= 0).astype(jnp.int32)
            within = block + beyond - after * (home_blocks + beyond)
            source = outer.at[after, :, pl.ds(within * BX, BX)]
            pltpu.make_async_copy(source, target, sems.at[slot]).start()

        @pl.when(jnp.logical_not(live))
        def _():
            pltpu.make_async_copy(zeros, target, sems.at[slot]).start()

    for slot in range(blocks):
        pltpu.make_async_copy(zeros, out.at[:, pl.ds(slot * BX, BX)], sems.at[slot]).wait()


def body(populations, design, fluid_mask, owner_after):
    count = lax.axis_size("block")
    home, width_y, width_z = design.shape
    home_blocks = home // BX
    slots = home_blocks + 2
    span = home + 2 * HALO
    plane = (width_y, width_z)
    vmem = pl.BlockSpec(memory_space=pltpu.VMEM)
    hbm = pl.BlockSpec(memory_space=pltpu.HBM)
    anywhere = pl.BlockSpec(memory_space=pl.ANY)
    smem = pl.BlockSpec(memory_space=pltpu.SMEM)
    cells = float(count * home * width_y * width_z)
    near_pairs = [(i, i ^ 1) for i in range(count)]
    far_pairs = [(i, (i + 1 if i % 2 else i - 1) % count) for i in range(count)]
    inner_pairs = far_pairs[1:-1]

    def planes(*lead, dtype=jnp.float32):
        return jax.ShapeDtypeStruct(lead + plane, dtype)

    def scratch(*lead, dtype=jnp.float32):
        return pltpu.VMEM(lead + plane, dtype)

    def call(kernel, name, ins, outs, scratches, limit, moved, *operands):
        return pl.pallas_call(
            kernel,
            out_shape=[shape for shape, _ in outs],
            in_specs=ins,
            out_specs=[spec for _, spec in outs],
            scratch_shapes=scratches,
            compiler_params=pltpu.CompilerParams(vmem_limit_bytes=limit * MIB),
            cost_estimate=pl.CostEstimate(flops=20 * moved, bytes_accessed=moved, transcendentals=0),
            name=name,
        )(*operands)

    populations, design, fluid_mask = [
        pltpu.with_memory_space_constraint(part, pltpu.HBM)
        for part in (populations, design, fluid_mask)
    ]
    own_near, own_far = call(
        functools.partial(edge_kernel, home),
        "edge_planes",
        [hbm] * 3,
        [(planes(23, RAW), vmem)] * 2,
        [
            scratch(2, 19, 1),
            scratch(2, HALO),
            scratch(2, HALO, dtype=jnp.int32),
            pltpu.SemaphoreType.DMA((8,)),
        ],
        4,
        1_000_000,
        populations,
        design,
        fluid_mask,
    )
    far = lax.ppermute(own_far, "block", far_pairs)
    near = lax.ppermute(own_near, "block", near_pairs)

    inner_shapes = (
        planes(49),
        planes(49),
        planes(19, 12),
        planes(16, home),
        planes(19, home),
        planes(home),
        planes(home, dtype=jnp.int32),
        planes(home, dtype=jnp.int32),
        planes(),
        planes(home),
    )
    (
        to_near,
        to_far,
        edges,
        inner_history,
        inner_final,
        inner_opens,
        inner_fluid,
        inner_words,
        inner_drag,
        marked,
    ) = call(
        functools.partial(interior_kernel, home),
        "interior_steps",
        [anywhere] + [hbm] * 3,
        [(shape, vmem) for shape in inner_shapes],
        [scratch(19, home), scratch(home), scratch(home, dtype=jnp.int32)]
        + [scratch(19, home)] * 2
        + [pltpu.SemaphoreType.DMA((3,))],
        16,
        6_000_000,
        own_near,
        populations,
        design,
        fluid_mask,
    )
    from_far = lax.ppermute(to_far, "block", far_pairs)
    from_near = lax.ppermute(to_near, "block", near_pairs)

    (where,) = call(
        functools.partial(count_kernel, home_blocks),
        "slot_counts",
        [smem],
        [(jax.ShapeDtypeStruct((3,), jnp.int32), smem)],
        [],
        2,
        20_000_000,
        owner_after,
    )

    boundary_shapes = (
        planes(19, home),
        planes(16, span),
        planes(span),
        planes(span, dtype=jnp.int32),
        planes(span, dtype=jnp.int32),
        planes(),
        planes(19, span),
        planes(19, span),
    )
    final, history, opens, fluid, words, drag, even_state, odd_state = call(
        functools.partial(boundary_kernel, home),
        "boundary_steps",
        [vmem] * 3 + [anywhere] + [vmem] * 5,
        [(shape, vmem) for shape in boundary_shapes],
        [pltpu.SemaphoreType.DMA((5,))],
        20,
        8_000_000,
        near,
        far,
        edges,
        inner_history,
        inner_final,
        inner_opens,
        inner_fluid,
        inner_words,
        inner_drag,
    )

    sums = [drag]
    distance = 1
    while distance < count:
        swap = [(i, i ^ distance) for i in range(count)]
        sums.append(sums[-1] + lax.ppermute(sums[-1], "block", swap))
        distance *= 2
    drag = sums[-1]

    gradient, outer, to_near, to_far = call(
        functools.partial(backward_kernel, home),
        "backward_steps",
        [vmem] * 11 + [anywhere],
        [(planes(home), vmem), (planes(2, 19, BX), vmem), (planes(BX), vmem), (planes(BX), vmem)],
        [
            scratch(19, span),
            scratch(19, span),
            scratch(span),
            scratch(2, 19, HALO),
            scratch(2, 19, HALO + 2),
            scratch(2, 4),
        ],
        20,
        8_000_000,
        history,
        opens,
        fluid,
        words,
        even_state,
        odd_state,
        near,
        far,
        from_near,
        from_far,
        marked,
        sums[1],
    )
    from_far = lax.ppermute(to_far, "block", inner_pairs)
    from_near = lax.ppermute(to_near, "block", near_pairs)

    ring = [(i, i + 1) for i in range(count - 1)]
    back = [(i + 1, i) for i in range(count - 1)]

    def place(outer):
        (out,) = call(
            place_kernel,
            "place_populations",
            [smem, anywhere, anywhere],
            [(planes(19, slots * BX), anywhere)],
            [scratch(19, BX), pltpu.SemaphoreType.DMA((slots,))],
            8,
            4_000_000,
            where,
            final,
            outer,
        )
        return out

    def place_far(_):
        wide = [lax.ppermute(final, "block", route) for route in (ring, back)]
        return place(jnp.stack(wide))

    def slope(kernel, name, reach, *messages):
        (out,) = call(
            functools.partial(kernel, home, cells),
            name,
            [smem] + [vmem] * 4,
            [(planes(slots * BX), vmem)],
            [scratch(home + 2 * reach)],
            4,
            1_000_000,
            where,
            drag,
            gradient,
            *messages,
        )
        return out

    def slope_near(*messages):
        return slope(near_gradient, "near_gradient", BX, *messages)

    def slope_far(*_):
        wide = [lax.ppermute(gradient, "block", route) for route in (ring, back)]
        return slope(far_gradient, "far_gradient", home, *wide)

    is_far = where[2] > 0
    populations_after = lax.cond(is_far, place_far, place, outer)
    sensitivity = lax.cond(is_far, slope_far, slope_near, from_near, from_far)
    return (populations_after, sensitivity)


def solution(mesh):
    placed = (
        P(None, ("group", "block"), None, None),
        P(("group", "block"), None, None),
        P(("group", "block"), None, None),
        P("group"),
    )
    return jax.shard_map(
        body,
        mesh=mesh,
        in_specs=placed,
        out_specs=(P(None, ("group", "block"), None, None), P(("group", "block"), None, None)),
        check_vma=False,
    )
```

time: 43.3 us -> 34.5 us (0.80)
  waiting for transfers between devices: 15.2 us -> 4 us
  starting transfers between devices: 11.4 us -> 14.3 us
  Pallas kernels: 13.8 us -> 13.3 us
    ppermute x4, waiting for transfers between devices: 9.34 us -> 3.98 us  [body(): sums.append(sums[-1] + lax.ppermute(sums[-1], 'block', swap))]
    ppermute x1, waiting for transfers between devices: 5.21 us -> 0.01 us  [body(): from_far = lax.ppermute(to_far, 'block', far_pairs)]
    ppermute x4, starting transfers between devices: 3.77 us -> 6.62 us  [body(): sums.append(sums[-1] + lax.ppermute(sums[-1], 'block', swap))]
    ppermute x2, waiting for transfers between devices: 0.64 us -> 0.01 us  [body(): from_near = lax.ppermute(to_near, 'block', near_pairs)]
    pallas_call x5 -> x7, Pallas kernels: 13.8 us -> 13.3 us  [call(): pl.pallas_call(kernel, out_shape=[shape for shape, _ in outs], in_specs=i...]
  transfers between devices with their start and end apart: 10 -> 10, of which waited for: 6 -> 2; matrix products, arithmetic and copies ran while one was open for 1% -> 2% of each run, Pallas kernels for 11% -> 33%
where the time goes in v1:
time: 34.5 us; the launch traced here: 34.3 us
  starting transfers between devices  14.3 us (41%)
  Pallas kernels  13.3 us (39%)
  waiting for transfers between devices  4 us (12%)
  between operations  1.44 us (4%)
  local copies, waits for them, and re-layouts  1.22 us (4%)
    pallas_call x7, Pallas kernels, call(): pl.pallas_call(kernel, out_shape=[shape for shape, _ in outs], in_specs=i...  13.3 us
    ppermute x4, starting transfers between devices, body(): sums.append(sums[-1] + lax.ppermute(sums[-1], 'block', swap))  6.62 us
    ppermute x1, starting transfers between devices, body(): far = lax.ppermute(own_far, 'block', far_pairs)  5.67 us
    ppermute x4, waiting for transfers between devices, body(): sums.append(sums[-1] + lax.ppermute(sums[-1], 'block', swap))  3.98 us
  transfers between devices with their start and end apart: 10, of which 2 were waited for; matrix products, arithmetic and copies ran while one was open for 2% of the time, Pallas kernels for 33%

profile of v1, /device:TPU:0, one launch (start us, length us, event | category | flops | bytes accessed | tf_op | source)
XLA Modules:
  0.0 34.3 jit_solution(14113959892447470979)
XLA Ops:
  0.6 1.2 %edge_planes.1 = (f32[23,2,8,128]{3,2,1,0:T(8,128)S(1)}, f32[23,2,8,128]{3,2,1,0:T(8,128)S(1)}) custom-call(f32[19,12,8,128]{3,2,1,0:T(8,128)} %pops_far.1, f32[12,8,128]{2,1,0:T(8,128)} %design.3, s32[12,8,128]{2,1,0:T(8,128)} %mask.3), custom_call_target="tpu_custom_call" | custom-call | flops 20000000 | bytes 1000000 | tf_op jit(solution)/shard_map/edge_planes/pallas_call | solution.py:688
  1.9 0.5 %collective-permute-start.4 = (f32[23,2,8,128]{3,2,1,0:T(8,128)S(1)}, f32[23,2,8,128]{3,2,1,0:T(8,128)S(1)}, u32[]{:S(2)}, u32[]{:S(2)}) collective-permute-start(f32[23,2,8,128]{3,2,1,0:T(8,128)S(1)} %get-tuple-element.71.own_near), channel_id=1, source_target_pairs={{0,1},{1,0},{2,3},{3,2},{4,5},{5,4},{6,7},{7,6},{8,9},{9,8},{10,11... | collective-permute-start | bytes 565256 | tf_op jit(solution)/shard_map/ppermute | solution.py:721
  2.4 5.7 %collective-permute-start.5 = (f32[23,2,8,128]{3,2,1,0:T(8,128)S(1)}, f32[23,2,8,128]{3,2,1,0:T(8,128)S(1)}, u32[]{:S(2)}, u32[]{:S(2)}) collective-permute-start(f32[23,2,8,128]{3,2,1,0:T(8,128)S(1)} %get-tuple-element.72), channel_id=1, source_target_pairs={{0,15},{1,2},{2,1},{3,4},{4,3},{5,6},{6,5},{7,8},{8,7},{9,10},{10,... | collective-permute-start | bytes 565256 | tf_op jit(solution)/shard_map/ppermute | solution.py:720
  8.1 3.8 %interior_steps.1 = (f32[49,8,128]{2,1,0:T(8,128)S(1)}, f32[49,8,128]{2,1,0:T(8,128)S(1)}, f32[19,12,8,128]{3,2,1,0:T(8,128)S(1)}, f32[16,12,8,128]{3,2,1,0:T(8,...) custom-call(f32[23,2,8,128]{3,2,1,0:T(8,128)S(1)} %get-tuple-element, ...), custom_call_target="tpu_custom_call" | custom-call | flops 120000000 | bytes 6000000 | tf_op jit(solution)/shard_map/interior_steps/pallas_call | solution.py:688
  11.8 0.1 collective-permute-start.6
  11.9 0.6 %collective-permute-start.7 = (f32[49,8,128]{2,1,0:T(8,128)S(1)}, f32[49,8,128]{2,1,0:T(8,128)S(1)}, u32[]{:S(2)}, u32[]{:S(2)}) collective-permute-start(f32[49,8,128]{2,1,0:T(8,128)S(1)} %get-tuple-element.88), channel_id=1, source_target_pairs={{0,15},{1,2},{2,1},{3,4},{4,3},{5,6},{6,5},{7,8},{8,7},{9,10},{10,... | collective-permute-start | bytes 602120 | tf_op jit(solution)/shard_map/ppermute | solution.py:761
  12.5 0.0 collective-permute-done.4.near
  12.5 0.0 collective-permute-done.5.far
  12.5 1.9 %boundary_steps.1 = (f32[19,12,8,128]{3,2,1,0:T(8,128)S(1)}, f32[16,18,8,128]{3,2,1,0:T(8,128)S(1)}, f32[18,8,128]{2,1,0:T(8,128)S(1)}, s32[18,8,128]{2,1,0:T(8,...) custom-call(f32[23,2,8,128]{3,2,1,0:T(8,128)S(1)} %collective-permut, ...), custom_call_target="tpu_custom_call" | custom-call | flops 160000000 | bytes 8000000 | tf_op jit(solution)/shard_map/boundary_steps/pallas_call | solution.py:688
  14.4 0.1 collective-permute-start.8
  14.5 1.2 %collective-permute-done.8 = f32[8,128]{1,0:T(8,128)S(1)} collective-permute-done((f32[8,128]{1,0:T(8,128)S(1)}, f32[8,128]{1,0:T(8,128)S(1)}, u32[]{:S(2)}, u32[]{:S(2)}) %collective-permute-start.8) | collective-permute-done | bytes 4128 | tf_op jit(solution)/shard_map/ppermute | solution.py:808
  15.6 1.5 %collective-permute-start.9 = (f32[8,128]{1,0:T(8,128)S(1)}, f32[8,128]{1,0:T(8,128)S(1)}, u32[]{:S(2)}, u32[]{:S(2)}) collective-permute-start(f32[8,128]{1,0:T(8,128)S(1)} %add.12.summed), channel_id=1, source_target_pairs={{0,2},{1,3},{2,0},{3,1},{4,6},{5,7},{6,4},{7,5},{8,10},{9,11},{10,... | collective-permute-start | bytes 12296 | tf_op jit(solution)/shard_map/ppermute | solution.py:808
  17.1 2.8 %collective-permute-done.9 = f32[8,128]{1,0:T(8,128)S(1)} collective-permute-done((f32[8,128]{1,0:T(8,128)S(1)}, f32[8,128]{1,0:T(8,128)S(1)}, u32[]{:S(2)}, u32[]{:S(2)}) %collective-permute-start.9) | collective-permute-done | bytes 4128 | tf_op jit(solution)/shard_map/ppermute | solution.py:808
  20.0 0.0 collective-permute-start.10
  20.0 0.0 collective-permute-done.6.from_near
  20.0 0.0 collective-permute-done.7.from_far
  20.0 0.0 copy-start
  20.0 3.2 %backward_steps.1 = (f32[12,8,128]{2,1,0:T(8,128)S(1)}, f32[2,19,4,8,128]{4,3,2,1,0:T(8,128)S(1)}, f32[4,8,128]{2,1,0:T(8,128)S(1)}, f32[4,8,128]{2,1,0:T(8,128)S(1)}) custom-call(f32[16,18,8,128]{3,2,1,0:T(8,128)S(1)} %get-tuple-element.81.history, f32[18,8,128]{2,1,0:T(8,128)S(1)} %get-tuple-element.82.opens, s32[18,8,128]{2,1,0:T(8,128)S(1)} %get-tuple-element.83.fluid, ...), custom_call_target="tpu_custom_call" | custom-call | flops 160000000 | bytes 8000000 | tf_op jit(solution)/shard_map/backward_steps/pallas_call | solution.py:688
  23.2 0.1 collective-permute-start.12
  23.4 0.7 %collective-permute-start.13 = (f32[4,8,128]{2,1,0:T(8,128)S(1)}, f32[4,8,128]{2,1,0:T(8,128)S(1)}, u32[]{:S(2)}, u32[]{:S(2)}) collective-permute-start(f32[4,8,128]{2,1,0:T(8,128)S(1)} %get-tuple-element.94), channel_id=1, source_target_pairs={{1,2},{2,1},{3,4},{4,3},{5,6},{6,5},{7,8},{8,7},{9,10},{10,9},{11,... | collective-permute-start | bytes 49160 | tf_op jit(solution)/shard_map/ppermute | solution.py:840
  24.1 5.0 %collective-permute-start.11 = (f32[8,128]{1,0:T(8,128)S(1)}, f32[8,128]{1,0:T(8,128)S(1)}, u32[]{:S(2)}, u32[]{:S(2)}) collective-permute-start(f32[8,128]{1,0:T(8,128)S(1)} %add.14), channel_id=1, source_target_pairs={{0,8},{1,9},{2,10},{3,11},{4,12},{5,13},{6,14},{7,15},{8,0},{9,1},... | collective-permute-start | bytes 12296 | tf_op jit(solution)/shard_map/ppermute | solution.py:808
  29.1 1.7 %slot_counts.1 = s32[3]{0:T(128)S(1)} custom-call(s32[48]{0:T(128)S(1)} %copy-done), custom_call_target="tpu_custom_call" | custom-call | flops 400000000 | bytes 20000000 | tf_op jit(solution)/shard_map/slot_counts/pallas_call | solution.py:688
  30.8 0.6 %slice.3 = s32[1]{0:T(128)} slice(s32[3]{0:T(128)S(1)} %slot_counts.1), slice={[2:3]} | slice | bytes 8 | tf_op jit(solution)/shard_map/slice | solution.py:888
  32.0 0.8 %conditional.2 = (f32[19,20,8,128]{3,2,1,0:T(8,128)S(1)}) conditional(s32[]{:T(128)} %bitcast.2, (s32[3]{0:T(128)S(1)}, f32[19,12,8,128]{3,2,1,0:T(8,128)S(1)}, f32[2,19,4,8,128]{4,3,2,1,0:T(8,128)S(1)}) %tuple.20, (f32[19,12,8,128]{3,2,1,0:T(8,128)S(1)}, s32[3]{0:T(128)S(1)}) %tuple.21), branch_computations={%region_0.0_spmd, %region_1.0_spmd} | conditional | flops 80466944 | bytes 15206744 | solution.py:889
  32.0 0.8 %place_populations.2 = f32[19,20,8,128]{3,2,1,0:T(8,128)S(1)} custom-call(s32[3]{0:T(128)S(1)} %get-tuple-element.28.where, f32[19,12,8,128]{3,2,1,0:T(8,128)S(1)} %get-tuple-element.29.final, f32[2,19,4,8,128]{4,3,2,1,0:T(8,128)S(1)} %get-tuple-element.34.outer), custom_call_target="tpu_custom_call" | custom-call | flops 80000000 | bytes 4000000 | tf_op jit(solution)/shard_map/cond/branch_0_fun/place_populations/pallas_call | solution.py:688
  32.9 0.0 copy-start.1
  32.9 0.0 collective-permute-done.12
  32.9 0.7 %conditional.3 = (f32[20,8,128]{2,1,0:T(8,128)S(1)}) conditional(s32[]{:T(128)} %bitcast.2, (s32[3]{0:T(128)S(1)}, f32[8,128]{1,0:T(8,128)S(1)}, f32[12,8,128]{2,1,0:T(8,128)S(1)}, f32[4,8,128]{2,1,0:T(8,128)S(1)}, f32[4,8,128]{2,1,0:T(8,128)S(1)}) %tuple.22, (f32[12,8,128]{2,1,0:T(8,128)S(1)}, s32[3]{0:T(128)S(1)}, f32[8,128]{1,0:T(8,128)S(1)}) %tuple.23), branch_computations={%region_2.0_spmd, %region_3.0_spmd} | conditional | flops 20000000 | bytes 1393304 | solution.py:890
  32.9 0.7 %near_gradient.1 = f32[20,8,128]{2,1,0:T(8,128)S(1)} custom-call(s32[3]{0:T(128)S(1)} %get-tuple-element.37.where, f32[8,128]{1,0:T(8,128)S(1)} %get-tuple-element.38.drag, f32[12,8,128]{2,1,0:T(8,128)S(1)} %get-tuple-element.39.gradient, f32[4,8,128]{2,1,0:T(8,128)S(1)} %get-tuple-element.40.from_near, f32[4,8,128]{2,1,0:T(8,128)S(1)} %get-tuple-element.41.from_far), custom_call_target="tpu_custom_call" | custom-call | flops 20000000 | bytes 1000000 | tf_op jit(solution)/shard_map/cond/branch_0_fun/near_gradient/pallas_call | solution.py:688
  33.7 0.0 copy-start.2
  33.7 0.3 copy-done.1
  34.0 0.3 copy-done.2
  (8 shorter events, 0.0 us)
Async XLA Ops:
  1.9 10.7 %collective-permute-start.4 = (f32[23,2,8,128]{3,2,1,0:T(8,128)S(1)}, f32[23,2,8,128]{3,2,1,0:T(8,128)S(1)}, u32[]{:S(2)}, u32[]{:S(2)}) collective-permute-start(f32[23,2,8,128]{3,2,1,0:T(8,128)S(1)} %get-tuple-element.71.own_near), channel_id=1, source_target_pairs={{0,1},{1,0},{2,3},{3,2},{4,5},{5,4},{6,7},{7,6},{8,9},{9,8},{10,11... | collective-permute-start | bytes 565256 | tf_op jit(solution)/shard_map/ppermute | solution.py:721
  2.4 10.1 %collective-permute-start.5 = (f32[23,2,8,128]{3,2,1,0:T(8,128)S(1)}, f32[23,2,8,128]{3,2,1,0:T(8,128)S(1)}, u32[]{:S(2)}, u32[]{:S(2)}) collective-permute-start(f32[23,2,8,128]{3,2,1,0:T(8,128)S(1)} %get-tuple-element.72), channel_id=1, source_target_pairs={{0,15},{1,2},{2,1},{3,4},{4,3},{5,6},{6,5},{7,8},{8,7},{9,10},{10,... | collective-permute-start | bytes 565256 | tf_op jit(solution)/shard_map/ppermute | solution.py:720
  11.8 8.1 %collective-permute-start.6 = (f32[49,8,128]{2,1,0:T(8,128)S(1)}, f32[49,8,128]{2,1,0:T(8,128)S(1)}, u32[]{:S(2)}, u32[]{:S(2)}) collective-permute-start(f32[49,8,128]{2,1,0:T(8,128)S(1)} %get-tuple-element.87), channel_id=1, source_target_pairs={{0,1},{1,0},{2,3},{3,2},{4,5},{5,4},{6,7},{7,6},{8,9},{9,8},{10,11... | collective-permute-start | bytes 602120 | tf_op jit(solution)/shard_map/ppermute | solution.py:762
  11.9 8.1 %collective-permute-start.7 = (f32[49,8,128]{2,1,0:T(8,128)S(1)}, f32[49,8,128]{2,1,0:T(8,128)S(1)}, u32[]{:S(2)}, u32[]{:S(2)}) collective-permute-start(f32[49,8,128]{2,1,0:T(8,128)S(1)} %get-tuple-element.88), channel_id=1, source_target_pairs={{0,15},{1,2},{2,1},{3,4},{4,3},{5,6},{6,5},{7,8},{8,7},{9,10},{10,... | collective-permute-start | bytes 602120 | tf_op jit(solution)/shard_map/ppermute | solution.py:761
  14.4 1.2 %collective-permute-start.8 = (f32[8,128]{1,0:T(8,128)S(1)}, f32[8,128]{1,0:T(8,128)S(1)}, u32[]{:S(2)}, u32[]{:S(2)}) collective-permute-start(f32[8,128]{1,0:T(8,128)S(1)} %get-tuple-element.90), channel_id=1, source_target_pairs={{0,1},{1,0},{2,3},{3,2},{4,5},{5,4},{6,7},{7,6},{8,9},{9,8},{10,11... | collective-permute-start | bytes 12296 | tf_op jit(solution)/shard_map/ppermute | solution.py:808
  15.6 4.3 %collective-permute-start.9 = (f32[8,128]{1,0:T(8,128)S(1)}, f32[8,128]{1,0:T(8,128)S(1)}, u32[]{:S(2)}, u32[]{:S(2)}) collective-permute-start(f32[8,128]{1,0:T(8,128)S(1)} %add.12.summed), channel_id=1, source_target_pairs={{0,2},{1,3},{2,0},{3,1},{4,6},{5,7},{6,4},{7,5},{8,10},{9,11},{10,... | collective-permute-start | bytes 12296 | tf_op jit(solution)/shard_map/ppermute | solution.py:808
  20.0 4.1 %collective-permute-start.10 = (f32[8,128]{1,0:T(8,128)S(1)}, f32[8,128]{1,0:T(8,128)S(1)}, u32[]{:S(2)}, u32[]{:S(2)}) collective-permute-start(f32[8,128]{1,0:T(8,128)S(1)} %add.13), channel_id=1, source_target_pairs={{0,4},{1,5},{2,6},{3,7},{4,0},{5,1},{6,2},{7,3},{8,12},{9,13},{10,... | collective-permute-start | bytes 12296 | tf_op jit(solution)/shard_map/ppermute | solution.py:808
  20.0 9.1 %copy-start = (s32[48]{0:T(128)S(1)}, s32[48]{0:T(128)}, u32[]{:S(2)}) copy-start(s32[48]{0:T(128)} %owner.1) | copy-start | bytes 580
  23.2 9.7 %collective-permute-start.12 = (f32[4,8,128]{2,1,0:T(8,128)S(1)}, f32[4,8,128]{2,1,0:T(8,128)S(1)}, u32[]{:S(2)}, u32[]{:S(2)}) collective-permute-start(f32[4,8,128]{2,1,0:T(8,128)S(1)} %get-tuple-element.93), channel_id=1, source_target_pairs={{0,1},{1,0},{2,3},{3,2},{4,5},{5,4},{6,7},{7,6},{8,9},{9,8},{10,11... | collective-permute-start | bytes 49160 | tf_op jit(solution)/shard_map/ppermute | solution.py:841
  23.4 9.5 %collective-permute-start.13 = (f32[4,8,128]{2,1,0:T(8,128)S(1)}, f32[4,8,128]{2,1,0:T(8,128)S(1)}, u32[]{:S(2)}, u32[]{:S(2)}) collective-permute-start(f32[4,8,128]{2,1,0:T(8,128)S(1)} %get-tuple-element.94), channel_id=1, source_target_pairs={{1,2},{2,1},{3,4},{4,3},{5,6},{6,5},{7,8},{8,7},{9,10},{10,9},{11,... | collective-permute-start | bytes 49160 | tf_op jit(solution)/shard_map/ppermute | solution.py:840
  24.1 8.8 %collective-permute-start.11 = (f32[8,128]{1,0:T(8,128)S(1)}, f32[8,128]{1,0:T(8,128)S(1)}, u32[]{:S(2)}, u32[]{:S(2)}) collective-permute-start(f32[8,128]{1,0:T(8,128)S(1)} %add.14), channel_id=1, source_target_pairs={{0,8},{1,9},{2,10},{3,11},{4,12},{5,13},{6,14},{7,15},{8,0},{9,1},... | collective-permute-start | bytes 12296 | tf_op jit(solution)/shard_map/ppermute | solution.py:808
  32.9 1.1 %copy-start.1 = (f32[19,20,8,128]{3,2,1,0:T(8,128)}, f32[19,20,8,128]{3,2,1,0:T(8,128)S(1)}, u32[]{:S(2)}) copy-start(f32[19,20,8,128]{3,2,1,0:T(8,128)S(1)} %get-tuple-element.95) | copy-start | bytes 4669444
  33.7 0.6 %copy-start.2 = (f32[20,8,128]{2,1,0:T(8,128)}, f32[20,8,128]{2,1,0:T(8,128)S(1)}, u32[]{:S(2)}) copy-start(f32[20,8,128]{2,1,0:T(8,128)S(1)} %get-tuple-element.96) | copy-start | bytes 245764

commit v2 on v1

--- a/solution.py
+++ b/solution.py
@@ -186,76 +186,59 @@
     return no + flag * (yes - no)
 
 
-def edge_kernel(home, pops, design, mask, near, far, third, designs, masks, sems):
+def edge_kernel(home, pops_far, design, mask, near, far, pops, marked, designs, masks, sems):
     up = parity()
-    copies = []
-    for side, (out, ahead) in enumerate(((near, up), (far, 1 - up))):
-        first = ahead * (home - HALO)
-        whole = ahead * (home - RAW)
-        copies.append(
-            [
-                pltpu.make_async_copy(
-                    pops.at[:, pl.ds(whole, RAW)], out.at[pl.ds(0, 19)], sems.at[4 * side]
-                ),
-                pltpu.make_async_copy(
-                    pops.at[:, pl.ds(first + RAW * (1 - ahead), 1)], third.at[side], sems.at[4 * side + 1]
-                ),
-                pltpu.make_async_copy(
-                    design.at[pl.ds(first, HALO)], designs.at[side], sems.at[4 * side + 2]
-                ),
-                pltpu.make_async_copy(mask.at[pl.ds(first, HALO)], masks.at[side], sems.at[4 * side + 3]),
-            ]
-        )
-    for side in copies:
-        for copy in side:
-            copy.start()
-    for side, (out, ahead) in enumerate(((near, up), (far, 1 - up))):
-        for copy in copies[side][1:]:
-            copy.wait()
-
-        def mark(plane):
-            return jnp.where(masks[side, plane] > 0, designs[side, plane], -1.0)
-
+    copies = [
+        pltpu.make_async_copy(source, target, sems.at[place])
+        for place, (source, target) in enumerate(((pops_far, pops), (design, designs), (mask, masks)))
+    ]
+    for copy in copies:
+        copy.start()
+    for copy in copies[1:]:
+        copy.wait()
+    for plane in range(home):
+        marked[plane] = jnp.where(masks[plane] > 0, designs[plane], -1.0)
+    copies[0].wait()
+    for out, ahead in ((near, up), (far, 1 - up)):
+        first = ahead * (home - RAW)
         for plane in range(RAW):
-            out[19, plane] = mark(ahead + plane)
-        last = mark(RAW * (1 - ahead))
+            for m in range(19):
+                out[m, plane] = pops[m, first + plane]
+            out[19, plane] = marked[first + plane]
+        third = ahead * (home - 1) + (1 - 2 * ahead) * RAW
+        last = marked[third]
         out[22, 1] = last
         _, open_rate = is_fluid_rate(last)
-        state = [third[side, m, 0] for m in range(19)]
+        state = [pops[m, third] for m in range(19)]
         density, flow = density_velocity(state)
         collided = collide(state, density, flow, open_rate)
         for slot in range(5):
             value = jnp.where(ahead > 0, collided[AHEAD[slot]], collided[BEHIND[slot]])
             out[20 + slot // 2, slot % 2] = value
-    for side in copies:
-        side[0].wait()
 
 
 def count_kernel(home_blocks, owner, where):
     rank = lax.axis_index("block")
-
-    def count(block, carry):
-        below, own = carry
+    below = jnp.int32(0)
+    own = jnp.int32(0)
+    for block in range(owner.shape[0]):
         holder = owner[block]
-        return below + (holder < rank).astype(jnp.int32), own + (holder == rank).astype(jnp.int32)
-
-    def stray(device, found):
+        below += (holder < rank).astype(jnp.int32)
+        own += (holder == rank).astype(jnp.int32)
+    stray = jnp.int32(0)
+    for device in range(owner.shape[0] // home_blocks):
         late = owner[home_blocks * device + 1] < device
         early = owner[home_blocks * device + home_blocks - 2] > device
-        return found | late.astype(jnp.int32) | early.astype(jnp.int32)
-
-    below, own = lax.fori_loop(0, owner.shape[0], count, (jnp.int32(0), jnp.int32(0)))
+        stray = stray | late.astype(jnp.int32) | early.astype(jnp.int32)
     where[0] = below - home_blocks * rank
     where[1] = own
-    where[2] = lax.fori_loop(0, owner.shape[0] // home_blocks, stray, jnp.int32(0))
+    where[2] = stray
 
 
 def interior_kernel(
     home,
-    own_near,
-    pops_far,
-    design,
-    mask,
+    pops,
+    marked,
     to_near,
     to_far,
     edges,
@@ -265,29 +248,13 @@
     fluid,
     words,
     drag,
-    marked,
-    pops,
-    designs,
-    masks,
     even,
     odd,
-    sems,
 ):
-    del own_near
     up = parity()
-    copies = [
-        pltpu.make_async_copy(source, target, sems.at[place])
-        for place, (source, target) in enumerate(((pops_far, pops), (design, designs), (mask, masks)))
-    ]
-    for copy in copies:
-        copy.start()
-    for copy in copies:
-        copy.wait()
 
     def start(plane):
-        mark = jnp.where(masks[plane] > 0, designs[plane], -1.0)
-        marked[plane] = mark
-        fluid[plane], open_rate = is_fluid_rate(mark)
+        fluid[plane], open_rate = is_fluid_rate(marked[plane])
         opens[plane] = open_rate
         state = [pops[m, plane] for m in range(19)]
         density, flow = density_velocity(state)
@@ -461,7 +428,45 @@
         copy.wait()
 
 
-def backward_kernel(
+def recall(history, step, plane):
+    return history[4 * step, plane], [history[4 * step + 1 + axis, plane] for axis in range(3)]
+
+
+def retreat(opens, words, share, source, target, plane, density, flow):
+    mirrored = pull(source, plane, words[plane])
+    adjoint = [mirrored[OPP[m]] for m in range(19)]
+    open_rate = opens[plane]
+    force_flow = [flow[0] + FORCE, flow[1], flow[2]]
+    x, y, z = [open_rate * part for part in force_flow]
+    plus, minus = pairs(adjoint)
+    mx, my, mz = [part * (1.0 / 12.0) for part in first_moments(minus, 2.0)]
+    xy_plus, xz_plus, yz_plus = plus[3] + plus[4], plus[5] + plus[6], plus[7] + plus[8]
+    axes = [2.0 * plus[k] for k in range(3)]
+    whole = 12.0 * adjoint[0] + (axes[0] + axes[1] + axes[2]) + (xy_plus + xz_plus + yz_plus)
+    third = whole * (1.0 / 3.0)
+    xx = axes[0] + (xy_plus + xz_plus) - third
+    yy = axes[1] + (xy_plus + yz_plus) - third
+    zz = axes[2] + (xz_plus + yz_plus) - third
+    xy, xz, yz = plus[3] - plus[4], plus[5] - plus[6], plus[7] - plus[8]
+    hx = 0.25 * (xx * x + xy * y + xz * z)
+    hy = 0.25 * (xy * x + yy * y + yz * z)
+    hz = 0.25 * (xz * x + yz * y + zz * z)
+    rate = 1.2 * open_rate
+    slope = [rate * (mx + hx), rate * (my + hy), rate * (mz + hz)]
+    pushed = slope[0] * force_flow[0] + slope[1] * force_flow[1] + slope[2] * force_flow[2]
+    share[plane] += density * pushed
+    if target is None:
+        return
+    level = whole * (1.2 / 36.0) + 1.2 * (
+        x * (mx + 0.5 * hx) + y * (my + 0.5 * hy) + z * (mz + 0.5 * hz)
+    )
+    level = level - (slope[0] * flow[0] + slope[1] * flow[1] + slope[2] * flow[2])
+    values = spread(level, slope)
+    for m in range(19):
+        target[OPP[m], plane] = values[m] - 0.2 * adjoint[m]
+
+
+def outer_kernel(
     home,
     history,
     opens,
@@ -473,25 +478,19 @@
     far,
     from_near,
     from_far,
-    marked,
     summed,
-    gradient,
+    counted,
     outer,
-    to_near,
-    to_far,
+    share,
+    odd,
     even,
-    odd,
-    share,
     first,
     second,
     second_flow,
 ):
-    del summed
+    del summed, counted
     span = home + 2 * HALO
     up = parity()
-
-    def recall(step, plane):
-        return history[4 * step, plane], [history[4 * step + 1 + axis, plane] for axis in range(3)]
 
     def seed(plane, density, flow):
         damping = 1.0 / opens[plane]
@@ -553,55 +552,40 @@
             outer[ahead, m, ahead * (BX - 1)] = message[30 + m]
 
     def seed_home(plane):
-        seed(plane, *recall(STEPS, plane))
+        seed(plane, *recall(history, STEPS, plane))
 
     each_plane(HALO, HALO + home, seed_home)
 
-    def retreat(step, source, target, plane, recalled=None):
-        mirrored = pull(source, plane, words[plane])
-        adjoint = [mirrored[OPP[m]] for m in range(19)]
-        density, flow = recalled or recall(step, plane)
-        open_rate = opens[plane]
-        force_flow = [flow[0] + FORCE, flow[1], flow[2]]
-        x, y, z = [open_rate * part for part in force_flow]
-        plus, minus = pairs(adjoint)
-        mx, my, mz = [part * (1.0 / 12.0) for part in first_moments(minus, 2.0)]
-        xy_plus, xz_plus, yz_plus = plus[3] + plus[4], plus[5] + plus[6], plus[7] + plus[8]
-        axes = [2.0 * plus[k] for k in range(3)]
-        whole = 12.0 * adjoint[0] + (axes[0] + axes[1] + axes[2]) + (xy_plus + xz_plus + yz_plus)
-        third = whole * (1.0 / 3.0)
-        xx = axes[0] + (xy_plus + xz_plus) - third
-        yy = axes[1] + (xy_plus + yz_plus) - third
-        zz = axes[2] + (xz_plus + yz_plus) - third
-        xy, xz, yz = plus[3] - plus[4], plus[5] - plus[6], plus[7] - plus[8]
-        hx = 0.25 * (xx * x + xy * y + xz * z)
-        hy = 0.25 * (xy * x + yy * y + yz * z)
-        hz = 0.25 * (xz * x + yz * y + zz * z)
-        rate = 1.2 * open_rate
-        slope = [rate * (mx + hx), rate * (my + hy), rate * (mz + hz)]
-        pushed = slope[0] * force_flow[0] + slope[1] * force_flow[1] + slope[2] * force_flow[2]
-        share[plane] += density * pushed
-        if target is None:
-            return
-        level = whole * (1.2 / 36.0) + 1.2 * (
-            x * (mx + 0.5 * hx) + y * (my + 0.5 * hy) + z * (mz + 0.5 * hz)
-        )
-        level = level - (slope[0] * flow[0] + slope[1] * flow[1] + slope[2] * flow[2])
-        values = spread(level, slope)
-        for m in range(19):
-            target[OPP[m], plane] = values[m] - 0.2 * adjoint[m]
-
     for side in range(2):
-        recalled = second_flow[side, 0], [second_flow[side, 1 + axis] for axis in range(3)]
-        retreat(2, even, odd, 1 + side * (span - 3), recalled)
-    each_plane(HALO - 1, HALO + home + 1, functools.partial(retreat, 2, even, odd))
-    each_plane(HALO - 1, HALO + home + 1, functools.partial(retreat, 1, odd, even))
-    each_plane(HALO, HALO + home, functools.partial(retreat, 0, even, None))
-
+        flow = [second_flow[side, 1 + axis] for axis in range(3)]
+        retreat(opens, words, share, even, odd, 1 + side * (span - 3), second_flow[side, 0], flow)
+
+    def step_two(plane):
+        retreat(opens, words, share, even, odd, plane, *recall(history, 2, plane))
+
+    each_plane(HALO - 1, HALO + home + 1, step_two)
+
+
+def gradient_kernel(
+    home, history, opens, words, share, odd, marked, summed, gradient, to_near, to_far, total, even
+):
+    del summed
+    up = parity()
+    for plane in range(share.shape[0]):
+        total[plane] = share[plane]
+
+    def step_one(plane):
+        retreat(opens, words, total, odd, even, plane, *recall(history, 1, plane))
+
+    def step_zero(plane):
+        retreat(opens, words, total, even, None, plane, *recall(history, 0, plane))
+
+    each_plane(HALO - 1, HALO + home + 1, step_one)
+    each_plane(HALO, HALO + home, step_zero)
     for plane in range(home):
         design = marked[plane]
         slope = 3.0 / ((1.6 + 3.4 * design) * (1.0 + 4.0 * design))
-        gradient[plane] = jnp.where(design >= 0.0, share[plane + HALO] * slope, 0.0)
+        gradient[plane] = jnp.where(design >= 0.0, total[plane + HALO] * slope, 0.0)
     for out, ahead in ((to_near, up), (to_far, 1 - up)):
         for plane in range(BX):
             out[plane] = gradient[ahead * (home - BX) + plane]
@@ -616,19 +600,25 @@
         out[plane] = jnp.where(live, joined[spot] * factor, 0.0)
 
 
-def near_gradient(home, cells, where, drag, gradient, from_near, from_far, out, joined):
+def near_gradient(home, cells, where, drag, gradient, from_near, from_far, out, joined, kept, sem):
     up = parity()
     for ahead, message in ((up, from_near), (1 - up, from_far)):
         joined[pl.ds(ahead * (BX + home), BX)] = message[...]
     joined[pl.ds(BX, home)] = gradient[...]
-    scaled(home, cells, where, drag, joined, out)
-
-
-def far_gradient(home, cells, where, drag, gradient, from_left, from_right, out, joined):
+    scaled(home, cells, where, drag, joined, kept)
+    copy = pltpu.make_async_copy(kept, out, sem)
+    copy.start()
+    copy.wait()
+
+
+def far_gradient(home, cells, where, drag, gradient, from_left, from_right, out, joined, kept, sem):
     joined[pl.ds(0, home)] = from_left[...]
     joined[pl.ds(home, home)] = gradient[...]
     joined[pl.ds(2 * home, home)] = from_right[...]
-    scaled(home, cells, where, drag, joined, out)
+    scaled(home, cells, where, drag, joined, kept)
+    copy = pltpu.make_async_copy(kept, out, sem)
+    copy.start()
+    copy.wait()
 
 
 def place_kernel(where, final, outer, out, zeros, sems):
@@ -696,26 +686,18 @@
             name=name,
         )(*operands)
 
-    populations, design, fluid_mask = [
-        pltpu.with_memory_space_constraint(part, pltpu.HBM)
-        for part in (populations, design, fluid_mask)
-    ]
-    own_near, own_far = call(
+    own_near, own_far, pops, marked = call(
         functools.partial(edge_kernel, home),
         "edge_planes",
         [hbm] * 3,
-        [(planes(23, RAW), vmem)] * 2,
-        [
-            scratch(2, 19, 1),
-            scratch(2, HALO),
-            scratch(2, HALO, dtype=jnp.int32),
-            pltpu.SemaphoreType.DMA((8,)),
-        ],
+        [(planes(23, RAW), vmem)] * 2 + [(planes(19, home), vmem), (planes(home), vmem)],
+        [scratch(home), scratch(home, dtype=jnp.int32), pltpu.SemaphoreType.DMA((3,))],
         4,
         1_000_000,
-        populations,
-        design,
-        fluid_mask,
+        *[
+            pltpu.with_memory_space_constraint(part, pltpu.HBM)
+            for part in (populations, design, fluid_mask)
+        ],
     )
     far = lax.ppermute(own_far, "block", far_pairs)
     near = lax.ppermute(own_near, "block", near_pairs)
@@ -730,7 +712,6 @@
         planes(home, dtype=jnp.int32),
         planes(home, dtype=jnp.int32),
         planes(),
-        planes(home),
     )
     (
         to_near,
@@ -742,21 +723,16 @@
         inner_fluid,
         inner_words,
         inner_drag,
-        marked,
     ) = call(
         functools.partial(interior_kernel, home),
         "interior_steps",
-        [anywhere] + [hbm] * 3,
+        [vmem] * 2,
         [(shape, vmem) for shape in inner_shapes],
-        [scratch(19, home), scratch(home), scratch(home, dtype=jnp.int32)]
-        + [scratch(19, home)] * 2
-        + [pltpu.SemaphoreType.DMA((3,))],
+        [scratch(19, home)] * 2,
         16,
         6_000_000,
-        own_near,
-        populations,
-        design,
-        fluid_mask,
+        pops,
+        marked,
     )
     from_far = lax.ppermute(to_far, "block", far_pairs)
     from_near = lax.ppermute(to_near, "block", near_pairs)
@@ -802,28 +778,26 @@
     )
 
     sums = [drag]
-    distance = 1
-    while distance < count:
-        swap = [(i, i ^ distance) for i in range(count)]
-        sums.append(sums[-1] + lax.ppermute(sums[-1], "block", swap))
-        distance *= 2
+    width = 1
+    while width < count:
+        fold = 4 if width >= 4 and width * 4 <= count else 2
+        parts = [sums[-1]]
+        for step in range(1, fold):
+            swap = [(i, i ^ (step * width)) for i in range(count)]
+            parts.append(lax.ppermute(sums[-1], "block", swap))
+        sums.append(sum(parts[1:], parts[0]))
+        width *= fold
     drag = sums[-1]
 
-    gradient, outer, to_near, to_far = call(
-        functools.partial(backward_kernel, home),
-        "backward_steps",
-        [vmem] * 11 + [anywhere],
-        [(planes(home), vmem), (planes(2, 19, BX), vmem), (planes(BX), vmem), (planes(BX), vmem)],
-        [
-            scratch(19, span),
-            scratch(19, span),
-            scratch(span),
-            scratch(2, 19, HALO),
-            scratch(2, 19, HALO + 2),
-            scratch(2, 4),
-        ],
+    is_far = where[2] > 0
+    outer, share, odd = call(
+        functools.partial(outer_kernel, home),
+        "outer_steps",
+        [vmem] * 10 + [anywhere] * 2,
+        [(planes(2, 19, BX), vmem), (planes(span), vmem), (planes(19, span), vmem)],
+        [scratch(19, span), scratch(2, 19, HALO), scratch(2, 19, HALO + 2), scratch(2, 4)],
         20,
-        8_000_000,
+        6_000_000,
         history,
         opens,
         fluid,
@@ -834,8 +808,24 @@
         far,
         from_near,
         from_far,
+        sums[2],
+        is_far.astype(jnp.int32).reshape(1),
+    )
+    gradient, to_near, to_far = call(
+        functools.partial(gradient_kernel, home),
+        "gradient_steps",
+        [vmem] * 6 + [anywhere],
+        [(planes(home), vmem), (planes(BX), vmem), (planes(BX), vmem)],
+        [scratch(span), scratch(19, span)],
+        20,
+        6_000_000,
+        history,
+        opens,
+        words,
+        share,
+        odd,
         marked,
-        sums[1],
+        drag,
     )
     from_far = lax.ppermute(to_far, "block", inner_pairs)
     from_near = lax.ppermute(to_near, "block", near_pairs)
@@ -848,7 +838,7 @@
             place_kernel,
             "place_populations",
             [smem, anywhere, anywhere],
-            [(planes(19, slots * BX), anywhere)],
+            [(pltpu.HBM((19, slots * BX) + plane, jnp.float32), hbm)],
             [scratch(19, BX), pltpu.SemaphoreType.DMA((slots,))],
             8,
             4_000_000,
@@ -867,8 +857,8 @@
             functools.partial(kernel, home, cells),
             name,
             [smem] + [vmem] * 4,
-            [(planes(slots * BX), vmem)],
-            [scratch(home + 2 * reach)],
+            [(pltpu.HBM((slots * BX,) + plane, jnp.float32), hbm)],
+            [scratch(home + 2 * reach), scratch(slots * BX), pltpu.SemaphoreType.DMA(())],
             4,
             1_000_000,
             where,
@@ -885,7 +875,6 @@
         wide = [lax.ppermute(gradient, "block", route) for route in (ring, back)]
         return slope(far_gradient, "far_gradient", home, *wide)
 
-    is_far = where[2] > 0
     populations_after = lax.cond(is_far, place_far, place, outer)
     sensitivity = lax.cond(is_far, slope_far, slope_near, from_near, from_far)
     return (populations_after, sensitivity)

time: 34.5 us -> 36.5 us (1.058)
  the two profiles are of different devices: /device:TPU:0 before, /device:TPU:1 now
where the time goes in v2:
time: 36.5 us; the launch traced here: 36.3 us
  starting transfers between devices  16.5 us (45%)
  Pallas kernels  13.2 us (36%)
  waiting for transfers between devices  4.53 us (12%)
  between operations  1.39 us (4%)
  local copies, waits for them, and re-layouts  0.59 us (2%)
    pallas_call x8, Pallas kernels, call(): pl.pallas_call(kernel, out_shape=[shape for shape, _ in outs], in_specs=i...  13.2 us
    ppermute x2, starting transfers between devices, body(): from_near = lax.ppermute(to_near, 'block', near_pairs)  5.76 us
    ppermute x5, starting transfers between devices, body(): parts.append(lax.ppermute(sums[-1], 'block', swap))  5.46 us
    ppermute x5, waiting for transfers between devices, body(): parts.append(lax.ppermute(sums[-1], 'block', swap))  3.77 us
    ppermute x1, starting transfers between devices, body(): far = lax.ppermute(own_far, 'block', far_pairs)  2.65 us
    ppermute x1, starting transfers between devices, body(): from_far = lax.ppermute(to_far, 'block', inner_pairs)  2.53 us
    ppermute x1, waiting for transfers between devices, body(): from_far = lax.ppermute(to_far, 'block', inner_pairs)  0.74 us
  transfers between devices with their start and end apart: 11, of which 4 were waited for; matrix products, arithmetic and copies ran while one was open for 2% of the time, Pallas kernels for 25%

profile of v2, /device:TPU:1, one launch (start us, length us, event | category | flops | bytes accessed | tf_op | source)
XLA Modules:
  0.0 36.3 jit_solution(16380701413488249203)
XLA Ops:
  0.6 1.3 %edge_planes.1 = (f32[23,2,8,128]{3,2,1,0:T(8,128)S(1)}, f32[23,2,8,128]{3,2,1,0:T(8,128)S(1)}, f32[19,12,8,128]{3,2,1,0:T(8,128)S(1)}, f32[12,8,128]{2,1,0:T(8,128)S(1)}) custom-call(f32[19,12,8,128]{3,2,1,0:T(8,128)} %pops_far.1, f32[12,8,128]{2,1,0:T(8,128)} %design.1, s32[12,8,128]{2,1,0:T(8,128)} %mask.1), custom_call_target="tpu_custom_call" | custom-call | flops 20000000 | bytes 1000000 | tf_op jit(solution)/shard_map/edge_planes/pallas_call | solution.py:678
  1.9 0.1 collective-permute-start.4
  2.0 2.7 %collective-permute-start.5 = (f32[23,2,8,128]{3,2,1,0:T(8,128)S(1)}, f32[23,2,8,128]{3,2,1,0:T(8,128)S(1)}, u32[]{:S(2)}, u32[]{:S(2)}) collective-permute-start(f32[23,2,8,128]{3,2,1,0:T(8,128)S(1)} %get-tuple-element.75), channel_id=1, source_target_pairs={{0,15},{1,2},{2,1},{3,4},{4,3},{5,6},{6,5},{7,8},{8,7},{9,10},{10,... | collective-permute-start | bytes 565256 | tf_op jit(solution)/shard_map/ppermute | solution.py:702
  4.7 2.5 %interior_steps.1 = (f32[49,8,128]{2,1,0:T(8,128)S(1)}, f32[49,8,128]{2,1,0:T(8,128)S(1)}, f32[19,12,8,128]{3,2,1,0:T(8,128)S(1)}, f32[16,12,8,128]{3,2,1,0:T(8,...) custom-call(f32[19,12,8,128]{3,2,1,0:T(8,128)S(1)} %get-tuple-elemen, ...), custom_call_target="tpu_custom_call" | custom-call | flops 120000000 | bytes 6000000 | tf_op jit(solution)/shard_map/interior_steps/pallas_call | solution.py:678
  7.2 3.5 %collective-permute-start.6 = (f32[49,8,128]{2,1,0:T(8,128)S(1)}, f32[49,8,128]{2,1,0:T(8,128)S(1)}, u32[]{:S(2)}, u32[]{:S(2)}) collective-permute-start(f32[49,8,128]{2,1,0:T(8,128)S(1)} %get-tuple-element.92), channel_id=1, source_target_pairs={{0,1},{1,0},{2,3},{3,2},{4,5},{5,4},{6,7},{7,6},{8,9},{9,8},{10,11... | collective-permute-start | bytes 602120 | tf_op jit(solution)/shard_map/ppermute | solution.py:738
  10.8 0.0 collective-permute-start.7
  10.8 0.0 collective-permute-done.4.near
  10.8 0.0 collective-permute-done.5.far
  10.8 0.0 copy-start
  10.8 1.9 %boundary_steps.1 = (f32[19,12,8,128]{3,2,1,0:T(8,128)S(1)}, f32[16,18,8,128]{3,2,1,0:T(8,128)S(1)}, f32[18,8,128]{2,1,0:T(8,128)S(1)}, s32[18,8,128]{2,1,0:T(8,...) custom-call(f32[23,2,8,128]{3,2,1,0:T(8,128)S(1)} %collective-permut, ...), custom_call_target="tpu_custom_call" | custom-call | flops 160000000 | bytes 8000000 | tf_op jit(solution)/shard_map/boundary_steps/pallas_call | solution.py:678
  12.7 0.7 %collective-permute-start.8 = (f32[8,128]{1,0:T(8,128)S(1)}, f32[8,128]{1,0:T(8,128)S(1)}, u32[]{:S(2)}, u32[]{:S(2)}) collective-permute-start(f32[8,128]{1,0:T(8,128)S(1)} %get-tuple-element.94), channel_id=1, source_target_pairs={{0,1},{1,0},{2,3},{3,2},{4,5},{5,4},{6,7},{7,6},{8,9},{9,8},{10,11... | collective-permute-start | bytes 12296 | tf_op jit(solution)/shard_map/ppermute | solution.py:787
  13.4 0.8 %collective-permute-done.8 = f32[8,128]{1,0:T(8,128)S(1)} collective-permute-done((f32[8,128]{1,0:T(8,128)S(1)}, f32[8,128]{1,0:T(8,128)S(1)}, u32[]{:S(2)}, u32[]{:S(2)}) %collective-permute-start.8) | collective-permute-done | bytes 4128 | tf_op jit(solution)/shard_map/ppermute | solution.py:787
  14.2 1.2 %collective-permute-start.9 = (f32[8,128]{1,0:T(8,128)S(1)}, f32[8,128]{1,0:T(8,128)S(1)}, u32[]{:S(2)}, u32[]{:S(2)}) collective-permute-start(f32[8,128]{1,0:T(8,128)S(1)} %add.15), channel_id=1, source_target_pairs={{0,2},{1,3},{2,0},{3,1},{4,6},{5,7},{6,4},{7,5},{8,10},{9,11},{10,... | collective-permute-start | bytes 12296 | tf_op jit(solution)/shard_map/ppermute | solution.py:787
  15.4 1.3 %slot_counts.1 = s32[3]{0:T(128)S(1)} custom-call(s32[48]{0:T(128)S(1)} %copy-done), custom_call_target="tpu_custom_call" | custom-call | flops 400000000 | bytes 20000000 | tf_op jit(solution)/shard_map/slot_counts/pallas_call | solution.py:678
  16.7 0.6 %slice.3 = s32[1]{0:T(128)} slice(s32[3]{0:T(128)S(1)} %slot_counts.1), slice={[2:3]} | slice | bytes 8 | tf_op jit(solution)/shard_map/slice | solution.py:792
  17.9 0.5 %collective-permute-done.9 = f32[8,128]{1,0:T(8,128)S(1)} collective-permute-done((f32[8,128]{1,0:T(8,128)S(1)}, f32[8,128]{1,0:T(8,128)S(1)}, u32[]{:S(2)}, u32[]{:S(2)}) %collective-permute-start.9) | collective-permute-done | bytes 4128 | tf_op jit(solution)/shard_map/ppermute | solution.py:787
  18.4 0.1 collective-permute-start.10
  18.5 3.4 %collective-permute-start.11 = (f32[8,128]{1,0:T(8,128)S(1)}, f32[8,128]{1,0:T(8,128)S(1)}, u32[]{:S(2)}, u32[]{:S(2)}) collective-permute-start(f32[8,128]{1,0:T(8,128)S(1)} %add.16.summed), channel_id=1, source_target_pairs={{0,8},{1,9},{2,10},{3,11},{4,12},{5,13},{6,14},{7,15},{8,0},{9,1},... | collective-permute-start | bytes 12296 | tf_op jit(solution)/shard_map/ppermute | solution.py:787
  21.9 0.1 collective-permute-start.12
  22.0 0.0 collective-permute-done.6.from_near
  22.0 1.6 %outer_steps.1 = (f32[2,19,4,8,128]{4,3,2,1,0:T(8,128)S(1)}, f32[18,8,128]{2,1,0:T(8,128)S(1)}, f32[19,18,8,128]{3,2,1,0:T(8,128)S(1)}) custom-call(f32[16,18,8,128]{3,2,1,0:T(8,128)S(1)} %get-tuple-element.86.history, f32[18,8,128]{2,1,0:T(8,128)S(1)} %get-tuple-element.87.opens, s32[18,8,128]{2,1,0:T(8,128)S(1)} %get-tuple-element.88.fluid, ...), custom_call_target="tpu_custom_call" | custom-call | flops 120000000 | bytes 6000000 | tf_op jit(solution)/shard_map/outer_steps/pallas_call | solution.py:678
  23.6 0.0 collective-permute-done.11
  23.6 2.5 %collective-permute-done.12 = f32[8,128]{1,0:T(8,128)S(1)} collective-permute-done((f32[8,128]{1,0:T(8,128)S(1)}, f32[8,128]{1,0:T(8,128)S(1)}, u32[]{:S(2)}, u32[]{:S(2)}) %collective-permute-start.12) | collective-permute-done | bytes 4128 | tf_op jit(solution)/shard_map/ppermute | solution.py:787
  26.1 1.6 %gradient_steps.1 = (f32[12,8,128]{2,1,0:T(8,128)S(1)}, f32[4,8,128]{2,1,0:T(8,128)S(1)}, f32[4,8,128]{2,1,0:T(8,128)S(1)}) custom-call(f32[16,18,8,128]{3,2,1,0:T(8,128)S(1)} %get-tuple-element.86.history, f32[18,8,128]{2,1,0:T(8,128)S(1)} %get-tuple-element.87.opens, s32[18,8,128]{2,1,0:T(8,128)S(1)} %get-tuple-element.89.words, ...), custom_call_target="tpu_custom_call" | custom-call | flops 120000000 | bytes 6000000 | tf_op jit(solution)/shard_map/gradient_steps/pallas_call | solution.py:678
  27.7 2.2 %collective-permute-start.13 = (f32[4,8,128]{2,1,0:T(8,128)S(1)}, f32[4,8,128]{2,1,0:T(8,128)S(1)}, u32[]{:S(2)}, u32[]{:S(2)}) collective-permute-start(f32[4,8,128]{2,1,0:T(8,128)S(1)} %get-tuple-element.99), channel_id=1, source_target_pairs={{0,1},{1,0},{2,3},{3,2},{4,5},{5,4},{6,7},{7,6},{8,9},{9,8},{10,11... | collective-permute-start | bytes 49160 | tf_op jit(solution)/shard_map/ppermute | solution.py:831
  29.9 2.5 %collective-permute-start.14 = (f32[4,8,128]{2,1,0:T(8,128)S(1)}, f32[4,8,128]{2,1,0:T(8,128)S(1)}, u32[]{:S(2)}, u32[]{:S(2)}) collective-permute-start(f32[4,8,128]{2,1,0:T(8,128)S(1)} %get-tuple-element.100), channel_id=1, source_target_pairs={{1,2},{2,1},{3,4},{4,3},{5,6},{6,5},{7,8},{8,7},{9,10},{10,9},{11,... | collective-permute-start | bytes 49160 | tf_op jit(solution)/shard_map/ppermute | solution.py:830
  32.5 1.7 %conditional.2 = (f32[19,20,8,128]{3,2,1,0:T(8,128)}) conditional(s32[]{:T(128)} %bitcast.2, (s32[3]{0:T(128)S(1)}, f32[19,12,8,128]{3,2,1,0:T(8,128)S(1)}, f32[2,19,4,8,128]{4,3,2,1,0:T(8,128)S(1)}) %tuple.20, (f32[19,12,8,128]{3,2,1,0:T(8,128)S(1)}, s32[3]{0:T(128)S(1)}) %tuple.21), branch_computations={%region_0.0_spmd, %region_1.0_spmd} | conditional | flops 80466944 | bytes 15206744 | solution.py:878
  32.5 1.7 %place_populations.2 = f32[19,20,8,128]{3,2,1,0:T(8,128)} custom-call(s32[3]{0:T(128)S(1)} %get-tuple-element.28.where, f32[19,12,8,128]{3,2,1,0:T(8,128)S(1)} %get-tuple-element.29.final, f32[2,19,4,8,128]{4,3,2,1,0:T(8,128)S(1)} %get-tuple-element.34.outer), custom_call_target="tpu_custom_call" | custom-call | flops 80000000 | bytes 4000000 | tf_op jit(solution)/shard_map/cond/branch_0_fun/place_populations/pallas_call | solution.py:678
  34.2 0.0 collective-permute-done.13
  34.2 0.7 %collective-permute-done.14 = f32[4,8,128]{2,1,0:T(8,128)S(1)} collective-permute-done((f32[4,8,128]{2,1,0:T(8,128)S(1)}, f32[4,8,128]{2,1,0:T(8,128)S(1)}, u32[]{:S(2)}, u32[]{:S(2)}) %collective-permute-start.14) | collective-permute-done | bytes 16416 | tf_op jit(solution)/shard_map/ppermute | solution.py:830
  35.0 1.4 %conditional.3 = (f32[20,8,128]{2,1,0:T(8,128)}) conditional(s32[]{:T(128)} %bitcast.2, (s32[3]{0:T(128)S(1)}, f32[8,128]{1,0:T(8,128)S(1)}, f32[12,8,128]{2,1,0:T(8,128)S(1)}, f32[4,8,128]{2,1,0:T(8,128)S(1)}, f32[4,8,128]{2,1,0:T(8,128)S(1)}) %tuple.22, (f32[12,8,128]{2,1,0:T(8,128)S(1)}, s32[3]{0:T(128)S(1)}, f32[8,128]{1,0:T(8,128)S(1)}) %tuple.23), branch_computations={%region_2.0_spmd, %region_3.0_spmd} | conditional | flops 20000000 | bytes 1393304 | solution.py:879
  35.0 1.3 %near_gradient.1 = f32[20,8,128]{2,1,0:T(8,128)} custom-call(s32[3]{0:T(128)S(1)} %get-tuple-element.37.where, f32[8,128]{1,0:T(8,128)S(1)} %get-tuple-element.38.drag, f32[12,8,128]{2,1,0:T(8,128)S(1)} %get-tuple-element.39.gradient, f32[4,8,128]{2,1,0:T(8,128)S(1)} %get-tuple-element.40.from_near, f32[4,8,128]{2,1,0:T(8,128)S(1)} %get-tuple-element.41.from_far), custom_call_target="tpu_custom_call" | custom-call | flops 20000000 | bytes 1000000 | tf_op jit(solution)/shard_map/cond/branch_0_fun/near_gradient/pallas_call | solution.py:678
  (6 shorter events, 0.0 us)
Async XLA Ops:
  1.9 8.9 %collective-permute-start.4 = (f32[23,2,8,128]{3,2,1,0:T(8,128)S(1)}, f32[23,2,8,128]{3,2,1,0:T(8,128)S(1)}, u32[]{:S(2)}, u32[]{:S(2)}) collective-permute-start(f32[23,2,8,128]{3,2,1,0:T(8,128)S(1)} %get-tuple-element.74), channel_id=1, source_target_pairs={{0,1},{1,0},{2,3},{3,2},{4,5},{5,4},{6,7},{7,6},{8,9},{9,8},{10,11... | collective-permute-start | bytes 565256 | tf_op jit(solution)/shard_map/ppermute | solution.py:703
  2.0 8.7 %collective-permute-start.5 = (f32[23,2,8,128]{3,2,1,0:T(8,128)S(1)}, f32[23,2,8,128]{3,2,1,0:T(8,128)S(1)}, u32[]{:S(2)}, u32[]{:S(2)}) collective-permute-start(f32[23,2,8,128]{3,2,1,0:T(8,128)S(1)} %get-tuple-element.75), channel_id=1, source_target_pairs={{0,15},{1,2},{2,1},{3,4},{4,3},{5,6},{6,5},{7,8},{8,7},{9,10},{10,... | collective-permute-start | bytes 565256 | tf_op jit(solution)/shard_map/ppermute | solution.py:702
  7.2 14.7 %collective-permute-start.6 = (f32[49,8,128]{2,1,0:T(8,128)S(1)}, f32[49,8,128]{2,1,0:T(8,128)S(1)}, u32[]{:S(2)}, u32[]{:S(2)}) collective-permute-start(f32[49,8,128]{2,1,0:T(8,128)S(1)} %get-tuple-element.92), channel_id=1, source_target_pairs={{0,1},{1,0},{2,3},{3,2},{4,5},{5,4},{6,7},{7,6},{8,9},{9,8},{10,11... | collective-permute-start | bytes 602120 | tf_op jit(solution)/shard_map/ppermute | solution.py:738
  10.8 11.2 %collective-permute-start.7 = (f32[49,8,128]{2,1,0:T(8,128)S(1)}, f32[49,8,128]{2,1,0:T(8,128)S(1)}, u32[]{:S(2)}, u32[]{:S(2)}) collective-permute-start(f32[49,8,128]{2,1,0:T(8,128)S(1)} %get-tuple-element.93), channel_id=1, source_target_pairs={{0,15},{1,2},{2,1},{3,4},{4,3},{5,6},{6,5},{7,8},{8,7},{9,10},{10,... | collective-permute-start | bytes 602120 | tf_op jit(solution)/shard_map/ppermute | solution.py:737
  10.8 4.6 %copy-start = (s32[48]{0:T(128)S(1)}, s32[48]{0:T(128)}, u32[]{:S(2)}) copy-start(s32[48]{0:T(128)} %owner.1) | copy-start | bytes 580
  12.7 1.5 %collective-permute-start.8 = (f32[8,128]{1,0:T(8,128)S(1)}, f32[8,128]{1,0:T(8,128)S(1)}, u32[]{:S(2)}, u32[]{:S(2)}) collective-permute-start(f32[8,128]{1,0:T(8,128)S(1)} %get-tuple-element.94), channel_id=1, source_target_pairs={{0,1},{1,0},{2,3},{3,2},{4,5},{5,4},{6,7},{7,6},{8,9},{9,8},{10,11... | collective-permute-start | bytes 12296 | tf_op jit(solution)/shard_map/ppermute | solution.py:787
  14.2 4.2 %collective-permute-start.9 = (f32[8,128]{1,0:T(8,128)S(1)}, f32[8,128]{1,0:T(8,128)S(1)}, u32[]{:S(2)}, u32[]{:S(2)}) collective-permute-start(f32[8,128]{1,0:T(8,128)S(1)} %add.15), channel_id=1, source_target_pairs={{0,2},{1,3},{2,0},{3,1},{4,6},{5,7},{6,4},{7,5},{8,10},{9,11},{10,... | collective-permute-start | bytes 12296 | tf_op jit(solution)/shard_map/ppermute | solution.py:787
  18.4 5.2 %collective-permute-start.10 = (f32[8,128]{1,0:T(8,128)S(1)}, f32[8,128]{1,0:T(8,128)S(1)}, u32[]{:S(2)}, u32[]{:S(2)}) collective-permute-start(f32[8,128]{1,0:T(8,128)S(1)} %add.16.summed), channel_id=1, source_target_pairs={{0,4},{1,5},{2,6},{3,7},{4,0},{5,1},{6,2},{7,3},{8,12},{9,13},{10,... | collective-permute-start | bytes 12296 | tf_op jit(solution)/shard_map/ppermute | solution.py:787
  18.5 5.1 %collective-permute-start.11 = (f32[8,128]{1,0:T(8,128)S(1)}, f32[8,128]{1,0:T(8,128)S(1)}, u32[]{:S(2)}, u32[]{:S(2)}) collective-permute-start(f32[8,128]{1,0:T(8,128)S(1)} %add.16.summed), channel_id=1, source_target_pairs={{0,8},{1,9},{2,10},{3,11},{4,12},{5,13},{6,14},{7,15},{8,0},{9,1},... | collective-permute-start | bytes 12296 | tf_op jit(solution)/shard_map/ppermute | solution.py:787
  21.9 4.3 %collective-permute-start.12 = (f32[8,128]{1,0:T(8,128)S(1)}, f32[8,128]{1,0:T(8,128)S(1)}, u32[]{:S(2)}, u32[]{:S(2)}) collective-permute-start(f32[8,128]{1,0:T(8,128)S(1)} %add.16.summed), channel_id=1, source_target_pairs={{0,12},{1,13},{2,14},{3,15},{4,8},{5,9},{6,10},{7,11},{8,4},{9,5},... | collective-permute-start | bytes 12296 | tf_op jit(solution)/shard_map/ppermute | solution.py:787
  27.7 6.5 %collective-permute-start.13 = (f32[4,8,128]{2,1,0:T(8,128)S(1)}, f32[4,8,128]{2,1,0:T(8,128)S(1)}, u32[]{:S(2)}, u32[]{:S(2)}) collective-permute-start(f32[4,8,128]{2,1,0:T(8,128)S(1)} %get-tuple-element.99), channel_id=1, source_target_pairs={{0,1},{1,0},{2,3},{3,2},{4,5},{5,4},{6,7},{7,6},{8,9},{9,8},{10,11... | collective-permute-start | bytes 49160 | tf_op jit(solution)/shard_map/ppermute | solution.py:831
  29.9 5.0 %collective-permute-start.14 = (f32[4,8,128]{2,1,0:T(8,128)S(1)}, f32[4,8,128]{2,1,0:T(8,128)S(1)}, u32[]{:S(2)}, u32[]{:S(2)}) collective-permute-start(f32[4,8,128]{2,1,0:T(8,128)S(1)} %get-tuple-element.100), channel_id=1, source_target_pairs={{1,2},{2,1},{3,4},{4,3},{5,6},{6,5},{7,8},{8,7},{9,10},{10,9},{11,... | collective-permute-start | bytes 49160 | tf_op jit(solution)/shard_map/ppermute | solution.py:830

commit v3 on v2

--- a/solution.py
+++ b/solution.py
@@ -412,7 +412,8 @@
     receive(1, odd)
     both(2, functools.partial(advance, 2, odd, even))
     receive(2, even)
-    drag[...] = inner_drag[...]
+    drag[...] = jnp.zeros_like(drag)
+    drag[0] = inner_drag[...]
 
     def finish(index, place, ahead):
         state = pull(even, index, words[index])
@@ -421,7 +422,7 @@
         here = fluid[index] > 0
         for m in range(19):
             final[m, index - HALO] = jnp.where(here, state[m], inner_final[m, index - HALO])
-        drag[...] += jnp.where(here, drag_terms(flow, opens[index]), 0.0)
+        drag[1 + place] += jnp.where(here, drag_terms(flow, opens[index]), 0.0)
 
     both(3, finish)
     for copy in copies:
@@ -600,28 +601,23 @@
         out[plane] = jnp.where(live, joined[spot] * factor, 0.0)
 
 
-def near_gradient(home, cells, where, drag, gradient, from_near, from_far, out, joined, kept, sem):
+def near_gradient(home, cells, where, drag, gradient, from_near, from_far, out, joined):
     up = parity()
     for ahead, message in ((up, from_near), (1 - up, from_far)):
         joined[pl.ds(ahead * (BX + home), BX)] = message[...]
     joined[pl.ds(BX, home)] = gradient[...]
-    scaled(home, cells, where, drag, joined, kept)
-    copy = pltpu.make_async_copy(kept, out, sem)
-    copy.start()
-    copy.wait()
-
-
-def far_gradient(home, cells, where, drag, gradient, from_left, from_right, out, joined, kept, sem):
+    scaled(home, cells, where, drag, joined, out)
+
+
+def far_gradient(home, cells, where, drag, gradient, from_left, from_right, out, joined):
     joined[pl.ds(0, home)] = from_left[...]
     joined[pl.ds(home, home)] = gradient[...]
     joined[pl.ds(2 * home, home)] = from_right[...]
-    scaled(home, cells, where, drag, joined, kept)
-    copy = pltpu.make_async_copy(kept, out, sem)
-    copy.start()
-    copy.wait()
-
-
-def place_kernel(where, final, outer, out, zeros, sems):
+    scaled(home, cells, where, drag, joined, out)
+
+
+def place_kernel(where, final, outer, later, out, zeros, sems):
+    del later
     blocks = out.shape[1] // BX
     home_blocks = final.shape[1] // BX
     beyond = outer.shape[2] // BX
@@ -754,7 +750,7 @@
         planes(span),
         planes(span, dtype=jnp.int32),
         planes(span, dtype=jnp.int32),
-        planes(),
+        planes(1 + STEPS),
         planes(19, span),
         planes(19, span),
     )
@@ -778,15 +774,11 @@
     )
 
     sums = [drag]
-    width = 1
-    while width < count:
-        fold = 4 if width >= 4 and width * 4 <= count else 2
-        parts = [sums[-1]]
-        for step in range(1, fold):
-            swap = [(i, i ^ (step * width)) for i in range(count)]
-            parts.append(lax.ppermute(sums[-1], "block", swap))
-        sums.append(sum(parts[1:], parts[0]))
-        width *= fold
+    distance = 1
+    while distance < count:
+        swap = [(i, i ^ distance) for i in range(count)]
+        sums.append(sums[-1] + lax.ppermute(sums[-1], "block", swap))
+        distance *= 2
     drag = sums[-1]
 
     is_far = where[2] > 0
@@ -797,7 +789,7 @@
         [(planes(2, 19, BX), vmem), (planes(span), vmem), (planes(19, span), vmem)],
         [scratch(19, span), scratch(2, 19, HALO), scratch(2, 19, HALO + 2), scratch(2, 4)],
         20,
-        6_000_000,
+        12_000_000,
         history,
         opens,
         fluid,
@@ -825,7 +817,7 @@
         share,
         odd,
         marked,
-        drag,
+        sums[3],
     )
     from_far = lax.ppermute(to_far, "block", inner_pairs)
     from_near = lax.ppermute(to_near, "block", near_pairs)
@@ -837,14 +829,15 @@
         (out,) = call(
             place_kernel,
             "place_populations",
-            [smem, anywhere, anywhere],
-            [(pltpu.HBM((19, slots * BX) + plane, jnp.float32), hbm)],
+            [smem, anywhere, anywhere, anywhere],
+            [(planes(19, slots * BX), anywhere)],
             [scratch(19, BX), pltpu.SemaphoreType.DMA((slots,))],
             8,
             4_000_000,
             where,
             final,
             outer,
+            to_near,
         )
         return out
 
@@ -857,8 +850,8 @@
             functools.partial(kernel, home, cells),
             name,
             [smem] + [vmem] * 4,
-            [(pltpu.HBM((slots * BX,) + plane, jnp.float32), hbm)],
-            [scratch(home + 2 * reach), scratch(slots * BX), pltpu.SemaphoreType.DMA(())],
+            [(planes(slots * BX), vmem)],
+            [scratch(home + 2 * reach)],
             4,
             1_000_000,
             where,

time: 36.5 us -> 33.5 us (0.918)
  the two profiles are of different devices: /device:TPU:1 before, /device:TPU:13 now
where the time goes in v3:
time: 33.5 us; the launch traced here: 33.3 us
  starting transfers between devices  13.6 us (41%)
  Pallas kernels  12.3 us (37%)
  waiting for transfers between devices  4.76 us (14%)
  between operations  1.43 us (4%)
  local copies, waits for them, and re-layouts  1.21 us (4%)
    pallas_call x8, Pallas kernels, call(): pl.pallas_call(kernel, out_shape=[shape for shape, _ in outs], in_specs=i...  12.3 us
    ppermute x4, starting transfers between devices, body(): sums.append(sums[-1] + lax.ppermute(sums[-1], 'block', swap))  5.33 us
    ppermute x1, waiting for transfers between devices, body(): from_far = lax.ppermute(to_far, 'block', inner_pairs)  3.14 us
    ppermute x2, starting transfers between devices, body(): from_near = lax.ppermute(to_near, 'block', near_pairs)  2.79 us
    ppermute x1, starting transfers between devices, body(): from_far = lax.ppermute(to_far, 'block', inner_pairs)  1.91 us
    ppermute x1, starting transfers between devices, body(): from_far = lax.ppermute(to_far, 'block', far_pairs)  1.62 us
    ppermute x1, starting transfers between devices, body(): far = lax.ppermute(own_far, 'block', far_pairs)  1.2 us
    ppermute x4, waiting for transfers between devices, body(): sums.append(sums[-1] + lax.ppermute(sums[-1], 'block', swap))  1.05 us
  transfers between devices with their start and end apart: 10, of which 4 were waited for; matrix products, arithmetic and copies ran while one was open for 2% of the time, Pallas kernels for 31%

profile of v3, /device:TPU:13, one launch (start us, length us, event | category | flops | bytes accessed | tf_op | source)
XLA Modules:
  0.0 33.3 jit_solution(17400389122622360364)
XLA Ops:
  0.6 1.3 %edge_planes.1 = (f32[23,2,8,128]{3,2,1,0:T(8,128)S(1)}, f32[23,2,8,128]{3,2,1,0:T(8,128)S(1)}, f32[19,12,8,128]{3,2,1,0:T(8,128)S(1)}, f32[12,8,128]{2,1,0:T(8,128)S(1)}) custom-call(f32[19,12,8,128]{3,2,1,0:T(8,128)} %pops_far.1, f32[12,8,128]{2,1,0:T(8,128)} %design.1, s32[12,8,128]{2,1,0:T(8,128)} %mask.1), custom_call_target="tpu_custom_call" | custom-call | flops 20000000 | bytes 1000000 | tf_op jit(solution)/shard_map/edge_planes/pallas_call | solution.py:674
  1.9 0.7 %collective-permute-start.4 = (f32[23,2,8,128]{3,2,1,0:T(8,128)S(1)}, f32[23,2,8,128]{3,2,1,0:T(8,128)S(1)}, u32[]{:S(2)}, u32[]{:S(2)}) collective-permute-start(f32[23,2,8,128]{3,2,1,0:T(8,128)S(1)} %get-tuple-element.80), channel_id=1, source_target_pairs={{0,1},{1,0},{2,3},{3,2},{4,5},{5,4},{6,7},{7,6},{8,9},{9,8},{10,11... | collective-permute-start | bytes 565256 | tf_op jit(solution)/shard_map/ppermute | solution.py:699
  2.7 1.2 %collective-permute-start.5 = (f32[23,2,8,128]{3,2,1,0:T(8,128)S(1)}, f32[23,2,8,128]{3,2,1,0:T(8,128)S(1)}, u32[]{:S(2)}, u32[]{:S(2)}) collective-permute-start(f32[23,2,8,128]{3,2,1,0:T(8,128)S(1)} %get-tuple-element.81), channel_id=1, source_target_pairs={{0,15},{1,2},{2,1},{3,4},{4,3},{5,6},{6,5},{7,8},{8,7},{9,10},{10,... | collective-permute-start | bytes 565256 | tf_op jit(solution)/shard_map/ppermute | solution.py:698
  3.9 2.5 %interior_steps.1 = (f32[49,8,128]{2,1,0:T(8,128)S(1)}, f32[49,8,128]{2,1,0:T(8,128)S(1)}, f32[19,12,8,128]{3,2,1,0:T(8,128)S(1)}, f32[16,12,8,128]{3,2,1,0:T(8,...) custom-call(f32[19,12,8,128]{3,2,1,0:T(8,128)S(1)} %get-tuple-elemen, ...), custom_call_target="tpu_custom_call" | custom-call | flops 120000000 | bytes 6000000 | tf_op jit(solution)/shard_map/interior_steps/pallas_call | solution.py:674
  6.4 0.1 collective-permute-start.6
  6.5 1.6 %collective-permute-start.7 = (f32[49,8,128]{2,1,0:T(8,128)S(1)}, f32[49,8,128]{2,1,0:T(8,128)S(1)}, u32[]{:S(2)}, u32[]{:S(2)}) collective-permute-start(f32[49,8,128]{2,1,0:T(8,128)S(1)} %get-tuple-element.99), channel_id=1, source_target_pairs={{0,15},{1,2},{2,1},{3,4},{4,3},{5,6},{6,5},{7,8},{8,7},{9,10},{10,... | collective-permute-start | bytes 602120 | tf_op jit(solution)/shard_map/ppermute | solution.py:733
  8.1 0.0 collective-permute-done.4.near
  8.1 0.6 %collective-permute-done.5.far = f32[23,2,8,128]{3,2,1,0:T(8,128)S(1)} collective-permute-done((f32[23,2,8,128]{3,2,1,0:T(8,128)S(1)}, f32[23,2,8,128]{3,2,1,0:T(8,128)S(1)}, u32[]{:S(2)}, u32[]{:S(2)}) %collective-permute-start.5) | collective-permute-done | bytes 188448 | tf_op jit(solution)/shard_map/ppermute | solution.py:698
  8.7 1.9 %boundary_steps.1 = (f32[19,12,8,128]{3,2,1,0:T(8,128)S(1)}, f32[16,18,8,128]{3,2,1,0:T(8,128)S(1)}, f32[18,8,128]{2,1,0:T(8,128)S(1)}, s32[18,8,128]{2,1,0:T(8,...) custom-call(f32[23,2,8,128]{3,2,1,0:T(8,128)S(1)} %collective-permut, ...), custom_call_target="tpu_custom_call" | custom-call | flops 160000000 | bytes 8000000 | tf_op jit(solution)/shard_map/boundary_steps/pallas_call | solution.py:674
  10.6 1.2 %collective-permute-start.8 = (f32[4,8,128]{2,1,0:T(8,128)S(1)}, f32[4,8,128]{2,1,0:T(8,128)S(1)}, u32[]{:S(2)}, u32[]{:S(2)}) collective-permute-start(f32[4,8,128]{2,1,0:T(8,128)S(1)} %get-tuple-element.100), channel_id=1, source_target_pairs={{0,1},{1,0},{2,3},{3,2},{4,5},{5,4},{6,7},{7,6},{8,9},{9,8},{10,11... | collective-permute-start | bytes 49160 | tf_op jit(solution)/shard_map/ppermute | solution.py:780
  11.7 0.8 %collective-permute-done.8 = f32[4,8,128]{2,1,0:T(8,128)S(1)} collective-permute-done((f32[4,8,128]{2,1,0:T(8,128)S(1)}, f32[4,8,128]{2,1,0:T(8,128)S(1)}, u32[]{:S(2)}, u32[]{:S(2)}) %collective-permute-start.8) | collective-permute-done | bytes 16416 | tf_op jit(solution)/shard_map/ppermute | solution.py:780
  12.6 0.5 %collective-permute-start.9 = (f32[4,8,128]{2,1,0:T(8,128)S(1)}, f32[4,8,128]{2,1,0:T(8,128)S(1)}, u32[]{:S(2)}, u32[]{:S(2)}) collective-permute-start(f32[4,8,128]{2,1,0:T(8,128)S(1)} %add.12), channel_id=1, source_target_pairs={{0,2},{1,3},{2,0},{3,1},{4,6},{5,7},{6,4},{7,5},{8,10},{9,11},{10,... | collective-permute-start | bytes 49160 | tf_op jit(solution)/shard_map/ppermute | solution.py:780
  13.0 1.3 %slot_counts.1 = s32[3]{0:T(128)S(1)} custom-call(s32[48]{0:T(128)S(1)} %copy-done), custom_call_target="tpu_custom_call" | custom-call | flops 400000000 | bytes 20000000 | tf_op jit(solution)/shard_map/slot_counts/pallas_call | solution.py:674
  14.3 0.6 %slice.3 = s32[1]{0:T(128)} slice(s32[3]{0:T(128)S(1)} %slot_counts.1), slice={[2:3]} | slice | bytes 8 | tf_op jit(solution)/shard_map/slice | solution.py:784
  15.6 0.8 %collective-permute-start.10 = (f32[4,8,128]{2,1,0:T(8,128)S(1)}, f32[4,8,128]{2,1,0:T(8,128)S(1)}, u32[]{:S(2)}, u32[]{:S(2)}) collective-permute-start(f32[4,8,128]{2,1,0:T(8,128)S(1)} %add.13.summed), channel_id=1, source_target_pairs={{0,4},{1,5},{2,6},{3,7},{4,0},{5,1},{6,2},{7,3},{8,12},{9,13},{10,... | collective-permute-start | bytes 49160 | tf_op jit(solution)/shard_map/ppermute | solution.py:780
  16.4 0.0 collective-permute-done.6.from_near
  16.4 0.0 collective-permute-done.7.from_far
  16.4 1.6 %outer_steps.1 = (f32[2,19,4,8,128]{4,3,2,1,0:T(8,128)S(1)}, f32[18,8,128]{2,1,0:T(8,128)S(1)}, f32[19,18,8,128]{3,2,1,0:T(8,128)S(1)}) custom-call(f32[16,18,8,128]{3,2,1,0:T(8,128)S(1)} %get-tuple-element.92.history, f32[18,8,128]{2,1,0:T(8,128)S(1)} %get-tuple-element.93.opens, s32[18,8,128]{2,1,0:T(8,128)S(1)} %get-tuple-element.94.fluid, ...), custom_call_target="tpu_custom_call" | custom-call | flops 240000000 | bytes 12000000 | tf_op jit(solution)/shard_map/outer_steps/pallas_call | solution.py:674
  18.0 0.2 collective-permute-done.10
  18.2 2.9 %collective-permute-start.11 = (f32[4,8,128]{2,1,0:T(8,128)S(1)}, f32[4,8,128]{2,1,0:T(8,128)S(1)}, u32[]{:S(2)}, u32[]{:S(2)}) collective-permute-start(f32[4,8,128]{2,1,0:T(8,128)S(1)} %add.14.summed), channel_id=1, source_target_pairs={{0,8},{1,9},{2,10},{3,11},{4,12},{5,13},{6,14},{7,15},{8,0},{9,1},... | collective-permute-start | bytes 49160 | tf_op jit(solution)/shard_map/ppermute | solution.py:780
  21.1 2.2 %gradient_steps.1 = (f32[12,8,128]{2,1,0:T(8,128)S(1)}, f32[4,8,128]{2,1,0:T(8,128)}, f32[4,8,128]{2,1,0:T(8,128)S(1)}) custom-call(f32[16,18,8,128]{3,2,1,0:T(8,128)S(1)} %get-tuple-element.92.history, f32[18,8,128]{2,1,0:T(8,128)S(1)} %get-tuple-element.93.opens, s32[18,8,128]{2,1,0:T(8,128)S(1)} %get-tuple-element.95.words, ...), custom_call_target="tpu_custom_call" | custom-call | flops 120000000 | bytes 6000000 | tf_op jit(solution)/shard_map/gradient_steps/pallas_call | solution.py:674
  23.3 2.7 %collective-permute-start.12 = (f32[4,8,128]{2,1,0:T(8,128)}, f32[4,8,128]{2,1,0:T(8,128)S(1)}, u32[]{:S(2)}, u32[]{:S(2)}) collective-permute-start(f32[4,8,128]{2,1,0:T(8,128)} %get-tuple-element.104), channel_id=1, source_target_pairs={{0,1},{1,0},{2,3},{3,2},{4,5},{5,4},{6,7},{7,6},{8,9},{9,8},{10,11... | collective-permute-start | bytes 49160 | tf_op jit(solution)/shard_map/ppermute | solution.py:823
  26.0 1.9 %collective-permute-start.13 = (f32[4,8,128]{2,1,0:T(8,128)S(1)}, f32[4,8,128]{2,1,0:T(8,128)S(1)}, u32[]{:S(2)}, u32[]{:S(2)}) collective-permute-start(f32[4,8,128]{2,1,0:T(8,128)S(1)} %get-tuple-element.106), channel_id=1, source_target_pairs={{1,2},{2,1},{3,4},{4,3},{5,6},{6,5},{7,8},{8,7},{9,10},{10,9},{11,... | collective-permute-start | bytes 49160 | tf_op jit(solution)/shard_map/ppermute | solution.py:822
  27.9 0.8 %conditional.2 = (f32[19,20,8,128]{3,2,1,0:T(8,128)S(1)}) conditional(s32[]{:T(128)} %bitcast.2, (s32[3]{0:T(128)S(1)}, f32[19,12,8,128]{3,2,1,0:T(8,128)S(1)}, f32[2,19,4,8,128]{4,3,2,1,0:T(8,128)S(1)}, f32[4,8,128]{2,1,0:T(8,128)}) %tuple.20, (f32[19,12,8,128]{3,2,1,0:T(8,128)S(1)}, s32[3]{0:T(128)S(1)}, f32[4,8,128]{2,1,0:T(8,128)}) %tuple.21), branch_computations={%region_0.0_spmd, %region_1.0_spmd} | conditional | flops 80466944 | bytes 15206744 | solution.py:871
  28.0 0.8 %place_populations.2 = f32[19,20,8,128]{3,2,1,0:T(8,128)S(1)} custom-call(s32[3]{0:T(128)S(1)} %get-tuple-element.32.where, f32[19,12,8,128]{3,2,1,0:T(8,128)S(1)} %get-tuple-element.33.final, f32[2,19,4,8,128]{4,3,2,1,0:T(8,128)S(1)} %get-tuple-element.38.outer, f32[4,8,128]{2,1,0:T(8,128)} %get-tuple-element.39.later), custom_call_target="tpu_custom_call" | custom-call | flops 80000000 | bytes 4000000 | tf_op jit(solution)/shard_map/cond/branch_0_fun/place_populations/pallas_call | solution.py:674
  28.8 0.0 copy-start.1
  28.8 0.0 collective-permute-done.11
  28.8 3.1 %collective-permute-done.13 = f32[4,8,128]{2,1,0:T(8,128)S(1)} collective-permute-done((f32[4,8,128]{2,1,0:T(8,128)S(1)}, f32[4,8,128]{2,1,0:T(8,128)S(1)}, u32[]{:S(2)}, u32[]{:S(2)}) %collective-permute-start.13) | collective-permute-done | bytes 16416 | tf_op jit(solution)/shard_map/ppermute | solution.py:822
  32.0 0.7 %conditional.3 = (f32[20,8,128]{2,1,0:T(8,128)S(1)}) conditional(s32[]{:T(128)} %bitcast.2, (s32[3]{0:T(128)S(1)}, f32[4,8,128]{2,1,0:T(8,128)S(1)}, f32[12,8,128]{2,1,0:T(8,128)S(1)}, f32[4,8,128]{2,1,0:T(8,128)S(1)}, f32[4,8,128]{2,1,0:T(8,128)S(1)}) %tuple.22, (f32[12,8,128]{2,1,0:T(8,128)S(1)}, s32[3]{0:T(128)S(1)}, ...), branch_computations={%region_2.0_spmd, %region_3.0_spmd} | conditional | flops 20000000 | bytes 1393304 | solution.py:872
  32.0 0.7 %near_gradient.1 = f32[20,8,128]{2,1,0:T(8,128)S(1)} custom-call(s32[3]{0:T(128)S(1)} %get-tuple-element.43.where, f32[4,8,128]{2,1,0:T(8,128)S(1)} %get-tuple-element.44.drag, f32[12,8,128]{2,1,0:T(8,128)S(1)} %get-tuple-element.45.gradient, f32[4,8,128]{2,1,0:T(8,128)S(1)} %get-tuple-element.46.from_near, f32[4,8,128]{2,1,0:T(8,128)S(1)} %get-tuple-element.47.from_far), custom_call_target="tpu_custom_call" | custom-call | flops 20000000 | bytes 1000000 | tf_op jit(solution)/shard_map/cond/branch_0_fun/near_gradient/pallas_call | solution.py:674
  32.7 0.0 copy-start.2
  32.7 0.6 %copy-done.2 = f32[20,8,128]{2,1,0:T(8,128)} copy-done((f32[20,8,128]{2,1,0:T(8,128)}, f32[20,8,128]{2,1,0:T(8,128)S(1)}, u32[]{:S(2)}) %copy-start.2) | copy-done | bytes 81944
  (9 shorter events, 0.0 us)
Async XLA Ops:
  1.9 6.2 %collective-permute-start.4 = (f32[23,2,8,128]{3,2,1,0:T(8,128)S(1)}, f32[23,2,8,128]{3,2,1,0:T(8,128)S(1)}, u32[]{:S(2)}, u32[]{:S(2)}) collective-permute-start(f32[23,2,8,128]{3,2,1,0:T(8,128)S(1)} %get-tuple-element.80), channel_id=1, source_target_pairs={{0,1},{1,0},{2,3},{3,2},{4,5},{5,4},{6,7},{7,6},{8,9},{9,8},{10,11... | collective-permute-start | bytes 565256 | tf_op jit(solution)/shard_map/ppermute | solution.py:699
  2.7 6.0 %collective-permute-start.5 = (f32[23,2,8,128]{3,2,1,0:T(8,128)S(1)}, f32[23,2,8,128]{3,2,1,0:T(8,128)S(1)}, u32[]{:S(2)}, u32[]{:S(2)}) collective-permute-start(f32[23,2,8,128]{3,2,1,0:T(8,128)S(1)} %get-tuple-element.81), channel_id=1, source_target_pairs={{0,15},{1,2},{2,1},{3,4},{4,3},{5,6},{6,5},{7,8},{8,7},{9,10},{10,... | collective-permute-start | bytes 565256 | tf_op jit(solution)/shard_map/ppermute | solution.py:698
  6.4 10.0 %collective-permute-start.6 = (f32[49,8,128]{2,1,0:T(8,128)S(1)}, f32[49,8,128]{2,1,0:T(8,128)S(1)}, u32[]{:S(2)}, u32[]{:S(2)}) collective-permute-start(f32[49,8,128]{2,1,0:T(8,128)S(1)} %get-tuple-element.98), channel_id=1, source_target_pairs={{0,1},{1,0},{2,3},{3,2},{4,5},{5,4},{6,7},{7,6},{8,9},{9,8},{10,11... | collective-permute-start | bytes 602120 | tf_op jit(solution)/shard_map/ppermute | solution.py:734
  6.5 9.9 %collective-permute-start.7 = (f32[49,8,128]{2,1,0:T(8,128)S(1)}, f32[49,8,128]{2,1,0:T(8,128)S(1)}, u32[]{:S(2)}, u32[]{:S(2)}) collective-permute-start(f32[49,8,128]{2,1,0:T(8,128)S(1)} %get-tuple-element.99), channel_id=1, source_target_pairs={{0,15},{1,2},{2,1},{3,4},{4,3},{5,6},{6,5},{7,8},{8,7},{9,10},{10,... | collective-permute-start | bytes 602120 | tf_op jit(solution)/shard_map/ppermute | solution.py:733
  8.7 4.4 %copy-start = (s32[48]{0:T(128)S(1)}, s32[48]{0:T(128)}, u32[]{:S(2)}) copy-start(s32[48]{0:T(128)} %owner.1) | copy-start | bytes 580
  10.6 2.0 %collective-permute-start.8 = (f32[4,8,128]{2,1,0:T(8,128)S(1)}, f32[4,8,128]{2,1,0:T(8,128)S(1)}, u32[]{:S(2)}, u32[]{:S(2)}) collective-permute-start(f32[4,8,128]{2,1,0:T(8,128)S(1)} %get-tuple-element.100), channel_id=1, source_target_pairs={{0,1},{1,0},{2,3},{3,2},{4,5},{5,4},{6,7},{7,6},{8,9},{9,8},{10,11... | collective-permute-start | bytes 49160 | tf_op jit(solution)/shard_map/ppermute | solution.py:780
  12.6 3.0 %collective-permute-start.9 = (f32[4,8,128]{2,1,0:T(8,128)S(1)}, f32[4,8,128]{2,1,0:T(8,128)S(1)}, u32[]{:S(2)}, u32[]{:S(2)}) collective-permute-start(f32[4,8,128]{2,1,0:T(8,128)S(1)} %add.12), channel_id=1, source_target_pairs={{0,2},{1,3},{2,0},{3,1},{4,6},{5,7},{6,4},{7,5},{8,10},{9,11},{10,... | collective-permute-start | bytes 49160 | tf_op jit(solution)/shard_map/ppermute | solution.py:780
  15.6 2.7 %collective-permute-start.10 = (f32[4,8,128]{2,1,0:T(8,128)S(1)}, f32[4,8,128]{2,1,0:T(8,128)S(1)}, u32[]{:S(2)}, u32[]{:S(2)}) collective-permute-start(f32[4,8,128]{2,1,0:T(8,128)S(1)} %add.13.summed), channel_id=1, source_target_pairs={{0,4},{1,5},{2,6},{3,7},{4,0},{5,1},{6,2},{7,3},{8,12},{9,13},{10,... | collective-permute-start | bytes 49160 | tf_op jit(solution)/shard_map/ppermute | solution.py:780
  18.2 10.5 %collective-permute-start.11 = (f32[4,8,128]{2,1,0:T(8,128)S(1)}, f32[4,8,128]{2,1,0:T(8,128)S(1)}, u32[]{:S(2)}, u32[]{:S(2)}) collective-permute-start(f32[4,8,128]{2,1,0:T(8,128)S(1)} %add.14.summed), channel_id=1, source_target_pairs={{0,8},{1,9},{2,10},{3,11},{4,12},{5,13},{6,14},{7,15},{8,0},{9,1},... | collective-permute-start | bytes 49160 | tf_op jit(solution)/shard_map/ppermute | solution.py:780
  23.3 5.5 %collective-permute-start.12 = (f32[4,8,128]{2,1,0:T(8,128)}, f32[4,8,128]{2,1,0:T(8,128)S(1)}, u32[]{:S(2)}, u32[]{:S(2)}) collective-permute-start(f32[4,8,128]{2,1,0:T(8,128)} %get-tuple-element.104), channel_id=1, source_target_pairs={{0,1},{1,0},{2,3},{3,2},{4,5},{5,4},{6,7},{7,6},{8,9},{9,8},{10,11... | collective-permute-start | bytes 49160 | tf_op jit(solution)/shard_map/ppermute | solution.py:823
  26.0 5.9 %collective-permute-start.13 = (f32[4,8,128]{2,1,0:T(8,128)S(1)}, f32[4,8,128]{2,1,0:T(8,128)S(1)}, u32[]{:S(2)}, u32[]{:S(2)}) collective-permute-start(f32[4,8,128]{2,1,0:T(8,128)S(1)} %get-tuple-element.106), channel_id=1, source_target_pairs={{1,2},{2,1},{3,4},{4,3},{5,6},{6,5},{7,8},{8,7},{9,10},{10,9},{11,... | collective-permute-start | bytes 49160 | tf_op jit(solution)/shard_map/ppermute | solution.py:822
  28.8 3.9 %copy-start.1 = (f32[19,20,8,128]{3,2,1,0:T(8,128)}, f32[19,20,8,128]{3,2,1,0:T(8,128)S(1)}, u32[]{:S(2)}) copy-start(f32[19,20,8,128]{3,2,1,0:T(8,128)S(1)} %get-tuple-element.107) | copy-start | bytes 4669444
  32.7 0.6 %copy-start.2 = (f32[20,8,128]{2,1,0:T(8,128)}, f32[20,8,128]{2,1,0:T(8,128)S(1)}, u32[]{:S(2)}) copy-start(f32[20,8,128]{2,1,0:T(8,128)S(1)} %get-tuple-element.108) | copy-start | bytes 245764

commit v4 on v3

--- a/solution.py
+++ b/solution.py
@@ -321,8 +321,8 @@
 
 def boundary_kernel(
     home,
+    far,
     near,
-    far,
     edges,
     inner_history,
     inner_final,
@@ -475,10 +475,10 @@
     words,
     even_state,
     odd_state,
+    far,
     near,
-    far,
+    from_far,
     from_near,
-    from_far,
     summed,
     counted,
     outer,
@@ -601,7 +601,7 @@
         out[plane] = jnp.where(live, joined[spot] * factor, 0.0)
 
 
-def near_gradient(home, cells, where, drag, gradient, from_near, from_far, out, joined):
+def near_gradient(home, cells, where, drag, gradient, from_far, from_near, out, joined):
     up = parity()
     for ahead, message in ((up, from_near), (1 - up, from_far)):
         joined[pl.ds(ahead * (BX + home), BX)] = message[...]
@@ -695,8 +695,8 @@
             for part in (populations, design, fluid_mask)
         ],
     )
+    near = lax.ppermute(own_near, "block", near_pairs)
     far = lax.ppermute(own_far, "block", far_pairs)
-    near = lax.ppermute(own_near, "block", near_pairs)
 
     inner_shapes = (
         planes(49),
@@ -730,8 +730,8 @@
         pops,
         marked,
     )
+    from_near = lax.ppermute(to_near, "block", near_pairs)
     from_far = lax.ppermute(to_far, "block", far_pairs)
-    from_near = lax.ppermute(to_near, "block", near_pairs)
 
     (where,) = call(
         functools.partial(count_kernel, home_blocks),
@@ -762,8 +762,8 @@
         [pltpu.SemaphoreType.DMA((5,))],
         20,
         8_000_000,
+        far,
         near,
-        far,
         edges,
         inner_history,
         inner_final,
@@ -796,10 +796,10 @@
         words,
         even_state,
         odd_state,
+        far,
         near,
-        far,
+        from_far,
         from_near,
-        from_far,
         sums[2],
         is_far.astype(jnp.int32).reshape(1),
     )
@@ -819,8 +819,8 @@
         marked,
         sums[3],
     )
+    from_near = lax.ppermute(to_near, "block", near_pairs)
     from_far = lax.ppermute(to_far, "block", inner_pairs)
-    from_near = lax.ppermute(to_near, "block", near_pairs)
 
     ring = [(i, i + 1) for i in range(count - 1)]
     back = [(i + 1, i) for i in range(count - 1)]
@@ -829,7 +829,7 @@
         (out,) = call(
             place_kernel,
             "place_populations",
-            [smem, anywhere, anywhere, anywhere],
+            [smem, anywhere, anywhere, vmem],
             [(planes(19, slots * BX), anywhere)],
             [scratch(19, BX), pltpu.SemaphoreType.DMA((slots,))],
             8,
@@ -837,7 +837,7 @@
             where,
             final,
             outer,
-            to_near,
+            gradient,
         )
         return out
 
@@ -869,7 +869,7 @@
         return slope(far_gradient, "far_gradient", home, *wide)
 
     populations_after = lax.cond(is_far, place_far, place, outer)
-    sensitivity = lax.cond(is_far, slope_far, slope_near, from_near, from_far)
+    sensitivity = lax.cond(is_far, slope_far, slope_near, from_far, from_near)
     return (populations_after, sensitivity)
 
 

time: 33.5 us -> 31.9 us (0.952)
  the two profiles are of different devices: /device:TPU:13 before, /device:TPU:8 now
where the time goes in v4:
time: 31.9 us; the launch traced here: 31.8 us
  starting transfers between devices  13.6 us (43%)
  Pallas kernels  11.7 us (37%)
  waiting for transfers between devices  3.86 us (12%)
  between operations  1.42 us (4%)
  local copies, waits for them, and re-layouts  1.21 us (4%)
    pallas_call x8, Pallas kernels, call(): pl.pallas_call(kernel, out_shape=[shape for shape, _ in outs], in_specs=i...  11.7 us
    ppermute x4, starting transfers between devices, body(): sums.append(sums[-1] + lax.ppermute(sums[-1], 'block', swap))  6.94 us
    ppermute x2, starting transfers between devices, body(): from_near = lax.ppermute(to_near, 'block', near_pairs)  1.93 us
    ppermute x1, starting transfers between devices, body(): from_far = lax.ppermute(to_far, 'block', inner_pairs)  1.92 us
    ppermute x1, waiting for transfers between devices, body(): from_far = lax.ppermute(to_far, 'block', inner_pairs)  1.86 us
    ppermute x4, waiting for transfers between devices, body(): sums.append(sums[-1] + lax.ppermute(sums[-1], 'block', swap))  1.86 us
    ppermute x1, starting transfers between devices, body(): from_far = lax.ppermute(to_far, 'block', far_pairs)  1.08 us
    ppermute x1, starting transfers between devices, body(): far = lax.ppermute(own_far, 'block', far_pairs)  0.91 us
  transfers between devices with their start and end apart: 10, of which 4 were waited for; matrix products, arithmetic and copies ran while one was open for 2% of the time, Pallas kernels for 30%

profile of v4, /device:TPU:8, one launch (start us, length us, event | category | flops | bytes accessed | tf_op | source)
XLA Modules:
  0.0 31.8 jit_solution(17083741598251847038)
XLA Ops:
  0.6 1.3 %edge_planes.1 = (f32[23,2,8,128]{3,2,1,0:T(8,128)S(1)}, f32[23,2,8,128]{3,2,1,0:T(8,128)S(1)}, f32[19,12,8,128]{3,2,1,0:T(8,128)S(1)}, f32[12,8,128]{2,1,0:T(8,128)S(1)}) custom-call(f32[19,12,8,128]{3,2,1,0:T(8,128)} %pops_far.1, f32[12,8,128]{2,1,0:T(8,128)} %design.1, s32[12,8,128]{2,1,0:T(8,128)} %mask.1), custom_call_target="tpu_custom_call" | custom-call | flops 20000000 | bytes 1000000 | tf_op jit(solution)/shard_map/edge_planes/pallas_call | solution.py:674
  1.9 0.9 %collective-permute-start.4 = (f32[23,2,8,128]{3,2,1,0:T(8,128)S(1)}, f32[23,2,8,128]{3,2,1,0:T(8,128)S(1)}, u32[]{:S(2)}, u32[]{:S(2)}) collective-permute-start(f32[23,2,8,128]{3,2,1,0:T(8,128)S(1)} %get-tuple-element.80), channel_id=1, source_target_pairs={{0,15},{1,2},{2,1},{3,4},{4,3},{5,6},{6,5},{7,8},{8,7},{9,10},{10,... | collective-permute-start | bytes 565256 | tf_op jit(solution)/shard_map/ppermute | solution.py:699
  2.8 0.8 %collective-permute-start.5 = (f32[23,2,8,128]{3,2,1,0:T(8,128)S(1)}, f32[23,2,8,128]{3,2,1,0:T(8,128)S(1)}, u32[]{:S(2)}, u32[]{:S(2)}) collective-permute-start(f32[23,2,8,128]{3,2,1,0:T(8,128)S(1)} %get-tuple-element.81), channel_id=1, source_target_pairs={{0,1},{1,0},{2,3},{3,2},{4,5},{5,4},{6,7},{7,6},{8,9},{9,8},{10,11... | collective-permute-start | bytes 565256 | tf_op jit(solution)/shard_map/ppermute | solution.py:698
  3.6 2.5 %interior_steps.1 = (f32[49,8,128]{2,1,0:T(8,128)S(1)}, f32[49,8,128]{2,1,0:T(8,128)S(1)}, f32[19,12,8,128]{3,2,1,0:T(8,128)S(1)}, f32[16,12,8,128]{3,2,1,0:T(8,...) custom-call(f32[19,12,8,128]{3,2,1,0:T(8,128)S(1)} %get-tuple-elemen, ...), custom_call_target="tpu_custom_call" | custom-call | flops 120000000 | bytes 6000000 | tf_op jit(solution)/shard_map/interior_steps/pallas_call | solution.py:674
  6.2 1.1 %collective-permute-start.6 = (f32[49,8,128]{2,1,0:T(8,128)S(1)}, f32[49,8,128]{2,1,0:T(8,128)S(1)}, u32[]{:S(2)}, u32[]{:S(2)}) collective-permute-start(f32[49,8,128]{2,1,0:T(8,128)S(1)} %get-tuple-element.98), channel_id=1, source_target_pairs={{0,15},{1,2},{2,1},{3,4},{4,3},{5,6},{6,5},{7,8},{8,7},{9,10},{10,... | collective-permute-start | bytes 602120 | tf_op jit(solution)/shard_map/ppermute | solution.py:734
  7.2 0.6 %collective-permute-start.7 = (f32[49,8,128]{2,1,0:T(8,128)S(1)}, f32[49,8,128]{2,1,0:T(8,128)S(1)}, u32[]{:S(2)}, u32[]{:S(2)}) collective-permute-start(f32[49,8,128]{2,1,0:T(8,128)S(1)} %get-tuple-element.99), channel_id=1, source_target_pairs={{0,1},{1,0},{2,3},{3,2},{4,5},{5,4},{6,7},{7,6},{8,9},{9,8},{10,11... | collective-permute-start | bytes 602120 | tf_op jit(solution)/shard_map/ppermute | solution.py:733
  7.9 0.1 collective-permute-done.4.far
  8.0 0.0 collective-permute-done.5.near
  8.0 1.9 %boundary_steps.1 = (f32[19,12,8,128]{3,2,1,0:T(8,128)S(1)}, f32[16,18,8,128]{3,2,1,0:T(8,128)S(1)}, f32[18,8,128]{2,1,0:T(8,128)S(1)}, s32[18,8,128]{2,1,0:T(8,...) custom-call(f32[23,2,8,128]{3,2,1,0:T(8,128)S(1)} %collective-permut, ...), custom_call_target="tpu_custom_call" | custom-call | flops 160000000 | bytes 8000000 | tf_op jit(solution)/shard_map/boundary_steps/pallas_call | solution.py:674
  9.9 1.0 %collective-permute-start.8 = (f32[4,8,128]{2,1,0:T(8,128)S(1)}, f32[4,8,128]{2,1,0:T(8,128)S(1)}, u32[]{:S(2)}, u32[]{:S(2)}) collective-permute-start(f32[4,8,128]{2,1,0:T(8,128)S(1)} %get-tuple-element.100), channel_id=1, source_target_pairs={{0,1},{1,0},{2,3},{3,2},{4,5},{5,4},{6,7},{7,6},{8,9},{9,8},{10,11... | collective-permute-start | bytes 49160 | tf_op jit(solution)/shard_map/ppermute | solution.py:780
  10.9 0.8 %collective-permute-done.8 = f32[4,8,128]{2,1,0:T(8,128)S(1)} collective-permute-done((f32[4,8,128]{2,1,0:T(8,128)S(1)}, f32[4,8,128]{2,1,0:T(8,128)S(1)}, u32[]{:S(2)}, u32[]{:S(2)}) %collective-permute-start.8) | collective-permute-done | bytes 16416 | tf_op jit(solution)/shard_map/ppermute | solution.py:780
  11.7 2.0 %collective-permute-start.9 = (f32[4,8,128]{2,1,0:T(8,128)S(1)}, f32[4,8,128]{2,1,0:T(8,128)S(1)}, u32[]{:S(2)}, u32[]{:S(2)}) collective-permute-start(f32[4,8,128]{2,1,0:T(8,128)S(1)} %add.12), channel_id=1, source_target_pairs={{0,2},{1,3},{2,0},{3,1},{4,6},{5,7},{6,4},{7,5},{8,10},{9,11},{10,... | collective-permute-start | bytes 49160 | tf_op jit(solution)/shard_map/ppermute | solution.py:780
  13.7 1.3 %slot_counts.1 = s32[3]{0:T(128)S(1)} custom-call(s32[48]{0:T(128)S(1)} %copy-done), custom_call_target="tpu_custom_call" | custom-call | flops 400000000 | bytes 20000000 | tf_op jit(solution)/shard_map/slot_counts/pallas_call | solution.py:674
  15.0 0.6 %slice.3 = s32[1]{0:T(128)} slice(s32[3]{0:T(128)S(1)} %slot_counts.1), slice={[2:3]} | slice | bytes 8 | tf_op jit(solution)/shard_map/slice | solution.py:784
  16.2 0.0 collective-permute-done.9
  16.2 1.1 %collective-permute-start.10 = (f32[4,8,128]{2,1,0:T(8,128)S(1)}, f32[4,8,128]{2,1,0:T(8,128)S(1)}, u32[]{:S(2)}, u32[]{:S(2)}) collective-permute-start(f32[4,8,128]{2,1,0:T(8,128)S(1)} %add.13.summed), channel_id=1, source_target_pairs={{0,4},{1,5},{2,6},{3,7},{4,0},{5,1},{6,2},{7,3},{8,12},{9,13},{10,... | collective-permute-start | bytes 49160 | tf_op jit(solution)/shard_map/ppermute | solution.py:780
  17.4 0.0 collective-permute-done.6.from_far
  17.4 1.6 %outer_steps.1 = (f32[2,19,4,8,128]{4,3,2,1,0:T(8,128)S(1)}, f32[18,8,128]{2,1,0:T(8,128)S(1)}, f32[19,18,8,128]{3,2,1,0:T(8,128)S(1)}) custom-call(f32[16,18,8,128]{3,2,1,0:T(8,128)S(1)} %get-tuple-element.92.history, f32[18,8,128]{2,1,0:T(8,128)S(1)} %get-tuple-element.93.opens, s32[18,8,128]{2,1,0:T(8,128)S(1)} %get-tuple-element.94.fluid, ...), custom_call_target="tpu_custom_call" | custom-call | flops 240000000 | bytes 12000000 | tf_op jit(solution)/shard_map/outer_steps/pallas_call | solution.py:674
  19.0 1.0 %collective-permute-done.10 = f32[4,8,128]{2,1,0:T(8,128)S(1)} collective-permute-done((f32[4,8,128]{2,1,0:T(8,128)S(1)}, f32[4,8,128]{2,1,0:T(8,128)S(1)}, u32[]{:S(2)}, u32[]{:S(2)}) %collective-permute-start.10) | collective-permute-done | bytes 16416 | tf_op jit(solution)/shard_map/ppermute | solution.py:780
  20.0 2.9 %collective-permute-start.11 = (f32[4,8,128]{2,1,0:T(8,128)S(1)}, f32[4,8,128]{2,1,0:T(8,128)S(1)}, u32[]{:S(2)}, u32[]{:S(2)}) collective-permute-start(f32[4,8,128]{2,1,0:T(8,128)S(1)} %add.14.summed), channel_id=1, source_target_pairs={{0,8},{1,9},{2,10},{3,11},{4,12},{5,13},{6,14},{7,15},{8,0},{9,1},... | collective-permute-start | bytes 49160 | tf_op jit(solution)/shard_map/ppermute | solution.py:780
  22.9 1.6 %gradient_steps.1 = (f32[12,8,128]{2,1,0:T(8,128)S(1)}, f32[4,8,128]{2,1,0:T(8,128)S(1)}, f32[4,8,128]{2,1,0:T(8,128)S(1)}) custom-call(f32[16,18,8,128]{3,2,1,0:T(8,128)S(1)} %get-tuple-element.92.history, f32[18,8,128]{2,1,0:T(8,128)S(1)} %get-tuple-element.93.opens, s32[18,8,128]{2,1,0:T(8,128)S(1)} %get-tuple-element.95.words, ...), custom_call_target="tpu_custom_call" | custom-call | flops 120000000 | bytes 6000000 | tf_op jit(solution)/shard_map/gradient_steps/pallas_call | solution.py:674
  24.5 1.9 %collective-permute-start.12 = (f32[4,8,128]{2,1,0:T(8,128)S(1)}, f32[4,8,128]{2,1,0:T(8,128)S(1)}, u32[]{:S(2)}, u32[]{:S(2)}) collective-permute-start(f32[4,8,128]{2,1,0:T(8,128)S(1)} %get-tuple-element.105), channel_id=1, source_target_pairs={{1,2},{2,1},{3,4},{4,3},{5,6},{6,5},{7,8},{8,7},{9,10},{10,9},{11,... | collective-permute-start | bytes 49160 | tf_op jit(solution)/shard_map/ppermute | solution.py:823
  26.4 1.3 %collective-permute-start.13 = (f32[4,8,128]{2,1,0:T(8,128)S(1)}, f32[4,8,128]{2,1,0:T(8,128)S(1)}, u32[]{:S(2)}, u32[]{:S(2)}) collective-permute-start(f32[4,8,128]{2,1,0:T(8,128)S(1)} %get-tuple-element.106), channel_id=1, source_target_pairs={{0,1},{1,0},{2,3},{3,2},{4,5},{5,4},{6,7},{7,6},{8,9},{9,8},{10,11... | collective-permute-start | bytes 49160 | tf_op jit(solution)/shard_map/ppermute | solution.py:822
  27.7 0.8 %conditional.2 = (f32[19,20,8,128]{3,2,1,0:T(8,128)S(1)}) conditional(s32[]{:T(128)} %bitcast.2, (s32[3]{0:T(128)S(1)}, f32[19,12,8,128]{3,2,1,0:T(8,128)S(1)}, f32[2,19,4,8,128]{4,3,2,1,0:T(8,128)S(1)}, f32[12,8,128]{2,1,0:T(8,128)S(1)}) %tuple.20, (f32[19,12,8,128]{3,2,1,0:T(8,128)S(1)}, s32[3]{0:T(128)S(1)}, f32[12,8,128]{2,1,0:T(8,128)S(1)}) %tuple.21), branch_computations={%region_0.0_spmd, %region_1.0_spmd} | conditional | flops 80466944 | bytes 15206744 | solution.py:871
  27.7 0.8 %place_populations.2 = f32[19,20,8,128]{3,2,1,0:T(8,128)S(1)} custom-call(s32[3]{0:T(128)S(1)} %get-tuple-element.32.where, f32[19,12,8,128]{3,2,1,0:T(8,128)S(1)} %get-tuple-element.33.final, f32[2,19,4,8,128]{4,3,2,1,0:T(8,128)S(1)} %get-tuple-element.38.outer, f32[12,8,128]{2,1,0:T(8,128)S(1)} %get-tuple-element.39.later), custom_call_target="tpu_custom_call" | custom-call | flops 80000000 | bytes 4000000 | tf_op jit(solution)/shard_map/cond/branch_0_fun/place_populations/pallas_call | solution.py:674
  28.5 0.0 copy-start.1
  28.5 0.0 collective-permute-done.11
  28.5 1.9 %collective-permute-done.12 = f32[4,8,128]{2,1,0:T(8,128)S(1)} collective-permute-done((f32[4,8,128]{2,1,0:T(8,128)S(1)}, f32[4,8,128]{2,1,0:T(8,128)S(1)}, u32[]{:S(2)}, u32[]{:S(2)}) %collective-permute-start.12) | collective-permute-done | bytes 16416 | tf_op jit(solution)/shard_map/ppermute | solution.py:823
  30.4 0.7 %conditional.3 = (f32[20,8,128]{2,1,0:T(8,128)S(1)}) conditional(s32[]{:T(128)} %bitcast.2, (s32[3]{0:T(128)S(1)}, f32[4,8,128]{2,1,0:T(8,128)S(1)}, f32[12,8,128]{2,1,0:T(8,128)S(1)}, f32[4,8,128]{2,1,0:T(8,128)S(1)}, f32[4,8,128]{2,1,0:T(8,128)S(1)}) %tuple.22, (f32[12,8,128]{2,1,0:T(8,128)S(1)}, s32[3]{0:T(128)S(1)}, ...), branch_computations={%region_2.0_spmd, %region_3.0_spmd} | conditional | flops 20000000 | bytes 1393304 | solution.py:872
  30.4 0.7 %near_gradient.1 = f32[20,8,128]{2,1,0:T(8,128)S(1)} custom-call(s32[3]{0:T(128)S(1)} %get-tuple-element.43.where, f32[4,8,128]{2,1,0:T(8,128)S(1)} %get-tuple-element.44.drag, f32[12,8,128]{2,1,0:T(8,128)S(1)} %get-tuple-element.45.gradient, f32[4,8,128]{2,1,0:T(8,128)S(1)} %get-tuple-element.46.from_far, f32[4,8,128]{2,1,0:T(8,128)S(1)} %get-tuple-element.47.from_near), custom_call_target="tpu_custom_call" | custom-call | flops 20000000 | bytes 1000000 | tf_op jit(solution)/shard_map/cond/branch_0_fun/near_gradient/pallas_call | solution.py:674
  31.1 0.0 copy-start.2
  31.2 0.6 %copy-done.2 = f32[20,8,128]{2,1,0:T(8,128)} copy-done((f32[20,8,128]{2,1,0:T(8,128)}, f32[20,8,128]{2,1,0:T(8,128)S(1)}, u32[]{:S(2)}) %copy-start.2) | copy-done | bytes 81944
  (9 shorter events, 0.0 us)
Async XLA Ops:
  1.9 6.1 %collective-permute-start.4 = (f32[23,2,8,128]{3,2,1,0:T(8,128)S(1)}, f32[23,2,8,128]{3,2,1,0:T(8,128)S(1)}, u32[]{:S(2)}, u32[]{:S(2)}) collective-permute-start(f32[23,2,8,128]{3,2,1,0:T(8,128)S(1)} %get-tuple-element.80), channel_id=1, source_target_pairs={{0,15},{1,2},{2,1},{3,4},{4,3},{5,6},{6,5},{7,8},{8,7},{9,10},{10,... | collective-permute-start | bytes 565256 | tf_op jit(solution)/shard_map/ppermute | solution.py:699
  2.8 5.2 %collective-permute-start.5 = (f32[23,2,8,128]{3,2,1,0:T(8,128)S(1)}, f32[23,2,8,128]{3,2,1,0:T(8,128)S(1)}, u32[]{:S(2)}, u32[]{:S(2)}) collective-permute-start(f32[23,2,8,128]{3,2,1,0:T(8,128)S(1)} %get-tuple-element.81), channel_id=1, source_target_pairs={{0,1},{1,0},{2,3},{3,2},{4,5},{5,4},{6,7},{7,6},{8,9},{9,8},{10,11... | collective-permute-start | bytes 565256 | tf_op jit(solution)/shard_map/ppermute | solution.py:698
  6.2 11.2 %collective-permute-start.6 = (f32[49,8,128]{2,1,0:T(8,128)S(1)}, f32[49,8,128]{2,1,0:T(8,128)S(1)}, u32[]{:S(2)}, u32[]{:S(2)}) collective-permute-start(f32[49,8,128]{2,1,0:T(8,128)S(1)} %get-tuple-element.98), channel_id=1, source_target_pairs={{0,15},{1,2},{2,1},{3,4},{4,3},{5,6},{6,5},{7,8},{8,7},{9,10},{10,... | collective-permute-start | bytes 602120 | tf_op jit(solution)/shard_map/ppermute | solution.py:734
  7.2 10.1 %collective-permute-start.7 = (f32[49,8,128]{2,1,0:T(8,128)S(1)}, f32[49,8,128]{2,1,0:T(8,128)S(1)}, u32[]{:S(2)}, u32[]{:S(2)}) collective-permute-start(f32[49,8,128]{2,1,0:T(8,128)S(1)} %get-tuple-element.99), channel_id=1, source_target_pairs={{0,1},{1,0},{2,3},{3,2},{4,5},{5,4},{6,7},{7,6},{8,9},{9,8},{10,11... | collective-permute-start | bytes 602120 | tf_op jit(solution)/shard_map/ppermute | solution.py:733
  8.0 5.7 %copy-start = (s32[48]{0:T(128)S(1)}, s32[48]{0:T(128)}, u32[]{:S(2)}) copy-start(s32[48]{0:T(128)} %owner.1) | copy-start | bytes 580
  9.9 1.8 %collective-permute-start.8 = (f32[4,8,128]{2,1,0:T(8,128)S(1)}, f32[4,8,128]{2,1,0:T(8,128)S(1)}, u32[]{:S(2)}, u32[]{:S(2)}) collective-permute-start(f32[4,8,128]{2,1,0:T(8,128)S(1)} %get-tuple-element.100), channel_id=1, source_target_pairs={{0,1},{1,0},{2,3},{3,2},{4,5},{5,4},{6,7},{7,6},{8,9},{9,8},{10,11... | collective-permute-start | bytes 49160 | tf_op jit(solution)/shard_map/ppermute | solution.py:780
  11.7 4.5 %collective-permute-start.9 = (f32[4,8,128]{2,1,0:T(8,128)S(1)}, f32[4,8,128]{2,1,0:T(8,128)S(1)}, u32[]{:S(2)}, u32[]{:S(2)}) collective-permute-start(f32[4,8,128]{2,1,0:T(8,128)S(1)} %add.12), channel_id=1, source_target_pairs={{0,2},{1,3},{2,0},{3,1},{4,6},{5,7},{6,4},{7,5},{8,10},{9,11},{10,... | collective-permute-start | bytes 49160 | tf_op jit(solution)/shard_map/ppermute | solution.py:780
  16.2 3.8 %collective-permute-start.10 = (f32[4,8,128]{2,1,0:T(8,128)S(1)}, f32[4,8,128]{2,1,0:T(8,128)S(1)}, u32[]{:S(2)}, u32[]{:S(2)}) collective-permute-start(f32[4,8,128]{2,1,0:T(8,128)S(1)} %add.13.summed), channel_id=1, source_target_pairs={{0,4},{1,5},{2,6},{3,7},{4,0},{5,1},{6,2},{7,3},{8,12},{9,13},{10,... | collective-permute-start | bytes 49160 | tf_op jit(solution)/shard_map/ppermute | solution.py:780
  20.0 8.5 %collective-permute-start.11 = (f32[4,8,128]{2,1,0:T(8,128)S(1)}, f32[4,8,128]{2,1,0:T(8,128)S(1)}, u32[]{:S(2)}, u32[]{:S(2)}) collective-permute-start(f32[4,8,128]{2,1,0:T(8,128)S(1)} %add.14.summed), channel_id=1, source_target_pairs={{0,8},{1,9},{2,10},{3,11},{4,12},{5,13},{6,14},{7,15},{8,0},{9,1},... | collective-permute-start | bytes 49160 | tf_op jit(solution)/shard_map/ppermute | solution.py:780
  24.5 6.0 %collective-permute-start.12 = (f32[4,8,128]{2,1,0:T(8,128)S(1)}, f32[4,8,128]{2,1,0:T(8,128)S(1)}, u32[]{:S(2)}, u32[]{:S(2)}) collective-permute-start(f32[4,8,128]{2,1,0:T(8,128)S(1)} %get-tuple-element.105), channel_id=1, source_target_pairs={{1,2},{2,1},{3,4},{4,3},{5,6},{6,5},{7,8},{8,7},{9,10},{10,9},{11,... | collective-permute-start | bytes 49160 | tf_op jit(solution)/shard_map/ppermute | solution.py:823
  26.4 4.0 %collective-permute-start.13 = (f32[4,8,128]{2,1,0:T(8,128)S(1)}, f32[4,8,128]{2,1,0:T(8,128)S(1)}, u32[]{:S(2)}, u32[]{:S(2)}) collective-permute-start(f32[4,8,128]{2,1,0:T(8,128)S(1)} %get-tuple-element.106), channel_id=1, source_target_pairs={{0,1},{1,0},{2,3},{3,2},{4,5},{5,4},{6,7},{7,6},{8,9},{9,8},{10,11... | collective-permute-start | bytes 49160 | tf_op jit(solution)/shard_map/ppermute | solution.py:822
  28.5 2.6 %copy-start.1 = (f32[19,20,8,128]{3,2,1,0:T(8,128)}, f32[19,20,8,128]{3,2,1,0:T(8,128)S(1)}, u32[]{:S(2)}) copy-start(f32[19,20,8,128]{3,2,1,0:T(8,128)S(1)} %get-tuple-element.107) | copy-start | bytes 4669444
  31.1 0.6 %copy-start.2 = (f32[20,8,128]{2,1,0:T(8,128)}, f32[20,8,128]{2,1,0:T(8,128)S(1)}, u32[]{:S(2)}) copy-start(f32[20,8,128]{2,1,0:T(8,128)S(1)} %get-tuple-element.108) | copy-start | bytes 245764

commit v5 on v4

--- a/solution.py
+++ b/solution.py
@@ -412,8 +412,7 @@
     receive(1, odd)
     both(2, functools.partial(advance, 2, odd, even))
     receive(2, even)
-    drag[...] = jnp.zeros_like(drag)
-    drag[0] = inner_drag[...]
+    drag[...] = inner_drag[...]
 
     def finish(index, place, ahead):
         state = pull(even, index, words[index])
@@ -422,7 +421,7 @@
         here = fluid[index] > 0
         for m in range(19):
             final[m, index - HALO] = jnp.where(here, state[m], inner_final[m, index - HALO])
-        drag[1 + place] += jnp.where(here, drag_terms(flow, opens[index]), 0.0)
+        drag[...] += jnp.where(here, drag_terms(flow, opens[index]), 0.0)
 
     both(3, finish)
     for copy in copies:
@@ -750,7 +749,7 @@
         planes(span),
         planes(span, dtype=jnp.int32),
         planes(span, dtype=jnp.int32),
-        planes(1 + STEPS),
+        planes(),
         planes(19, span),
         planes(19, span),
     )
@@ -773,13 +772,8 @@
         inner_drag,
     )
 
-    sums = [drag]
-    distance = 1
-    while distance < count:
-        swap = [(i, i ^ distance) for i in range(count)]
-        sums.append(sums[-1] + lax.ppermute(sums[-1], "block", swap))
-        distance *= 2
-    drag = sums[-1]
+    copies = jnp.broadcast_to(drag[None], (count,) + drag.shape)
+    drag = lax.all_to_all(copies, "block", 0, 0)
 
     is_far = where[2] > 0
     outer, share, odd = call(
@@ -800,7 +794,7 @@
         near,
         from_far,
         from_near,
-        sums[2],
+        inner_drag,
         is_far.astype(jnp.int32).reshape(1),
     )
     gradient, to_near, to_far = call(
@@ -817,7 +811,7 @@
         share,
         odd,
         marked,
-        sums[3],
+        inner_drag,
     )
     from_near = lax.ppermute(to_near, "block", near_pairs)
     from_far = lax.ppermute(to_far, "block", inner_pairs)

time: 31.9 us -> 38.1 us (1.19)
  the two profiles are of different devices: /device:TPU:8 before, /device:TPU:0 now
where the time goes in v5:
time: 38.1 us; the launch traced here: 37.6 us
  starting transfers between devices  15.7 us (41%)
  Pallas kernels  13.9 us (36%)
  local copies, waits for them, and re-layouts  6.41 us (17%)
  between operations  1.51 us (4%)
    pallas_call x8, Pallas kernels, call(): pl.pallas_call(kernel, out_shape=[shape for shape, _ in outs], in_specs=i...  13.9 us
    ppermute x1, starting transfers between devices, body(): far = lax.ppermute(own_far, 'block', far_pairs)  5.51 us
    all_to_all x1, starting transfers between devices, body(): drag = lax.all_to_all(copies, 'block', 0, 0)  5.49 us
    unnamed x20, local copies, waits for them, and re-layouts  4.55 us
    ppermute x2, starting transfers between devices, body(): from_near = lax.ppermute(to_near, 'block', near_pairs)  3.3 us
    slice x1, local copies, waits for them, and re-layouts, body(): is_far = where[2] > 0  1.23 us
  transfers between devices with their start and end apart: 7, of which 0 were waited for; matrix products, arithmetic and copies ran while one was open for 5% of the time, Pallas kernels for 31%

profile of v5, /device:TPU:0, one launch (start us, length us, event | category | flops | bytes accessed | tf_op | source)
XLA Modules:
  0.0 37.6 jit_solution(7089614642305371729)
XLA Ops:
  0.6 1.3 %edge_planes.1 = (f32[23,2,8,128]{3,2,1,0:T(8,128)S(1)}, f32[23,2,8,128]{3,2,1,0:T(8,128)S(1)}, f32[19,12,8,128]{3,2,1,0:T(8,128)S(1)}, f32[12,8,128]{2,1,0:T(8,128)S(1)}) custom-call(f32[19,12,8,128]{3,2,1,0:T(8,128)} %pops_far.1, f32[12,8,128]{2,1,0:T(8,128)} %design.1, s32[12,8,128]{2,1,0:T(8,128)} %mask.1), custom_call_target="tpu_custom_call" | custom-call | flops 20000000 | bytes 1000000 | tf_op jit(solution)/shard_map/edge_planes/pallas_call | solution.py:673
  1.9 5.5 %collective-permute-start.4 = (f32[23,2,8,128]{3,2,1,0:T(8,128)S(1)}, f32[23,2,8,128]{3,2,1,0:T(8,128)S(1)}, u32[]{:S(2)}, u32[]{:S(2)}) collective-permute-start(f32[23,2,8,128]{3,2,1,0:T(8,128)S(1)} %get-tuple-element.80), channel_id=1, source_target_pairs={{0,15},{1,2},{2,1},{3,4},{4,3},{5,6},{6,5},{7,8},{8,7},{9,10},{10,... | collective-permute-start | bytes 565256 | tf_op jit(solution)/shard_map/ppermute | solution.py:698
  7.4 0.0 collective-permute-start.5
  7.4 3.3 %interior_steps.1 = (f32[49,8,128]{2,1,0:T(8,128)}, f32[49,8,128]{2,1,0:T(8,128)}, f32[19,12,8,128]{3,2,1,0:T(8,128)S(1)}, f32[16,12,8,128]{3,2,1,0:T(8,128)S(1)...) custom-call(f32[19,12,8,128]{3,2,1,0:T(8,128)S(1)} %get-tuple-elemen, ...), custom_call_target="tpu_custom_call" | custom-call | flops 120000000 | bytes 6000000 | tf_op jit(solution)/shard_map/interior_steps/pallas_call | solution.py:673
  10.7 0.8 %collective-permute-start.6 = (f32[49,8,128]{2,1,0:T(8,128)}, f32[49,8,128]{2,1,0:T(8,128)S(1)}, u32[]{:S(2)}, u32[]{:S(2)}) collective-permute-start(f32[49,8,128]{2,1,0:T(8,128)} %get-tuple-element.98), channel_id=1, source_target_pairs={{0,15},{1,2},{2,1},{3,4},{4,3},{5,6},{6,5},{7,8},{8,7},{9,10},{10,... | collective-permute-start | bytes 602120 | tf_op jit(solution)/shard_map/ppermute | solution.py:733
  11.5 0.0 collective-permute-start.7
  11.5 0.0 collective-permute-done.4.far
  11.5 0.0 collective-permute-done.5.near
  11.5 2.8 %boundary_steps.1 = (f32[19,12,8,128]{3,2,1,0:T(8,128)}, f32[16,18,8,128]{3,2,1,0:T(8,128)S(1)}, f32[18,8,128]{2,1,0:T(8,128)S(1)}, s32[18,8,128]{2,1,0:T(8,128)...) custom-call(f32[23,2,8,128]{3,2,1,0:T(8,128)S(1)} %collective-permut, ...), custom_call_target="tpu_custom_call" | custom-call | flops 160000000 | bytes 8000000 | tf_op jit(solution)/shard_map/boundary_steps/pallas_call | solution.py:673
  14.4 0.0 copy-start
  14.4 1.1 %copy-done = f32[19,18,8,128]{3,2,1,0:T(8,128)} copy-done((f32[19,18,8,128]{3,2,1,0:T(8,128)}, f32[19,18,8,128]{3,2,1,0:T(8,128)S(1)}, u32[]{:S(2)}) %copy-start) | copy-done | bytes 1400856
  15.5 0.6 %copy-done.2 = s32[18,8,128]{2,1,0:T(8,128)} copy-done((s32[18,8,128]{2,1,0:T(8,128)}, s32[18,8,128]{2,1,0:T(8,128)S(1)}, u32[]{:S(2)}) %copy-start.2) | copy-done | bytes 73752
  16.1 0.6 %broadcast_in_dim.2 = f32[16,8,128]{2,1,0:T(8,128)} broadcast(f32[8,128]{1,0:T(8,128)S(1)} %get-tuple-element.104), dimensions={1,2} | broadcast | bytes 69632 | tf_op jit(solution)/shard_map/broadcast_in_dim | solution.py:775
  16.7 5.5 %all-to-all-start = ((f32[16,8,128]{2,1,0:T(8,128)}), f32[16,8,128]{2,1,0:T(8,128)}, u32[]{:S(2)}, u32[]{:S(2)}) async-start(f32[16,8,128]{2,1,0:T(8,128)} %broadcast_in_dim.2), calls=%async_computation | async-start | bytes 131072 | tf_op jit(solution)/shard_map/all_to_all | solution.py:776
  22.2 0.0 copy-start.6
  22.2 0.6 %copy-done.6 = s32[48]{0:T(128)S(1)} copy-done((s32[48]{0:T(128)S(1)}, s32[48]{0:T(128)}, u32[]{:S(2)}) %copy-start.6) | copy-done | bytes 216
  22.9 1.2 %slot_counts.1 = s32[3]{0:T(128)} custom-call(s32[48]{0:T(128)S(1)} %copy-done.6), custom_call_target="tpu_custom_call" | custom-call | flops 400000000 | bytes 20000000 | tf_op jit(solution)/shard_map/slot_counts/pallas_call | solution.py:673
  24.1 1.2 %slice.3 = s32[1]{0:T(128)} slice(s32[3]{0:T(128)} %slot_counts.1), slice={[2:3]} | slice | bytes 8 | tf_op jit(solution)/shard_map/slice | solution.py:778
  26.0 0.0 copy-start.3
  26.0 0.9 %copy-done.3 = s32[18,8,128]{2,1,0:T(8,128)S(1)} copy-done((s32[18,8,128]{2,1,0:T(8,128)S(1)}, s32[18,8,128]{2,1,0:T(8,128)}, u32[]{:S(2)}) %copy-start.3) | copy-done | bytes 73752
  26.9 0.7 %copy-done.5 = f32[8,128]{1,0:T(8,128)S(1)} copy-done((f32[8,128]{1,0:T(8,128)S(1)}, f32[8,128]{1,0:T(8,128)}, u32[]{:S(2)}) %copy-start.5) | copy-done | bytes 4120
  27.6 1.6 %outer_steps.1 = (f32[2,19,4,8,128]{4,3,2,1,0:T(8,128)S(1)}, f32[18,8,128]{2,1,0:T(8,128)S(1)}, f32[19,18,8,128]{3,2,1,0:T(8,128)S(1)}) custom-call(f32[16,18,8,128]{3,2,1,0:T(8,128)S(1)} %get-tuple-element.92.history, f32[18,8,128]{2,1,0:T(8,128)S(1)} %get-tuple-element.93.opens, s32[18,8,128]{2,1,0:T(8,128)S(1)} %copy-done.3, ...), custom_call_target="tpu_custom_call" | custom-call | flops 240000000 | bytes 12000000 | tf_op jit(solution)/shard_map/outer_steps/pallas_call | solution.py:673
  29.2 1.6 %gradient_steps.1 = (f32[12,8,128]{2,1,0:T(8,128)S(1)}, f32[4,8,128]{2,1,0:T(8,128)S(1)}, f32[4,8,128]{2,1,0:T(8,128)S(1)}) custom-call(f32[16,18,8,128]{3,2,1,0:T(8,128)S(1)} %get-tuple-element.92.history, f32[18,8,128]{2,1,0:T(8,128)S(1)} %get-tuple-element.93.opens, s32[18,8,128]{2,1,0:T(8,128)S(1)} %get-tuple-element.95.words, ...), custom_call_target="tpu_custom_call" | custom-call | flops 120000000 | bytes 6000000 | tf_op jit(solution)/shard_map/gradient_steps/pallas_call | solution.py:673
  30.8 0.7 %collective-permute-start.8 = (f32[4,8,128]{2,1,0:T(8,128)S(1)}, f32[4,8,128]{2,1,0:T(8,128)S(1)}, u32[]{:S(2)}, u32[]{:S(2)}) collective-permute-start(f32[4,8,128]{2,1,0:T(8,128)S(1)} %get-tuple-element.105), channel_id=1, source_target_pairs={{1,2},{2,1},{3,4},{4,3},{5,6},{6,5},{7,8},{8,7},{9,10},{10,9},{11,... | collective-permute-start | bytes 49160 | tf_op jit(solution)/shard_map/ppermute | solution.py:817
  31.5 3.3 %collective-permute-start.9 = (f32[4,8,128]{2,1,0:T(8,128)S(1)}, f32[4,8,128]{2,1,0:T(8,128)S(1)}, u32[]{:S(2)}, u32[]{:S(2)}) collective-permute-start(f32[4,8,128]{2,1,0:T(8,128)S(1)} %get-tuple-element.106), channel_id=1, source_target_pairs={{0,1},{1,0},{2,3},{3,2},{4,5},{5,4},{6,7},{7,6},{8,9},{9,8},{10,11... | collective-permute-start | bytes 49160 | tf_op jit(solution)/shard_map/ppermute | solution.py:816
  34.8 0.9 %conditional.2 = (f32[19,20,8,128]{3,2,1,0:T(8,128)S(1)}) conditional(s32[]{:T(128)} %bitcast.2, (s32[3]{0:T(128)}, f32[19,12,8,128]{3,2,1,0:T(8,128)S(1)}, f32[2,19,4,8,128]{4,3,2,1,0:T(8,128)S(1)}, f32[12,8,128]{2,1,0:T(8,128)S(1)}) %tuple.29, (f32[19,12,8,128]{3,2,1,0:T(8,128)S(1)}, s32[3]{0:T(128)}, f32[12,8,128]{2,1,0:T(8,128)S(1)}) %tuple.30), branch_computations={%region_0.0_spmd, %region_1.0_spmd} | conditional | flops 80466944 | bytes 15206744 | solution.py:865
  34.8 0.9 %place_populations.2 = f32[19,20,8,128]{3,2,1,0:T(8,128)S(1)} custom-call(s32[3]{0:T(128)} %get-tuple-element.32.where, f32[19,12,8,128]{3,2,1,0:T(8,128)S(1)} %get-tuple-element.33.final, f32[2,19,4,8,128]{4,3,2,1,0:T(8,128)S(1)} %get-tuple-element.38.outer, f32[12,8,128]{2,1,0:T(8,128)S(1)} %get-tuple-element.39.later), custom_call_target="tpu_custom_call" | custom-call | flops 80000000 | bytes 4000000 | tf_op jit(solution)/shard_map/cond/branch_0_fun/place_populations/pallas_call | solution.py:673
  35.7 0.0 copy-start.8
  35.8 1.1 %conditional.3 = (f32[20,8,128]{2,1,0:T(8,128)S(1)}) conditional(s32[]{:T(128)} %bitcast.2, (s32[3]{0:T(128)}, f32[16,8,128]{2,1,0:T(8,128)}, f32[12,8,128]{2,1,0:T(8,128)S(1)}, f32[4,8,128]{2,1,0:T(8,128)S(1)}, f32[4,8,128]{2,1,0:T(8,128)S(1)}) %tuple.22, (f32[12,8,128]{2,1,0:T(8,128)S(1)}, s32[3]{0:T(128)}, f32[16,8,128]{2,1,0:T(8,128)}) %tuple.23), branch_computations={%region_2.0_spmd, %region_3.0_spmd} | conditional | flops 20000000 | bytes 1393304 | solution.py:866
  35.8 1.1 %near_gradient.1 = f32[20,8,128]{2,1,0:T(8,128)S(1)} custom-call(s32[3]{0:T(128)} %get-tuple-element.43.where, f32[16,8,128]{2,1,0:T(8,128)} %get-tuple-element.44.drag, f32[12,8,128]{2,1,0:T(8,128)S(1)} %get-tuple-element.45.gradient, f32[4,8,128]{2,1,0:T(8,128)S(1)} %get-tuple-element.46.from_far, f32[4,8,128]{2,1,0:T(8,128)S(1)} %get-tuple-element.47.from_near), custom_call_target="tpu_custom_call" | custom-call | flops 20000000 | bytes 1000000 | tf_op jit(solution)/shard_map/cond/branch_0_fun/near_gradient/pallas_call | solution.py:673
  36.9 0.0 copy-start.9
  36.9 0.6 %copy-done.9 = f32[20,8,128]{2,1,0:T(8,128)} copy-done((f32[20,8,128]{2,1,0:T(8,128)}, f32[20,8,128]{2,1,0:T(8,128)S(1)}, u32[]{:S(2)}) %copy-start.9) | copy-done | bytes 81944
  (14 shorter events, 0.0 us)
Async XLA Ops:
  1.9 9.6 %collective-permute-start.4 = (f32[23,2,8,128]{3,2,1,0:T(8,128)S(1)}, f32[23,2,8,128]{3,2,1,0:T(8,128)S(1)}, u32[]{:S(2)}, u32[]{:S(2)}) collective-permute-start(f32[23,2,8,128]{3,2,1,0:T(8,128)S(1)} %get-tuple-element.80), channel_id=1, source_target_pairs={{0,15},{1,2},{2,1},{3,4},{4,3},{5,6},{6,5},{7,8},{8,7},{9,10},{10,... | collective-permute-start | bytes 565256 | tf_op jit(solution)/shard_map/ppermute | solution.py:698
  7.4 4.1 %collective-permute-start.5 = (f32[23,2,8,128]{3,2,1,0:T(8,128)S(1)}, f32[23,2,8,128]{3,2,1,0:T(8,128)S(1)}, u32[]{:S(2)}, u32[]{:S(2)}) collective-permute-start(f32[23,2,8,128]{3,2,1,0:T(8,128)S(1)} %get-tuple-element.81), channel_id=1, source_target_pairs={{0,1},{1,0},{2,3},{3,2},{4,5},{5,4},{6,7},{7,6},{8,9},{9,8},{10,11... | collective-permute-start | bytes 565256 | tf_op jit(solution)/shard_map/ppermute | solution.py:697
  10.7 3.6 %copy-start.4 = (f32[8,128]{1,0:T(8,128)}, f32[8,128]{1,0:T(8,128)S(1)}, u32[]{:S(2)}) copy-start(f32[8,128]{1,0:T(8,128)S(1)} %get-tuple-element.90.inner_drag.summed) | copy-start | bytes 12292
  10.7 15.3 %collective-permute-start.6 = (f32[49,8,128]{2,1,0:T(8,128)}, f32[49,8,128]{2,1,0:T(8,128)S(1)}, u32[]{:S(2)}, u32[]{:S(2)}) collective-permute-start(f32[49,8,128]{2,1,0:T(8,128)} %get-tuple-element.98), channel_id=1, source_target_pairs={{0,15},{1,2},{2,1},{3,4},{4,3},{5,6},{6,5},{7,8},{8,7},{9,10},{10,... | collective-permute-start | bytes 602120 | tf_op jit(solution)/shard_map/ppermute | solution.py:733
  11.5 14.5 %collective-permute-start.7 = (f32[49,8,128]{2,1,0:T(8,128)}, f32[49,8,128]{2,1,0:T(8,128)S(1)}, u32[]{:S(2)}, u32[]{:S(2)}) collective-permute-start(f32[49,8,128]{2,1,0:T(8,128)} %get-tuple-element.99), channel_id=1, source_target_pairs={{0,1},{1,0},{2,3},{3,2},{4,5},{5,4},{6,7},{7,6},{8,9},{9,8},{10,11... | collective-permute-start | bytes 602120 | tf_op jit(solution)/shard_map/ppermute | solution.py:732
  14.4 1.1 %copy-start = (f32[19,18,8,128]{3,2,1,0:T(8,128)}, f32[19,18,8,128]{3,2,1,0:T(8,128)S(1)}, u32[]{:S(2)}) copy-start(f32[19,18,8,128]{3,2,1,0:T(8,128)S(1)} %get-tuple-element.97.odd_state) | copy-start | bytes 4202500
  15.5 0.6 %copy-start.2 = (s32[18,8,128]{2,1,0:T(8,128)}, s32[18,8,128]{2,1,0:T(8,128)S(1)}, u32[]{:S(2)}) copy-start(s32[18,8,128]{2,1,0:T(8,128)S(1)} %get-tuple-element.94.fluid) | copy-start | bytes 221188
  16.7 19.0 %all-to-all-start = ((f32[16,8,128]{2,1,0:T(8,128)}), f32[16,8,128]{2,1,0:T(8,128)}, u32[]{:S(2)}, u32[]{:S(2)}) async-start(f32[16,8,128]{2,1,0:T(8,128)} %broadcast_in_dim.2), calls=%async_computation | async-start | bytes 131072 | tf_op jit(solution)/shard_map/all_to_all | solution.py:776
  22.2 0.7 %copy-start.6 = (s32[48]{0:T(128)S(1)}, s32[48]{0:T(128)}, u32[]{:S(2)}) copy-start(s32[48]{0:T(128)} %owner.1) | copy-start | bytes 580
  22.9 3.2 %copy-start.1 = (f32[19,18,8,128]{3,2,1,0:T(8,128)S(1)}, f32[19,18,8,128]{3,2,1,0:T(8,128)}, u32[]{:S(2)}) copy-start(f32[19,18,8,128]{3,2,1,0:T(8,128)} %copy-done) | copy-start | bytes 4202500
  26.0 0.9 %copy-start.3 = (s32[18,8,128]{2,1,0:T(8,128)S(1)}, s32[18,8,128]{2,1,0:T(8,128)}, u32[]{:S(2)}) copy-start(s32[18,8,128]{2,1,0:T(8,128)} %copy-done.2) | copy-start | bytes 221188
  26.9 0.7 %copy-start.5 = (f32[8,128]{1,0:T(8,128)S(1)}, f32[8,128]{1,0:T(8,128)}, u32[]{:S(2)}) copy-start(f32[8,128]{1,0:T(8,128)} %copy-done.4) | copy-start | bytes 12292
  29.2 5.6 %copy-start.7 = (f32[19,12,8,128]{3,2,1,0:T(8,128)S(1)}, f32[19,12,8,128]{3,2,1,0:T(8,128)}, u32[]{:S(2)}) copy-start(f32[19,12,8,128]{3,2,1,0:T(8,128)} %get-tuple-element.91) | copy-start | bytes 2801668
  30.8 4.9 %collective-permute-start.8 = (f32[4,8,128]{2,1,0:T(8,128)S(1)}, f32[4,8,128]{2,1,0:T(8,128)S(1)}, u32[]{:S(2)}, u32[]{:S(2)}) collective-permute-start(f32[4,8,128]{2,1,0:T(8,128)S(1)} %get-tuple-element.105), channel_id=1, source_target_pairs={{1,2},{2,1},{3,4},{4,3},{5,6},{6,5},{7,8},{8,7},{9,10},{10,9},{11,... | collective-permute-start | bytes 49160 | tf_op jit(solution)/shard_map/ppermute | solution.py:817
  31.5 4.3 %collective-permute-start.9 = (f32[4,8,128]{2,1,0:T(8,128)S(1)}, f32[4,8,128]{2,1,0:T(8,128)S(1)}, u32[]{:S(2)}, u32[]{:S(2)}) collective-permute-start(f32[4,8,128]{2,1,0:T(8,128)S(1)} %get-tuple-element.106), channel_id=1, source_target_pairs={{0,1},{1,0},{2,3},{3,2},{4,5},{5,4},{6,7},{7,6},{8,9},{9,8},{10,11... | collective-permute-start | bytes 49160 | tf_op jit(solution)/shard_map/ppermute | solution.py:816
  35.7 1.2 %copy-start.8 = (f32[19,20,8,128]{3,2,1,0:T(8,128)}, f32[19,20,8,128]{3,2,1,0:T(8,128)S(1)}, u32[]{:S(2)}) copy-start(f32[19,20,8,128]{3,2,1,0:T(8,128)S(1)} %get-tuple-element.107) | copy-start | bytes 4669444
  36.9 0.6 %copy-start.9 = (f32[20,8,128]{2,1,0:T(8,128)}, f32[20,8,128]{2,1,0:T(8,128)S(1)}, u32[]{:S(2)}) copy-start(f32[20,8,128]{2,1,0:T(8,128)S(1)} %get-tuple-element.108) | copy-start | bytes 245764

commit v6 on v4

--- a/solution.py
+++ b/solution.py
@@ -147,15 +147,24 @@
     return jnp.where(here > 0, word, 0)
 
 
-def each_plane(low, high, body):
-    def two(index, carry):
-        body(low + 2 * index)
-        body(low + 2 * index + 1)
+def run(bodies):
+    for body in bodies:
+        next(body)
+    for body in bodies:
+        next(body, None)
+
+
+def each_plane(low, high, body, width=2):
+    groups = (high - low) // width
+
+    def group(index, carry):
+        run([body(low + width * index + place) for place in range(width)])
         return carry
 
-    lax.fori_loop(0, (high - low) // 2, two, 0)
-    if (high - low) % 2:
-        body(high - 1)
+    lax.fori_loop(0, groups, group, 0)
+    rest = range(low + groups * width, high)
+    if rest:
+        run([body(plane) for plane in rest])
 
 
 def is_fluid_rate(mark):
@@ -254,30 +263,39 @@
     up = parity()
 
     def start(plane):
-        fluid[plane], open_rate = is_fluid_rate(marked[plane])
-        opens[plane] = open_rate
+        is_fluid, open_rate = is_fluid_rate(marked[plane])
         state = [pops[m, plane] for m in range(19)]
         density, flow = density_velocity(state)
+        collided = collide(state, density, flow, open_rate)
+        yield
+        fluid[plane] = is_fluid
+        opens[plane] = open_rate
         remember(history, 0, plane, density, flow)
-        store(even, plane, collide(state, density, flow, open_rate))
+        store(even, plane, collided)
 
     def link(plane):
-        words[plane] = link_word(fluid[plane - 1], fluid[plane], fluid[plane + 1])
+        word = link_word(fluid[plane - 1], fluid[plane], fluid[plane + 1])
+        yield
+        words[plane] = word
 
     def advance(step, source, target, plane):
         state = pull(source, plane, words[plane])
         density, flow = density_velocity(state)
+        collided = collide(state, density, flow, opens[plane])
+        yield
         remember(history, step, plane, density, flow)
-        store(target, plane, collide(state, density, flow, opens[plane]))
+        store(target, plane, collided)
 
     def finish(plane):
         state = pull(even, plane, words[plane])
         density, flow = density_velocity(state)
+        here = fluid[plane] > 0
+        placed = [jnp.where(here, state[m], pops[m, plane]) for m in range(19)]
+        part = jnp.where(here, drag_terms(flow, opens[plane]), 0.0)
+        yield
         remember(history, 3, plane, density, flow)
-        here = fluid[plane] > 0
-        for m in range(19):
-            final[m, plane] = jnp.where(here, state[m], pops[m, plane])
-        drag[...] += jnp.where(here, drag_terms(flow, opens[plane]), 0.0)
+        store(final, plane, placed)
+        drag[...] += part
 
     def keep(step, source):
         for m in range(19):
@@ -371,14 +389,19 @@
         for slot in range(5):
             even[AHEAD[slot] + ahead, ahead * (span - 1)] = side[20 + slot // 2, slot % 2]
 
+    def begin(plane, ahead, side):
+        index = plane + 1 + ahead * (home + RAW)
+        is_fluid, open_rate = is_fluid_rate(side[19, plane])
+        state = [side[m, plane] for m in range(19)]
+        density, flow = density_velocity(state)
+        collided = collide(state, density, flow, open_rate)
+        yield
+        fluid[index] = is_fluid
+        opens[index] = open_rate
+        store(even, index, collided)
+
     def start(plane, carry):
-        for ahead, side in sides:
-            index = plane + 1 + ahead * (home + RAW)
-            fluid[index], open_rate = is_fluid_rate(side[19, plane])
-            opens[index] = open_rate
-            state = [side[m, plane] for m in range(19)]
-            density, flow = density_velocity(state)
-            store(even, index, collide(state, density, flow, open_rate))
+        run([begin(plane, *side) for side in sides])
         return carry
 
     lax.fori_loop(0, RAW, start, 0)
@@ -391,20 +414,23 @@
 
     def both(step, body):
         def two(place, carry):
-            body(step + place, place, 0)
-            body(span - 3 - step + place, place, 1)
+            run([body(step + place, place, 0), body(span - 3 - step + place, place, 1)])
             return carry
 
         lax.fori_loop(0, 3, two, 0)
 
     def link(index, place, ahead):
-        words[index] = link_word(fluid[index - 1], fluid[index], fluid[index + 1])
+        word = link_word(fluid[index - 1], fluid[index], fluid[index + 1])
+        yield
+        words[index] = word
 
     def advance(step, source, target, index, place, ahead):
         state = pull(source, index, words[index])
         density, flow = density_velocity(state)
+        collided = collide(state, density, flow, opens[index])
+        yield
         remember(history, step, index, density, flow)
-        store(target, index, collide(state, density, flow, opens[index]))
+        store(target, index, collided)
 
     both(1, link)
     receive(0, even)
@@ -418,11 +444,13 @@
     def finish(index, place, ahead):
         state = pull(even, index, words[index])
         density, flow = density_velocity(state)
+        here = fluid[index] > 0
+        placed = [jnp.where(here, state[m], inner_final[m, index - HALO]) for m in range(19)]
+        part = jnp.where(here, drag_terms(flow, opens[index]), 0.0)
+        yield
         remember(history, 3, index, density, flow)
-        here = fluid[index] > 0
-        for m in range(19):
-            final[m, index - HALO] = jnp.where(here, state[m], inner_final[m, index - HALO])
-        drag[1 + place] += jnp.where(here, drag_terms(flow, opens[index]), 0.0)
+        store(final, index - HALO, placed)
+        drag[1 + place] += part
 
     both(3, finish)
     for copy in copies:
@@ -455,16 +483,20 @@
     rate = 1.2 * open_rate
     slope = [rate * (mx + hx), rate * (my + hy), rate * (mz + hz)]
     pushed = slope[0] * force_flow[0] + slope[1] * force_flow[1] + slope[2] * force_flow[2]
-    share[plane] += density * pushed
+    gained = share[plane] + density * pushed
     if target is None:
+        yield
+        share[plane] = gained
         return
     level = whole * (1.2 / 36.0) + 1.2 * (
         x * (mx + 0.5 * hx) + y * (my + 0.5 * hy) + z * (mz + 0.5 * hz)
     )
     level = level - (slope[0] * flow[0] + slope[1] * flow[1] + slope[2] * flow[2])
-    values = spread(level, slope)
+    values = [part - 0.2 * old for part, old in zip(spread(level, slope), adjoint)]
+    yield
+    share[plane] = gained
     for m in range(19):
-        target[OPP[m], plane] = values[m] - 0.2 * adjoint[m]
+        target[OPP[m], plane] = values[m]
 
 
 def outer_kernel(
@@ -496,10 +528,11 @@
     def seed(plane, density, flow):
         damping = 1.0 / opens[plane]
         square = flow[0] * flow[0] + flow[1] * flow[1] + flow[2] * flow[2]
-        share[plane] = -square * damping
         factor = 2.0 * damping / density
         slope = [part * factor for part in flow]
         values = spread(-square * factor, slope)
+        yield
+        share[plane] = -square * damping
         for m in range(19):
             even[OPP[m], plane] = values[m]
 
@@ -540,7 +573,7 @@
                 word = words[index] + ahead * (edge_word - words[index])
             state = pull(two, spot, word)
             density, flow = density_velocity(state)
-            seed(index, density, flow)
+            run([seed(index, density, flow)])
             here = fluid[index] > 0
             for m in range(19):
                 if place == 1:
@@ -553,16 +586,18 @@
             outer[ahead, m, ahead * (BX - 1)] = message[30 + m]
 
     def seed_home(plane):
-        seed(plane, *recall(history, STEPS, plane))
+        return seed(plane, *recall(history, STEPS, plane))
 
     each_plane(HALO, HALO + home, seed_home)
 
-    for side in range(2):
+    def ends(side):
         flow = [second_flow[side, 1 + axis] for axis in range(3)]
-        retreat(opens, words, share, even, odd, 1 + side * (span - 3), second_flow[side, 0], flow)
+        return retreat(opens, words, share, even, odd, 1 + side * (span - 3), second_flow[side, 0], flow)
+
+    run([ends(0), ends(1)])
 
     def step_two(plane):
-        retreat(opens, words, share, even, odd, plane, *recall(history, 2, plane))
+        return retreat(opens, words, share, even, odd, plane, *recall(history, 2, plane))
 
     each_plane(HALO - 1, HALO + home + 1, step_two)
 
@@ -576,10 +611,10 @@
         total[plane] = share[plane]
 
     def step_one(plane):
-        retreat(opens, words, total, odd, even, plane, *recall(history, 1, plane))
+        return retreat(opens, words, total, odd, even, plane, *recall(history, 1, plane))
 
     def step_zero(plane):
-        retreat(opens, words, total, even, None, plane, *recall(history, 0, plane))
+        return retreat(opens, words, total, even, None, plane, *recall(history, 0, plane))
 
     each_plane(HALO - 1, HALO + home + 1, step_one)
     each_plane(HALO, HALO + home, step_zero)

time: 31.9 us -> 32 us (level)
  transfers between devices with their start and end apart: 10 -> 10, of which waited for: 4 -> 4; matrix products, arithmetic and copies ran while one was open for 2% -> 2% of each run, Pallas kernels for 30% -> 31%
where the time goes in v6:
time: 32 us; the launch traced here: 31.8 us
  starting transfers between devices  13.6 us (42%)
  Pallas kernels  11.7 us (37%)
  waiting for transfers between devices  3.85 us (12%)
  between operations  1.41 us (4%)
  local copies, waits for them, and re-layouts  1.21 us (4%)
    pallas_call x8, Pallas kernels, call(): pl.pallas_call(kernel, out_shape=[shape for shape, _ in outs], in_specs=i...  11.7 us
    ppermute x4, starting transfers between devices, body(): sums.append(sums[-1] + lax.ppermute(sums[-1], 'block', swap))  6.94 us
    ppermute x2, starting transfers between devices, body(): from_near = lax.ppermute(to_near, 'block', near_pairs)  1.93 us
    ppermute x1, starting transfers between devices, body(): from_far = lax.ppermute(to_far, 'block', inner_pairs)  1.92 us
    ppermute x1, waiting for transfers between devices, body(): from_far = lax.ppermute(to_far, 'block', inner_pairs)  1.86 us
    ppermute x4, waiting for transfers between devices, body(): sums.append(sums[-1] + lax.ppermute(sums[-1], 'block', swap))  1.85 us
    ppermute x1, starting transfers between devices, body(): from_far = lax.ppermute(to_far, 'block', far_pairs)  1.08 us
    ppermute x1, starting transfers between devices, body(): far = lax.ppermute(own_far, 'block', far_pairs)  0.91 us
  transfers between devices with their start and end apart: 10, of which 4 were waited for; matrix products, arithmetic and copies ran while one was open for 2% of the time, Pallas kernels for 31%

profile of v6, /device:TPU:8, one launch (start us, length us, event | category | flops | bytes accessed | tf_op | source)
XLA Modules:
  0.0 31.8 jit_solution(6657650297098783490)
XLA Ops:
  0.6 1.3 %edge_planes.1 = (f32[23,2,8,128]{3,2,1,0:T(8,128)S(1)}, f32[23,2,8,128]{3,2,1,0:T(8,128)S(1)}, f32[19,12,8,128]{3,2,1,0:T(8,128)S(1)}, f32[12,8,128]{2,1,0:T(8,128)S(1)}) custom-call(f32[19,12,8,128]{3,2,1,0:T(8,128)} %pops_far.1, f32[12,8,128]{2,1,0:T(8,128)} %design.1, s32[12,8,128]{2,1,0:T(8,128)} %mask.1), custom_call_target="tpu_custom_call" | custom-call | flops 20000000 | bytes 1000000 | tf_op jit(solution)/shard_map/edge_planes/pallas_call | solution.py:709
  1.9 0.9 %collective-permute-start.4 = (f32[23,2,8,128]{3,2,1,0:T(8,128)S(1)}, f32[23,2,8,128]{3,2,1,0:T(8,128)S(1)}, u32[]{:S(2)}, u32[]{:S(2)}) collective-permute-start(f32[23,2,8,128]{3,2,1,0:T(8,128)S(1)} %get-tuple-element.80), channel_id=1, source_target_pairs={{0,15},{1,2},{2,1},{3,4},{4,3},{5,6},{6,5},{7,8},{8,7},{9,10},{10,... | collective-permute-start | bytes 565256 | tf_op jit(solution)/shard_map/ppermute | solution.py:734
  2.8 0.8 %collective-permute-start.5 = (f32[23,2,8,128]{3,2,1,0:T(8,128)S(1)}, f32[23,2,8,128]{3,2,1,0:T(8,128)S(1)}, u32[]{:S(2)}, u32[]{:S(2)}) collective-permute-start(f32[23,2,8,128]{3,2,1,0:T(8,128)S(1)} %get-tuple-element.81), channel_id=1, source_target_pairs={{0,1},{1,0},{2,3},{3,2},{4,5},{5,4},{6,7},{7,6},{8,9},{9,8},{10,11... | collective-permute-start | bytes 565256 | tf_op jit(solution)/shard_map/ppermute | solution.py:733
  3.6 2.5 %interior_steps.1 = (f32[49,8,128]{2,1,0:T(8,128)S(1)}, f32[49,8,128]{2,1,0:T(8,128)S(1)}, f32[19,12,8,128]{3,2,1,0:T(8,128)S(1)}, f32[16,12,8,128]{3,2,1,0:T(8,...) custom-call(f32[19,12,8,128]{3,2,1,0:T(8,128)S(1)} %get-tuple-elemen, ...), custom_call_target="tpu_custom_call" | custom-call | flops 120000000 | bytes 6000000 | tf_op jit(solution)/shard_map/interior_steps/pallas_call | solution.py:709
  6.2 1.1 %collective-permute-start.6 = (f32[49,8,128]{2,1,0:T(8,128)S(1)}, f32[49,8,128]{2,1,0:T(8,128)S(1)}, u32[]{:S(2)}, u32[]{:S(2)}) collective-permute-start(f32[49,8,128]{2,1,0:T(8,128)S(1)} %get-tuple-element.98), channel_id=1, source_target_pairs={{0,15},{1,2},{2,1},{3,4},{4,3},{5,6},{6,5},{7,8},{8,7},{9,10},{10,... | collective-permute-start | bytes 602120 | tf_op jit(solution)/shard_map/ppermute | solution.py:769
  7.3 0.6 %collective-permute-start.7 = (f32[49,8,128]{2,1,0:T(8,128)S(1)}, f32[49,8,128]{2,1,0:T(8,128)S(1)}, u32[]{:S(2)}, u32[]{:S(2)}) collective-permute-start(f32[49,8,128]{2,1,0:T(8,128)S(1)} %get-tuple-element.99), channel_id=1, source_target_pairs={{0,1},{1,0},{2,3},{3,2},{4,5},{5,4},{6,7},{7,6},{8,9},{9,8},{10,11... | collective-permute-start | bytes 602120 | tf_op jit(solution)/shard_map/ppermute | solution.py:768
  7.9 0.1 collective-permute-done.4.far
  8.0 0.0 collective-permute-done.5.near
  8.0 1.9 %boundary_steps.1 = (f32[19,12,8,128]{3,2,1,0:T(8,128)S(1)}, f32[16,18,8,128]{3,2,1,0:T(8,128)S(1)}, f32[18,8,128]{2,1,0:T(8,128)S(1)}, s32[18,8,128]{2,1,0:T(8,...) custom-call(f32[23,2,8,128]{3,2,1,0:T(8,128)S(1)} %collective-permut, ...), custom_call_target="tpu_custom_call" | custom-call | flops 160000000 | bytes 8000000 | tf_op jit(solution)/shard_map/boundary_steps/pallas_call | solution.py:709
  9.9 1.0 %collective-permute-start.8 = (f32[4,8,128]{2,1,0:T(8,128)S(1)}, f32[4,8,128]{2,1,0:T(8,128)S(1)}, u32[]{:S(2)}, u32[]{:S(2)}) collective-permute-start(f32[4,8,128]{2,1,0:T(8,128)S(1)} %get-tuple-element.100), channel_id=1, source_target_pairs={{0,1},{1,0},{2,3},{3,2},{4,5},{5,4},{6,7},{7,6},{8,9},{9,8},{10,11... | collective-permute-start | bytes 49160 | tf_op jit(solution)/shard_map/ppermute | solution.py:815
  10.9 0.8 %collective-permute-done.8 = f32[4,8,128]{2,1,0:T(8,128)S(1)} collective-permute-done((f32[4,8,128]{2,1,0:T(8,128)S(1)}, f32[4,8,128]{2,1,0:T(8,128)S(1)}, u32[]{:S(2)}, u32[]{:S(2)}) %collective-permute-start.8) | collective-permute-done | bytes 16416 | tf_op jit(solution)/shard_map/ppermute | solution.py:815
  11.7 2.0 %collective-permute-start.9 = (f32[4,8,128]{2,1,0:T(8,128)S(1)}, f32[4,8,128]{2,1,0:T(8,128)S(1)}, u32[]{:S(2)}, u32[]{:S(2)}) collective-permute-start(f32[4,8,128]{2,1,0:T(8,128)S(1)} %add.12), channel_id=1, source_target_pairs={{0,2},{1,3},{2,0},{3,1},{4,6},{5,7},{6,4},{7,5},{8,10},{9,11},{10,... | collective-permute-start | bytes 49160 | tf_op jit(solution)/shard_map/ppermute | solution.py:815
  13.7 1.3 %slot_counts.1 = s32[3]{0:T(128)S(1)} custom-call(s32[48]{0:T(128)S(1)} %copy-done), custom_call_target="tpu_custom_call" | custom-call | flops 400000000 | bytes 20000000 | tf_op jit(solution)/shard_map/slot_counts/pallas_call | solution.py:709
  15.0 0.6 %slice.3 = s32[1]{0:T(128)} slice(s32[3]{0:T(128)S(1)} %slot_counts.1), slice={[2:3]} | slice | bytes 8 | tf_op jit(solution)/shard_map/slice | solution.py:819
  16.2 0.0 collective-permute-done.9
  16.2 1.1 %collective-permute-start.10 = (f32[4,8,128]{2,1,0:T(8,128)S(1)}, f32[4,8,128]{2,1,0:T(8,128)S(1)}, u32[]{:S(2)}, u32[]{:S(2)}) collective-permute-start(f32[4,8,128]{2,1,0:T(8,128)S(1)} %add.13.summed), channel_id=1, source_target_pairs={{0,4},{1,5},{2,6},{3,7},{4,0},{5,1},{6,2},{7,3},{8,12},{9,13},{10,... | collective-permute-start | bytes 49160 | tf_op jit(solution)/shard_map/ppermute | solution.py:815
  17.4 0.0 collective-permute-done.6.from_far
  17.4 1.6 %outer_steps.1 = (f32[2,19,4,8,128]{4,3,2,1,0:T(8,128)S(1)}, f32[18,8,128]{2,1,0:T(8,128)S(1)}, f32[19,18,8,128]{3,2,1,0:T(8,128)S(1)}) custom-call(f32[16,18,8,128]{3,2,1,0:T(8,128)S(1)} %get-tuple-element.92.history, f32[18,8,128]{2,1,0:T(8,128)S(1)} %get-tuple-element.93.opens, s32[18,8,128]{2,1,0:T(8,128)S(1)} %get-tuple-element.94.fluid, ...), custom_call_target="tpu_custom_call" | custom-call | flops 240000000 | bytes 12000000 | tf_op jit(solution)/shard_map/outer_steps/pallas_call | solution.py:709
  19.0 1.0 %collective-permute-done.10 = f32[4,8,128]{2,1,0:T(8,128)S(1)} collective-permute-done((f32[4,8,128]{2,1,0:T(8,128)S(1)}, f32[4,8,128]{2,1,0:T(8,128)S(1)}, u32[]{:S(2)}, u32[]{:S(2)}) %collective-permute-start.10) | collective-permute-done | bytes 16416 | tf_op jit(solution)/shard_map/ppermute | solution.py:815
  20.0 2.9 %collective-permute-start.11 = (f32[4,8,128]{2,1,0:T(8,128)S(1)}, f32[4,8,128]{2,1,0:T(8,128)S(1)}, u32[]{:S(2)}, u32[]{:S(2)}) collective-permute-start(f32[4,8,128]{2,1,0:T(8,128)S(1)} %add.14.summed), channel_id=1, source_target_pairs={{0,8},{1,9},{2,10},{3,11},{4,12},{5,13},{6,14},{7,15},{8,0},{9,1},... | collective-permute-start | bytes 49160 | tf_op jit(solution)/shard_map/ppermute | solution.py:815
  22.9 1.6 %gradient_steps.1 = (f32[12,8,128]{2,1,0:T(8,128)S(1)}, f32[4,8,128]{2,1,0:T(8,128)S(1)}, f32[4,8,128]{2,1,0:T(8,128)S(1)}) custom-call(f32[16,18,8,128]{3,2,1,0:T(8,128)S(1)} %get-tuple-element.92.history, f32[18,8,128]{2,1,0:T(8,128)S(1)} %get-tuple-element.93.opens, s32[18,8,128]{2,1,0:T(8,128)S(1)} %get-tuple-element.95.words, ...), custom_call_target="tpu_custom_call" | custom-call | flops 120000000 | bytes 6000000 | tf_op jit(solution)/shard_map/gradient_steps/pallas_call | solution.py:709
  24.5 1.9 %collective-permute-start.12 = (f32[4,8,128]{2,1,0:T(8,128)S(1)}, f32[4,8,128]{2,1,0:T(8,128)S(1)}, u32[]{:S(2)}, u32[]{:S(2)}) collective-permute-start(f32[4,8,128]{2,1,0:T(8,128)S(1)} %get-tuple-element.105), channel_id=1, source_target_pairs={{1,2},{2,1},{3,4},{4,3},{5,6},{6,5},{7,8},{8,7},{9,10},{10,9},{11,... | collective-permute-start | bytes 49160 | tf_op jit(solution)/shard_map/ppermute | solution.py:858
  26.4 1.3 %collective-permute-start.13 = (f32[4,8,128]{2,1,0:T(8,128)S(1)}, f32[4,8,128]{2,1,0:T(8,128)S(1)}, u32[]{:S(2)}, u32[]{:S(2)}) collective-permute-start(f32[4,8,128]{2,1,0:T(8,128)S(1)} %get-tuple-element.106), channel_id=1, source_target_pairs={{0,1},{1,0},{2,3},{3,2},{4,5},{5,4},{6,7},{7,6},{8,9},{9,8},{10,11... | collective-permute-start | bytes 49160 | tf_op jit(solution)/shard_map/ppermute | solution.py:857
  27.7 0.8 %conditional.2 = (f32[19,20,8,128]{3,2,1,0:T(8,128)S(1)}) conditional(s32[]{:T(128)} %bitcast.2, (s32[3]{0:T(128)S(1)}, f32[19,12,8,128]{3,2,1,0:T(8,128)S(1)}, f32[2,19,4,8,128]{4,3,2,1,0:T(8,128)S(1)}, f32[12,8,128]{2,1,0:T(8,128)S(1)}) %tuple.20, (f32[19,12,8,128]{3,2,1,0:T(8,128)S(1)}, s32[3]{0:T(128)S(1)}, f32[12,8,128]{2,1,0:T(8,128)S(1)}) %tuple.21), branch_computations={%region_0.0_spmd, %region_1.0_spmd} | conditional | flops 80466944 | bytes 15206744 | solution.py:906
  27.7 0.8 %place_populations.2 = f32[19,20,8,128]{3,2,1,0:T(8,128)S(1)} custom-call(s32[3]{0:T(128)S(1)} %get-tuple-element.32.where, f32[19,12,8,128]{3,2,1,0:T(8,128)S(1)} %get-tuple-element.33.final, f32[2,19,4,8,128]{4,3,2,1,0:T(8,128)S(1)} %get-tuple-element.38.outer, f32[12,8,128]{2,1,0:T(8,128)S(1)} %get-tuple-element.39.later), custom_call_target="tpu_custom_call" | custom-call | flops 80000000 | bytes 4000000 | tf_op jit(solution)/shard_map/cond/branch_0_fun/place_populations/pallas_call | solution.py:709
  28.5 0.0 copy-start.1
  28.6 1.9 %collective-permute-done.12 = f32[4,8,128]{2,1,0:T(8,128)S(1)} collective-permute-done((f32[4,8,128]{2,1,0:T(8,128)S(1)}, f32[4,8,128]{2,1,0:T(8,128)S(1)}, u32[]{:S(2)}, u32[]{:S(2)}) %collective-permute-start.12) | collective-permute-done | bytes 16416 | tf_op jit(solution)/shard_map/ppermute | solution.py:858
  30.4 0.0 collective-permute-done.13
  30.4 0.7 %conditional.3 = (f32[20,8,128]{2,1,0:T(8,128)S(1)}) conditional(s32[]{:T(128)} %bitcast.2, (s32[3]{0:T(128)S(1)}, f32[4,8,128]{2,1,0:T(8,128)S(1)}, f32[12,8,128]{2,1,0:T(8,128)S(1)}, f32[4,8,128]{2,1,0:T(8,128)S(1)}, f32[4,8,128]{2,1,0:T(8,128)S(1)}) %tuple.22, (f32[12,8,128]{2,1,0:T(8,128)S(1)}, s32[3]{0:T(128)S(1)}, ...), branch_computations={%region_2.0_spmd, %region_3.0_spmd} | conditional | flops 20000000 | bytes 1393304 | solution.py:907
  30.4 0.7 %near_gradient.1 = f32[20,8,128]{2,1,0:T(8,128)S(1)} custom-call(s32[3]{0:T(128)S(1)} %get-tuple-element.43.where, f32[4,8,128]{2,1,0:T(8,128)S(1)} %get-tuple-element.44.drag, f32[12,8,128]{2,1,0:T(8,128)S(1)} %get-tuple-element.45.gradient, f32[4,8,128]{2,1,0:T(8,128)S(1)} %get-tuple-element.46.from_far, f32[4,8,128]{2,1,0:T(8,128)S(1)} %get-tuple-element.47.from_near), custom_call_target="tpu_custom_call" | custom-call | flops 20000000 | bytes 1000000 | tf_op jit(solution)/shard_map/cond/branch_0_fun/near_gradient/pallas_call | solution.py:709
  31.2 0.0 copy-start.2
  31.2 0.6 %copy-done.2 = f32[20,8,128]{2,1,0:T(8,128)} copy-done((f32[20,8,128]{2,1,0:T(8,128)}, f32[20,8,128]{2,1,0:T(8,128)S(1)}, u32[]{:S(2)}) %copy-start.2) | copy-done | bytes 81944
  (9 shorter events, 0.0 us)
Async XLA Ops:
  1.9 6.1 %collective-permute-start.4 = (f32[23,2,8,128]{3,2,1,0:T(8,128)S(1)}, f32[23,2,8,128]{3,2,1,0:T(8,128)S(1)}, u32[]{:S(2)}, u32[]{:S(2)}) collective-permute-start(f32[23,2,8,128]{3,2,1,0:T(8,128)S(1)} %get-tuple-element.80), channel_id=1, source_target_pairs={{0,15},{1,2},{2,1},{3,4},{4,3},{5,6},{6,5},{7,8},{8,7},{9,10},{10,... | collective-permute-start | bytes 565256 | tf_op jit(solution)/shard_map/ppermute | solution.py:734
  2.8 5.2 %collective-permute-start.5 = (f32[23,2,8,128]{3,2,1,0:T(8,128)S(1)}, f32[23,2,8,128]{3,2,1,0:T(8,128)S(1)}, u32[]{:S(2)}, u32[]{:S(2)}) collective-permute-start(f32[23,2,8,128]{3,2,1,0:T(8,128)S(1)} %get-tuple-element.81), channel_id=1, source_target_pairs={{0,1},{1,0},{2,3},{3,2},{4,5},{5,4},{6,7},{7,6},{8,9},{9,8},{10,11... | collective-permute-start | bytes 565256 | tf_op jit(solution)/shard_map/ppermute | solution.py:733
  6.2 11.2 %collective-permute-start.6 = (f32[49,8,128]{2,1,0:T(8,128)S(1)}, f32[49,8,128]{2,1,0:T(8,128)S(1)}, u32[]{:S(2)}, u32[]{:S(2)}) collective-permute-start(f32[49,8,128]{2,1,0:T(8,128)S(1)} %get-tuple-element.98), channel_id=1, source_target_pairs={{0,15},{1,2},{2,1},{3,4},{4,3},{5,6},{6,5},{7,8},{8,7},{9,10},{10,... | collective-permute-start | bytes 602120 | tf_op jit(solution)/shard_map/ppermute | solution.py:769
  7.3 10.1 %collective-permute-start.7 = (f32[49,8,128]{2,1,0:T(8,128)S(1)}, f32[49,8,128]{2,1,0:T(8,128)S(1)}, u32[]{:S(2)}, u32[]{:S(2)}) collective-permute-start(f32[49,8,128]{2,1,0:T(8,128)S(1)} %get-tuple-element.99), channel_id=1, source_target_pairs={{0,1},{1,0},{2,3},{3,2},{4,5},{5,4},{6,7},{7,6},{8,9},{9,8},{10,11... | collective-permute-start | bytes 602120 | tf_op jit(solution)/shard_map/ppermute | solution.py:768
  8.0 5.7 %copy-start = (s32[48]{0:T(128)S(1)}, s32[48]{0:T(128)}, u32[]{:S(2)}) copy-start(s32[48]{0:T(128)} %owner.1) | copy-start | bytes 580
  9.9 1.8 %collective-permute-start.8 = (f32[4,8,128]{2,1,0:T(8,128)S(1)}, f32[4,8,128]{2,1,0:T(8,128)S(1)}, u32[]{:S(2)}, u32[]{:S(2)}) collective-permute-start(f32[4,8,128]{2,1,0:T(8,128)S(1)} %get-tuple-element.100), channel_id=1, source_target_pairs={{0,1},{1,0},{2,3},{3,2},{4,5},{5,4},{6,7},{7,6},{8,9},{9,8},{10,11... | collective-permute-start | bytes 49160 | tf_op jit(solution)/shard_map/ppermute | solution.py:815
  11.7 4.5 %collective-permute-start.9 = (f32[4,8,128]{2,1,0:T(8,128)S(1)}, f32[4,8,128]{2,1,0:T(8,128)S(1)}, u32[]{:S(2)}, u32[]{:S(2)}) collective-permute-start(f32[4,8,128]{2,1,0:T(8,128)S(1)} %add.12), channel_id=1, source_target_pairs={{0,2},{1,3},{2,0},{3,1},{4,6},{5,7},{6,4},{7,5},{8,10},{9,11},{10,... | collective-permute-start | bytes 49160 | tf_op jit(solution)/shard_map/ppermute | solution.py:815
  16.2 3.8 %collective-permute-start.10 = (f32[4,8,128]{2,1,0:T(8,128)S(1)}, f32[4,8,128]{2,1,0:T(8,128)S(1)}, u32[]{:S(2)}, u32[]{:S(2)}) collective-permute-start(f32[4,8,128]{2,1,0:T(8,128)S(1)} %add.13.summed), channel_id=1, source_target_pairs={{0,4},{1,5},{2,6},{3,7},{4,0},{5,1},{6,2},{7,3},{8,12},{9,13},{10,... | collective-permute-start | bytes 49160 | tf_op jit(solution)/shard_map/ppermute | solution.py:815
  20.0 8.5 %collective-permute-start.11 = (f32[4,8,128]{2,1,0:T(8,128)S(1)}, f32[4,8,128]{2,1,0:T(8,128)S(1)}, u32[]{:S(2)}, u32[]{:S(2)}) collective-permute-start(f32[4,8,128]{2,1,0:T(8,128)S(1)} %add.14.summed), channel_id=1, source_target_pairs={{0,8},{1,9},{2,10},{3,11},{4,12},{5,13},{6,14},{7,15},{8,0},{9,1},... | collective-permute-start | bytes 49160 | tf_op jit(solution)/shard_map/ppermute | solution.py:815
  24.5 6.0 %collective-permute-start.12 = (f32[4,8,128]{2,1,0:T(8,128)S(1)}, f32[4,8,128]{2,1,0:T(8,128)S(1)}, u32[]{:S(2)}, u32[]{:S(2)}) collective-permute-start(f32[4,8,128]{2,1,0:T(8,128)S(1)} %get-tuple-element.105), channel_id=1, source_target_pairs={{1,2},{2,1},{3,4},{4,3},{5,6},{6,5},{7,8},{8,7},{9,10},{10,9},{11,... | collective-permute-start | bytes 49160 | tf_op jit(solution)/shard_map/ppermute | solution.py:858
  26.4 4.0 %collective-permute-start.13 = (f32[4,8,128]{2,1,0:T(8,128)S(1)}, f32[4,8,128]{2,1,0:T(8,128)S(1)}, u32[]{:S(2)}, u32[]{:S(2)}) collective-permute-start(f32[4,8,128]{2,1,0:T(8,128)S(1)} %get-tuple-element.106), channel_id=1, source_target_pairs={{0,1},{1,0},{2,3},{3,2},{4,5},{5,4},{6,7},{7,6},{8,9},{9,8},{10,11... | collective-permute-start | bytes 49160 | tf_op jit(solution)/shard_map/ppermute | solution.py:857
  28.5 2.6 %copy-start.1 = (f32[19,20,8,128]{3,2,1,0:T(8,128)}, f32[19,20,8,128]{3,2,1,0:T(8,128)S(1)}, u32[]{:S(2)}) copy-start(f32[19,20,8,128]{3,2,1,0:T(8,128)S(1)} %get-tuple-element.107) | copy-start | bytes 4669444
  31.2 0.6 %copy-start.2 = (f32[20,8,128]{2,1,0:T(8,128)}, f32[20,8,128]{2,1,0:T(8,128)S(1)}, u32[]{:S(2)}) copy-start(f32[20,8,128]{2,1,0:T(8,128)S(1)} %get-tuple-element.108) | copy-start | bytes 245764

commit v7 on v6

--- a/solution.py
+++ b/solution.py
@@ -154,7 +154,7 @@
         next(body, None)
 
 
-def each_plane(low, high, body, width=2):
+def each_plane(low, high, body, width=4):
     groups = (high - low) // width
 
     def group(index, carry):
@@ -400,11 +400,7 @@
         opens[index] = open_rate
         store(even, index, collided)
 
-    def start(plane, carry):
-        run([begin(plane, *side) for side in sides])
-        return carry
-
-    lax.fori_loop(0, RAW, start, 0)
+    run([begin(plane, *side) for plane in range(RAW) for side in sides])
 
     def receive(step, target):
         for m in range(19):
@@ -413,11 +409,13 @@
                 target[m, HALO + home - 2 - step + side] = edges[m, 4 * step + 2 + side]
 
     def both(step, body):
-        def two(place, carry):
-            run([body(step + place, place, 0), body(span - 3 - step + place, place, 1)])
-            return carry
-
-        lax.fori_loop(0, 3, two, 0)
+        run(
+            [
+                body(first + place, place, ahead)
+                for place in range(3)
+                for ahead, first in enumerate((step, span - 3 - step))
+            ]
+        )
 
     def link(index, place, ahead):
         word = link_word(fluid[index - 1], fluid[index], fluid[index + 1])

time: 32 us -> 30.7 us (0.959)
  the two profiles are of different devices: /device:TPU:8 before, /device:TPU:10 now
where the time goes in v7:
time: 30.7 us; the launch traced here: 30.6 us
  starting transfers between devices  13.6 us (44%)
  Pallas kernels  9.49 us (31%)
  waiting for transfers between devices  4.77 us (16%)
  between operations  1.42 us (5%)
  local copies, waits for them, and re-layouts  1.21 us (4%)
    pallas_call x8, Pallas kernels, call(): pl.pallas_call(kernel, out_shape=[shape for shape, _ in outs], in_specs=i...  9.49 us
    ppermute x4, starting transfers between devices, body(): sums.append(sums[-1] + lax.ppermute(sums[-1], 'block', swap))  7.01 us
    ppermute x4, waiting for transfers between devices, body(): sums.append(sums[-1] + lax.ppermute(sums[-1], 'block', swap))  2.05 us
    ppermute x2, starting transfers between devices, body(): from_near = lax.ppermute(to_near, 'block', near_pairs)  1.93 us
    ppermute x1, starting transfers between devices, body(): from_far = lax.ppermute(to_far, 'block', inner_pairs)  1.92 us
    ppermute x1, waiting for transfers between devices, body(): from_far = lax.ppermute(to_far, 'block', inner_pairs)  1.86 us
    ppermute x1, starting transfers between devices, body(): from_far = lax.ppermute(to_far, 'block', far_pairs)  1.07 us
    ppermute x1, starting transfers between devices, body(): far = lax.ppermute(own_far, 'block', far_pairs)  0.91 us
  transfers between devices with their start and end apart: 10, of which 4 were waited for; matrix products, arithmetic and copies ran while one was open for 2% of the time, Pallas kernels for 24%

profile of v7, /device:TPU:10, one launch (start us, length us, event | category | flops | bytes accessed | tf_op | source)
XLA Modules:
  0.0 30.6 jit_solution(14763989963456390851)
XLA Ops:
  0.6 1.3 %edge_planes.1 = (f32[23,2,8,128]{3,2,1,0:T(8,128)S(1)}, f32[23,2,8,128]{3,2,1,0:T(8,128)S(1)}, f32[19,12,8,128]{3,2,1,0:T(8,128)S(1)}, f32[12,8,128]{2,1,0:T(8,128)S(1)}) custom-call(f32[19,12,8,128]{3,2,1,0:T(8,128)} %pops_far.1, f32[12,8,128]{2,1,0:T(8,128)} %design.1, s32[12,8,128]{2,1,0:T(8,128)} %mask.1), custom_call_target="tpu_custom_call" | custom-call | flops 20000000 | bytes 1000000 | tf_op jit(solution)/shard_map/edge_planes/pallas_call | solution.py:707
  1.9 0.9 %collective-permute-start.4 = (f32[23,2,8,128]{3,2,1,0:T(8,128)S(1)}, f32[23,2,8,128]{3,2,1,0:T(8,128)S(1)}, u32[]{:S(2)}, u32[]{:S(2)}) collective-permute-start(f32[23,2,8,128]{3,2,1,0:T(8,128)S(1)} %get-tuple-element.80), channel_id=1, source_target_pairs={{0,15},{1,2},{2,1},{3,4},{4,3},{5,6},{6,5},{7,8},{8,7},{9,10},{10,... | collective-permute-start | bytes 565256 | tf_op jit(solution)/shard_map/ppermute | solution.py:732
  2.8 0.8 %collective-permute-start.5 = (f32[23,2,8,128]{3,2,1,0:T(8,128)S(1)}, f32[23,2,8,128]{3,2,1,0:T(8,128)S(1)}, u32[]{:S(2)}, u32[]{:S(2)}) collective-permute-start(f32[23,2,8,128]{3,2,1,0:T(8,128)S(1)} %get-tuple-element.81), channel_id=1, source_target_pairs={{0,1},{1,0},{2,3},{3,2},{4,5},{5,4},{6,7},{7,6},{8,9},{9,8},{10,11... | collective-permute-start | bytes 565256 | tf_op jit(solution)/shard_map/ppermute | solution.py:731
  3.6 1.8 %interior_steps.1 = (f32[49,8,128]{2,1,0:T(8,128)S(1)}, f32[49,8,128]{2,1,0:T(8,128)S(1)}, f32[19,12,8,128]{3,2,1,0:T(8,128)S(1)}, f32[16,12,8,128]{3,2,1,0:T(8,...) custom-call(f32[19,12,8,128]{3,2,1,0:T(8,128)S(1)} %get-tuple-elemen, ...), custom_call_target="tpu_custom_call" | custom-call | flops 120000000 | bytes 6000000 | tf_op jit(solution)/shard_map/interior_steps/pallas_call | solution.py:707
  5.5 1.1 %collective-permute-start.6 = (f32[49,8,128]{2,1,0:T(8,128)S(1)}, f32[49,8,128]{2,1,0:T(8,128)S(1)}, u32[]{:S(2)}, u32[]{:S(2)}) collective-permute-start(f32[49,8,128]{2,1,0:T(8,128)S(1)} %get-tuple-element.98), channel_id=1, source_target_pairs={{0,15},{1,2},{2,1},{3,4},{4,3},{5,6},{6,5},{7,8},{8,7},{9,10},{10,... | collective-permute-start | bytes 602120 | tf_op jit(solution)/shard_map/ppermute | solution.py:767
  6.5 0.6 %collective-permute-start.7 = (f32[49,8,128]{2,1,0:T(8,128)S(1)}, f32[49,8,128]{2,1,0:T(8,128)S(1)}, u32[]{:S(2)}, u32[]{:S(2)}) collective-permute-start(f32[49,8,128]{2,1,0:T(8,128)S(1)} %get-tuple-element.99), channel_id=1, source_target_pairs={{0,1},{1,0},{2,3},{3,2},{4,5},{5,4},{6,7},{7,6},{8,9},{9,8},{10,11... | collective-permute-start | bytes 602120 | tf_op jit(solution)/shard_map/ppermute | solution.py:766
  7.2 0.8 %collective-permute-done.4.far = f32[23,2,8,128]{3,2,1,0:T(8,128)S(1)} collective-permute-done((f32[23,2,8,128]{3,2,1,0:T(8,128)S(1)}, f32[23,2,8,128]{3,2,1,0:T(8,128)S(1)}, u32[]{:S(2)}, u32[]{:S(2)}) %collective-permute-start.4) | collective-permute-done | bytes 188448 | tf_op jit(solution)/shard_map/ppermute | solution.py:732
  8.0 1.1 %boundary_steps.1 = (f32[19,12,8,128]{3,2,1,0:T(8,128)S(1)}, f32[16,18,8,128]{3,2,1,0:T(8,128)S(1)}, f32[18,8,128]{2,1,0:T(8,128)S(1)}, s32[18,8,128]{2,1,0:T(8,...) custom-call(f32[23,2,8,128]{3,2,1,0:T(8,128)S(1)} %collective-permut, ...), custom_call_target="tpu_custom_call" | custom-call | flops 160000000 | bytes 8000000 | tf_op jit(solution)/shard_map/boundary_steps/pallas_call | solution.py:707
  9.1 1.0 %collective-permute-start.8 = (f32[4,8,128]{2,1,0:T(8,128)S(1)}, f32[4,8,128]{2,1,0:T(8,128)S(1)}, u32[]{:S(2)}, u32[]{:S(2)}) collective-permute-start(f32[4,8,128]{2,1,0:T(8,128)S(1)} %get-tuple-element.100), channel_id=1, source_target_pairs={{0,1},{1,0},{2,3},{3,2},{4,5},{5,4},{6,7},{7,6},{8,9},{9,8},{10,11... | collective-permute-start | bytes 49160 | tf_op jit(solution)/shard_map/ppermute | solution.py:813
  10.1 0.8 %collective-permute-done.8 = f32[4,8,128]{2,1,0:T(8,128)S(1)} collective-permute-done((f32[4,8,128]{2,1,0:T(8,128)S(1)}, f32[4,8,128]{2,1,0:T(8,128)S(1)}, u32[]{:S(2)}, u32[]{:S(2)}) %collective-permute-start.8) | collective-permute-done | bytes 16416 | tf_op jit(solution)/shard_map/ppermute | solution.py:813
  10.9 2.0 %collective-permute-start.9 = (f32[4,8,128]{2,1,0:T(8,128)S(1)}, f32[4,8,128]{2,1,0:T(8,128)S(1)}, u32[]{:S(2)}, u32[]{:S(2)}) collective-permute-start(f32[4,8,128]{2,1,0:T(8,128)S(1)} %add.12), channel_id=1, source_target_pairs={{0,2},{1,3},{2,0},{3,1},{4,6},{5,7},{6,4},{7,5},{8,10},{9,11},{10,... | collective-permute-start | bytes 49160 | tf_op jit(solution)/shard_map/ppermute | solution.py:813
  12.9 1.3 %slot_counts.1 = s32[3]{0:T(128)S(1)} custom-call(s32[48]{0:T(128)S(1)} %copy-done), custom_call_target="tpu_custom_call" | custom-call | flops 400000000 | bytes 20000000 | tf_op jit(solution)/shard_map/slot_counts/pallas_call | solution.py:707
  14.2 0.6 %slice.3 = s32[1]{0:T(128)} slice(s32[3]{0:T(128)S(1)} %slot_counts.1), slice={[2:3]} | slice | bytes 8 | tf_op jit(solution)/shard_map/slice | solution.py:817
  15.4 1.2 %collective-permute-start.10 = (f32[4,8,128]{2,1,0:T(8,128)S(1)}, f32[4,8,128]{2,1,0:T(8,128)S(1)}, u32[]{:S(2)}, u32[]{:S(2)}) collective-permute-start(f32[4,8,128]{2,1,0:T(8,128)S(1)} %add.13.summed), channel_id=1, source_target_pairs={{0,4},{1,5},{2,6},{3,7},{4,0},{5,1},{6,2},{7,3},{8,12},{9,13},{10,... | collective-permute-start | bytes 49160 | tf_op jit(solution)/shard_map/ppermute | solution.py:813
  16.6 0.0 collective-permute-done.6.from_far
  16.6 0.0 collective-permute-done.7.from_near
  16.6 1.4 %outer_steps.1 = (f32[2,19,4,8,128]{4,3,2,1,0:T(8,128)S(1)}, f32[18,8,128]{2,1,0:T(8,128)S(1)}, f32[19,18,8,128]{3,2,1,0:T(8,128)S(1)}) custom-call(f32[16,18,8,128]{3,2,1,0:T(8,128)S(1)} %get-tuple-element.92.history, f32[18,8,128]{2,1,0:T(8,128)S(1)} %get-tuple-element.93.opens, s32[18,8,128]{2,1,0:T(8,128)S(1)} %get-tuple-element.94.fluid, ...), custom_call_target="tpu_custom_call" | custom-call | flops 240000000 | bytes 12000000 | tf_op jit(solution)/shard_map/outer_steps/pallas_call | solution.py:707
  18.0 1.2 %collective-permute-done.10 = f32[4,8,128]{2,1,0:T(8,128)S(1)} collective-permute-done((f32[4,8,128]{2,1,0:T(8,128)S(1)}, f32[4,8,128]{2,1,0:T(8,128)S(1)}, u32[]{:S(2)}, u32[]{:S(2)}) %collective-permute-start.10) | collective-permute-done | bytes 16416 | tf_op jit(solution)/shard_map/ppermute | solution.py:813
  19.2 2.9 %collective-permute-start.11 = (f32[4,8,128]{2,1,0:T(8,128)S(1)}, f32[4,8,128]{2,1,0:T(8,128)S(1)}, u32[]{:S(2)}, u32[]{:S(2)}) collective-permute-start(f32[4,8,128]{2,1,0:T(8,128)S(1)} %add.14.summed), channel_id=1, source_target_pairs={{0,8},{1,9},{2,10},{3,11},{4,12},{5,13},{6,14},{7,15},{8,0},{9,1},... | collective-permute-start | bytes 49160 | tf_op jit(solution)/shard_map/ppermute | solution.py:813
  22.1 1.1 %gradient_steps.1 = (f32[12,8,128]{2,1,0:T(8,128)S(1)}, f32[4,8,128]{2,1,0:T(8,128)S(1)}, f32[4,8,128]{2,1,0:T(8,128)S(1)}) custom-call(f32[16,18,8,128]{3,2,1,0:T(8,128)S(1)} %get-tuple-element.92.history, f32[18,8,128]{2,1,0:T(8,128)S(1)} %get-tuple-element.93.opens, s32[18,8,128]{2,1,0:T(8,128)S(1)} %get-tuple-element.95.words, ...), custom_call_target="tpu_custom_call" | custom-call | flops 120000000 | bytes 6000000 | tf_op jit(solution)/shard_map/gradient_steps/pallas_call | solution.py:707
  23.2 1.9 %collective-permute-start.12 = (f32[4,8,128]{2,1,0:T(8,128)S(1)}, f32[4,8,128]{2,1,0:T(8,128)S(1)}, u32[]{:S(2)}, u32[]{:S(2)}) collective-permute-start(f32[4,8,128]{2,1,0:T(8,128)S(1)} %get-tuple-element.105), channel_id=1, source_target_pairs={{1,2},{2,1},{3,4},{4,3},{5,6},{6,5},{7,8},{8,7},{9,10},{10,9},{11,... | collective-permute-start | bytes 49160 | tf_op jit(solution)/shard_map/ppermute | solution.py:856
  25.2 1.3 %collective-permute-start.13 = (f32[4,8,128]{2,1,0:T(8,128)S(1)}, f32[4,8,128]{2,1,0:T(8,128)S(1)}, u32[]{:S(2)}, u32[]{:S(2)}) collective-permute-start(f32[4,8,128]{2,1,0:T(8,128)S(1)} %get-tuple-element.106), channel_id=1, source_target_pairs={{0,1},{1,0},{2,3},{3,2},{4,5},{5,4},{6,7},{7,6},{8,9},{9,8},{10,11... | collective-permute-start | bytes 49160 | tf_op jit(solution)/shard_map/ppermute | solution.py:855
  26.5 0.8 %conditional.2 = (f32[19,20,8,128]{3,2,1,0:T(8,128)S(1)}) conditional(s32[]{:T(128)} %bitcast.2, (s32[3]{0:T(128)S(1)}, f32[19,12,8,128]{3,2,1,0:T(8,128)S(1)}, f32[2,19,4,8,128]{4,3,2,1,0:T(8,128)S(1)}, f32[12,8,128]{2,1,0:T(8,128)S(1)}) %tuple.20, (f32[19,12,8,128]{3,2,1,0:T(8,128)S(1)}, s32[3]{0:T(128)S(1)}, f32[12,8,128]{2,1,0:T(8,128)S(1)}) %tuple.21), branch_computations={%region_0.0_spmd, %region_1.0_spmd} | conditional | flops 80466944 | bytes 15206744 | solution.py:904
  26.5 0.8 %place_populations.2 = f32[19,20,8,128]{3,2,1,0:T(8,128)S(1)} custom-call(s32[3]{0:T(128)S(1)} %get-tuple-element.32.where, f32[19,12,8,128]{3,2,1,0:T(8,128)S(1)} %get-tuple-element.33.final, f32[2,19,4,8,128]{4,3,2,1,0:T(8,128)S(1)} %get-tuple-element.38.outer, f32[12,8,128]{2,1,0:T(8,128)S(1)} %get-tuple-element.39.later), custom_call_target="tpu_custom_call" | custom-call | flops 80000000 | bytes 4000000 | tf_op jit(solution)/shard_map/cond/branch_0_fun/place_populations/pallas_call | solution.py:707
  27.3 0.0 copy-start.1
  27.3 0.0 collective-permute-done.11
  27.3 1.9 %collective-permute-done.12 = f32[4,8,128]{2,1,0:T(8,128)S(1)} collective-permute-done((f32[4,8,128]{2,1,0:T(8,128)S(1)}, f32[4,8,128]{2,1,0:T(8,128)S(1)}, u32[]{:S(2)}, u32[]{:S(2)}) %collective-permute-start.12) | collective-permute-done | bytes 16416 | tf_op jit(solution)/shard_map/ppermute | solution.py:856
  29.2 0.0 collective-permute-done.13
  29.2 0.7 %conditional.3 = (f32[20,8,128]{2,1,0:T(8,128)S(1)}) conditional(s32[]{:T(128)} %bitcast.2, (s32[3]{0:T(128)S(1)}, f32[4,8,128]{2,1,0:T(8,128)S(1)}, f32[12,8,128]{2,1,0:T(8,128)S(1)}, f32[4,8,128]{2,1,0:T(8,128)S(1)}, f32[4,8,128]{2,1,0:T(8,128)S(1)}) %tuple.22, (f32[12,8,128]{2,1,0:T(8,128)S(1)}, s32[3]{0:T(128)S(1)}, ...), branch_computations={%region_2.0_spmd, %region_3.0_spmd} | conditional | flops 20000000 | bytes 1393304 | solution.py:905
  29.2 0.7 %near_gradient.1 = f32[20,8,128]{2,1,0:T(8,128)S(1)} custom-call(s32[3]{0:T(128)S(1)} %get-tuple-element.43.where, f32[4,8,128]{2,1,0:T(8,128)S(1)} %get-tuple-element.44.drag, f32[12,8,128]{2,1,0:T(8,128)S(1)} %get-tuple-element.45.gradient, f32[4,8,128]{2,1,0:T(8,128)S(1)} %get-tuple-element.46.from_far, f32[4,8,128]{2,1,0:T(8,128)S(1)} %get-tuple-element.47.from_near), custom_call_target="tpu_custom_call" | custom-call | flops 20000000 | bytes 1000000 | tf_op jit(solution)/shard_map/cond/branch_0_fun/near_gradient/pallas_call | solution.py:707
  29.9 0.0 copy-start.2
  29.9 0.6 %copy-done.2 = f32[20,8,128]{2,1,0:T(8,128)} copy-done((f32[20,8,128]{2,1,0:T(8,128)}, f32[20,8,128]{2,1,0:T(8,128)S(1)}, u32[]{:S(2)}) %copy-start.2) | copy-done | bytes 81944
  (9 shorter events, 0.0 us)
Async XLA Ops:
  1.9 6.1 %collective-permute-start.4 = (f32[23,2,8,128]{3,2,1,0:T(8,128)S(1)}, f32[23,2,8,128]{3,2,1,0:T(8,128)S(1)}, u32[]{:S(2)}, u32[]{:S(2)}) collective-permute-start(f32[23,2,8,128]{3,2,1,0:T(8,128)S(1)} %get-tuple-element.80), channel_id=1, source_target_pairs={{0,15},{1,2},{2,1},{3,4},{4,3},{5,6},{6,5},{7,8},{8,7},{9,10},{10,... | collective-permute-start | bytes 565256 | tf_op jit(solution)/shard_map/ppermute | solution.py:732
  2.8 5.2 %collective-permute-start.5 = (f32[23,2,8,128]{3,2,1,0:T(8,128)S(1)}, f32[23,2,8,128]{3,2,1,0:T(8,128)S(1)}, u32[]{:S(2)}, u32[]{:S(2)}) collective-permute-start(f32[23,2,8,128]{3,2,1,0:T(8,128)S(1)} %get-tuple-element.81), channel_id=1, source_target_pairs={{0,1},{1,0},{2,3},{3,2},{4,5},{5,4},{6,7},{7,6},{8,9},{9,8},{10,11... | collective-permute-start | bytes 565256 | tf_op jit(solution)/shard_map/ppermute | solution.py:731
  5.5 11.2 %collective-permute-start.6 = (f32[49,8,128]{2,1,0:T(8,128)S(1)}, f32[49,8,128]{2,1,0:T(8,128)S(1)}, u32[]{:S(2)}, u32[]{:S(2)}) collective-permute-start(f32[49,8,128]{2,1,0:T(8,128)S(1)} %get-tuple-element.98), channel_id=1, source_target_pairs={{0,15},{1,2},{2,1},{3,4},{4,3},{5,6},{6,5},{7,8},{8,7},{9,10},{10,... | collective-permute-start | bytes 602120 | tf_op jit(solution)/shard_map/ppermute | solution.py:767
  6.5 10.1 %collective-permute-start.7 = (f32[49,8,128]{2,1,0:T(8,128)S(1)}, f32[49,8,128]{2,1,0:T(8,128)S(1)}, u32[]{:S(2)}, u32[]{:S(2)}) collective-permute-start(f32[49,8,128]{2,1,0:T(8,128)S(1)} %get-tuple-element.99), channel_id=1, source_target_pairs={{0,1},{1,0},{2,3},{3,2},{4,5},{5,4},{6,7},{7,6},{8,9},{9,8},{10,11... | collective-permute-start | bytes 602120 | tf_op jit(solution)/shard_map/ppermute | solution.py:766
  8.0 4.9 %copy-start = (s32[48]{0:T(128)S(1)}, s32[48]{0:T(128)}, u32[]{:S(2)}) copy-start(s32[48]{0:T(128)} %owner.1) | copy-start | bytes 580
  9.1 1.8 %collective-permute-start.8 = (f32[4,8,128]{2,1,0:T(8,128)S(1)}, f32[4,8,128]{2,1,0:T(8,128)S(1)}, u32[]{:S(2)}, u32[]{:S(2)}) collective-permute-start(f32[4,8,128]{2,1,0:T(8,128)S(1)} %get-tuple-element.100), channel_id=1, source_target_pairs={{0,1},{1,0},{2,3},{3,2},{4,5},{5,4},{6,7},{7,6},{8,9},{9,8},{10,11... | collective-permute-start | bytes 49160 | tf_op jit(solution)/shard_map/ppermute | solution.py:813
  10.9 4.5 %collective-permute-start.9 = (f32[4,8,128]{2,1,0:T(8,128)S(1)}, f32[4,8,128]{2,1,0:T(8,128)S(1)}, u32[]{:S(2)}, u32[]{:S(2)}) collective-permute-start(f32[4,8,128]{2,1,0:T(8,128)S(1)} %add.12), channel_id=1, source_target_pairs={{0,2},{1,3},{2,0},{3,1},{4,6},{5,7},{6,4},{7,5},{8,10},{9,11},{10,... | collective-permute-start | bytes 49160 | tf_op jit(solution)/shard_map/ppermute | solution.py:813
  15.4 3.8 %collective-permute-start.10 = (f32[4,8,128]{2,1,0:T(8,128)S(1)}, f32[4,8,128]{2,1,0:T(8,128)S(1)}, u32[]{:S(2)}, u32[]{:S(2)}) collective-permute-start(f32[4,8,128]{2,1,0:T(8,128)S(1)} %add.13.summed), channel_id=1, source_target_pairs={{0,4},{1,5},{2,6},{3,7},{4,0},{5,1},{6,2},{7,3},{8,12},{9,13},{10,... | collective-permute-start | bytes 49160 | tf_op jit(solution)/shard_map/ppermute | solution.py:813
  19.2 8.1 %collective-permute-start.11 = (f32[4,8,128]{2,1,0:T(8,128)S(1)}, f32[4,8,128]{2,1,0:T(8,128)S(1)}, u32[]{:S(2)}, u32[]{:S(2)}) collective-permute-start(f32[4,8,128]{2,1,0:T(8,128)S(1)} %add.14.summed), channel_id=1, source_target_pairs={{0,8},{1,9},{2,10},{3,11},{4,12},{5,13},{6,14},{7,15},{8,0},{9,1},... | collective-permute-start | bytes 49160 | tf_op jit(solution)/shard_map/ppermute | solution.py:813
  23.2 6.0 %collective-permute-start.12 = (f32[4,8,128]{2,1,0:T(8,128)S(1)}, f32[4,8,128]{2,1,0:T(8,128)S(1)}, u32[]{:S(2)}, u32[]{:S(2)}) collective-permute-start(f32[4,8,128]{2,1,0:T(8,128)S(1)} %get-tuple-element.105), channel_id=1, source_target_pairs={{1,2},{2,1},{3,4},{4,3},{5,6},{6,5},{7,8},{8,7},{9,10},{10,9},{11,... | collective-permute-start | bytes 49160 | tf_op jit(solution)/shard_map/ppermute | solution.py:856
  25.2 4.0 %collective-permute-start.13 = (f32[4,8,128]{2,1,0:T(8,128)S(1)}, f32[4,8,128]{2,1,0:T(8,128)S(1)}, u32[]{:S(2)}, u32[]{:S(2)}) collective-permute-start(f32[4,8,128]{2,1,0:T(8,128)S(1)} %get-tuple-element.106), channel_id=1, source_target_pairs={{0,1},{1,0},{2,3},{3,2},{4,5},{5,4},{6,7},{7,6},{8,9},{9,8},{10,11... | collective-permute-start | bytes 49160 | tf_op jit(solution)/shard_map/ppermute | solution.py:855
  27.3 2.6 %copy-start.1 = (f32[19,20,8,128]{3,2,1,0:T(8,128)}, f32[19,20,8,128]{3,2,1,0:T(8,128)S(1)}, u32[]{:S(2)}) copy-start(f32[19,20,8,128]{3,2,1,0:T(8,128)S(1)} %get-tuple-element.107) | copy-start | bytes 4669444
  29.9 0.6 %copy-start.2 = (f32[20,8,128]{2,1,0:T(8,128)}, f32[20,8,128]{2,1,0:T(8,128)S(1)}, u32[]{:S(2)}) copy-start(f32[20,8,128]{2,1,0:T(8,128)S(1)} %get-tuple-element.108) | copy-start | bytes 245764

commit v8 on v7

--- a/solution.py
+++ b/solution.py
@@ -154,7 +154,7 @@
         next(body, None)
 
 
-def each_plane(low, high, body, width=4):
+def each_plane(low, high, body, width=6):
     groups = (high - low) // width
 
     def group(index, carry):
@@ -197,17 +197,24 @@
 
 def edge_kernel(home, pops_far, design, mask, near, far, pops, marked, designs, masks, sems):
     up = parity()
+    cuts = ((0, HALO), (home - HALO, HALO), (HALO, home - 2 * HALO))
     copies = [
-        pltpu.make_async_copy(source, target, sems.at[place])
-        for place, (source, target) in enumerate(((pops_far, pops), (design, designs), (mask, masks)))
+        pltpu.make_async_copy(design, designs, sems.at[0]),
+        pltpu.make_async_copy(mask, masks, sems.at[1]),
+    ] + [
+        pltpu.make_async_copy(
+            pops_far.at[:, pl.ds(first, planes)], pops.at[:, pl.ds(first, planes)], sems.at[2 + place]
+        )
+        for place, (first, planes) in enumerate(cuts)
     ]
     for copy in copies:
         copy.start()
-    for copy in copies[1:]:
+    for copy in copies[:2]:
         copy.wait()
     for plane in range(home):
         marked[plane] = jnp.where(masks[plane] > 0, designs[plane], -1.0)
-    copies[0].wait()
+    for copy in copies[2:4]:
+        copy.wait()
     for out, ahead in ((near, up), (far, 1 - up)):
         first = ahead * (home - RAW)
         for plane in range(RAW):
@@ -224,6 +231,7 @@
         for slot in range(5):
             value = jnp.where(ahead > 0, collided[AHEAD[slot]], collided[BEHIND[slot]])
             out[20 + slot // 2, slot % 2] = value
+    copies[4].wait()
 
 
 def count_kernel(home_blocks, owner, where):
@@ -534,52 +542,73 @@
         for m in range(19):
             even[OPP[m], plane] = values[m]
 
-    for ahead, raw, message in ((up, near, from_near), (1 - up, far, from_far)):
-        one = first.at[ahead]
+    sides = ((up, near, from_near), (1 - up, far, from_far))
+    edge_words = []
+    for ahead, _, message in sides:
         for m in range(19):
             for place in range(HALO):
-                one[m, place] = odd_state[m, ahead * (span - HALO) + place]
+                first[ahead, m, place] = odd_state[m, ahead * (span - HALO) + place]
+            for place in range(2):
+                second[ahead, m, 3 - 3 * ahead + place] = even_state[m, 2 + ahead * (span - 6) + place]
+            second[ahead, m, 1 + 2 * ahead] = message[10 + m]
         for slot in range(5):
-            one[AHEAD[slot] + ahead, ahead * RAW] = message[slot]
+            first[ahead, AHEAD[slot] + ahead, ahead * RAW] = message[slot]
+            second[ahead, AHEAD[slot] + ahead, 4 * ahead] = message[5 + slot]
+        beyond = (message[29] >= 0.0).astype(jnp.int32)
+        within = fluid[1 + ahead * (span - 3)]
+        edge_words.append(
+            link_word(
+                beyond + ahead * (within - beyond),
+                fluid[ahead * (span - 1)],
+                within + ahead * (beyond - within),
+            )
+        )
+
+    def second_out(ahead):
         index = 1 + ahead * (span - 3)
-        state = pull(one, 1, words[index])
+        state = pull(first.at[ahead], 1, words[index])
         density, flow = density_velocity(state)
+        collided = collide(state, density, flow, opens[index])
+        yield
         for place, part in enumerate([density] + flow):
             second_flow[ahead, place] = part
+        store(second.at[ahead], 2, collided)
+
+    run([second_out(side[0]) for side in sides])
+
+    def last_step(ahead, raw, message, edge_word, place):
+        spot = 1 + place
+        index = place + ahead * (span - 3)
         two = second.at[ahead]
-        store(two, 2, collide(state, density, flow, opens[index]))
+        word = words[index]
+        if place == 0:
+            word = edge_word + ahead * (word - edge_word)
+        if place == 2:
+            word = word + ahead * (edge_word - word)
+        state = pull(two, spot, word)
+        density, flow = density_velocity(state)
+        seeded = seed(index, density, flow)
+        next(seeded)
+        here = fluid[index] > 0
+        placed = []
         for m in range(19):
-            for place in range(2):
-                two[m, 3 - 3 * ahead + place] = even_state[m, 2 + ahead * (span - 6) + place]
-            two[m, 1 + 2 * ahead] = message[10 + m]
-        for slot in range(5):
-            two[AHEAD[slot] + ahead, 4 * ahead] = message[5 + slot]
-        beyond = (message[29] >= 0.0).astype(jnp.int32)
-        within = fluid[1 + ahead * (span - 3)]
-        edge_word = link_word(
-            beyond + ahead * (within - beyond),
-            fluid[ahead * (span - 1)],
-            within + ahead * (beyond - within),
-        )
-        for place in range(HALO):
-            spot = 1 + place
-            index = place + ahead * (span - 3)
-            word = words[index] if place == 1 else None
-            if place == 0:
-                word = edge_word + ahead * (words[index] - edge_word)
-            if place == 2:
-                word = words[index] + ahead * (edge_word - words[index])
-            state = pull(two, spot, word)
-            density, flow = density_velocity(state)
-            run([seed(index, density, flow)])
-            here = fluid[index] > 0
-            for m in range(19):
-                if place == 1:
-                    initial = raw[m, ahead]
-                else:
-                    kept = two[m, spot]
-                    initial = jnp.where((ahead > 0) == (place == 2), kept, raw[m, place // 2])
-                outer[ahead, m, spot - ahead] = jnp.where(here, state[m], initial)
+            if place == 1:
+                initial = raw[m, ahead]
+            else:
+                initial = jnp.where((ahead > 0) == (place == 2), two[m, spot], raw[m, place // 2])
+            placed.append(jnp.where(here, state[m], initial))
+        yield
+        next(seeded, None)
+        store(outer.at[ahead], spot - ahead, placed)
+
+    run(
+        [
+            last_step(*side, edge_word, place)
+            for place in range(HALO)
+            for side, edge_word in zip(sides, edge_words)
+        ]
+    )
+    for ahead, _, message in sides:
         for m in range(19):
             outer[ahead, m, ahead * (BX - 1)] = message[30 + m]
 
@@ -720,7 +749,7 @@
         "edge_planes",
         [hbm] * 3,
         [(planes(23, RAW), vmem)] * 2 + [(planes(19, home), vmem), (planes(home), vmem)],
-        [scratch(home), scratch(home, dtype=jnp.int32), pltpu.SemaphoreType.DMA((3,))],
+        [scratch(home), scratch(home, dtype=jnp.int32), pltpu.SemaphoreType.DMA((5,))],
         4,
         1_000_000,
         *[

time: 30.7 us -> 31.9 us (1.039)
  the two profiles are of different devices: /device:TPU:10 before, /device:TPU:8 now
where the time goes in v8:
time: 31.9 us; the launch traced here: 31.7 us
  starting transfers between devices  12.2 us (38%)
  Pallas kernels  8.85 us (28%)
  waiting for transfers between devices  7.94 us (25%)
  between operations  1.42 us (4%)
  local copies, waits for them, and re-layouts  1.21 us (4%)
    pallas_call x8, Pallas kernels, call(): pl.pallas_call(kernel, out_shape=[shape for shape, _ in outs], in_specs=i...  8.85 us
    ppermute x4, starting transfers between devices, body(): sums.append(sums[-1] + lax.ppermute(sums[-1], 'block', swap))  5.87 us
    ppermute x4, waiting for transfers between devices, body(): sums.append(sums[-1] + lax.ppermute(sums[-1], 'block', swap))  4.48 us
    ppermute x1, waiting for transfers between devices, body(): from_far = lax.ppermute(to_far, 'block', inner_pairs)  2.11 us
    ppermute x1, starting transfers between devices, body(): from_far = lax.ppermute(to_far, 'block', inner_pairs)  1.92 us
    ppermute x2, starting transfers between devices, body(): from_near = lax.ppermute(to_near, 'block', near_pairs)  1.68 us
    ppermute x1, waiting for transfers between devices, body(): far = lax.ppermute(own_far, 'block', far_pairs)  1.35 us
    ppermute x1, starting transfers between devices, body(): from_far = lax.ppermute(to_far, 'block', far_pairs)  1.08 us
  transfers between devices with their start and end apart: 10, of which 5 were waited for; matrix products, arithmetic and copies ran while one was open for 2% of the time, Pallas kernels for 21%

profile of v8, /device:TPU:8, one launch (start us, length us, event | category | flops | bytes accessed | tf_op | source)
XLA Modules:
  0.0 31.7 jit_solution(6518985612121459722)
XLA Ops:
  0.6 1.4 %edge_planes.1 = (f32[23,2,8,128]{3,2,1,0:T(8,128)S(1)}, f32[23,2,8,128]{3,2,1,0:T(8,128)S(1)}, f32[19,12,8,128]{3,2,1,0:T(8,128)S(1)}, f32[12,8,128]{2,1,0:T(8,128)S(1)}) custom-call(f32[19,12,8,128]{3,2,1,0:T(8,128)} %pops_far.1, f32[12,8,128]{2,1,0:T(8,128)} %design.1, s32[12,8,128]{2,1,0:T(8,128)} %mask.1), custom_call_target="tpu_custom_call" | custom-call | flops 20000000 | bytes 1000000 | tf_op jit(solution)/shard_map/edge_planes/pallas_call | solution.py:736
  2.0 0.9 %collective-permute-start.4 = (f32[23,2,8,128]{3,2,1,0:T(8,128)S(1)}, f32[23,2,8,128]{3,2,1,0:T(8,128)S(1)}, u32[]{:S(2)}, u32[]{:S(2)}) collective-permute-start(f32[23,2,8,128]{3,2,1,0:T(8,128)S(1)} %get-tuple-element.80), channel_id=1, source_target_pairs={{0,15},{1,2},{2,1},{3,4},{4,3},{5,6},{6,5},{7,8},{8,7},{9,10},{10,... | collective-permute-start | bytes 565256 | tf_op jit(solution)/shard_map/ppermute | solution.py:761
  2.9 0.8 %collective-permute-start.5 = (f32[23,2,8,128]{3,2,1,0:T(8,128)S(1)}, f32[23,2,8,128]{3,2,1,0:T(8,128)S(1)}, u32[]{:S(2)}, u32[]{:S(2)}) collective-permute-start(f32[23,2,8,128]{3,2,1,0:T(8,128)S(1)} %get-tuple-element.81), channel_id=1, source_target_pairs={{0,1},{1,0},{2,3},{3,2},{4,5},{5,4},{6,7},{7,6},{8,9},{9,8},{10,11... | collective-permute-start | bytes 565256 | tf_op jit(solution)/shard_map/ppermute | solution.py:760
  3.7 1.3 %interior_steps.1 = (f32[49,8,128]{2,1,0:T(8,128)S(1)}, f32[49,8,128]{2,1,0:T(8,128)S(1)}, f32[19,12,8,128]{3,2,1,0:T(8,128)S(1)}, f32[16,12,8,128]{3,2,1,0:T(8,...) custom-call(f32[19,12,8,128]{3,2,1,0:T(8,128)S(1)} %get-tuple-elemen, ...), custom_call_target="tpu_custom_call" | custom-call | flops 120000000 | bytes 6000000 | tf_op jit(solution)/shard_map/interior_steps/pallas_call | solution.py:736
  5.0 1.1 %collective-permute-start.6 = (f32[49,8,128]{2,1,0:T(8,128)S(1)}, f32[49,8,128]{2,1,0:T(8,128)S(1)}, u32[]{:S(2)}, u32[]{:S(2)}) collective-permute-start(f32[49,8,128]{2,1,0:T(8,128)S(1)} %get-tuple-element.98), channel_id=1, source_target_pairs={{0,15},{1,2},{2,1},{3,4},{4,3},{5,6},{6,5},{7,8},{8,7},{9,10},{10,... | collective-permute-start | bytes 602120 | tf_op jit(solution)/shard_map/ppermute | solution.py:796
  6.1 0.6 %collective-permute-start.7 = (f32[49,8,128]{2,1,0:T(8,128)S(1)}, f32[49,8,128]{2,1,0:T(8,128)S(1)}, u32[]{:S(2)}, u32[]{:S(2)}) collective-permute-start(f32[49,8,128]{2,1,0:T(8,128)S(1)} %get-tuple-element.99), channel_id=1, source_target_pairs={{0,1},{1,0},{2,3},{3,2},{4,5},{5,4},{6,7},{7,6},{8,9},{9,8},{10,11... | collective-permute-start | bytes 602120 | tf_op jit(solution)/shard_map/ppermute | solution.py:795
  6.7 1.4 %collective-permute-done.4.far = f32[23,2,8,128]{3,2,1,0:T(8,128)S(1)} collective-permute-done((f32[23,2,8,128]{3,2,1,0:T(8,128)S(1)}, f32[23,2,8,128]{3,2,1,0:T(8,128)S(1)}, u32[]{:S(2)}, u32[]{:S(2)}) %collective-permute-start.4) | collective-permute-done | bytes 188448 | tf_op jit(solution)/shard_map/ppermute | solution.py:761
  8.1 0.0 collective-permute-done.5.near
  8.1 1.1 %boundary_steps.1 = (f32[19,12,8,128]{3,2,1,0:T(8,128)S(1)}, f32[16,18,8,128]{3,2,1,0:T(8,128)S(1)}, f32[18,8,128]{2,1,0:T(8,128)S(1)}, s32[18,8,128]{2,1,0:T(8,...) custom-call(f32[23,2,8,128]{3,2,1,0:T(8,128)S(1)} %collective-permut, ...), custom_call_target="tpu_custom_call" | custom-call | flops 160000000 | bytes 8000000 | tf_op jit(solution)/shard_map/boundary_steps/pallas_call | solution.py:736
  9.2 3.3 %collective-permute-start.8 = (f32[4,8,128]{2,1,0:T(8,128)S(1)}, f32[4,8,128]{2,1,0:T(8,128)S(1)}, u32[]{:S(2)}, u32[]{:S(2)}) collective-permute-start(f32[4,8,128]{2,1,0:T(8,128)S(1)} %get-tuple-element.100), channel_id=1, source_target_pairs={{0,1},{1,0},{2,3},{3,2},{4,5},{5,4},{6,7},{7,6},{8,9},{9,8},{10,11... | collective-permute-start | bytes 49160 | tf_op jit(solution)/shard_map/ppermute | solution.py:842
  12.4 0.8 %collective-permute-done.8 = f32[4,8,128]{2,1,0:T(8,128)S(1)} collective-permute-done((f32[4,8,128]{2,1,0:T(8,128)S(1)}, f32[4,8,128]{2,1,0:T(8,128)S(1)}, u32[]{:S(2)}, u32[]{:S(2)}) %collective-permute-start.8) | collective-permute-done | bytes 16416 | tf_op jit(solution)/shard_map/ppermute | solution.py:842
  13.3 0.0 collective-permute-start.9
  13.3 1.3 %slot_counts.1 = s32[3]{0:T(128)S(1)} custom-call(s32[48]{0:T(128)S(1)} %copy-done), custom_call_target="tpu_custom_call" | custom-call | flops 400000000 | bytes 20000000 | tf_op jit(solution)/shard_map/slot_counts/pallas_call | solution.py:736
  14.6 0.6 %slice.3 = s32[1]{0:T(128)} slice(s32[3]{0:T(128)S(1)} %slot_counts.1), slice={[2:3]} | slice | bytes 8 | tf_op jit(solution)/shard_map/slice | solution.py:846
  15.8 1.2 %collective-permute-done.9 = f32[4,8,128]{2,1,0:T(8,128)S(1)} collective-permute-done((f32[4,8,128]{2,1,0:T(8,128)S(1)}, f32[4,8,128]{2,1,0:T(8,128)S(1)}, u32[]{:S(2)}, u32[]{:S(2)}) %collective-permute-start.9) | collective-permute-done | bytes 16416 | tf_op jit(solution)/shard_map/ppermute | solution.py:842
  17.0 0.0 collective-permute-start.10
  17.0 0.0 collective-permute-done.6.from_far
  17.0 0.0 collective-permute-done.7.from_near
  17.1 1.3 %outer_steps.1 = (f32[2,19,4,8,128]{4,3,2,1,0:T(8,128)S(1)}, f32[18,8,128]{2,1,0:T(8,128)S(1)}, f32[19,18,8,128]{3,2,1,0:T(8,128)S(1)}) custom-call(f32[16,18,8,128]{3,2,1,0:T(8,128)S(1)} %get-tuple-element.92.history, f32[18,8,128]{2,1,0:T(8,128)S(1)} %get-tuple-element.93.opens, s32[18,8,128]{2,1,0:T(8,128)S(1)} %get-tuple-element.94.fluid, ...), custom_call_target="tpu_custom_call" | custom-call | flops 240000000 | bytes 12000000 | tf_op jit(solution)/shard_map/outer_steps/pallas_call | solution.py:736
  18.3 2.4 %collective-permute-done.10 = f32[4,8,128]{2,1,0:T(8,128)S(1)} collective-permute-done((f32[4,8,128]{2,1,0:T(8,128)S(1)}, f32[4,8,128]{2,1,0:T(8,128)S(1)}, u32[]{:S(2)}, u32[]{:S(2)}) %collective-permute-start.10) | collective-permute-done | bytes 16416 | tf_op jit(solution)/shard_map/ppermute | solution.py:842
  20.8 2.6 %collective-permute-start.11 = (f32[4,8,128]{2,1,0:T(8,128)S(1)}, f32[4,8,128]{2,1,0:T(8,128)S(1)}, u32[]{:S(2)}, u32[]{:S(2)}) collective-permute-start(f32[4,8,128]{2,1,0:T(8,128)S(1)} %add.14.summed), channel_id=1, source_target_pairs={{0,8},{1,9},{2,10},{3,11},{4,12},{5,13},{6,14},{7,15},{8,0},{9,1},... | collective-permute-start | bytes 49160 | tf_op jit(solution)/shard_map/ppermute | solution.py:842
  23.4 1.0 %gradient_steps.1 = (f32[12,8,128]{2,1,0:T(8,128)S(1)}, f32[4,8,128]{2,1,0:T(8,128)S(1)}, f32[4,8,128]{2,1,0:T(8,128)S(1)}) custom-call(f32[16,18,8,128]{3,2,1,0:T(8,128)S(1)} %get-tuple-element.92.history, f32[18,8,128]{2,1,0:T(8,128)S(1)} %get-tuple-element.93.opens, s32[18,8,128]{2,1,0:T(8,128)S(1)} %get-tuple-element.95.words, ...), custom_call_target="tpu_custom_call" | custom-call | flops 120000000 | bytes 6000000 | tf_op jit(solution)/shard_map/gradient_steps/pallas_call | solution.py:736
  24.4 1.9 %collective-permute-start.12 = (f32[4,8,128]{2,1,0:T(8,128)S(1)}, f32[4,8,128]{2,1,0:T(8,128)S(1)}, u32[]{:S(2)}, u32[]{:S(2)}) collective-permute-start(f32[4,8,128]{2,1,0:T(8,128)S(1)} %get-tuple-element.105), channel_id=1, source_target_pairs={{1,2},{2,1},{3,4},{4,3},{5,6},{6,5},{7,8},{8,7},{9,10},{10,9},{11,... | collective-permute-start | bytes 49160 | tf_op jit(solution)/shard_map/ppermute | solution.py:885
  26.3 1.1 %collective-permute-start.13 = (f32[4,8,128]{2,1,0:T(8,128)S(1)}, f32[4,8,128]{2,1,0:T(8,128)S(1)}, u32[]{:S(2)}, u32[]{:S(2)}) collective-permute-start(f32[4,8,128]{2,1,0:T(8,128)S(1)} %get-tuple-element.106), channel_id=1, source_target_pairs={{0,1},{1,0},{2,3},{3,2},{4,5},{5,4},{6,7},{7,6},{8,9},{9,8},{10,11... | collective-permute-start | bytes 49160 | tf_op jit(solution)/shard_map/ppermute | solution.py:884
  27.4 0.8 %conditional.2 = (f32[19,20,8,128]{3,2,1,0:T(8,128)S(1)}) conditional(s32[]{:T(128)} %bitcast.2, (s32[3]{0:T(128)S(1)}, f32[19,12,8,128]{3,2,1,0:T(8,128)S(1)}, f32[2,19,4,8,128]{4,3,2,1,0:T(8,128)S(1)}, f32[12,8,128]{2,1,0:T(8,128)S(1)}) %tuple.20, (f32[19,12,8,128]{3,2,1,0:T(8,128)S(1)}, s32[3]{0:T(128)S(1)}, f32[12,8,128]{2,1,0:T(8,128)S(1)}) %tuple.21), branch_computations={%region_0.0_spmd, %region_1.0_spmd} | conditional | flops 80466944 | bytes 15206744 | solution.py:933
  27.4 0.8 %place_populations.2 = f32[19,20,8,128]{3,2,1,0:T(8,128)S(1)} custom-call(s32[3]{0:T(128)S(1)} %get-tuple-element.32.where, f32[19,12,8,128]{3,2,1,0:T(8,128)S(1)} %get-tuple-element.33.final, f32[2,19,4,8,128]{4,3,2,1,0:T(8,128)S(1)} %get-tuple-element.38.outer, f32[12,8,128]{2,1,0:T(8,128)S(1)} %get-tuple-element.39.later), custom_call_target="tpu_custom_call" | custom-call | flops 80000000 | bytes 4000000 | tf_op jit(solution)/shard_map/cond/branch_0_fun/place_populations/pallas_call | solution.py:736
  28.2 0.0 copy-start.1
  28.2 2.1 %collective-permute-done.12 = f32[4,8,128]{2,1,0:T(8,128)S(1)} collective-permute-done((f32[4,8,128]{2,1,0:T(8,128)S(1)}, f32[4,8,128]{2,1,0:T(8,128)S(1)}, u32[]{:S(2)}, u32[]{:S(2)}) %collective-permute-start.12) | collective-permute-done | bytes 16416 | tf_op jit(solution)/shard_map/ppermute | solution.py:885
  30.3 0.7 %conditional.3 = (f32[20,8,128]{2,1,0:T(8,128)S(1)}) conditional(s32[]{:T(128)} %bitcast.2, (s32[3]{0:T(128)S(1)}, f32[4,8,128]{2,1,0:T(8,128)S(1)}, f32[12,8,128]{2,1,0:T(8,128)S(1)}, f32[4,8,128]{2,1,0:T(8,128)S(1)}, f32[4,8,128]{2,1,0:T(8,128)S(1)}) %tuple.22, (f32[12,8,128]{2,1,0:T(8,128)S(1)}, s32[3]{0:T(128)S(1)}, ...), branch_computations={%region_2.0_spmd, %region_3.0_spmd} | conditional | flops 20000000 | bytes 1393304 | solution.py:934
  30.3 0.7 %near_gradient.1 = f32[20,8,128]{2,1,0:T(8,128)S(1)} custom-call(s32[3]{0:T(128)S(1)} %get-tuple-element.43.where, f32[4,8,128]{2,1,0:T(8,128)S(1)} %get-tuple-element.44.drag, f32[12,8,128]{2,1,0:T(8,128)S(1)} %get-tuple-element.45.gradient, f32[4,8,128]{2,1,0:T(8,128)S(1)} %get-tuple-element.46.from_far, f32[4,8,128]{2,1,0:T(8,128)S(1)} %get-tuple-element.47.from_near), custom_call_target="tpu_custom_call" | custom-call | flops 20000000 | bytes 1000000 | tf_op jit(solution)/shard_map/cond/branch_0_fun/near_gradient/pallas_call | solution.py:736
  31.1 0.0 copy-start.2
  31.1 0.6 %copy-done.2 = f32[20,8,128]{2,1,0:T(8,128)} copy-done((f32[20,8,128]{2,1,0:T(8,128)}, f32[20,8,128]{2,1,0:T(8,128)S(1)}, u32[]{:S(2)}) %copy-start.2) | copy-done | bytes 81944
  (9 shorter events, 0.0 us)
Async XLA Ops:
  2.0 6.1 %collective-permute-start.4 = (f32[23,2,8,128]{3,2,1,0:T(8,128)S(1)}, f32[23,2,8,128]{3,2,1,0:T(8,128)S(1)}, u32[]{:S(2)}, u32[]{:S(2)}) collective-permute-start(f32[23,2,8,128]{3,2,1,0:T(8,128)S(1)} %get-tuple-element.80), channel_id=1, source_target_pairs={{0,15},{1,2},{2,1},{3,4},{4,3},{5,6},{6,5},{7,8},{8,7},{9,10},{10,... | collective-permute-start | bytes 565256 | tf_op jit(solution)/shard_map/ppermute | solution.py:761
  2.9 5.2 %collective-permute-start.5 = (f32[23,2,8,128]{3,2,1,0:T(8,128)S(1)}, f32[23,2,8,128]{3,2,1,0:T(8,128)S(1)}, u32[]{:S(2)}, u32[]{:S(2)}) collective-permute-start(f32[23,2,8,128]{3,2,1,0:T(8,128)S(1)} %get-tuple-element.81), channel_id=1, source_target_pairs={{0,1},{1,0},{2,3},{3,2},{4,5},{5,4},{6,7},{7,6},{8,9},{9,8},{10,11... | collective-permute-start | bytes 565256 | tf_op jit(solution)/shard_map/ppermute | solution.py:760
  5.0 12.0 %collective-permute-start.6 = (f32[49,8,128]{2,1,0:T(8,128)S(1)}, f32[49,8,128]{2,1,0:T(8,128)S(1)}, u32[]{:S(2)}, u32[]{:S(2)}) collective-permute-start(f32[49,8,128]{2,1,0:T(8,128)S(1)} %get-tuple-element.98), channel_id=1, source_target_pairs={{0,15},{1,2},{2,1},{3,4},{4,3},{5,6},{6,5},{7,8},{8,7},{9,10},{10,... | collective-permute-start | bytes 602120 | tf_op jit(solution)/shard_map/ppermute | solution.py:796
  6.1 10.9 %collective-permute-start.7 = (f32[49,8,128]{2,1,0:T(8,128)S(1)}, f32[49,8,128]{2,1,0:T(8,128)S(1)}, u32[]{:S(2)}, u32[]{:S(2)}) collective-permute-start(f32[49,8,128]{2,1,0:T(8,128)S(1)} %get-tuple-element.99), channel_id=1, source_target_pairs={{0,1},{1,0},{2,3},{3,2},{4,5},{5,4},{6,7},{7,6},{8,9},{9,8},{10,11... | collective-permute-start | bytes 602120 | tf_op jit(solution)/shard_map/ppermute | solution.py:795
  8.1 5.2 %copy-start = (s32[48]{0:T(128)S(1)}, s32[48]{0:T(128)}, u32[]{:S(2)}) copy-start(s32[48]{0:T(128)} %owner.1) | copy-start | bytes 580
  9.2 4.1 %collective-permute-start.8 = (f32[4,8,128]{2,1,0:T(8,128)S(1)}, f32[4,8,128]{2,1,0:T(8,128)S(1)}, u32[]{:S(2)}, u32[]{:S(2)}) collective-permute-start(f32[4,8,128]{2,1,0:T(8,128)S(1)} %get-tuple-element.100), channel_id=1, source_target_pairs={{0,1},{1,0},{2,3},{3,2},{4,5},{5,4},{6,7},{7,6},{8,9},{9,8},{10,11... | collective-permute-start | bytes 49160 | tf_op jit(solution)/shard_map/ppermute | solution.py:842
  13.3 3.7 %collective-permute-start.9 = (f32[4,8,128]{2,1,0:T(8,128)S(1)}, f32[4,8,128]{2,1,0:T(8,128)S(1)}, u32[]{:S(2)}, u32[]{:S(2)}) collective-permute-start(f32[4,8,128]{2,1,0:T(8,128)S(1)} %add.12), channel_id=1, source_target_pairs={{0,2},{1,3},{2,0},{3,1},{4,6},{5,7},{6,4},{7,5},{8,10},{9,11},{10,... | collective-permute-start | bytes 49160 | tf_op jit(solution)/shard_map/ppermute | solution.py:842
  17.0 3.7 %collective-permute-start.10 = (f32[4,8,128]{2,1,0:T(8,128)S(1)}, f32[4,8,128]{2,1,0:T(8,128)S(1)}, u32[]{:S(2)}, u32[]{:S(2)}) collective-permute-start(f32[4,8,128]{2,1,0:T(8,128)S(1)} %add.13.summed), channel_id=1, source_target_pairs={{0,4},{1,5},{2,6},{3,7},{4,0},{5,1},{6,2},{7,3},{8,12},{9,13},{10,... | collective-permute-start | bytes 49160 | tf_op jit(solution)/shard_map/ppermute | solution.py:842
  20.8 7.4 %collective-permute-start.11 = (f32[4,8,128]{2,1,0:T(8,128)S(1)}, f32[4,8,128]{2,1,0:T(8,128)S(1)}, u32[]{:S(2)}, u32[]{:S(2)}) collective-permute-start(f32[4,8,128]{2,1,0:T(8,128)S(1)} %add.14.summed), channel_id=1, source_target_pairs={{0,8},{1,9},{2,10},{3,11},{4,12},{5,13},{6,14},{7,15},{8,0},{9,1},... | collective-permute-start | bytes 49160 | tf_op jit(solution)/shard_map/ppermute | solution.py:842
  24.4 6.0 %collective-permute-start.12 = (f32[4,8,128]{2,1,0:T(8,128)S(1)}, f32[4,8,128]{2,1,0:T(8,128)S(1)}, u32[]{:S(2)}, u32[]{:S(2)}) collective-permute-start(f32[4,8,128]{2,1,0:T(8,128)S(1)} %get-tuple-element.105), channel_id=1, source_target_pairs={{1,2},{2,1},{3,4},{4,3},{5,6},{6,5},{7,8},{8,7},{9,10},{10,9},{11,... | collective-permute-start | bytes 49160 | tf_op jit(solution)/shard_map/ppermute | solution.py:885
  26.3 4.0 %collective-permute-start.13 = (f32[4,8,128]{2,1,0:T(8,128)S(1)}, f32[4,8,128]{2,1,0:T(8,128)S(1)}, u32[]{:S(2)}, u32[]{:S(2)}) collective-permute-start(f32[4,8,128]{2,1,0:T(8,128)S(1)} %get-tuple-element.106), channel_id=1, source_target_pairs={{0,1},{1,0},{2,3},{3,2},{4,5},{5,4},{6,7},{7,6},{8,9},{9,8},{10,11... | collective-permute-start | bytes 49160 | tf_op jit(solution)/shard_map/ppermute | solution.py:884
  28.2 2.9 %copy-start.1 = (f32[19,20,8,128]{3,2,1,0:T(8,128)}, f32[19,20,8,128]{3,2,1,0:T(8,128)S(1)}, u32[]{:S(2)}) copy-start(f32[19,20,8,128]{3,2,1,0:T(8,128)S(1)} %get-tuple-element.107) | copy-start | bytes 4669444
  31.1 0.6 %copy-start.2 = (f32[20,8,128]{2,1,0:T(8,128)}, f32[20,8,128]{2,1,0:T(8,128)S(1)}, u32[]{:S(2)}) copy-start(f32[20,8,128]{2,1,0:T(8,128)S(1)} %get-tuple-element.108) | copy-start | bytes 245764

commit v9 on v8

--- a/solution.py
+++ b/solution.py
@@ -234,7 +234,7 @@
     copies[4].wait()
 
 
-def count_kernel(home_blocks, owner, where):
+def count_blocks(home_blocks, owner, where):
     rank = lax.axis_index("block")
     below = jnp.int32(0)
     own = jnp.int32(0)
@@ -254,6 +254,7 @@
 
 def interior_kernel(
     home,
+    owner_far,
     pops,
     marked,
     to_near,
@@ -265,10 +266,15 @@
     fluid,
     words,
     drag,
+    where,
     even,
     odd,
+    owner,
+    sem,
 ):
     up = parity()
+    copy = pltpu.make_async_copy(owner_far, owner, sem)
+    copy.start()
 
     def start(plane):
         is_fluid, open_rate = is_fluid_rate(marked[plane])
@@ -343,6 +349,8 @@
             final[m, home - STEPS + plane] = pops[m, home - STEPS + plane]
         for out, ahead in ((to_near, up), (to_far, 1 - up)):
             out[30 + m] = final[m, STEPS + ahead * (home - 1 - 2 * STEPS)]
+    copy.wait()
+    count_blocks(home // BX, owner, where)
 
 
 def boundary_kernel(
@@ -713,8 +721,7 @@
 def body(populations, design, fluid_mask, owner_after):
     count = lax.axis_size("block")
     home, width_y, width_z = design.shape
-    home_blocks = home // BX
-    slots = home_blocks + 2
+    slots = home // BX + 2
     span = home + 2 * HALO
     plane = (width_y, width_z)
     vmem = pl.BlockSpec(memory_space=pltpu.VMEM)
@@ -781,30 +788,22 @@
         inner_fluid,
         inner_words,
         inner_drag,
+        where,
     ) = call(
         functools.partial(interior_kernel, home),
         "interior_steps",
-        [vmem] * 2,
-        [(shape, vmem) for shape in inner_shapes],
-        [scratch(19, home)] * 2,
+        [hbm] + [vmem] * 2,
+        [(shape, vmem) for shape in inner_shapes] + [(jax.ShapeDtypeStruct((3,), jnp.int32), smem)],
+        [scratch(19, home)] * 2
+        + [pltpu.SMEM(owner_after.shape, jnp.int32), pltpu.SemaphoreType.DMA(())],
         16,
         6_000_000,
+        pltpu.with_memory_space_constraint(owner_after, pltpu.HBM),
         pops,
         marked,
     )
     from_near = lax.ppermute(to_near, "block", near_pairs)
     from_far = lax.ppermute(to_far, "block", far_pairs)
-
-    (where,) = call(
-        functools.partial(count_kernel, home_blocks),
-        "slot_counts",
-        [smem],
-        [(jax.ShapeDtypeStruct((3,), jnp.int32), smem)],
-        [],
-        2,
-        20_000_000,
-        owner_after,
-    )
 
     boundary_shapes = (
         planes(19, home),

time: 31.9 us -> 30 us (0.940)
  the two profiles are of different devices: /device:TPU:8 before, /device:TPU:0 now
where the time goes in v9:
time: 30 us; the launch traced here: 29.9 us
  starting transfers between devices  12.7 us (42%)
  Pallas kernels  8.32 us (28%)
  waiting for transfers between devices  6.16 us (21%)
  between operations  1.42 us (5%)
  local copies, waits for them, and re-layouts  1.21 us (4%)
    pallas_call x7, Pallas kernels, call(): pl.pallas_call(kernel, out_shape=[shape for shape, _ in outs], in_specs=i...  8.32 us
    ppermute x4, waiting for transfers between devices, body(): sums.append(sums[-1] + lax.ppermute(sums[-1], 'block', swap))  5.78 us
    ppermute x1, starting transfers between devices, body(): far = lax.ppermute(own_far, 'block', far_pairs)  5.51 us
    ppermute x2, starting transfers between devices, body(): from_near = lax.ppermute(to_near, 'block', near_pairs)  3.4 us
    ppermute x4, starting transfers between devices, body(): sums.append(sums[-1] + lax.ppermute(sums[-1], 'block', swap))  2.3 us
    ppermute x1, starting transfers between devices, body(): from_far = lax.ppermute(to_far, 'block', far_pairs)  0.82 us
    ppermute x1, starting transfers between devices, body(): from_far = lax.ppermute(to_far, 'block', inner_pairs)  0.66 us
    unnamed x4, local copies, waits for them, and re-layouts  0.63 us
  transfers between devices with their start and end apart: 10, of which 4 were waited for; matrix products, arithmetic and copies ran while one was open for 2% of the time, Pallas kernels for 21%

profile of v9, /device:TPU:0, one launch (start us, length us, event | category | flops | bytes accessed | tf_op | source)
XLA Modules:
  0.0 29.9 jit_solution(16835119442602474688)
XLA Ops:
  0.6 1.4 %edge_planes.1 = (f32[23,2,8,128]{3,2,1,0:T(8,128)S(1)}, f32[23,2,8,128]{3,2,1,0:T(8,128)S(1)}, f32[19,12,8,128]{3,2,1,0:T(8,128)S(1)}, f32[12,8,128]{2,1,0:T(8,128)S(1)}) custom-call(f32[19,12,8,128]{3,2,1,0:T(8,128)} %pops_far.1, f32[12,8,128]{2,1,0:T(8,128)} %design.1, s32[12,8,128]{2,1,0:T(8,128)} %mask.1), custom_call_target="tpu_custom_call" | custom-call | flops 20000000 | bytes 1000000 | tf_op jit(solution)/shard_map/edge_planes/pallas_call | solution.py:743
  2.0 5.5 %collective-permute-start.4 = (f32[23,2,8,128]{3,2,1,0:T(8,128)S(1)}, f32[23,2,8,128]{3,2,1,0:T(8,128)S(1)}, u32[]{:S(2)}, u32[]{:S(2)}) collective-permute-start(f32[23,2,8,128]{3,2,1,0:T(8,128)S(1)} %get-tuple-element.84), channel_id=1, source_target_pairs={{0,15},{1,2},{2,1},{3,4},{4,3},{5,6},{6,5},{7,8},{8,7},{9,10},{10,... | collective-permute-start | bytes 565256 | tf_op jit(solution)/shard_map/ppermute | solution.py:768
  7.5 0.0 collective-permute-start.5
  7.5 2.1 %interior_steps.1 = (f32[49,8,128]{2,1,0:T(8,128)S(1)}, f32[49,8,128]{2,1,0:T(8,128)S(1)}, f32[19,12,8,128]{3,2,1,0:T(8,128)S(1)}, f32[16,12,8,128]{3,2,1,0:T(8,...) custom-call(s32[48]{0:T(128)} %owner_far.1, ...), custom_call_target="tpu_custom_call" | custom-call | flops 120000000 | bytes 6000000 | tf_op jit(solution)/shard_map/interior_steps/pallas_call | solution.py:743
  9.6 0.8 %collective-permute-start.6 = (f32[49,8,128]{2,1,0:T(8,128)S(1)}, f32[49,8,128]{2,1,0:T(8,128)S(1)}, u32[]{:S(2)}, u32[]{:S(2)}) collective-permute-start(f32[49,8,128]{2,1,0:T(8,128)S(1)} %get-tuple-element.100), channel_id=1, source_target_pairs={{0,15},{1,2},{2,1},{3,4},{4,3},{5,6},{6,5},{7,8},{8,7},{9,10},{10,... | collective-permute-start | bytes 602120 | tf_op jit(solution)/shard_map/ppermute | solution.py:806
  10.4 0.0 collective-permute-start.7
  10.4 0.4 %collective-permute-done.4.far = f32[23,2,8,128]{3,2,1,0:T(8,128)S(1)} collective-permute-done((f32[23,2,8,128]{3,2,1,0:T(8,128)S(1)}, f32[23,2,8,128]{3,2,1,0:T(8,128)S(1)}, u32[]{:S(2)}, u32[]{:S(2)}) %collective-permute-start.4) | collective-permute-done | bytes 188448 | tf_op jit(solution)/shard_map/ppermute | solution.py:768
  10.8 0.0 collective-permute-done.5.near
  10.8 1.1 %boundary_steps.1 = (f32[19,12,8,128]{3,2,1,0:T(8,128)S(1)}, f32[16,18,8,128]{3,2,1,0:T(8,128)S(1)}, f32[18,8,128]{2,1,0:T(8,128)S(1)}, s32[18,8,128]{2,1,0:T(8,...) custom-call(f32[23,2,8,128]{3,2,1,0:T(8,128)S(1)} %collective-permut, ...), custom_call_target="tpu_custom_call" | custom-call | flops 160000000 | bytes 8000000 | tf_op jit(solution)/shard_map/boundary_steps/pallas_call | solution.py:743
  11.9 0.2 collective-permute-start.8
  12.1 1.0 %collective-permute-done.8 = f32[4,8,128]{2,1,0:T(8,128)S(1)} collective-permute-done((f32[4,8,128]{2,1,0:T(8,128)S(1)}, f32[4,8,128]{2,1,0:T(8,128)S(1)}, u32[]{:S(2)}, u32[]{:S(2)}) %collective-permute-start.8) | collective-permute-done | bytes 16416 | tf_op jit(solution)/shard_map/ppermute | solution.py:841
  13.1 1.3 %collective-permute-start.9 = (f32[4,8,128]{2,1,0:T(8,128)S(1)}, f32[4,8,128]{2,1,0:T(8,128)S(1)}, u32[]{:S(2)}, u32[]{:S(2)}) collective-permute-start(f32[4,8,128]{2,1,0:T(8,128)S(1)} %add.12), channel_id=1, source_target_pairs={{0,2},{1,3},{2,0},{3,1},{4,6},{5,7},{6,4},{7,5},{8,10},{9,11},{10,... | collective-permute-start | bytes 49160 | tf_op jit(solution)/shard_map/ppermute | solution.py:841
  14.4 0.6 %slice.3 = s32[1]{0:T(128)} slice(s32[3]{0:T(128)S(1)} %get-tuple-element.83), slice={[2:3]} | slice | bytes 8 | tf_op jit(solution)/shard_map/slice | solution.py:845
  15.6 2.3 %collective-permute-done.9 = f32[4,8,128]{2,1,0:T(8,128)S(1)} collective-permute-done((f32[4,8,128]{2,1,0:T(8,128)S(1)}, f32[4,8,128]{2,1,0:T(8,128)S(1)}, u32[]{:S(2)}, u32[]{:S(2)}) %collective-permute-start.9) | collective-permute-done | bytes 16416 | tf_op jit(solution)/shard_map/ppermute | solution.py:841
  18.0 0.0 collective-permute-start.10
  18.0 0.0 collective-permute-done.6.from_far
  18.0 1.3 %outer_steps.1 = (f32[2,19,4,8,128]{4,3,2,1,0:T(8,128)S(1)}, f32[18,8,128]{2,1,0:T(8,128)S(1)}, f32[19,18,8,128]{3,2,1,0:T(8,128)S(1)}) custom-call(f32[16,18,8,128]{3,2,1,0:T(8,128)S(1)} %get-tuple-element.94.history, f32[18,8,128]{2,1,0:T(8,128)S(1)} %get-tuple-element.95.opens, s32[18,8,128]{2,1,0:T(8,128)S(1)} %get-tuple-element.96.fluid, ...), custom_call_target="tpu_custom_call" | custom-call | flops 240000000 | bytes 12000000 | tf_op jit(solution)/shard_map/outer_steps/pallas_call | solution.py:743
  19.3 2.4 %collective-permute-done.10 = f32[4,8,128]{2,1,0:T(8,128)S(1)} collective-permute-done((f32[4,8,128]{2,1,0:T(8,128)S(1)}, f32[4,8,128]{2,1,0:T(8,128)S(1)}, u32[]{:S(2)}, u32[]{:S(2)}) %collective-permute-start.10) | collective-permute-done | bytes 16416 | tf_op jit(solution)/shard_map/ppermute | solution.py:841
  21.7 0.8 %collective-permute-start.11 = (f32[4,8,128]{2,1,0:T(8,128)S(1)}, f32[4,8,128]{2,1,0:T(8,128)S(1)}, u32[]{:S(2)}, u32[]{:S(2)}) collective-permute-start(f32[4,8,128]{2,1,0:T(8,128)S(1)} %add.14.summed), channel_id=1, source_target_pairs={{0,8},{1,9},{2,10},{3,11},{4,12},{5,13},{6,14},{7,15},{8,0},{9,1},... | collective-permute-start | bytes 49160 | tf_op jit(solution)/shard_map/ppermute | solution.py:841
  22.5 1.0 %gradient_steps.1 = (f32[12,8,128]{2,1,0:T(8,128)S(1)}, f32[4,8,128]{2,1,0:T(8,128)S(1)}, f32[4,8,128]{2,1,0:T(8,128)S(1)}) custom-call(f32[16,18,8,128]{3,2,1,0:T(8,128)S(1)} %get-tuple-element.94.history, f32[18,8,128]{2,1,0:T(8,128)S(1)} %get-tuple-element.95.opens, s32[18,8,128]{2,1,0:T(8,128)S(1)} %get-tuple-element.97.words, ...), custom_call_target="tpu_custom_call" | custom-call | flops 120000000 | bytes 6000000 | tf_op jit(solution)/shard_map/gradient_steps/pallas_call | solution.py:743
  23.5 0.7 %collective-permute-start.12 = (f32[4,8,128]{2,1,0:T(8,128)S(1)}, f32[4,8,128]{2,1,0:T(8,128)S(1)}, u32[]{:S(2)}, u32[]{:S(2)}) collective-permute-start(f32[4,8,128]{2,1,0:T(8,128)S(1)} %get-tuple-element.107), channel_id=1, source_target_pairs={{1,2},{2,1},{3,4},{4,3},{5,6},{6,5},{7,8},{8,7},{9,10},{10,9},{11,... | collective-permute-start | bytes 49160 | tf_op jit(solution)/shard_map/ppermute | solution.py:884
  24.2 3.4 %collective-permute-start.13 = (f32[4,8,128]{2,1,0:T(8,128)S(1)}, f32[4,8,128]{2,1,0:T(8,128)S(1)}, u32[]{:S(2)}, u32[]{:S(2)}) collective-permute-start(f32[4,8,128]{2,1,0:T(8,128)S(1)} %get-tuple-element.108), channel_id=1, source_target_pairs={{0,1},{1,0},{2,3},{3,2},{4,5},{5,4},{6,7},{7,6},{8,9},{9,8},{10,11... | collective-permute-start | bytes 49160 | tf_op jit(solution)/shard_map/ppermute | solution.py:883
  27.6 0.8 %conditional.2 = (f32[19,20,8,128]{3,2,1,0:T(8,128)S(1)}) conditional(s32[]{:T(128)} %bitcast.2, (s32[3]{0:T(128)S(1)}, f32[19,12,8,128]{3,2,1,0:T(8,128)S(1)}, f32[2,19,4,8,128]{4,3,2,1,0:T(8,128)S(1)}, f32[12,8,128]{2,1,0:T(8,128)S(1)}) %tuple.20, (f32[19,12,8,128]{3,2,1,0:T(8,128)S(1)}, s32[3]{0:T(128)S(1)}, f32[12,8,128]{2,1,0:T(8,128)S(1)}) %tuple.21), branch_computations={%region_0.0_spmd, %region_1.0_spmd} | conditional | flops 80466944 | bytes 15206744 | solution.py:932
  27.6 0.8 %place_populations.2 = f32[19,20,8,128]{3,2,1,0:T(8,128)S(1)} custom-call(s32[3]{0:T(128)S(1)} %get-tuple-element.32.where, f32[19,12,8,128]{3,2,1,0:T(8,128)S(1)} %get-tuple-element.33.final, f32[2,19,4,8,128]{4,3,2,1,0:T(8,128)S(1)} %get-tuple-element.38.outer, f32[12,8,128]{2,1,0:T(8,128)S(1)} %get-tuple-element.39.later), custom_call_target="tpu_custom_call" | custom-call | flops 80000000 | bytes 4000000 | tf_op jit(solution)/shard_map/cond/branch_0_fun/place_populations/pallas_call | solution.py:743
  28.4 0.0 copy-start
  28.4 0.0 collective-permute-done.11
  28.5 0.0 collective-permute-done.13
  28.5 0.7 %conditional.3 = (f32[20,8,128]{2,1,0:T(8,128)S(1)}) conditional(s32[]{:T(128)} %bitcast.2, (s32[3]{0:T(128)S(1)}, f32[4,8,128]{2,1,0:T(8,128)S(1)}, f32[12,8,128]{2,1,0:T(8,128)S(1)}, f32[4,8,128]{2,1,0:T(8,128)S(1)}, f32[4,8,128]{2,1,0:T(8,128)S(1)}) %tuple.22, (f32[12,8,128]{2,1,0:T(8,128)S(1)}, s32[3]{0:T(128)S(1)}, ...), branch_computations={%region_2.0_spmd, %region_3.0_spmd} | conditional | flops 20000000 | bytes 1393304 | solution.py:933
  28.5 0.7 %near_gradient.1 = f32[20,8,128]{2,1,0:T(8,128)S(1)} custom-call(s32[3]{0:T(128)S(1)} %get-tuple-element.43.where, f32[4,8,128]{2,1,0:T(8,128)S(1)} %get-tuple-element.44.drag, f32[12,8,128]{2,1,0:T(8,128)S(1)} %get-tuple-element.45.gradient, f32[4,8,128]{2,1,0:T(8,128)S(1)} %get-tuple-element.46.from_far, f32[4,8,128]{2,1,0:T(8,128)S(1)} %get-tuple-element.47.from_near), custom_call_target="tpu_custom_call" | custom-call | flops 20000000 | bytes 1000000 | tf_op jit(solution)/shard_map/cond/branch_0_fun/near_gradient/pallas_call | solution.py:743
  29.2 0.0 copy-start.1
  29.2 0.3 %copy-done = f32[19,20,8,128]{3,2,1,0:T(8,128)} copy-done((f32[19,20,8,128]{3,2,1,0:T(8,128)}, f32[19,20,8,128]{3,2,1,0:T(8,128)S(1)}, u32[]{:S(2)}) %copy-start) | copy-done | bytes 1556504
  29.6 0.3 copy-done.1
  (6 shorter events, 0.0 us)
Async XLA Ops:
  2.0 8.8 %collective-permute-start.4 = (f32[23,2,8,128]{3,2,1,0:T(8,128)S(1)}, f32[23,2,8,128]{3,2,1,0:T(8,128)S(1)}, u32[]{:S(2)}, u32[]{:S(2)}) collective-permute-start(f32[23,2,8,128]{3,2,1,0:T(8,128)S(1)} %get-tuple-element.84), channel_id=1, source_target_pairs={{0,15},{1,2},{2,1},{3,4},{4,3},{5,6},{6,5},{7,8},{8,7},{9,10},{10,... | collective-permute-start | bytes 565256 | tf_op jit(solution)/shard_map/ppermute | solution.py:768
  7.5 3.3 %collective-permute-start.5 = (f32[23,2,8,128]{3,2,1,0:T(8,128)S(1)}, f32[23,2,8,128]{3,2,1,0:T(8,128)S(1)}, u32[]{:S(2)}, u32[]{:S(2)}) collective-permute-start(f32[23,2,8,128]{3,2,1,0:T(8,128)S(1)} %get-tuple-element.85), channel_id=1, source_target_pairs={{0,1},{1,0},{2,3},{3,2},{4,5},{5,4},{6,7},{7,6},{8,9},{9,8},{10,11... | collective-permute-start | bytes 565256 | tf_op jit(solution)/shard_map/ppermute | solution.py:767
  9.6 8.4 %collective-permute-start.6 = (f32[49,8,128]{2,1,0:T(8,128)S(1)}, f32[49,8,128]{2,1,0:T(8,128)S(1)}, u32[]{:S(2)}, u32[]{:S(2)}) collective-permute-start(f32[49,8,128]{2,1,0:T(8,128)S(1)} %get-tuple-element.100), channel_id=1, source_target_pairs={{0,15},{1,2},{2,1},{3,4},{4,3},{5,6},{6,5},{7,8},{8,7},{9,10},{10,... | collective-permute-start | bytes 602120 | tf_op jit(solution)/shard_map/ppermute | solution.py:806
  10.4 7.6 %collective-permute-start.7 = (f32[49,8,128]{2,1,0:T(8,128)S(1)}, f32[49,8,128]{2,1,0:T(8,128)S(1)}, u32[]{:S(2)}, u32[]{:S(2)}) collective-permute-start(f32[49,8,128]{2,1,0:T(8,128)S(1)} %get-tuple-element.101), channel_id=1, source_target_pairs={{0,1},{1,0},{2,3},{3,2},{4,5},{5,4},{6,7},{7,6},{8,9},{9,8},{10,11... | collective-permute-start | bytes 602120 | tf_op jit(solution)/shard_map/ppermute | solution.py:805
  11.9 1.2 %collective-permute-start.8 = (f32[4,8,128]{2,1,0:T(8,128)S(1)}, f32[4,8,128]{2,1,0:T(8,128)S(1)}, u32[]{:S(2)}, u32[]{:S(2)}) collective-permute-start(f32[4,8,128]{2,1,0:T(8,128)S(1)} %get-tuple-element.102), channel_id=1, source_target_pairs={{0,1},{1,0},{2,3},{3,2},{4,5},{5,4},{6,7},{7,6},{8,9},{9,8},{10,11... | collective-permute-start | bytes 49160 | tf_op jit(solution)/shard_map/ppermute | solution.py:841
  13.1 4.8 %collective-permute-start.9 = (f32[4,8,128]{2,1,0:T(8,128)S(1)}, f32[4,8,128]{2,1,0:T(8,128)S(1)}, u32[]{:S(2)}, u32[]{:S(2)}) collective-permute-start(f32[4,8,128]{2,1,0:T(8,128)S(1)} %add.12), channel_id=1, source_target_pairs={{0,2},{1,3},{2,0},{3,1},{4,6},{5,7},{6,4},{7,5},{8,10},{9,11},{10,... | collective-permute-start | bytes 49160 | tf_op jit(solution)/shard_map/ppermute | solution.py:841
  18.0 3.7 %collective-permute-start.10 = (f32[4,8,128]{2,1,0:T(8,128)S(1)}, f32[4,8,128]{2,1,0:T(8,128)S(1)}, u32[]{:S(2)}, u32[]{:S(2)}) collective-permute-start(f32[4,8,128]{2,1,0:T(8,128)S(1)} %add.13.summed), channel_id=1, source_target_pairs={{0,4},{1,5},{2,6},{3,7},{4,0},{5,1},{6,2},{7,3},{8,12},{9,13},{10,... | collective-permute-start | bytes 49160 | tf_op jit(solution)/shard_map/ppermute | solution.py:841
  21.7 6.7 %collective-permute-start.11 = (f32[4,8,128]{2,1,0:T(8,128)S(1)}, f32[4,8,128]{2,1,0:T(8,128)S(1)}, u32[]{:S(2)}, u32[]{:S(2)}) collective-permute-start(f32[4,8,128]{2,1,0:T(8,128)S(1)} %add.14.summed), channel_id=1, source_target_pairs={{0,8},{1,9},{2,10},{3,11},{4,12},{5,13},{6,14},{7,15},{8,0},{9,1},... | collective-permute-start | bytes 49160 | tf_op jit(solution)/shard_map/ppermute | solution.py:841
  23.5 4.9 %collective-permute-start.12 = (f32[4,8,128]{2,1,0:T(8,128)S(1)}, f32[4,8,128]{2,1,0:T(8,128)S(1)}, u32[]{:S(2)}, u32[]{:S(2)}) collective-permute-start(f32[4,8,128]{2,1,0:T(8,128)S(1)} %get-tuple-element.107), channel_id=1, source_target_pairs={{1,2},{2,1},{3,4},{4,3},{5,6},{6,5},{7,8},{8,7},{9,10},{10,9},{11,... | collective-permute-start | bytes 49160 | tf_op jit(solution)/shard_map/ppermute | solution.py:884
  24.2 4.3 %collective-permute-start.13 = (f32[4,8,128]{2,1,0:T(8,128)S(1)}, f32[4,8,128]{2,1,0:T(8,128)S(1)}, u32[]{:S(2)}, u32[]{:S(2)}) collective-permute-start(f32[4,8,128]{2,1,0:T(8,128)S(1)} %get-tuple-element.108), channel_id=1, source_target_pairs={{0,1},{1,0},{2,3},{3,2},{4,5},{5,4},{6,7},{7,6},{8,9},{9,8},{10,11... | collective-permute-start | bytes 49160 | tf_op jit(solution)/shard_map/ppermute | solution.py:883
  28.4 1.1 %copy-start = (f32[19,20,8,128]{3,2,1,0:T(8,128)}, f32[19,20,8,128]{3,2,1,0:T(8,128)S(1)}, u32[]{:S(2)}) copy-start(f32[19,20,8,128]{3,2,1,0:T(8,128)S(1)} %get-tuple-element.109) | copy-start | bytes 4669444
  29.2 0.6 %copy-start.1 = (f32[20,8,128]{2,1,0:T(8,128)}, f32[20,8,128]{2,1,0:T(8,128)S(1)}, u32[]{:S(2)}) copy-start(f32[20,8,128]{2,1,0:T(8,128)S(1)} %get-tuple-element.110) | copy-start | bytes 245764

commit v10 on v9

--- a/solution.py
+++ b/solution.py
@@ -834,12 +834,11 @@
         inner_drag,
     )
 
+    distances = [1 << bit for bit in range(count.bit_length() - 1)]
     sums = [drag]
-    distance = 1
-    while distance < count:
+    for distance in distances[:1] + distances[2:] + distances[1:2]:
         swap = [(i, i ^ distance) for i in range(count)]
         sums.append(sums[-1] + lax.ppermute(sums[-1], "block", swap))
-        distance *= 2
     drag = sums[-1]
 
     is_far = where[2] > 0

time: 30 us -> 30.1 us (level)
  the two profiles are of different devices: /device:TPU:0 before, /device:TPU:26 now
where the time goes in v10:
time: 30.1 us; the launch traced here: 30 us
  waiting for transfers between devices  10.2 us (34%)
  starting transfers between devices  8.83 us (29%)
  Pallas kernels  8.32 us (28%)
  between operations  1.39 us (5%)
  local copies, waits for them, and re-layouts  1.21 us (4%)
    pallas_call x7, Pallas kernels, call(): pl.pallas_call(kernel, out_shape=[shape for shape, _ in outs], in_specs=i...  8.32 us
    ppermute x4, waiting for transfers between devices, body(): sums.append(sums[-1] + lax.ppermute(sums[-1], 'block', swap))  5.97 us
    ppermute x4, starting transfers between devices, body(): sums.append(sums[-1] + lax.ppermute(sums[-1], 'block', swap))  3.94 us
    ppermute x1, waiting for transfers between devices, body(): from_far = lax.ppermute(to_far, 'block', inner_pairs)  2.98 us
    ppermute x1, starting transfers between devices, body(): from_far = lax.ppermute(to_far, 'block', inner_pairs)  1.92 us
    ppermute x1, waiting for transfers between devices, body(): far = lax.ppermute(own_far, 'block', far_pairs)  1.22 us
    ppermute x1, starting transfers between devices, body(): from_far = lax.ppermute(to_far, 'block', far_pairs)  1.08 us
    ppermute x1, starting transfers between devices, body(): far = lax.ppermute(own_far, 'block', far_pairs)  0.91 us
  transfers between devices with their start and end apart: 10, of which 5 were waited for; matrix products, arithmetic and copies ran while one was open for 2% of the time, Pallas kernels for 21%

profile of v10, /device:TPU:26, one launch (start us, length us, event | category | flops | bytes accessed | tf_op | source)
XLA Modules:
  0.0 30.0 jit_solution(6833394768830103747)
XLA Ops:
  0.6 1.4 %edge_planes.1 = (f32[23,2,8,128]{3,2,1,0:T(8,128)S(1)}, f32[23,2,8,128]{3,2,1,0:T(8,128)S(1)}, f32[19,12,8,128]{3,2,1,0:T(8,128)S(1)}, f32[12,8,128]{2,1,0:T(8,128)S(1)}) custom-call(f32[19,12,8,128]{3,2,1,0:T(8,128)} %pops_far.1, f32[12,8,128]{2,1,0:T(8,128)} %design.1, s32[12,8,128]{2,1,0:T(8,128)} %mask.1), custom_call_target="tpu_custom_call" | custom-call | flops 20000000 | bytes 1000000 | tf_op jit(solution)/shard_map/edge_planes/pallas_call | solution.py:743
  2.0 0.9 %collective-permute-start.4 = (f32[23,2,8,128]{3,2,1,0:T(8,128)S(1)}, f32[23,2,8,128]{3,2,1,0:T(8,128)S(1)}, u32[]{:S(2)}, u32[]{:S(2)}) collective-permute-start(f32[23,2,8,128]{3,2,1,0:T(8,128)S(1)} %get-tuple-element.84), channel_id=1, source_target_pairs={{0,15},{1,2},{2,1},{3,4},{4,3},{5,6},{6,5},{7,8},{8,7},{9,10},{10,... | collective-permute-start | bytes 565256 | tf_op jit(solution)/shard_map/ppermute | solution.py:768
  2.9 0.8 %collective-permute-start.5 = (f32[23,2,8,128]{3,2,1,0:T(8,128)S(1)}, f32[23,2,8,128]{3,2,1,0:T(8,128)S(1)}, u32[]{:S(2)}, u32[]{:S(2)}) collective-permute-start(f32[23,2,8,128]{3,2,1,0:T(8,128)S(1)} %get-tuple-element.85), channel_id=1, source_target_pairs={{0,1},{1,0},{2,3},{3,2},{4,5},{5,4},{6,7},{7,6},{8,9},{9,8},{10,11... | collective-permute-start | bytes 565256 | tf_op jit(solution)/shard_map/ppermute | solution.py:767
  3.7 2.1 %interior_steps.1 = (f32[49,8,128]{2,1,0:T(8,128)S(1)}, f32[49,8,128]{2,1,0:T(8,128)S(1)}, f32[19,12,8,128]{3,2,1,0:T(8,128)S(1)}, f32[16,12,8,128]{3,2,1,0:T(8,...) custom-call(s32[48]{0:T(128)} %owner_far.1, ...), custom_call_target="tpu_custom_call" | custom-call | flops 120000000 | bytes 6000000 | tf_op jit(solution)/shard_map/interior_steps/pallas_call | solution.py:743
  5.8 1.1 %collective-permute-start.6 = (f32[49,8,128]{2,1,0:T(8,128)S(1)}, f32[49,8,128]{2,1,0:T(8,128)S(1)}, u32[]{:S(2)}, u32[]{:S(2)}) collective-permute-start(f32[49,8,128]{2,1,0:T(8,128)S(1)} %get-tuple-element.100), channel_id=1, source_target_pairs={{0,15},{1,2},{2,1},{3,4},{4,3},{5,6},{6,5},{7,8},{8,7},{9,10},{10,... | collective-permute-start | bytes 602120 | tf_op jit(solution)/shard_map/ppermute | solution.py:806
  6.8 0.0 collective-permute-start.7
  6.9 1.2 %collective-permute-done.4.far = f32[23,2,8,128]{3,2,1,0:T(8,128)S(1)} collective-permute-done((f32[23,2,8,128]{3,2,1,0:T(8,128)S(1)}, f32[23,2,8,128]{3,2,1,0:T(8,128)S(1)}, u32[]{:S(2)}, u32[]{:S(2)}) %collective-permute-start.4) | collective-permute-done | bytes 188448 | tf_op jit(solution)/shard_map/ppermute | solution.py:768
  8.1 0.0 collective-permute-done.5.near
  8.1 1.1 %boundary_steps.1 = (f32[19,12,8,128]{3,2,1,0:T(8,128)S(1)}, f32[16,18,8,128]{3,2,1,0:T(8,128)S(1)}, f32[18,8,128]{2,1,0:T(8,128)S(1)}, s32[18,8,128]{2,1,0:T(8,...) custom-call(f32[23,2,8,128]{3,2,1,0:T(8,128)S(1)} %collective-permut, ...), custom_call_target="tpu_custom_call" | custom-call | flops 160000000 | bytes 8000000 | tf_op jit(solution)/shard_map/boundary_steps/pallas_call | solution.py:743
  9.2 1.0 %collective-permute-start.8 = (f32[4,8,128]{2,1,0:T(8,128)S(1)}, f32[4,8,128]{2,1,0:T(8,128)S(1)}, u32[]{:S(2)}, u32[]{:S(2)}) collective-permute-start(f32[4,8,128]{2,1,0:T(8,128)S(1)} %get-tuple-element.102), channel_id=1, source_target_pairs={{0,1},{1,0},{2,3},{3,2},{4,5},{5,4},{6,7},{7,6},{8,9},{9,8},{10,11... | collective-permute-start | bytes 49160 | tf_op jit(solution)/shard_map/ppermute | solution.py:841
  10.1 0.8 %collective-permute-done.8 = f32[4,8,128]{2,1,0:T(8,128)S(1)} collective-permute-done((f32[4,8,128]{2,1,0:T(8,128)S(1)}, f32[4,8,128]{2,1,0:T(8,128)S(1)}, u32[]{:S(2)}, u32[]{:S(2)}) %collective-permute-start.8) | collective-permute-done | bytes 16416 | tf_op jit(solution)/shard_map/ppermute | solution.py:841
  11.0 0.4 %collective-permute-start.9 = (f32[4,8,128]{2,1,0:T(8,128)S(1)}, f32[4,8,128]{2,1,0:T(8,128)S(1)}, u32[]{:S(2)}, u32[]{:S(2)}) collective-permute-start(f32[4,8,128]{2,1,0:T(8,128)S(1)} %add.12), channel_id=1, source_target_pairs={{0,4},{1,5},{2,6},{3,7},{4,0},{5,1},{6,2},{7,3},{8,12},{9,13},{10,... | collective-permute-start | bytes 49160 | tf_op jit(solution)/shard_map/ppermute | solution.py:841
  11.4 0.6 %slice.3 = s32[1]{0:T(128)} slice(s32[3]{0:T(128)S(1)} %get-tuple-element.83), slice={[2:3]} | slice | bytes 8 | tf_op jit(solution)/shard_map/slice | solution.py:844
  12.7 2.1 %collective-permute-done.9 = f32[4,8,128]{2,1,0:T(8,128)S(1)} collective-permute-done((f32[4,8,128]{2,1,0:T(8,128)S(1)}, f32[4,8,128]{2,1,0:T(8,128)S(1)}, u32[]{:S(2)}, u32[]{:S(2)}) %collective-permute-start.9) | collective-permute-done | bytes 16416 | tf_op jit(solution)/shard_map/ppermute | solution.py:841
  14.7 0.3 %collective-permute-start.10 = (f32[4,8,128]{2,1,0:T(8,128)S(1)}, f32[4,8,128]{2,1,0:T(8,128)S(1)}, u32[]{:S(2)}, u32[]{:S(2)}) collective-permute-start(f32[4,8,128]{2,1,0:T(8,128)S(1)} %add.13.summed), channel_id=1, source_target_pairs={{0,8},{1,9},{2,10},{3,11},{4,12},{5,13},{6,14},{7,15},{8,0},{9,1},... | collective-permute-start | bytes 49160 | tf_op jit(solution)/shard_map/ppermute | solution.py:841
  15.1 0.0 collective-permute-done.6.from_far
  15.1 1.3 %outer_steps.1 = (f32[2,19,4,8,128]{4,3,2,1,0:T(8,128)S(1)}, f32[18,8,128]{2,1,0:T(8,128)S(1)}, f32[19,18,8,128]{3,2,1,0:T(8,128)S(1)}) custom-call(f32[16,18,8,128]{3,2,1,0:T(8,128)S(1)} %get-tuple-element.94.history, f32[18,8,128]{2,1,0:T(8,128)S(1)} %get-tuple-element.95.opens, s32[18,8,128]{2,1,0:T(8,128)S(1)} %get-tuple-element.96.fluid, ...), custom_call_target="tpu_custom_call" | custom-call | flops 240000000 | bytes 12000000 | tf_op jit(solution)/shard_map/outer_steps/pallas_call | solution.py:743
  16.3 3.1 %collective-permute-done.10 = f32[4,8,128]{2,1,0:T(8,128)S(1)} collective-permute-done((f32[4,8,128]{2,1,0:T(8,128)S(1)}, f32[4,8,128]{2,1,0:T(8,128)S(1)}, u32[]{:S(2)}, u32[]{:S(2)}) %collective-permute-start.10) | collective-permute-done | bytes 16416 | tf_op jit(solution)/shard_map/ppermute | solution.py:841
  19.4 2.2 %collective-permute-start.11 = (f32[4,8,128]{2,1,0:T(8,128)S(1)}, f32[4,8,128]{2,1,0:T(8,128)S(1)}, u32[]{:S(2)}, u32[]{:S(2)}) collective-permute-start(f32[4,8,128]{2,1,0:T(8,128)S(1)} %add.14.summed), channel_id=1, source_target_pairs={{0,2},{1,3},{2,0},{3,1},{4,6},{5,7},{6,4},{7,5},{8,10},{9,11},{10,... | collective-permute-start | bytes 49160 | tf_op jit(solution)/shard_map/ppermute | solution.py:841
  21.6 1.0 %gradient_steps.1 = (f32[12,8,128]{2,1,0:T(8,128)S(1)}, f32[4,8,128]{2,1,0:T(8,128)S(1)}, f32[4,8,128]{2,1,0:T(8,128)S(1)}) custom-call(f32[16,18,8,128]{3,2,1,0:T(8,128)S(1)} %get-tuple-element.94.history, f32[18,8,128]{2,1,0:T(8,128)S(1)} %get-tuple-element.95.opens, s32[18,8,128]{2,1,0:T(8,128)S(1)} %get-tuple-element.97.words, ...), custom_call_target="tpu_custom_call" | custom-call | flops 120000000 | bytes 6000000 | tf_op jit(solution)/shard_map/gradient_steps/pallas_call | solution.py:743
  22.6 1.9 %collective-permute-start.12 = (f32[4,8,128]{2,1,0:T(8,128)S(1)}, f32[4,8,128]{2,1,0:T(8,128)S(1)}, u32[]{:S(2)}, u32[]{:S(2)}) collective-permute-start(f32[4,8,128]{2,1,0:T(8,128)S(1)} %get-tuple-element.107), channel_id=1, source_target_pairs={{1,2},{2,1},{3,4},{4,3},{5,6},{6,5},{7,8},{8,7},{9,10},{10,9},{11,... | collective-permute-start | bytes 49160 | tf_op jit(solution)/shard_map/ppermute | solution.py:883
  24.6 0.2 collective-permute-start.13
  24.7 0.8 %conditional.2 = (f32[19,20,8,128]{3,2,1,0:T(8,128)S(1)}) conditional(s32[]{:T(128)} %bitcast.2, (s32[3]{0:T(128)S(1)}, f32[19,12,8,128]{3,2,1,0:T(8,128)S(1)}, f32[2,19,4,8,128]{4,3,2,1,0:T(8,128)S(1)}, f32[12,8,128]{2,1,0:T(8,128)S(1)}) %tuple.20, (f32[19,12,8,128]{3,2,1,0:T(8,128)S(1)}, s32[3]{0:T(128)S(1)}, f32[12,8,128]{2,1,0:T(8,128)S(1)}) %tuple.21), branch_computations={%region_0.0_spmd, %region_1.0_spmd} | conditional | flops 80466944 | bytes 15206744 | solution.py:931
  24.7 0.8 %place_populations.2 = f32[19,20,8,128]{3,2,1,0:T(8,128)S(1)} custom-call(s32[3]{0:T(128)S(1)} %get-tuple-element.32.where, f32[19,12,8,128]{3,2,1,0:T(8,128)S(1)} %get-tuple-element.33.final, f32[2,19,4,8,128]{4,3,2,1,0:T(8,128)S(1)} %get-tuple-element.38.outer, f32[12,8,128]{2,1,0:T(8,128)S(1)} %get-tuple-element.39.later), custom_call_target="tpu_custom_call" | custom-call | flops 80000000 | bytes 4000000 | tf_op jit(solution)/shard_map/cond/branch_0_fun/place_populations/pallas_call | solution.py:743
  25.6 0.0 copy-start
  25.6 0.0 collective-permute-done.11
  25.6 3.0 %collective-permute-done.12 = f32[4,8,128]{2,1,0:T(8,128)S(1)} collective-permute-done((f32[4,8,128]{2,1,0:T(8,128)S(1)}, f32[4,8,128]{2,1,0:T(8,128)S(1)}, u32[]{:S(2)}, u32[]{:S(2)}) %collective-permute-start.12) | collective-permute-done | bytes 16416 | tf_op jit(solution)/shard_map/ppermute | solution.py:883
  28.6 0.0 collective-permute-done.13
  28.6 0.7 %conditional.3 = (f32[20,8,128]{2,1,0:T(8,128)S(1)}) conditional(s32[]{:T(128)} %bitcast.2, (s32[3]{0:T(128)S(1)}, f32[4,8,128]{2,1,0:T(8,128)S(1)}, f32[12,8,128]{2,1,0:T(8,128)S(1)}, f32[4,8,128]{2,1,0:T(8,128)S(1)}, f32[4,8,128]{2,1,0:T(8,128)S(1)}) %tuple.22, (f32[12,8,128]{2,1,0:T(8,128)S(1)}, s32[3]{0:T(128)S(1)}, ...), branch_computations={%region_2.0_spmd, %region_3.0_spmd} | conditional | flops 20000000 | bytes 1393304 | solution.py:932
  28.6 0.7 %near_gradient.1 = f32[20,8,128]{2,1,0:T(8,128)S(1)} custom-call(s32[3]{0:T(128)S(1)} %get-tuple-element.43.where, f32[4,8,128]{2,1,0:T(8,128)S(1)} %get-tuple-element.44.drag, f32[12,8,128]{2,1,0:T(8,128)S(1)} %get-tuple-element.45.gradient, f32[4,8,128]{2,1,0:T(8,128)S(1)} %get-tuple-element.46.from_far, f32[4,8,128]{2,1,0:T(8,128)S(1)} %get-tuple-element.47.from_near), custom_call_target="tpu_custom_call" | custom-call | flops 20000000 | bytes 1000000 | tf_op jit(solution)/shard_map/cond/branch_0_fun/near_gradient/pallas_call | solution.py:743
  29.3 0.0 copy-start.1
  29.3 0.6 %copy-done.1 = f32[20,8,128]{2,1,0:T(8,128)} copy-done((f32[20,8,128]{2,1,0:T(8,128)}, f32[20,8,128]{2,1,0:T(8,128)S(1)}, u32[]{:S(2)}) %copy-start.1) | copy-done | bytes 81944
  (6 shorter events, 0.0 us)
Async XLA Ops:
  2.0 6.1 %collective-permute-start.4 = (f32[23,2,8,128]{3,2,1,0:T(8,128)S(1)}, f32[23,2,8,128]{3,2,1,0:T(8,128)S(1)}, u32[]{:S(2)}, u32[]{:S(2)}) collective-permute-start(f32[23,2,8,128]{3,2,1,0:T(8,128)S(1)} %get-tuple-element.84), channel_id=1, source_target_pairs={{0,15},{1,2},{2,1},{3,4},{4,3},{5,6},{6,5},{7,8},{8,7},{9,10},{10,... | collective-permute-start | bytes 565256 | tf_op jit(solution)/shard_map/ppermute | solution.py:768
  2.9 5.2 %collective-permute-start.5 = (f32[23,2,8,128]{3,2,1,0:T(8,128)S(1)}, f32[23,2,8,128]{3,2,1,0:T(8,128)S(1)}, u32[]{:S(2)}, u32[]{:S(2)}) collective-permute-start(f32[23,2,8,128]{3,2,1,0:T(8,128)S(1)} %get-tuple-element.85), channel_id=1, source_target_pairs={{0,1},{1,0},{2,3},{3,2},{4,5},{5,4},{6,7},{7,6},{8,9},{9,8},{10,11... | collective-permute-start | bytes 565256 | tf_op jit(solution)/shard_map/ppermute | solution.py:767
  5.8 9.3 %collective-permute-start.6 = (f32[49,8,128]{2,1,0:T(8,128)S(1)}, f32[49,8,128]{2,1,0:T(8,128)S(1)}, u32[]{:S(2)}, u32[]{:S(2)}) collective-permute-start(f32[49,8,128]{2,1,0:T(8,128)S(1)} %get-tuple-element.100), channel_id=1, source_target_pairs={{0,15},{1,2},{2,1},{3,4},{4,3},{5,6},{6,5},{7,8},{8,7},{9,10},{10,... | collective-permute-start | bytes 602120 | tf_op jit(solution)/shard_map/ppermute | solution.py:806
  6.8 8.2 %collective-permute-start.7 = (f32[49,8,128]{2,1,0:T(8,128)S(1)}, f32[49,8,128]{2,1,0:T(8,128)S(1)}, u32[]{:S(2)}, u32[]{:S(2)}) collective-permute-start(f32[49,8,128]{2,1,0:T(8,128)S(1)} %get-tuple-element.101), channel_id=1, source_target_pairs={{0,1},{1,0},{2,3},{3,2},{4,5},{5,4},{6,7},{7,6},{8,9},{9,8},{10,11... | collective-permute-start | bytes 602120 | tf_op jit(solution)/shard_map/ppermute | solution.py:805
  9.2 1.8 %collective-permute-start.8 = (f32[4,8,128]{2,1,0:T(8,128)S(1)}, f32[4,8,128]{2,1,0:T(8,128)S(1)}, u32[]{:S(2)}, u32[]{:S(2)}) collective-permute-start(f32[4,8,128]{2,1,0:T(8,128)S(1)} %get-tuple-element.102), channel_id=1, source_target_pairs={{0,1},{1,0},{2,3},{3,2},{4,5},{5,4},{6,7},{7,6},{8,9},{9,8},{10,11... | collective-permute-start | bytes 49160 | tf_op jit(solution)/shard_map/ppermute | solution.py:841
  11.0 3.7 %collective-permute-start.9 = (f32[4,8,128]{2,1,0:T(8,128)S(1)}, f32[4,8,128]{2,1,0:T(8,128)S(1)}, u32[]{:S(2)}, u32[]{:S(2)}) collective-permute-start(f32[4,8,128]{2,1,0:T(8,128)S(1)} %add.12), channel_id=1, source_target_pairs={{0,4},{1,5},{2,6},{3,7},{4,0},{5,1},{6,2},{7,3},{8,12},{9,13},{10,... | collective-permute-start | bytes 49160 | tf_op jit(solution)/shard_map/ppermute | solution.py:841
  14.7 4.7 %collective-permute-start.10 = (f32[4,8,128]{2,1,0:T(8,128)S(1)}, f32[4,8,128]{2,1,0:T(8,128)S(1)}, u32[]{:S(2)}, u32[]{:S(2)}) collective-permute-start(f32[4,8,128]{2,1,0:T(8,128)S(1)} %add.13.summed), channel_id=1, source_target_pairs={{0,8},{1,9},{2,10},{3,11},{4,12},{5,13},{6,14},{7,15},{8,0},{9,1},... | collective-permute-start | bytes 49160 | tf_op jit(solution)/shard_map/ppermute | solution.py:841
  19.4 6.2 %collective-permute-start.11 = (f32[4,8,128]{2,1,0:T(8,128)S(1)}, f32[4,8,128]{2,1,0:T(8,128)S(1)}, u32[]{:S(2)}, u32[]{:S(2)}) collective-permute-start(f32[4,8,128]{2,1,0:T(8,128)S(1)} %add.14.summed), channel_id=1, source_target_pairs={{0,2},{1,3},{2,0},{3,1},{4,6},{5,7},{6,4},{7,5},{8,10},{9,11},{10,... | collective-permute-start | bytes 49160 | tf_op jit(solution)/shard_map/ppermute | solution.py:841
  22.6 6.0 %collective-permute-start.12 = (f32[4,8,128]{2,1,0:T(8,128)S(1)}, f32[4,8,128]{2,1,0:T(8,128)S(1)}, u32[]{:S(2)}, u32[]{:S(2)}) collective-permute-start(f32[4,8,128]{2,1,0:T(8,128)S(1)} %get-tuple-element.107), channel_id=1, source_target_pairs={{1,2},{2,1},{3,4},{4,3},{5,6},{6,5},{7,8},{8,7},{9,10},{10,9},{11,... | collective-permute-start | bytes 49160 | tf_op jit(solution)/shard_map/ppermute | solution.py:883
  24.6 4.0 %collective-permute-start.13 = (f32[4,8,128]{2,1,0:T(8,128)S(1)}, f32[4,8,128]{2,1,0:T(8,128)S(1)}, u32[]{:S(2)}, u32[]{:S(2)}) collective-permute-start(f32[4,8,128]{2,1,0:T(8,128)S(1)} %get-tuple-element.108), channel_id=1, source_target_pairs={{0,1},{1,0},{2,3},{3,2},{4,5},{5,4},{6,7},{7,6},{8,9},{9,8},{10,11... | collective-permute-start | bytes 49160 | tf_op jit(solution)/shard_map/ppermute | solution.py:882
  25.6 3.8 %copy-start = (f32[19,20,8,128]{3,2,1,0:T(8,128)}, f32[19,20,8,128]{3,2,1,0:T(8,128)S(1)}, u32[]{:S(2)}) copy-start(f32[19,20,8,128]{3,2,1,0:T(8,128)S(1)} %get-tuple-element.109) | copy-start | bytes 4669444
  29.3 0.6 %copy-start.1 = (f32[20,8,128]{2,1,0:T(8,128)}, f32[20,8,128]{2,1,0:T(8,128)S(1)}, u32[]{:S(2)}) copy-start(f32[20,8,128]{2,1,0:T(8,128)S(1)} %get-tuple-element.110) | copy-start | bytes 245764

commit v11 on v10

--- a/solution.py
+++ b/solution.py
@@ -452,8 +452,7 @@
     receive(1, odd)
     both(2, functools.partial(advance, 2, odd, even))
     receive(2, even)
-    drag[...] = jnp.zeros_like(drag)
-    drag[0] = inner_drag[...]
+    drag[...] = inner_drag[...]
 
     def finish(index, place, ahead):
         state = pull(even, index, words[index])
@@ -464,7 +463,7 @@
         yield
         remember(history, 3, index, density, flow)
         store(final, index - HALO, placed)
-        drag[1 + place] += part
+        drag[...] += part
 
     both(3, finish)
     for copy in copies:
@@ -811,7 +810,7 @@
         planes(span),
         planes(span, dtype=jnp.int32),
         planes(span, dtype=jnp.int32),
-        planes(1 + STEPS),
+        planes(),
         planes(19, span),
         planes(19, span),
     )

time: 30.1 us -> 31 us (1.030)
  the two profiles are of different devices: /device:TPU:26 before, /device:TPU:0 now
where the time goes in v11:
time: 31 us; the launch traced here: 30.8 us
  starting transfers between devices  13.8 us (45%)
  Pallas kernels  8.29 us (27%)
  waiting for transfers between devices  6.12 us (20%)
  between operations  1.38 us (4%)
  local copies, waits for them, and re-layouts  1.21 us (4%)
    pallas_call x7, Pallas kernels, call(): pl.pallas_call(kernel, out_shape=[shape for shape, _ in outs], in_specs=i...  8.29 us
    ppermute x4, waiting for transfers between devices, body(): sums.append(sums[-1] + lax.ppermute(sums[-1], 'block', swap))  5.74 us
    ppermute x1, starting transfers between devices, body(): far = lax.ppermute(own_far, 'block', far_pairs)  5.51 us
    ppermute x4, starting transfers between devices, body(): sums.append(sums[-1] + lax.ppermute(sums[-1], 'block', swap))  3.85 us
    ppermute x2, starting transfers between devices, body(): from_near = lax.ppermute(to_near, 'block', near_pairs)  2.93 us
    ppermute x1, starting transfers between devices, body(): from_far = lax.ppermute(to_far, 'block', far_pairs)  0.82 us
    ppermute x1, starting transfers between devices, body(): from_far = lax.ppermute(to_far, 'block', inner_pairs)  0.66 us
    unnamed x4, local copies, waits for them, and re-layouts  0.63 us
  transfers between devices with their start and end apart: 10, of which 5 were waited for; matrix products, arithmetic and copies ran while one was open for 2% of the time, Pallas kernels for 17%

profile of v11, /device:TPU:0, one launch (start us, length us, event | category | flops | bytes accessed | tf_op | source)
XLA Modules:
  0.0 30.8 jit_solution(580864708672521037)
XLA Ops:
  0.6 1.4 %edge_planes.1 = (f32[23,2,8,128]{3,2,1,0:T(8,128)S(1)}, f32[23,2,8,128]{3,2,1,0:T(8,128)S(1)}, f32[19,12,8,128]{3,2,1,0:T(8,128)S(1)}, f32[12,8,128]{2,1,0:T(8,128)S(1)}) custom-call(f32[19,12,8,128]{3,2,1,0:T(8,128)} %pops_far.1, f32[12,8,128]{2,1,0:T(8,128)} %design.1, s32[12,8,128]{2,1,0:T(8,128)} %mask.1), custom_call_target="tpu_custom_call" | custom-call | flops 20000000 | bytes 1000000 | tf_op jit(solution)/shard_map/edge_planes/pallas_call | solution.py:742
  2.0 5.5 %collective-permute-start.4 = (f32[23,2,8,128]{3,2,1,0:T(8,128)S(1)}, f32[23,2,8,128]{3,2,1,0:T(8,128)S(1)}, u32[]{:S(2)}, u32[]{:S(2)}) collective-permute-start(f32[23,2,8,128]{3,2,1,0:T(8,128)S(1)} %get-tuple-element.84), channel_id=1, source_target_pairs={{0,15},{1,2},{2,1},{3,4},{4,3},{5,6},{6,5},{7,8},{8,7},{9,10},{10,... | collective-permute-start | bytes 565256 | tf_op jit(solution)/shard_map/ppermute | solution.py:767
  7.5 0.0 collective-permute-start.5
  7.5 2.1 %interior_steps.1 = (f32[49,8,128]{2,1,0:T(8,128)S(1)}, f32[49,8,128]{2,1,0:T(8,128)S(1)}, f32[19,12,8,128]{3,2,1,0:T(8,128)S(1)}, f32[16,12,8,128]{3,2,1,0:T(8,...) custom-call(s32[48]{0:T(128)} %owner_far.1, ...), custom_call_target="tpu_custom_call" | custom-call | flops 120000000 | bytes 6000000 | tf_op jit(solution)/shard_map/interior_steps/pallas_call | solution.py:742
  9.6 0.8 %collective-permute-start.6 = (f32[49,8,128]{2,1,0:T(8,128)S(1)}, f32[49,8,128]{2,1,0:T(8,128)S(1)}, u32[]{:S(2)}, u32[]{:S(2)}) collective-permute-start(f32[49,8,128]{2,1,0:T(8,128)S(1)} %get-tuple-element.100), channel_id=1, source_target_pairs={{0,15},{1,2},{2,1},{3,4},{4,3},{5,6},{6,5},{7,8},{8,7},{9,10},{10,... | collective-permute-start | bytes 602120 | tf_op jit(solution)/shard_map/ppermute | solution.py:805
  10.4 0.0 collective-permute-start.7
  10.4 0.4 %collective-permute-done.4.far = f32[23,2,8,128]{3,2,1,0:T(8,128)S(1)} collective-permute-done((f32[23,2,8,128]{3,2,1,0:T(8,128)S(1)}, f32[23,2,8,128]{3,2,1,0:T(8,128)S(1)}, u32[]{:S(2)}, u32[]{:S(2)}) %collective-permute-start.4) | collective-permute-done | bytes 188448 | tf_op jit(solution)/shard_map/ppermute | solution.py:767
  10.8 0.0 collective-permute-done.5.near
  10.8 1.1 %boundary_steps.1 = (f32[19,12,8,128]{3,2,1,0:T(8,128)S(1)}, f32[16,18,8,128]{3,2,1,0:T(8,128)S(1)}, f32[18,8,128]{2,1,0:T(8,128)S(1)}, s32[18,8,128]{2,1,0:T(8,...) custom-call(f32[23,2,8,128]{3,2,1,0:T(8,128)S(1)} %collective-permut, ...), custom_call_target="tpu_custom_call" | custom-call | flops 160000000 | bytes 8000000 | tf_op jit(solution)/shard_map/boundary_steps/pallas_call | solution.py:742
  11.8 0.2 collective-permute-start.8
  12.0 1.0 %collective-permute-done.8 = f32[8,128]{1,0:T(8,128)S(1)} collective-permute-done((f32[8,128]{1,0:T(8,128)S(1)}, f32[8,128]{1,0:T(8,128)S(1)}, u32[]{:S(2)}, u32[]{:S(2)}) %collective-permute-start.8) | collective-permute-done | bytes 4128 | tf_op jit(solution)/shard_map/ppermute | solution.py:840
  13.1 0.9 %collective-permute-start.9 = (f32[8,128]{1,0:T(8,128)S(1)}, f32[8,128]{1,0:T(8,128)S(1)}, u32[]{:S(2)}, u32[]{:S(2)}) collective-permute-start(f32[8,128]{1,0:T(8,128)S(1)} %add.12), channel_id=1, source_target_pairs={{0,4},{1,5},{2,6},{3,7},{4,0},{5,1},{6,2},{7,3},{8,12},{9,13},{10,... | collective-permute-start | bytes 12296 | tf_op jit(solution)/shard_map/ppermute | solution.py:840
  14.0 0.6 %slice.3 = s32[1]{0:T(128)} slice(s32[3]{0:T(128)S(1)} %get-tuple-element.83), slice={[2:3]} | slice | bytes 8 | tf_op jit(solution)/shard_map/slice | solution.py:843
  15.2 1.5 %collective-permute-done.9 = f32[8,128]{1,0:T(8,128)S(1)} collective-permute-done((f32[8,128]{1,0:T(8,128)S(1)}, f32[8,128]{1,0:T(8,128)S(1)}, u32[]{:S(2)}, u32[]{:S(2)}) %collective-permute-start.9) | collective-permute-done | bytes 4128 | tf_op jit(solution)/shard_map/ppermute | solution.py:840
  16.7 1.9 %collective-permute-start.10 = (f32[8,128]{1,0:T(8,128)S(1)}, f32[8,128]{1,0:T(8,128)S(1)}, u32[]{:S(2)}, u32[]{:S(2)}) collective-permute-start(f32[8,128]{1,0:T(8,128)S(1)} %add.13.summed), channel_id=1, source_target_pairs={{0,8},{1,9},{2,10},{3,11},{4,12},{5,13},{6,14},{7,15},{8,0},{9,1},... | collective-permute-start | bytes 12296 | tf_op jit(solution)/shard_map/ppermute | solution.py:840
  18.6 0.0 collective-permute-done.6.from_far
  18.6 0.0 collective-permute-done.7.from_near
  18.6 1.3 %outer_steps.1 = (f32[2,19,4,8,128]{4,3,2,1,0:T(8,128)S(1)}, f32[18,8,128]{2,1,0:T(8,128)S(1)}, f32[19,18,8,128]{3,2,1,0:T(8,128)S(1)}) custom-call(f32[16,18,8,128]{3,2,1,0:T(8,128)S(1)} %get-tuple-element.94.history, f32[18,8,128]{2,1,0:T(8,128)S(1)} %get-tuple-element.95.opens, s32[18,8,128]{2,1,0:T(8,128)S(1)} %get-tuple-element.96.fluid, ...), custom_call_target="tpu_custom_call" | custom-call | flops 240000000 | bytes 12000000 | tf_op jit(solution)/shard_map/outer_steps/pallas_call | solution.py:742
  19.9 1.3 %collective-permute-done.10 = f32[8,128]{1,0:T(8,128)S(1)} collective-permute-done((f32[8,128]{1,0:T(8,128)S(1)}, f32[8,128]{1,0:T(8,128)S(1)}, u32[]{:S(2)}, u32[]{:S(2)}) %collective-permute-start.10) | collective-permute-done | bytes 4128 | tf_op jit(solution)/shard_map/ppermute | solution.py:840
  21.2 1.0 %gradient_steps.1 = (f32[12,8,128]{2,1,0:T(8,128)S(1)}, f32[4,8,128]{2,1,0:T(8,128)S(1)}, f32[4,8,128]{2,1,0:T(8,128)S(1)}) custom-call(f32[16,18,8,128]{3,2,1,0:T(8,128)S(1)} %get-tuple-element.94.history, f32[18,8,128]{2,1,0:T(8,128)S(1)} %get-tuple-element.95.opens, s32[18,8,128]{2,1,0:T(8,128)S(1)} %get-tuple-element.97.words, ...), custom_call_target="tpu_custom_call" | custom-call | flops 120000000 | bytes 6000000 | tf_op jit(solution)/shard_map/gradient_steps/pallas_call | solution.py:742
  22.2 0.7 %collective-permute-start.12 = (f32[4,8,128]{2,1,0:T(8,128)S(1)}, f32[4,8,128]{2,1,0:T(8,128)S(1)}, u32[]{:S(2)}, u32[]{:S(2)}) collective-permute-start(f32[4,8,128]{2,1,0:T(8,128)S(1)} %get-tuple-element.107), channel_id=1, source_target_pairs={{1,2},{2,1},{3,4},{4,3},{5,6},{6,5},{7,8},{8,7},{9,10},{10,9},{11,... | collective-permute-start | bytes 49160 | tf_op jit(solution)/shard_map/ppermute | solution.py:882
  22.9 2.9 %collective-permute-start.13 = (f32[4,8,128]{2,1,0:T(8,128)S(1)}, f32[4,8,128]{2,1,0:T(8,128)S(1)}, u32[]{:S(2)}, u32[]{:S(2)}) collective-permute-start(f32[4,8,128]{2,1,0:T(8,128)S(1)} %get-tuple-element.108), channel_id=1, source_target_pairs={{0,1},{1,0},{2,3},{3,2},{4,5},{5,4},{6,7},{7,6},{8,9},{9,8},{10,11... | collective-permute-start | bytes 49160 | tf_op jit(solution)/shard_map/ppermute | solution.py:881
  25.8 0.8 %collective-permute-start.11 = (f32[8,128]{1,0:T(8,128)S(1)}, f32[8,128]{1,0:T(8,128)S(1)}, u32[]{:S(2)}, u32[]{:S(2)}) collective-permute-start(f32[8,128]{1,0:T(8,128)S(1)} %add.14.summed), channel_id=1, source_target_pairs={{0,2},{1,3},{2,0},{3,1},{4,6},{5,7},{6,4},{7,5},{8,10},{9,11},{10,... | collective-permute-start | bytes 12296 | tf_op jit(solution)/shard_map/ppermute | solution.py:840
  26.7 0.8 %conditional.2 = (f32[19,20,8,128]{3,2,1,0:T(8,128)S(1)}) conditional(s32[]{:T(128)} %bitcast.2, (s32[3]{0:T(128)S(1)}, f32[19,12,8,128]{3,2,1,0:T(8,128)S(1)}, f32[2,19,4,8,128]{4,3,2,1,0:T(8,128)S(1)}, f32[12,8,128]{2,1,0:T(8,128)S(1)}) %tuple.20, (f32[19,12,8,128]{3,2,1,0:T(8,128)S(1)}, s32[3]{0:T(128)S(1)}, f32[12,8,128]{2,1,0:T(8,128)S(1)}) %tuple.21), branch_computations={%region_0.0_spmd, %region_1.0_spmd} | conditional | flops 80466944 | bytes 15206744 | solution.py:930
  26.7 0.8 %place_populations.2 = f32[19,20,8,128]{3,2,1,0:T(8,128)S(1)} custom-call(s32[3]{0:T(128)S(1)} %get-tuple-element.32.where, f32[19,12,8,128]{3,2,1,0:T(8,128)S(1)} %get-tuple-element.33.final, f32[2,19,4,8,128]{4,3,2,1,0:T(8,128)S(1)} %get-tuple-element.38.outer, f32[12,8,128]{2,1,0:T(8,128)S(1)} %get-tuple-element.39.later), custom_call_target="tpu_custom_call" | custom-call | flops 80000000 | bytes 4000000 | tf_op jit(solution)/shard_map/cond/branch_0_fun/place_populations/pallas_call | solution.py:742
  27.5 0.0 copy-start
  27.5 1.9 %collective-permute-done.11 = f32[8,128]{1,0:T(8,128)S(1)} collective-permute-done((f32[8,128]{1,0:T(8,128)S(1)}, f32[8,128]{1,0:T(8,128)S(1)}, u32[]{:S(2)}, u32[]{:S(2)}) %collective-permute-start.11) | collective-permute-done | bytes 4128 | tf_op jit(solution)/shard_map/ppermute | solution.py:840
  29.4 0.0 collective-permute-done.12
  29.4 0.7 %conditional.3 = (f32[20,8,128]{2,1,0:T(8,128)S(1)}) conditional(s32[]{:T(128)} %bitcast.2, (s32[3]{0:T(128)S(1)}, f32[8,128]{1,0:T(8,128)S(1)}, f32[12,8,128]{2,1,0:T(8,128)S(1)}, f32[4,8,128]{2,1,0:T(8,128)S(1)}, f32[4,8,128]{2,1,0:T(8,128)S(1)}) %tuple.22, (f32[12,8,128]{2,1,0:T(8,128)S(1)}, s32[3]{0:T(128)S(1)}, f32[8,128]{1,0:T(8,128)S(1)}) %tuple.23), branch_computations={%region_2.0_spmd, %region_3.0_spmd} | conditional | flops 20000000 | bytes 1393304 | solution.py:931
  29.5 0.7 %near_gradient.1 = f32[20,8,128]{2,1,0:T(8,128)S(1)} custom-call(s32[3]{0:T(128)S(1)} %get-tuple-element.43.where, f32[8,128]{1,0:T(8,128)S(1)} %get-tuple-element.44.drag, f32[12,8,128]{2,1,0:T(8,128)S(1)} %get-tuple-element.45.gradient, f32[4,8,128]{2,1,0:T(8,128)S(1)} %get-tuple-element.46.from_far, f32[4,8,128]{2,1,0:T(8,128)S(1)} %get-tuple-element.47.from_near), custom_call_target="tpu_custom_call" | custom-call | flops 20000000 | bytes 1000000 | tf_op jit(solution)/shard_map/cond/branch_0_fun/near_gradient/pallas_call | solution.py:742
  30.2 0.0 copy-start.1
  30.2 0.6 %copy-done.1 = f32[20,8,128]{2,1,0:T(8,128)} copy-done((f32[20,8,128]{2,1,0:T(8,128)}, f32[20,8,128]{2,1,0:T(8,128)S(1)}, u32[]{:S(2)}) %copy-start.1) | copy-done | bytes 81944
  (6 shorter events, 0.0 us)
Async XLA Ops:
  2.0 8.8 %collective-permute-start.4 = (f32[23,2,8,128]{3,2,1,0:T(8,128)S(1)}, f32[23,2,8,128]{3,2,1,0:T(8,128)S(1)}, u32[]{:S(2)}, u32[]{:S(2)}) collective-permute-start(f32[23,2,8,128]{3,2,1,0:T(8,128)S(1)} %get-tuple-element.84), channel_id=1, source_target_pairs={{0,15},{1,2},{2,1},{3,4},{4,3},{5,6},{6,5},{7,8},{8,7},{9,10},{10,... | collective-permute-start | bytes 565256 | tf_op jit(solution)/shard_map/ppermute | solution.py:767
  7.5 3.3 %collective-permute-start.5 = (f32[23,2,8,128]{3,2,1,0:T(8,128)S(1)}, f32[23,2,8,128]{3,2,1,0:T(8,128)S(1)}, u32[]{:S(2)}, u32[]{:S(2)}) collective-permute-start(f32[23,2,8,128]{3,2,1,0:T(8,128)S(1)} %get-tuple-element.85), channel_id=1, source_target_pairs={{0,1},{1,0},{2,3},{3,2},{4,5},{5,4},{6,7},{7,6},{8,9},{9,8},{10,11... | collective-permute-start | bytes 565256 | tf_op jit(solution)/shard_map/ppermute | solution.py:766
  9.6 9.0 %collective-permute-start.6 = (f32[49,8,128]{2,1,0:T(8,128)S(1)}, f32[49,8,128]{2,1,0:T(8,128)S(1)}, u32[]{:S(2)}, u32[]{:S(2)}) collective-permute-start(f32[49,8,128]{2,1,0:T(8,128)S(1)} %get-tuple-element.100), channel_id=1, source_target_pairs={{0,15},{1,2},{2,1},{3,4},{4,3},{5,6},{6,5},{7,8},{8,7},{9,10},{10,... | collective-permute-start | bytes 602120 | tf_op jit(solution)/shard_map/ppermute | solution.py:805
  10.4 8.2 %collective-permute-start.7 = (f32[49,8,128]{2,1,0:T(8,128)S(1)}, f32[49,8,128]{2,1,0:T(8,128)S(1)}, u32[]{:S(2)}, u32[]{:S(2)}) collective-permute-start(f32[49,8,128]{2,1,0:T(8,128)S(1)} %get-tuple-element.101), channel_id=1, source_target_pairs={{0,1},{1,0},{2,3},{3,2},{4,5},{5,4},{6,7},{7,6},{8,9},{9,8},{10,11... | collective-permute-start | bytes 602120 | tf_op jit(solution)/shard_map/ppermute | solution.py:804
  11.8 1.2 %collective-permute-start.8 = (f32[8,128]{1,0:T(8,128)S(1)}, f32[8,128]{1,0:T(8,128)S(1)}, u32[]{:S(2)}, u32[]{:S(2)}) collective-permute-start(f32[8,128]{1,0:T(8,128)S(1)} %get-tuple-element.102), channel_id=1, source_target_pairs={{0,1},{1,0},{2,3},{3,2},{4,5},{5,4},{6,7},{7,6},{8,9},{9,8},{10,11... | collective-permute-start | bytes 12296 | tf_op jit(solution)/shard_map/ppermute | solution.py:840
  13.1 3.6 %collective-permute-start.9 = (f32[8,128]{1,0:T(8,128)S(1)}, f32[8,128]{1,0:T(8,128)S(1)}, u32[]{:S(2)}, u32[]{:S(2)}) collective-permute-start(f32[8,128]{1,0:T(8,128)S(1)} %add.12), channel_id=1, source_target_pairs={{0,4},{1,5},{2,6},{3,7},{4,0},{5,1},{6,2},{7,3},{8,12},{9,13},{10,... | collective-permute-start | bytes 12296 | tf_op jit(solution)/shard_map/ppermute | solution.py:840
  16.7 4.5 %collective-permute-start.10 = (f32[8,128]{1,0:T(8,128)S(1)}, f32[8,128]{1,0:T(8,128)S(1)}, u32[]{:S(2)}, u32[]{:S(2)}) collective-permute-start(f32[8,128]{1,0:T(8,128)S(1)} %add.13.summed), channel_id=1, source_target_pairs={{0,8},{1,9},{2,10},{3,11},{4,12},{5,13},{6,14},{7,15},{8,0},{9,1},... | collective-permute-start | bytes 12296 | tf_op jit(solution)/shard_map/ppermute | solution.py:840
  22.2 7.2 %collective-permute-start.12 = (f32[4,8,128]{2,1,0:T(8,128)S(1)}, f32[4,8,128]{2,1,0:T(8,128)S(1)}, u32[]{:S(2)}, u32[]{:S(2)}) collective-permute-start(f32[4,8,128]{2,1,0:T(8,128)S(1)} %get-tuple-element.107), channel_id=1, source_target_pairs={{1,2},{2,1},{3,4},{4,3},{5,6},{6,5},{7,8},{8,7},{9,10},{10,9},{11,... | collective-permute-start | bytes 49160 | tf_op jit(solution)/shard_map/ppermute | solution.py:882
  22.9 6.5 %collective-permute-start.13 = (f32[4,8,128]{2,1,0:T(8,128)S(1)}, f32[4,8,128]{2,1,0:T(8,128)S(1)}, u32[]{:S(2)}, u32[]{:S(2)}) collective-permute-start(f32[4,8,128]{2,1,0:T(8,128)S(1)} %get-tuple-element.108), channel_id=1, source_target_pairs={{0,1},{1,0},{2,3},{3,2},{4,5},{5,4},{6,7},{7,6},{8,9},{9,8},{10,11... | collective-permute-start | bytes 49160 | tf_op jit(solution)/shard_map/ppermute | solution.py:881
  25.8 3.6 %collective-permute-start.11 = (f32[8,128]{1,0:T(8,128)S(1)}, f32[8,128]{1,0:T(8,128)S(1)}, u32[]{:S(2)}, u32[]{:S(2)}) collective-permute-start(f32[8,128]{1,0:T(8,128)S(1)} %add.14.summed), channel_id=1, source_target_pairs={{0,2},{1,3},{2,0},{3,1},{4,6},{5,7},{6,4},{7,5},{8,10},{9,11},{10,... | collective-permute-start | bytes 12296 | tf_op jit(solution)/shard_map/ppermute | solution.py:840
  27.5 2.7 %copy-start = (f32[19,20,8,128]{3,2,1,0:T(8,128)}, f32[19,20,8,128]{3,2,1,0:T(8,128)S(1)}, u32[]{:S(2)}) copy-start(f32[19,20,8,128]{3,2,1,0:T(8,128)S(1)} %get-tuple-element.109) | copy-start | bytes 4669444
  30.2 0.6 %copy-start.1 = (f32[20,8,128]{2,1,0:T(8,128)}, f32[20,8,128]{2,1,0:T(8,128)S(1)}, u32[]{:S(2)}) copy-start(f32[20,8,128]{2,1,0:T(8,128)S(1)} %get-tuple-element.110) | copy-start | bytes 245764

commit v12 on v10

--- a/solution.py
+++ b/solution.py
@@ -836,7 +836,7 @@
 
     distances = [1 << bit for bit in range(count.bit_length() - 1)]
     sums = [drag]
-    for distance in distances[:1] + distances[2:] + distances[1:2]:
+    for distance in distances[:1] + distances[2:3] + distances[1:2] + distances[3:]:
         swap = [(i, i ^ distance) for i in range(count)]
         sums.append(sums[-1] + lax.ppermute(sums[-1], "block", swap))
     drag = sums[-1]

time: 30.1 us -> 30 us (level)
  the two profiles are of different devices: /device:TPU:26 before, /device:TPU:0 now
where the time goes in v12:
time: 30 us; the launch traced here: 29.9 us
  starting transfers between devices  15 us (50%)
  Pallas kernels  8.32 us (28%)
  waiting for transfers between devices  3.88 us (13%)
  between operations  1.4 us (5%)
  local copies, waits for them, and re-layouts  1.21 us (4%)
    pallas_call x7, Pallas kernels, call(): pl.pallas_call(kernel, out_shape=[shape for shape, _ in outs], in_specs=i...  8.32 us
    ppermute x1, starting transfers between devices, body(): far = lax.ppermute(own_far, 'block', far_pairs)  5.51 us
    ppermute x4, starting transfers between devices, body(): sums.append(sums[-1] + lax.ppermute(sums[-1], 'block', swap))  4.6 us
    ppermute x4, waiting for transfers between devices, body(): sums.append(sums[-1] + lax.ppermute(sums[-1], 'block', swap))  3.51 us
    ppermute x2, starting transfers between devices, body(): from_near = lax.ppermute(to_near, 'block', near_pairs)  3.4 us
    ppermute x1, starting transfers between devices, body(): from_far = lax.ppermute(to_far, 'block', far_pairs)  0.82 us
    ppermute x1, starting transfers between devices, body(): from_far = lax.ppermute(to_far, 'block', inner_pairs)  0.66 us
    unnamed x4, local copies, waits for them, and re-layouts  0.63 us
  transfers between devices with their start and end apart: 10, of which 4 were waited for; matrix products, arithmetic and copies ran while one was open for 2% of the time, Pallas kernels for 21%

profile of v12, /device:TPU:0, one launch (start us, length us, event | category | flops | bytes accessed | tf_op | source)
XLA Modules:
  0.0 29.9 jit_solution(13787651361613467704)
XLA Ops:
  0.6 1.4 %edge_planes.1 = (f32[23,2,8,128]{3,2,1,0:T(8,128)S(1)}, f32[23,2,8,128]{3,2,1,0:T(8,128)S(1)}, f32[19,12,8,128]{3,2,1,0:T(8,128)S(1)}, f32[12,8,128]{2,1,0:T(8,128)S(1)}) custom-call(f32[19,12,8,128]{3,2,1,0:T(8,128)} %pops_far.1, f32[12,8,128]{2,1,0:T(8,128)} %design.1, s32[12,8,128]{2,1,0:T(8,128)} %mask.1), custom_call_target="tpu_custom_call" | custom-call | flops 20000000 | bytes 1000000 | tf_op jit(solution)/shard_map/edge_planes/pallas_call | solution.py:743
  2.0 5.5 %collective-permute-start.4 = (f32[23,2,8,128]{3,2,1,0:T(8,128)S(1)}, f32[23,2,8,128]{3,2,1,0:T(8,128)S(1)}, u32[]{:S(2)}, u32[]{:S(2)}) collective-permute-start(f32[23,2,8,128]{3,2,1,0:T(8,128)S(1)} %get-tuple-element.84), channel_id=1, source_target_pairs={{0,15},{1,2},{2,1},{3,4},{4,3},{5,6},{6,5},{7,8},{8,7},{9,10},{10,... | collective-permute-start | bytes 565256 | tf_op jit(solution)/shard_map/ppermute | solution.py:768
  7.5 0.0 collective-permute-start.5
  7.5 2.1 %interior_steps.1 = (f32[49,8,128]{2,1,0:T(8,128)S(1)}, f32[49,8,128]{2,1,0:T(8,128)S(1)}, f32[19,12,8,128]{3,2,1,0:T(8,128)S(1)}, f32[16,12,8,128]{3,2,1,0:T(8,...) custom-call(s32[48]{0:T(128)} %owner_far.1, ...), custom_call_target="tpu_custom_call" | custom-call | flops 120000000 | bytes 6000000 | tf_op jit(solution)/shard_map/interior_steps/pallas_call | solution.py:743
  9.6 0.8 %collective-permute-start.6 = (f32[49,8,128]{2,1,0:T(8,128)S(1)}, f32[49,8,128]{2,1,0:T(8,128)S(1)}, u32[]{:S(2)}, u32[]{:S(2)}) collective-permute-start(f32[49,8,128]{2,1,0:T(8,128)S(1)} %get-tuple-element.100), channel_id=1, source_target_pairs={{0,15},{1,2},{2,1},{3,4},{4,3},{5,6},{6,5},{7,8},{8,7},{9,10},{10,... | collective-permute-start | bytes 602120 | tf_op jit(solution)/shard_map/ppermute | solution.py:806
  10.4 0.0 collective-permute-start.7
  10.4 0.4 %collective-permute-done.4.far = f32[23,2,8,128]{3,2,1,0:T(8,128)S(1)} collective-permute-done((f32[23,2,8,128]{3,2,1,0:T(8,128)S(1)}, f32[23,2,8,128]{3,2,1,0:T(8,128)S(1)}, u32[]{:S(2)}, u32[]{:S(2)}) %collective-permute-start.4) | collective-permute-done | bytes 188448 | tf_op jit(solution)/shard_map/ppermute | solution.py:768
  10.8 0.0 collective-permute-done.5.near
  10.8 1.1 %boundary_steps.1 = (f32[19,12,8,128]{3,2,1,0:T(8,128)S(1)}, f32[16,18,8,128]{3,2,1,0:T(8,128)S(1)}, f32[18,8,128]{2,1,0:T(8,128)S(1)}, s32[18,8,128]{2,1,0:T(8,...) custom-call(f32[23,2,8,128]{3,2,1,0:T(8,128)S(1)} %collective-permut, ...), custom_call_target="tpu_custom_call" | custom-call | flops 160000000 | bytes 8000000 | tf_op jit(solution)/shard_map/boundary_steps/pallas_call | solution.py:743
  11.9 0.2 collective-permute-start.8
  12.1 1.0 %collective-permute-done.8 = f32[4,8,128]{2,1,0:T(8,128)S(1)} collective-permute-done((f32[4,8,128]{2,1,0:T(8,128)S(1)}, f32[4,8,128]{2,1,0:T(8,128)S(1)}, u32[]{:S(2)}, u32[]{:S(2)}) %collective-permute-start.8) | collective-permute-done | bytes 16416 | tf_op jit(solution)/shard_map/ppermute | solution.py:841
  13.1 0.9 %collective-permute-start.9 = (f32[4,8,128]{2,1,0:T(8,128)S(1)}, f32[4,8,128]{2,1,0:T(8,128)S(1)}, u32[]{:S(2)}, u32[]{:S(2)}) collective-permute-start(f32[4,8,128]{2,1,0:T(8,128)S(1)} %add.12), channel_id=1, source_target_pairs={{0,4},{1,5},{2,6},{3,7},{4,0},{5,1},{6,2},{7,3},{8,12},{9,13},{10,... | collective-permute-start | bytes 49160 | tf_op jit(solution)/shard_map/ppermute | solution.py:841
  14.0 0.6 %slice.3 = s32[1]{0:T(128)} slice(s32[3]{0:T(128)S(1)} %get-tuple-element.83), slice={[2:3]} | slice | bytes 8 | tf_op jit(solution)/shard_map/slice | solution.py:844
  15.2 1.6 %collective-permute-done.9 = f32[4,8,128]{2,1,0:T(8,128)S(1)} collective-permute-done((f32[4,8,128]{2,1,0:T(8,128)S(1)}, f32[4,8,128]{2,1,0:T(8,128)S(1)}, u32[]{:S(2)}, u32[]{:S(2)}) %collective-permute-start.9) | collective-permute-done | bytes 16416 | tf_op jit(solution)/shard_map/ppermute | solution.py:841
  16.9 1.6 %collective-permute-start.10 = (f32[4,8,128]{2,1,0:T(8,128)S(1)}, f32[4,8,128]{2,1,0:T(8,128)S(1)}, u32[]{:S(2)}, u32[]{:S(2)}) collective-permute-start(f32[4,8,128]{2,1,0:T(8,128)S(1)} %add.13.summed), channel_id=1, source_target_pairs={{0,2},{1,3},{2,0},{3,1},{4,6},{5,7},{6,4},{7,5},{8,10},{9,11},{10,... | collective-permute-start | bytes 49160 | tf_op jit(solution)/shard_map/ppermute | solution.py:841
  18.5 0.0 collective-permute-done.6.from_far
  18.5 1.3 %outer_steps.1 = (f32[2,19,4,8,128]{4,3,2,1,0:T(8,128)S(1)}, f32[18,8,128]{2,1,0:T(8,128)S(1)}, f32[19,18,8,128]{3,2,1,0:T(8,128)S(1)}) custom-call(f32[16,18,8,128]{3,2,1,0:T(8,128)S(1)} %get-tuple-element.94.history, f32[18,8,128]{2,1,0:T(8,128)S(1)} %get-tuple-element.95.opens, s32[18,8,128]{2,1,0:T(8,128)S(1)} %get-tuple-element.96.fluid, ...), custom_call_target="tpu_custom_call" | custom-call | flops 240000000 | bytes 12000000 | tf_op jit(solution)/shard_map/outer_steps/pallas_call | solution.py:743
  19.7 0.9 %collective-permute-done.10 = f32[4,8,128]{2,1,0:T(8,128)S(1)} collective-permute-done((f32[4,8,128]{2,1,0:T(8,128)S(1)}, f32[4,8,128]{2,1,0:T(8,128)S(1)}, u32[]{:S(2)}, u32[]{:S(2)}) %collective-permute-start.10) | collective-permute-done | bytes 16416 | tf_op jit(solution)/shard_map/ppermute | solution.py:841
  20.6 1.9 %collective-permute-start.11 = (f32[4,8,128]{2,1,0:T(8,128)S(1)}, f32[4,8,128]{2,1,0:T(8,128)S(1)}, u32[]{:S(2)}, u32[]{:S(2)}) collective-permute-start(f32[4,8,128]{2,1,0:T(8,128)S(1)} %add.14.summed), channel_id=1, source_target_pairs={{0,8},{1,9},{2,10},{3,11},{4,12},{5,13},{6,14},{7,15},{8,0},{9,1},... | collective-permute-start | bytes 49160 | tf_op jit(solution)/shard_map/ppermute | solution.py:841
  22.5 1.0 %gradient_steps.1 = (f32[12,8,128]{2,1,0:T(8,128)S(1)}, f32[4,8,128]{2,1,0:T(8,128)S(1)}, f32[4,8,128]{2,1,0:T(8,128)S(1)}) custom-call(f32[16,18,8,128]{3,2,1,0:T(8,128)S(1)} %get-tuple-element.94.history, f32[18,8,128]{2,1,0:T(8,128)S(1)} %get-tuple-element.95.opens, s32[18,8,128]{2,1,0:T(8,128)S(1)} %get-tuple-element.97.words, ...), custom_call_target="tpu_custom_call" | custom-call | flops 120000000 | bytes 6000000 | tf_op jit(solution)/shard_map/gradient_steps/pallas_call | solution.py:743
  23.5 0.7 %collective-permute-start.12 = (f32[4,8,128]{2,1,0:T(8,128)S(1)}, f32[4,8,128]{2,1,0:T(8,128)S(1)}, u32[]{:S(2)}, u32[]{:S(2)}) collective-permute-start(f32[4,8,128]{2,1,0:T(8,128)S(1)} %get-tuple-element.107), channel_id=1, source_target_pairs={{1,2},{2,1},{3,4},{4,3},{5,6},{6,5},{7,8},{8,7},{9,10},{10,9},{11,... | collective-permute-start | bytes 49160 | tf_op jit(solution)/shard_map/ppermute | solution.py:883
  24.2 3.4 %collective-permute-start.13 = (f32[4,8,128]{2,1,0:T(8,128)S(1)}, f32[4,8,128]{2,1,0:T(8,128)S(1)}, u32[]{:S(2)}, u32[]{:S(2)}) collective-permute-start(f32[4,8,128]{2,1,0:T(8,128)S(1)} %get-tuple-element.108), channel_id=1, source_target_pairs={{0,1},{1,0},{2,3},{3,2},{4,5},{5,4},{6,7},{7,6},{8,9},{9,8},{10,11... | collective-permute-start | bytes 49160 | tf_op jit(solution)/shard_map/ppermute | solution.py:882
  27.6 0.8 %conditional.2 = (f32[19,20,8,128]{3,2,1,0:T(8,128)S(1)}) conditional(s32[]{:T(128)} %bitcast.2, (s32[3]{0:T(128)S(1)}, f32[19,12,8,128]{3,2,1,0:T(8,128)S(1)}, f32[2,19,4,8,128]{4,3,2,1,0:T(8,128)S(1)}, f32[12,8,128]{2,1,0:T(8,128)S(1)}) %tuple.20, (f32[19,12,8,128]{3,2,1,0:T(8,128)S(1)}, s32[3]{0:T(128)S(1)}, f32[12,8,128]{2,1,0:T(8,128)S(1)}) %tuple.21), branch_computations={%region_0.0_spmd, %region_1.0_spmd} | conditional | flops 80466944 | bytes 15206744 | solution.py:931
  27.6 0.8 %place_populations.2 = f32[19,20,8,128]{3,2,1,0:T(8,128)S(1)} custom-call(s32[3]{0:T(128)S(1)} %get-tuple-element.32.where, f32[19,12,8,128]{3,2,1,0:T(8,128)S(1)} %get-tuple-element.33.final, f32[2,19,4,8,128]{4,3,2,1,0:T(8,128)S(1)} %get-tuple-element.38.outer, f32[12,8,128]{2,1,0:T(8,128)S(1)} %get-tuple-element.39.later), custom_call_target="tpu_custom_call" | custom-call | flops 80000000 | bytes 4000000 | tf_op jit(solution)/shard_map/cond/branch_0_fun/place_populations/pallas_call | solution.py:743
  28.4 0.0 copy-start
  28.4 0.0 collective-permute-done.11
  28.5 0.0 collective-permute-done.13
  28.5 0.7 %conditional.3 = (f32[20,8,128]{2,1,0:T(8,128)S(1)}) conditional(s32[]{:T(128)} %bitcast.2, (s32[3]{0:T(128)S(1)}, f32[4,8,128]{2,1,0:T(8,128)S(1)}, f32[12,8,128]{2,1,0:T(8,128)S(1)}, f32[4,8,128]{2,1,0:T(8,128)S(1)}, f32[4,8,128]{2,1,0:T(8,128)S(1)}) %tuple.22, (f32[12,8,128]{2,1,0:T(8,128)S(1)}, s32[3]{0:T(128)S(1)}, ...), branch_computations={%region_2.0_spmd, %region_3.0_spmd} | conditional | flops 20000000 | bytes 1393304 | solution.py:932
  28.5 0.7 %near_gradient.1 = f32[20,8,128]{2,1,0:T(8,128)S(1)} custom-call(s32[3]{0:T(128)S(1)} %get-tuple-element.43.where, f32[4,8,128]{2,1,0:T(8,128)S(1)} %get-tuple-element.44.drag, f32[12,8,128]{2,1,0:T(8,128)S(1)} %get-tuple-element.45.gradient, f32[4,8,128]{2,1,0:T(8,128)S(1)} %get-tuple-element.46.from_far, f32[4,8,128]{2,1,0:T(8,128)S(1)} %get-tuple-element.47.from_near), custom_call_target="tpu_custom_call" | custom-call | flops 20000000 | bytes 1000000 | tf_op jit(solution)/shard_map/cond/branch_0_fun/near_gradient/pallas_call | solution.py:743
  29.2 0.0 copy-start.1
  29.2 0.3 %copy-done = f32[19,20,8,128]{3,2,1,0:T(8,128)} copy-done((f32[19,20,8,128]{3,2,1,0:T(8,128)}, f32[19,20,8,128]{3,2,1,0:T(8,128)S(1)}, u32[]{:S(2)}) %copy-start) | copy-done | bytes 1556504
  29.6 0.3 copy-done.1
  (6 shorter events, 0.0 us)
Async XLA Ops:
  2.0 8.8 %collective-permute-start.4 = (f32[23,2,8,128]{3,2,1,0:T(8,128)S(1)}, f32[23,2,8,128]{3,2,1,0:T(8,128)S(1)}, u32[]{:S(2)}, u32[]{:S(2)}) collective-permute-start(f32[23,2,8,128]{3,2,1,0:T(8,128)S(1)} %get-tuple-element.84), channel_id=1, source_target_pairs={{0,15},{1,2},{2,1},{3,4},{4,3},{5,6},{6,5},{7,8},{8,7},{9,10},{10,... | collective-permute-start | bytes 565256 | tf_op jit(solution)/shard_map/ppermute | solution.py:768
  7.5 3.3 %collective-permute-start.5 = (f32[23,2,8,128]{3,2,1,0:T(8,128)S(1)}, f32[23,2,8,128]{3,2,1,0:T(8,128)S(1)}, u32[]{:S(2)}, u32[]{:S(2)}) collective-permute-start(f32[23,2,8,128]{3,2,1,0:T(8,128)S(1)} %get-tuple-element.85), channel_id=1, source_target_pairs={{0,1},{1,0},{2,3},{3,2},{4,5},{5,4},{6,7},{7,6},{8,9},{9,8},{10,11... | collective-permute-start | bytes 565256 | tf_op jit(solution)/shard_map/ppermute | solution.py:767
  9.6 8.9 %collective-permute-start.6 = (f32[49,8,128]{2,1,0:T(8,128)S(1)}, f32[49,8,128]{2,1,0:T(8,128)S(1)}, u32[]{:S(2)}, u32[]{:S(2)}) collective-permute-start(f32[49,8,128]{2,1,0:T(8,128)S(1)} %get-tuple-element.100), channel_id=1, source_target_pairs={{0,15},{1,2},{2,1},{3,4},{4,3},{5,6},{6,5},{7,8},{8,7},{9,10},{10,... | collective-permute-start | bytes 602120 | tf_op jit(solution)/shard_map/ppermute | solution.py:806
  10.4 8.1 %collective-permute-start.7 = (f32[49,8,128]{2,1,0:T(8,128)S(1)}, f32[49,8,128]{2,1,0:T(8,128)S(1)}, u32[]{:S(2)}, u32[]{:S(2)}) collective-permute-start(f32[49,8,128]{2,1,0:T(8,128)S(1)} %get-tuple-element.101), channel_id=1, source_target_pairs={{0,1},{1,0},{2,3},{3,2},{4,5},{5,4},{6,7},{7,6},{8,9},{9,8},{10,11... | collective-permute-start | bytes 602120 | tf_op jit(solution)/shard_map/ppermute | solution.py:805
  11.9 1.2 %collective-permute-start.8 = (f32[4,8,128]{2,1,0:T(8,128)S(1)}, f32[4,8,128]{2,1,0:T(8,128)S(1)}, u32[]{:S(2)}, u32[]{:S(2)}) collective-permute-start(f32[4,8,128]{2,1,0:T(8,128)S(1)} %get-tuple-element.102), channel_id=1, source_target_pairs={{0,1},{1,0},{2,3},{3,2},{4,5},{5,4},{6,7},{7,6},{8,9},{9,8},{10,11... | collective-permute-start | bytes 49160 | tf_op jit(solution)/shard_map/ppermute | solution.py:841
  13.1 3.7 %collective-permute-start.9 = (f32[4,8,128]{2,1,0:T(8,128)S(1)}, f32[4,8,128]{2,1,0:T(8,128)S(1)}, u32[]{:S(2)}, u32[]{:S(2)}) collective-permute-start(f32[4,8,128]{2,1,0:T(8,128)S(1)} %add.12), channel_id=1, source_target_pairs={{0,4},{1,5},{2,6},{3,7},{4,0},{5,1},{6,2},{7,3},{8,12},{9,13},{10,... | collective-permute-start | bytes 49160 | tf_op jit(solution)/shard_map/ppermute | solution.py:841
  16.9 3.7 %collective-permute-start.10 = (f32[4,8,128]{2,1,0:T(8,128)S(1)}, f32[4,8,128]{2,1,0:T(8,128)S(1)}, u32[]{:S(2)}, u32[]{:S(2)}) collective-permute-start(f32[4,8,128]{2,1,0:T(8,128)S(1)} %add.13.summed), channel_id=1, source_target_pairs={{0,2},{1,3},{2,0},{3,1},{4,6},{5,7},{6,4},{7,5},{8,10},{9,11},{10,... | collective-permute-start | bytes 49160 | tf_op jit(solution)/shard_map/ppermute | solution.py:841
  20.6 7.8 %collective-permute-start.11 = (f32[4,8,128]{2,1,0:T(8,128)S(1)}, f32[4,8,128]{2,1,0:T(8,128)S(1)}, u32[]{:S(2)}, u32[]{:S(2)}) collective-permute-start(f32[4,8,128]{2,1,0:T(8,128)S(1)} %add.14.summed), channel_id=1, source_target_pairs={{0,8},{1,9},{2,10},{3,11},{4,12},{5,13},{6,14},{7,15},{8,0},{9,1},... | collective-permute-start | bytes 49160 | tf_op jit(solution)/shard_map/ppermute | solution.py:841
  23.5 4.9 %collective-permute-start.12 = (f32[4,8,128]{2,1,0:T(8,128)S(1)}, f32[4,8,128]{2,1,0:T(8,128)S(1)}, u32[]{:S(2)}, u32[]{:S(2)}) collective-permute-start(f32[4,8,128]{2,1,0:T(8,128)S(1)} %get-tuple-element.107), channel_id=1, source_target_pairs={{1,2},{2,1},{3,4},{4,3},{5,6},{6,5},{7,8},{8,7},{9,10},{10,9},{11,... | collective-permute-start | bytes 49160 | tf_op jit(solution)/shard_map/ppermute | solution.py:883
  24.2 4.3 %collective-permute-start.13 = (f32[4,8,128]{2,1,0:T(8,128)S(1)}, f32[4,8,128]{2,1,0:T(8,128)S(1)}, u32[]{:S(2)}, u32[]{:S(2)}) collective-permute-start(f32[4,8,128]{2,1,0:T(8,128)S(1)} %get-tuple-element.108), channel_id=1, source_target_pairs={{0,1},{1,0},{2,3},{3,2},{4,5},{5,4},{6,7},{7,6},{8,9},{9,8},{10,11... | collective-permute-start | bytes 49160 | tf_op jit(solution)/shard_map/ppermute | solution.py:882
  28.4 1.1 %copy-start = (f32[19,20,8,128]{3,2,1,0:T(8,128)}, f32[19,20,8,128]{3,2,1,0:T(8,128)S(1)}, u32[]{:S(2)}) copy-start(f32[19,20,8,128]{3,2,1,0:T(8,128)S(1)} %get-tuple-element.109) | copy-start | bytes 4669444
  29.2 0.6 %copy-start.1 = (f32[20,8,128]{2,1,0:T(8,128)}, f32[20,8,128]{2,1,0:T(8,128)S(1)}, u32[]{:S(2)}) copy-start(f32[20,8,128]{2,1,0:T(8,128)S(1)} %get-tuple-element.110) | copy-start | bytes 245764

commit v13 on v12

--- a/solution.py
+++ b/solution.py
@@ -154,7 +154,7 @@
         next(body, None)
 
 
-def each_plane(low, high, body, width=6):
+def each_plane(low, high, body, width=7):
     groups = (high - low) // width
 
     def group(index, carry):

time: 30 us -> 29.9 us (level)
  waiting for transfers between devices: 3.88 us -> 3.43 us
    ppermute x1, waiting for transfers between devices: 0.36 us -> 0.01 us  [body(): far = lax.ppermute(own_far, 'block', far_pairs)]
  transfers between devices with their start and end apart: 10 -> 10, of which waited for: 4 -> 3; matrix products, arithmetic and copies ran while one was open for 2% -> 2% of each run, Pallas kernels for 21% -> 22%
where the time goes in v13:
time: 29.9 us; the launch traced here: 29.7 us
  starting transfers between devices  15.1 us (51%)
  Pallas kernels  8.54 us (29%)
  waiting for transfers between devices  3.43 us (11%)
  between operations  1.41 us (5%)
  local copies, waits for them, and re-layouts  1.21 us (4%)
    pallas_call x7, Pallas kernels, call(): pl.pallas_call(kernel, out_shape=[shape for shape, _ in outs], in_specs=i...  8.54 us
    ppermute x1, starting transfers between devices, body(): far = lax.ppermute(own_far, 'block', far_pairs)  5.51 us
    ppermute x4, starting transfers between devices, body(): sums.append(sums[-1] + lax.ppermute(sums[-1], 'block', swap))  4.7 us
    ppermute x4, waiting for transfers between devices, body(): sums.append(sums[-1] + lax.ppermute(sums[-1], 'block', swap))  3.41 us
    ppermute x2, starting transfers between devices, body(): from_near = lax.ppermute(to_near, 'block', near_pairs)  3.4 us
    ppermute x1, starting transfers between devices, body(): from_far = lax.ppermute(to_far, 'block', far_pairs)  0.81 us
    ppermute x1, starting transfers between devices, body(): from_far = lax.ppermute(to_far, 'block', inner_pairs)  0.66 us
    unnamed x4, local copies, waits for them, and re-layouts  0.63 us
  transfers between devices with their start and end apart: 10, of which 3 were waited for; matrix products, arithmetic and copies ran while one was open for 2% of the time, Pallas kernels for 22%

profile of v13, /device:TPU:0, one launch (start us, length us, event | category | flops | bytes accessed | tf_op | source)
XLA Modules:
  0.0 29.7 jit_solution(7531716283033271544)
XLA Ops:
  0.6 1.4 %edge_planes.1 = (f32[23,2,8,128]{3,2,1,0:T(8,128)S(1)}, f32[23,2,8,128]{3,2,1,0:T(8,128)S(1)}, f32[19,12,8,128]{3,2,1,0:T(8,128)S(1)}, f32[12,8,128]{2,1,0:T(8,128)S(1)}) custom-call(f32[19,12,8,128]{3,2,1,0:T(8,128)} %pops_far.1, f32[12,8,128]{2,1,0:T(8,128)} %design.1, s32[12,8,128]{2,1,0:T(8,128)} %mask.1), custom_call_target="tpu_custom_call" | custom-call | flops 20000000 | bytes 1000000 | tf_op jit(solution)/shard_map/edge_planes/pallas_call | solution.py:743
  2.0 5.5 %collective-permute-start.4 = (f32[23,2,8,128]{3,2,1,0:T(8,128)S(1)}, f32[23,2,8,128]{3,2,1,0:T(8,128)S(1)}, u32[]{:S(2)}, u32[]{:S(2)}) collective-permute-start(f32[23,2,8,128]{3,2,1,0:T(8,128)S(1)} %get-tuple-element.84), channel_id=1, source_target_pairs={{0,15},{1,2},{2,1},{3,4},{4,3},{5,6},{6,5},{7,8},{8,7},{9,10},{10,... | collective-permute-start | bytes 565256 | tf_op jit(solution)/shard_map/ppermute | solution.py:768
  7.5 0.0 collective-permute-start.5
  7.5 2.5 %interior_steps.1 = (f32[49,8,128]{2,1,0:T(8,128)S(1)}, f32[49,8,128]{2,1,0:T(8,128)S(1)}, f32[19,12,8,128]{3,2,1,0:T(8,128)S(1)}, f32[16,12,8,128]{3,2,1,0:T(8,...) custom-call(s32[48]{0:T(128)} %owner_far.1, ...), custom_call_target="tpu_custom_call" | custom-call | flops 120000000 | bytes 6000000 | tf_op jit(solution)/shard_map/interior_steps/pallas_call | solution.py:743
  10.0 0.8 %collective-permute-start.6 = (f32[49,8,128]{2,1,0:T(8,128)S(1)}, f32[49,8,128]{2,1,0:T(8,128)S(1)}, u32[]{:S(2)}, u32[]{:S(2)}) collective-permute-start(f32[49,8,128]{2,1,0:T(8,128)S(1)} %get-tuple-element.100), channel_id=1, source_target_pairs={{0,15},{1,2},{2,1},{3,4},{4,3},{5,6},{6,5},{7,8},{8,7},{9,10},{10,... | collective-permute-start | bytes 602120 | tf_op jit(solution)/shard_map/ppermute | solution.py:806
  10.8 0.0 collective-permute-start.7
  10.8 0.0 collective-permute-done.4.far
  10.8 1.1 %boundary_steps.1 = (f32[19,12,8,128]{3,2,1,0:T(8,128)S(1)}, f32[16,18,8,128]{3,2,1,0:T(8,128)S(1)}, f32[18,8,128]{2,1,0:T(8,128)S(1)}, s32[18,8,128]{2,1,0:T(8,...) custom-call(f32[23,2,8,128]{3,2,1,0:T(8,128)S(1)} %collective-permut, ...), custom_call_target="tpu_custom_call" | custom-call | flops 160000000 | bytes 8000000 | tf_op jit(solution)/shard_map/boundary_steps/pallas_call | solution.py:743
  11.9 0.6 %collective-permute-start.8 = (f32[4,8,128]{2,1,0:T(8,128)S(1)}, f32[4,8,128]{2,1,0:T(8,128)S(1)}, u32[]{:S(2)}, u32[]{:S(2)}) collective-permute-start(f32[4,8,128]{2,1,0:T(8,128)S(1)} %get-tuple-element.102), channel_id=1, source_target_pairs={{0,1},{1,0},{2,3},{3,2},{4,5},{5,4},{6,7},{7,6},{8,9},{9,8},{10,11... | collective-permute-start | bytes 49160 | tf_op jit(solution)/shard_map/ppermute | solution.py:841
  12.5 0.8 %collective-permute-done.8 = f32[4,8,128]{2,1,0:T(8,128)S(1)} collective-permute-done((f32[4,8,128]{2,1,0:T(8,128)S(1)}, f32[4,8,128]{2,1,0:T(8,128)S(1)}, u32[]{:S(2)}, u32[]{:S(2)}) %collective-permute-start.8) | collective-permute-done | bytes 16416 | tf_op jit(solution)/shard_map/ppermute | solution.py:841
  13.3 0.7 %collective-permute-start.9 = (f32[4,8,128]{2,1,0:T(8,128)S(1)}, f32[4,8,128]{2,1,0:T(8,128)S(1)}, u32[]{:S(2)}, u32[]{:S(2)}) collective-permute-start(f32[4,8,128]{2,1,0:T(8,128)S(1)} %add.12), channel_id=1, source_target_pairs={{0,4},{1,5},{2,6},{3,7},{4,0},{5,1},{6,2},{7,3},{8,12},{9,13},{10,... | collective-permute-start | bytes 49160 | tf_op jit(solution)/shard_map/ppermute | solution.py:841
  14.0 0.6 %slice.3 = s32[1]{0:T(128)} slice(s32[3]{0:T(128)S(1)} %get-tuple-element.83), slice={[2:3]} | slice | bytes 8 | tf_op jit(solution)/shard_map/slice | solution.py:844
  15.2 1.8 %collective-permute-done.9 = f32[4,8,128]{2,1,0:T(8,128)S(1)} collective-permute-done((f32[4,8,128]{2,1,0:T(8,128)S(1)}, f32[4,8,128]{2,1,0:T(8,128)S(1)}, u32[]{:S(2)}, u32[]{:S(2)}) %collective-permute-start.9) | collective-permute-done | bytes 16416 | tf_op jit(solution)/shard_map/ppermute | solution.py:841
  17.1 1.8 %collective-permute-start.10 = (f32[4,8,128]{2,1,0:T(8,128)S(1)}, f32[4,8,128]{2,1,0:T(8,128)S(1)}, u32[]{:S(2)}, u32[]{:S(2)}) collective-permute-start(f32[4,8,128]{2,1,0:T(8,128)S(1)} %add.13.summed), channel_id=1, source_target_pairs={{0,2},{1,3},{2,0},{3,1},{4,6},{5,7},{6,4},{7,5},{8,10},{9,11},{10,... | collective-permute-start | bytes 49160 | tf_op jit(solution)/shard_map/ppermute | solution.py:841
  18.9 0.0 collective-permute-done.6.from_far
  18.9 0.0 collective-permute-done.7.from_near
  18.9 1.2 %outer_steps.1 = (f32[2,19,4,8,128]{4,3,2,1,0:T(8,128)S(1)}, f32[18,8,128]{2,1,0:T(8,128)S(1)}, f32[19,18,8,128]{3,2,1,0:T(8,128)S(1)}) custom-call(f32[16,18,8,128]{3,2,1,0:T(8,128)S(1)} %get-tuple-element.94.history, f32[18,8,128]{2,1,0:T(8,128)S(1)} %get-tuple-element.95.opens, s32[18,8,128]{2,1,0:T(8,128)S(1)} %get-tuple-element.96.fluid, ...), custom_call_target="tpu_custom_call" | custom-call | flops 240000000 | bytes 12000000 | tf_op jit(solution)/shard_map/outer_steps/pallas_call | solution.py:743
  20.1 0.7 %collective-permute-done.10 = f32[4,8,128]{2,1,0:T(8,128)S(1)} collective-permute-done((f32[4,8,128]{2,1,0:T(8,128)S(1)}, f32[4,8,128]{2,1,0:T(8,128)S(1)}, u32[]{:S(2)}, u32[]{:S(2)}) %collective-permute-start.10) | collective-permute-done | bytes 16416 | tf_op jit(solution)/shard_map/ppermute | solution.py:841
  20.8 1.7 %collective-permute-start.11 = (f32[4,8,128]{2,1,0:T(8,128)S(1)}, f32[4,8,128]{2,1,0:T(8,128)S(1)}, u32[]{:S(2)}, u32[]{:S(2)}) collective-permute-start(f32[4,8,128]{2,1,0:T(8,128)S(1)} %add.14.summed), channel_id=1, source_target_pairs={{0,8},{1,9},{2,10},{3,11},{4,12},{5,13},{6,14},{7,15},{8,0},{9,1},... | collective-permute-start | bytes 49160 | tf_op jit(solution)/shard_map/ppermute | solution.py:841
  22.5 0.9 %gradient_steps.1 = (f32[12,8,128]{2,1,0:T(8,128)S(1)}, f32[4,8,128]{2,1,0:T(8,128)S(1)}, f32[4,8,128]{2,1,0:T(8,128)S(1)}) custom-call(f32[16,18,8,128]{3,2,1,0:T(8,128)S(1)} %get-tuple-element.94.history, f32[18,8,128]{2,1,0:T(8,128)S(1)} %get-tuple-element.95.opens, s32[18,8,128]{2,1,0:T(8,128)S(1)} %get-tuple-element.97.words, ...), custom_call_target="tpu_custom_call" | custom-call | flops 120000000 | bytes 6000000 | tf_op jit(solution)/shard_map/gradient_steps/pallas_call | solution.py:743
  23.4 0.7 %collective-permute-start.12 = (f32[4,8,128]{2,1,0:T(8,128)S(1)}, f32[4,8,128]{2,1,0:T(8,128)S(1)}, u32[]{:S(2)}, u32[]{:S(2)}) collective-permute-start(f32[4,8,128]{2,1,0:T(8,128)S(1)} %get-tuple-element.107), channel_id=1, source_target_pairs={{1,2},{2,1},{3,4},{4,3},{5,6},{6,5},{7,8},{8,7},{9,10},{10,9},{11,... | collective-permute-start | bytes 49160 | tf_op jit(solution)/shard_map/ppermute | solution.py:883
  24.1 3.4 %collective-permute-start.13 = (f32[4,8,128]{2,1,0:T(8,128)S(1)}, f32[4,8,128]{2,1,0:T(8,128)S(1)}, u32[]{:S(2)}, u32[]{:S(2)}) collective-permute-start(f32[4,8,128]{2,1,0:T(8,128)S(1)} %get-tuple-element.108), channel_id=1, source_target_pairs={{0,1},{1,0},{2,3},{3,2},{4,5},{5,4},{6,7},{7,6},{8,9},{9,8},{10,11... | collective-permute-start | bytes 49160 | tf_op jit(solution)/shard_map/ppermute | solution.py:882
  27.5 0.8 %conditional.2 = (f32[19,20,8,128]{3,2,1,0:T(8,128)S(1)}) conditional(s32[]{:T(128)} %bitcast.2, (s32[3]{0:T(128)S(1)}, f32[19,12,8,128]{3,2,1,0:T(8,128)S(1)}, f32[2,19,4,8,128]{4,3,2,1,0:T(8,128)S(1)}, f32[12,8,128]{2,1,0:T(8,128)S(1)}) %tuple.20, (f32[19,12,8,128]{3,2,1,0:T(8,128)S(1)}, s32[3]{0:T(128)S(1)}, f32[12,8,128]{2,1,0:T(8,128)S(1)}) %tuple.21), branch_computations={%region_0.0_spmd, %region_1.0_spmd} | conditional | flops 80466944 | bytes 15206744 | solution.py:931
  27.5 0.8 %place_populations.2 = f32[19,20,8,128]{3,2,1,0:T(8,128)S(1)} custom-call(s32[3]{0:T(128)S(1)} %get-tuple-element.32.where, f32[19,12,8,128]{3,2,1,0:T(8,128)S(1)} %get-tuple-element.33.final, f32[2,19,4,8,128]{4,3,2,1,0:T(8,128)S(1)} %get-tuple-element.38.outer, f32[12,8,128]{2,1,0:T(8,128)S(1)} %get-tuple-element.39.later), custom_call_target="tpu_custom_call" | custom-call | flops 80000000 | bytes 4000000 | tf_op jit(solution)/shard_map/cond/branch_0_fun/place_populations/pallas_call | solution.py:743
  28.3 0.0 copy-start
  28.3 0.0 collective-permute-done.11
  28.3 0.0 collective-permute-done.13
  28.3 0.7 %conditional.3 = (f32[20,8,128]{2,1,0:T(8,128)S(1)}) conditional(s32[]{:T(128)} %bitcast.2, (s32[3]{0:T(128)S(1)}, f32[4,8,128]{2,1,0:T(8,128)S(1)}, f32[12,8,128]{2,1,0:T(8,128)S(1)}, f32[4,8,128]{2,1,0:T(8,128)S(1)}, f32[4,8,128]{2,1,0:T(8,128)S(1)}) %tuple.22, (f32[12,8,128]{2,1,0:T(8,128)S(1)}, s32[3]{0:T(128)S(1)}, ...), branch_computations={%region_2.0_spmd, %region_3.0_spmd} | conditional | flops 20000000 | bytes 1393304 | solution.py:932
  28.4 0.7 %near_gradient.1 = f32[20,8,128]{2,1,0:T(8,128)S(1)} custom-call(s32[3]{0:T(128)S(1)} %get-tuple-element.43.where, f32[4,8,128]{2,1,0:T(8,128)S(1)} %get-tuple-element.44.drag, f32[12,8,128]{2,1,0:T(8,128)S(1)} %get-tuple-element.45.gradient, f32[4,8,128]{2,1,0:T(8,128)S(1)} %get-tuple-element.46.from_far, f32[4,8,128]{2,1,0:T(8,128)S(1)} %get-tuple-element.47.from_near), custom_call_target="tpu_custom_call" | custom-call | flops 20000000 | bytes 1000000 | tf_op jit(solution)/shard_map/cond/branch_0_fun/near_gradient/pallas_call | solution.py:743
  29.1 0.0 copy-start.1
  29.1 0.3 %copy-done = f32[19,20,8,128]{3,2,1,0:T(8,128)} copy-done((f32[19,20,8,128]{3,2,1,0:T(8,128)}, f32[19,20,8,128]{3,2,1,0:T(8,128)S(1)}, u32[]{:S(2)}) %copy-start) | copy-done | bytes 1556504
  29.4 0.3 copy-done.1
  (6 shorter events, 0.0 us)
Async XLA Ops:
  2.0 8.8 %collective-permute-start.4 = (f32[23,2,8,128]{3,2,1,0:T(8,128)S(1)}, f32[23,2,8,128]{3,2,1,0:T(8,128)S(1)}, u32[]{:S(2)}, u32[]{:S(2)}) collective-permute-start(f32[23,2,8,128]{3,2,1,0:T(8,128)S(1)} %get-tuple-element.84), channel_id=1, source_target_pairs={{0,15},{1,2},{2,1},{3,4},{4,3},{5,6},{6,5},{7,8},{8,7},{9,10},{10,... | collective-permute-start | bytes 565256 | tf_op jit(solution)/shard_map/ppermute | solution.py:768
  7.5 3.3 %collective-permute-start.5 = (f32[23,2,8,128]{3,2,1,0:T(8,128)S(1)}, f32[23,2,8,128]{3,2,1,0:T(8,128)S(1)}, u32[]{:S(2)}, u32[]{:S(2)}) collective-permute-start(f32[23,2,8,128]{3,2,1,0:T(8,128)S(1)} %get-tuple-element.85), channel_id=1, source_target_pairs={{0,1},{1,0},{2,3},{3,2},{4,5},{5,4},{6,7},{7,6},{8,9},{9,8},{10,11... | collective-permute-start | bytes 565256 | tf_op jit(solution)/shard_map/ppermute | solution.py:767
  10.0 8.9 %collective-permute-start.6 = (f32[49,8,128]{2,1,0:T(8,128)S(1)}, f32[49,8,128]{2,1,0:T(8,128)S(1)}, u32[]{:S(2)}, u32[]{:S(2)}) collective-permute-start(f32[49,8,128]{2,1,0:T(8,128)S(1)} %get-tuple-element.100), channel_id=1, source_target_pairs={{0,15},{1,2},{2,1},{3,4},{4,3},{5,6},{6,5},{7,8},{8,7},{9,10},{10,... | collective-permute-start | bytes 602120 | tf_op jit(solution)/shard_map/ppermute | solution.py:806
  10.8 8.1 %collective-permute-start.7 = (f32[49,8,128]{2,1,0:T(8,128)S(1)}, f32[49,8,128]{2,1,0:T(8,128)S(1)}, u32[]{:S(2)}, u32[]{:S(2)}) collective-permute-start(f32[49,8,128]{2,1,0:T(8,128)S(1)} %get-tuple-element.101), channel_id=1, source_target_pairs={{0,1},{1,0},{2,3},{3,2},{4,5},{5,4},{6,7},{7,6},{8,9},{9,8},{10,11... | collective-permute-start | bytes 602120 | tf_op jit(solution)/shard_map/ppermute | solution.py:805
  11.9 1.4 %collective-permute-start.8 = (f32[4,8,128]{2,1,0:T(8,128)S(1)}, f32[4,8,128]{2,1,0:T(8,128)S(1)}, u32[]{:S(2)}, u32[]{:S(2)}) collective-permute-start(f32[4,8,128]{2,1,0:T(8,128)S(1)} %get-tuple-element.102), channel_id=1, source_target_pairs={{0,1},{1,0},{2,3},{3,2},{4,5},{5,4},{6,7},{7,6},{8,9},{9,8},{10,11... | collective-permute-start | bytes 49160 | tf_op jit(solution)/shard_map/ppermute | solution.py:841
  13.3 3.7 %collective-permute-start.9 = (f32[4,8,128]{2,1,0:T(8,128)S(1)}, f32[4,8,128]{2,1,0:T(8,128)S(1)}, u32[]{:S(2)}, u32[]{:S(2)}) collective-permute-start(f32[4,8,128]{2,1,0:T(8,128)S(1)} %add.12), channel_id=1, source_target_pairs={{0,4},{1,5},{2,6},{3,7},{4,0},{5,1},{6,2},{7,3},{8,12},{9,13},{10,... | collective-permute-start | bytes 49160 | tf_op jit(solution)/shard_map/ppermute | solution.py:841
  17.1 3.7 %collective-permute-start.10 = (f32[4,8,128]{2,1,0:T(8,128)S(1)}, f32[4,8,128]{2,1,0:T(8,128)S(1)}, u32[]{:S(2)}, u32[]{:S(2)}) collective-permute-start(f32[4,8,128]{2,1,0:T(8,128)S(1)} %add.13.summed), channel_id=1, source_target_pairs={{0,2},{1,3},{2,0},{3,1},{4,6},{5,7},{6,4},{7,5},{8,10},{9,11},{10,... | collective-permute-start | bytes 49160 | tf_op jit(solution)/shard_map/ppermute | solution.py:841
  20.8 7.5 %collective-permute-start.11 = (f32[4,8,128]{2,1,0:T(8,128)S(1)}, f32[4,8,128]{2,1,0:T(8,128)S(1)}, u32[]{:S(2)}, u32[]{:S(2)}) collective-permute-start(f32[4,8,128]{2,1,0:T(8,128)S(1)} %add.14.summed), channel_id=1, source_target_pairs={{0,8},{1,9},{2,10},{3,11},{4,12},{5,13},{6,14},{7,15},{8,0},{9,1},... | collective-permute-start | bytes 49160 | tf_op jit(solution)/shard_map/ppermute | solution.py:841
  23.4 4.9 %collective-permute-start.12 = (f32[4,8,128]{2,1,0:T(8,128)S(1)}, f32[4,8,128]{2,1,0:T(8,128)S(1)}, u32[]{:S(2)}, u32[]{:S(2)}) collective-permute-start(f32[4,8,128]{2,1,0:T(8,128)S(1)} %get-tuple-element.107), channel_id=1, source_target_pairs={{1,2},{2,1},{3,4},{4,3},{5,6},{6,5},{7,8},{8,7},{9,10},{10,9},{11,... | collective-permute-start | bytes 49160 | tf_op jit(solution)/shard_map/ppermute | solution.py:883
  24.1 4.3 %collective-permute-start.13 = (f32[4,8,128]{2,1,0:T(8,128)S(1)}, f32[4,8,128]{2,1,0:T(8,128)S(1)}, u32[]{:S(2)}, u32[]{:S(2)}) collective-permute-start(f32[4,8,128]{2,1,0:T(8,128)S(1)} %get-tuple-element.108), channel_id=1, source_target_pairs={{0,1},{1,0},{2,3},{3,2},{4,5},{5,4},{6,7},{7,6},{8,9},{9,8},{10,11... | collective-permute-start | bytes 49160 | tf_op jit(solution)/shard_map/ppermute | solution.py:882
  28.3 1.1 %copy-start = (f32[19,20,8,128]{3,2,1,0:T(8,128)}, f32[19,20,8,128]{3,2,1,0:T(8,128)S(1)}, u32[]{:S(2)}) copy-start(f32[19,20,8,128]{3,2,1,0:T(8,128)S(1)} %get-tuple-element.109) | copy-start | bytes 4669444
  29.1 0.6 %copy-start.1 = (f32[20,8,128]{2,1,0:T(8,128)}, f32[20,8,128]{2,1,0:T(8,128)S(1)}, u32[]{:S(2)}) copy-start(f32[20,8,128]{2,1,0:T(8,128)S(1)} %get-tuple-element.110) | copy-start | bytes 245764

commit v14 on v13

--- a/solution.py
+++ b/solution.py
@@ -623,7 +623,7 @@
     def seed_home(plane):
         return seed(plane, *recall(history, STEPS, plane))
 
-    each_plane(HALO, HALO + home, seed_home)
+    each_plane(HALO, HALO + home, seed_home, home)
 
     def ends(side):
         flow = [second_flow[side, 1 + axis] for axis in range(3)]
@@ -634,7 +634,7 @@
     def step_two(plane):
         return retreat(opens, words, share, even, odd, plane, *recall(history, 2, plane))
 
-    each_plane(HALO - 1, HALO + home + 1, step_two)
+    each_plane(HALO - 1, HALO + home + 1, step_two, home + 2)
 
 
 def gradient_kernel(
@@ -651,8 +651,8 @@
     def step_zero(plane):
         return retreat(opens, words, total, even, None, plane, *recall(history, 0, plane))
 
-    each_plane(HALO - 1, HALO + home + 1, step_one)
-    each_plane(HALO, HALO + home, step_zero)
+    each_plane(HALO - 1, HALO + home + 1, step_one, home + 2)
+    each_plane(HALO, HALO + home, step_zero, home)
     for plane in range(home):
         design = marked[plane]
         slope = 3.0 / ((1.6 + 3.4 * design) * (1.0 + 4.0 * design))

time: 29.9 us -> 29.8 us (level)
  transfers between devices with their start and end apart: 10 -> 10, of which waited for: 3 -> 3; matrix products, arithmetic and copies ran while one was open for 2% -> 2% of each run, Pallas kernels for 22% -> 21%
where the time goes in v14:
time: 29.8 us; the launch traced here: 29.6 us
  starting transfers between devices  15.1 us (51%)
  Pallas kernels  8.29 us (28%)
  waiting for transfers between devices  3.57 us (12%)
  between operations  1.4 us (5%)
  local copies, waits for them, and re-layouts  1.21 us (4%)
    pallas_call x7, Pallas kernels, call(): pl.pallas_call(kernel, out_shape=[shape for shape, _ in outs], in_specs=i...  8.29 us
    ppermute x1, starting transfers between devices, body(): far = lax.ppermute(own_far, 'block', far_pairs)  5.51 us
    ppermute x4, starting transfers between devices, body(): sums.append(sums[-1] + lax.ppermute(sums[-1], 'block', swap))  4.7 us
    ppermute x4, waiting for transfers between devices, body(): sums.append(sums[-1] + lax.ppermute(sums[-1], 'block', swap))  3.55 us
    ppermute x2, starting transfers between devices, body(): from_near = lax.ppermute(to_near, 'block', near_pairs)  3.4 us
    ppermute x1, starting transfers between devices, body(): from_far = lax.ppermute(to_far, 'block', far_pairs)  0.81 us
    ppermute x1, starting transfers between devices, body(): from_far = lax.ppermute(to_far, 'block', inner_pairs)  0.66 us
    unnamed x4, local copies, waits for them, and re-layouts  0.63 us
  transfers between devices with their start and end apart: 10, of which 3 were waited for; matrix products, arithmetic and copies ran while one was open for 2% of the time, Pallas kernels for 21%

profile of v14, /device:TPU:0, one launch (start us, length us, event | category | flops | bytes accessed | tf_op | source)
XLA Modules:
  0.0 29.6 jit_solution(11085041724475862341)
XLA Ops:
  0.6 1.4 %edge_planes.1 = (f32[23,2,8,128]{3,2,1,0:T(8,128)S(1)}, f32[23,2,8,128]{3,2,1,0:T(8,128)S(1)}, f32[19,12,8,128]{3,2,1,0:T(8,128)S(1)}, f32[12,8,128]{2,1,0:T(8,128)S(1)}) custom-call(f32[19,12,8,128]{3,2,1,0:T(8,128)} %pops_far.1, f32[12,8,128]{2,1,0:T(8,128)} %design.1, s32[12,8,128]{2,1,0:T(8,128)} %mask.1), custom_call_target="tpu_custom_call" | custom-call | flops 20000000 | bytes 1000000 | tf_op jit(solution)/shard_map/edge_planes/pallas_call | solution.py:743
  2.0 5.5 %collective-permute-start.4 = (f32[23,2,8,128]{3,2,1,0:T(8,128)S(1)}, f32[23,2,8,128]{3,2,1,0:T(8,128)S(1)}, u32[]{:S(2)}, u32[]{:S(2)}) collective-permute-start(f32[23,2,8,128]{3,2,1,0:T(8,128)S(1)} %get-tuple-element.84), channel_id=1, source_target_pairs={{0,15},{1,2},{2,1},{3,4},{4,3},{5,6},{6,5},{7,8},{8,7},{9,10},{10,... | collective-permute-start | bytes 565256 | tf_op jit(solution)/shard_map/ppermute | solution.py:768
  7.5 0.0 collective-permute-start.5
  7.5 2.5 %interior_steps.1 = (f32[49,8,128]{2,1,0:T(8,128)S(1)}, f32[49,8,128]{2,1,0:T(8,128)S(1)}, f32[19,12,8,128]{3,2,1,0:T(8,128)S(1)}, f32[16,12,8,128]{3,2,1,0:T(8,...) custom-call(s32[48]{0:T(128)} %owner_far.1, ...), custom_call_target="tpu_custom_call" | custom-call | flops 120000000 | bytes 6000000 | tf_op jit(solution)/shard_map/interior_steps/pallas_call | solution.py:743
  10.0 0.8 %collective-permute-start.6 = (f32[49,8,128]{2,1,0:T(8,128)S(1)}, f32[49,8,128]{2,1,0:T(8,128)S(1)}, u32[]{:S(2)}, u32[]{:S(2)}) collective-permute-start(f32[49,8,128]{2,1,0:T(8,128)S(1)} %get-tuple-element.100), channel_id=1, source_target_pairs={{0,15},{1,2},{2,1},{3,4},{4,3},{5,6},{6,5},{7,8},{8,7},{9,10},{10,... | collective-permute-start | bytes 602120 | tf_op jit(solution)/shard_map/ppermute | solution.py:806
  10.8 0.0 collective-permute-start.7
  10.8 0.0 collective-permute-done.4.far
  10.8 0.0 collective-permute-done.5.near
  10.8 1.1 %boundary_steps.1 = (f32[19,12,8,128]{3,2,1,0:T(8,128)S(1)}, f32[16,18,8,128]{3,2,1,0:T(8,128)S(1)}, f32[18,8,128]{2,1,0:T(8,128)S(1)}, s32[18,8,128]{2,1,0:T(8,...) custom-call(f32[23,2,8,128]{3,2,1,0:T(8,128)S(1)} %collective-permut, ...), custom_call_target="tpu_custom_call" | custom-call | flops 160000000 | bytes 8000000 | tf_op jit(solution)/shard_map/boundary_steps/pallas_call | solution.py:743
  11.9 0.6 %collective-permute-start.8 = (f32[4,8,128]{2,1,0:T(8,128)S(1)}, f32[4,8,128]{2,1,0:T(8,128)S(1)}, u32[]{:S(2)}, u32[]{:S(2)}) collective-permute-start(f32[4,8,128]{2,1,0:T(8,128)S(1)} %get-tuple-element.102), channel_id=1, source_target_pairs={{0,1},{1,0},{2,3},{3,2},{4,5},{5,4},{6,7},{7,6},{8,9},{9,8},{10,11... | collective-permute-start | bytes 49160 | tf_op jit(solution)/shard_map/ppermute | solution.py:841
  12.5 0.8 %collective-permute-done.8 = f32[4,8,128]{2,1,0:T(8,128)S(1)} collective-permute-done((f32[4,8,128]{2,1,0:T(8,128)S(1)}, f32[4,8,128]{2,1,0:T(8,128)S(1)}, u32[]{:S(2)}, u32[]{:S(2)}) %collective-permute-start.8) | collective-permute-done | bytes 16416 | tf_op jit(solution)/shard_map/ppermute | solution.py:841
  13.3 0.7 %collective-permute-start.9 = (f32[4,8,128]{2,1,0:T(8,128)S(1)}, f32[4,8,128]{2,1,0:T(8,128)S(1)}, u32[]{:S(2)}, u32[]{:S(2)}) collective-permute-start(f32[4,8,128]{2,1,0:T(8,128)S(1)} %add.12), channel_id=1, source_target_pairs={{0,4},{1,5},{2,6},{3,7},{4,0},{5,1},{6,2},{7,3},{8,12},{9,13},{10,... | collective-permute-start | bytes 49160 | tf_op jit(solution)/shard_map/ppermute | solution.py:841
  14.0 0.6 %slice.3 = s32[1]{0:T(128)} slice(s32[3]{0:T(128)S(1)} %get-tuple-element.83), slice={[2:3]} | slice | bytes 8 | tf_op jit(solution)/shard_map/slice | solution.py:844
  15.2 1.8 %collective-permute-done.9 = f32[4,8,128]{2,1,0:T(8,128)S(1)} collective-permute-done((f32[4,8,128]{2,1,0:T(8,128)S(1)}, f32[4,8,128]{2,1,0:T(8,128)S(1)}, u32[]{:S(2)}, u32[]{:S(2)}) %collective-permute-start.9) | collective-permute-done | bytes 16416 | tf_op jit(solution)/shard_map/ppermute | solution.py:841
  17.1 1.8 %collective-permute-start.10 = (f32[4,8,128]{2,1,0:T(8,128)S(1)}, f32[4,8,128]{2,1,0:T(8,128)S(1)}, u32[]{:S(2)}, u32[]{:S(2)}) collective-permute-start(f32[4,8,128]{2,1,0:T(8,128)S(1)} %add.13.summed), channel_id=1, source_target_pairs={{0,2},{1,3},{2,0},{3,1},{4,6},{5,7},{6,4},{7,5},{8,10},{9,11},{10,... | collective-permute-start | bytes 49160 | tf_op jit(solution)/shard_map/ppermute | solution.py:841
  18.9 0.0 collective-permute-done.6.from_far
  18.9 0.0 collective-permute-done.7.from_near
  18.9 1.1 %outer_steps.1 = (f32[2,19,4,8,128]{4,3,2,1,0:T(8,128)S(1)}, f32[18,8,128]{2,1,0:T(8,128)S(1)}, f32[19,18,8,128]{3,2,1,0:T(8,128)S(1)}) custom-call(f32[16,18,8,128]{3,2,1,0:T(8,128)S(1)} %get-tuple-element.94.history, f32[18,8,128]{2,1,0:T(8,128)S(1)} %get-tuple-element.95.opens, s32[18,8,128]{2,1,0:T(8,128)S(1)} %get-tuple-element.96.fluid, ...), custom_call_target="tpu_custom_call" | custom-call | flops 240000000 | bytes 12000000 | tf_op jit(solution)/shard_map/outer_steps/pallas_call | solution.py:743
  19.9 0.9 %collective-permute-done.10 = f32[4,8,128]{2,1,0:T(8,128)S(1)} collective-permute-done((f32[4,8,128]{2,1,0:T(8,128)S(1)}, f32[4,8,128]{2,1,0:T(8,128)S(1)}, u32[]{:S(2)}, u32[]{:S(2)}) %collective-permute-start.10) | collective-permute-done | bytes 16416 | tf_op jit(solution)/shard_map/ppermute | solution.py:841
  20.8 1.7 %collective-permute-start.11 = (f32[4,8,128]{2,1,0:T(8,128)S(1)}, f32[4,8,128]{2,1,0:T(8,128)S(1)}, u32[]{:S(2)}, u32[]{:S(2)}) collective-permute-start(f32[4,8,128]{2,1,0:T(8,128)S(1)} %add.14.summed), channel_id=1, source_target_pairs={{0,8},{1,9},{2,10},{3,11},{4,12},{5,13},{6,14},{7,15},{8,0},{9,1},... | collective-permute-start | bytes 49160 | tf_op jit(solution)/shard_map/ppermute | solution.py:841
  22.5 0.8 %gradient_steps.1 = (f32[12,8,128]{2,1,0:T(8,128)S(1)}, f32[4,8,128]{2,1,0:T(8,128)S(1)}, f32[4,8,128]{2,1,0:T(8,128)S(1)}) custom-call(f32[16,18,8,128]{3,2,1,0:T(8,128)S(1)} %get-tuple-element.94.history, f32[18,8,128]{2,1,0:T(8,128)S(1)} %get-tuple-element.95.opens, s32[18,8,128]{2,1,0:T(8,128)S(1)} %get-tuple-element.97.words, ...), custom_call_target="tpu_custom_call" | custom-call | flops 120000000 | bytes 6000000 | tf_op jit(solution)/shard_map/gradient_steps/pallas_call | solution.py:743
  23.3 0.7 %collective-permute-start.12 = (f32[4,8,128]{2,1,0:T(8,128)S(1)}, f32[4,8,128]{2,1,0:T(8,128)S(1)}, u32[]{:S(2)}, u32[]{:S(2)}) collective-permute-start(f32[4,8,128]{2,1,0:T(8,128)S(1)} %get-tuple-element.107), channel_id=1, source_target_pairs={{1,2},{2,1},{3,4},{4,3},{5,6},{6,5},{7,8},{8,7},{9,10},{10,9},{11,... | collective-permute-start | bytes 49160 | tf_op jit(solution)/shard_map/ppermute | solution.py:883
  23.9 3.4 %collective-permute-start.13 = (f32[4,8,128]{2,1,0:T(8,128)S(1)}, f32[4,8,128]{2,1,0:T(8,128)S(1)}, u32[]{:S(2)}, u32[]{:S(2)}) collective-permute-start(f32[4,8,128]{2,1,0:T(8,128)S(1)} %get-tuple-element.108), channel_id=1, source_target_pairs={{0,1},{1,0},{2,3},{3,2},{4,5},{5,4},{6,7},{7,6},{8,9},{9,8},{10,11... | collective-permute-start | bytes 49160 | tf_op jit(solution)/shard_map/ppermute | solution.py:882
  27.3 0.8 %conditional.2 = (f32[19,20,8,128]{3,2,1,0:T(8,128)S(1)}) conditional(s32[]{:T(128)} %bitcast.2, (s32[3]{0:T(128)S(1)}, f32[19,12,8,128]{3,2,1,0:T(8,128)S(1)}, f32[2,19,4,8,128]{4,3,2,1,0:T(8,128)S(1)}, f32[12,8,128]{2,1,0:T(8,128)S(1)}) %tuple.20, (f32[19,12,8,128]{3,2,1,0:T(8,128)S(1)}, s32[3]{0:T(128)S(1)}, f32[12,8,128]{2,1,0:T(8,128)S(1)}) %tuple.21), branch_computations={%region_0.0_spmd, %region_1.0_spmd} | conditional | flops 80466944 | bytes 15206744 | solution.py:931
  27.3 0.8 %place_populations.2 = f32[19,20,8,128]{3,2,1,0:T(8,128)S(1)} custom-call(s32[3]{0:T(128)S(1)} %get-tuple-element.32.where, f32[19,12,8,128]{3,2,1,0:T(8,128)S(1)} %get-tuple-element.33.final, f32[2,19,4,8,128]{4,3,2,1,0:T(8,128)S(1)} %get-tuple-element.38.outer, f32[12,8,128]{2,1,0:T(8,128)S(1)} %get-tuple-element.39.later), custom_call_target="tpu_custom_call" | custom-call | flops 80000000 | bytes 4000000 | tf_op jit(solution)/shard_map/cond/branch_0_fun/place_populations/pallas_call | solution.py:743
  28.2 0.0 copy-start
  28.2 0.0 collective-permute-done.11
  28.2 0.7 %conditional.3 = (f32[20,8,128]{2,1,0:T(8,128)S(1)}) conditional(s32[]{:T(128)} %bitcast.2, (s32[3]{0:T(128)S(1)}, f32[4,8,128]{2,1,0:T(8,128)S(1)}, f32[12,8,128]{2,1,0:T(8,128)S(1)}, f32[4,8,128]{2,1,0:T(8,128)S(1)}, f32[4,8,128]{2,1,0:T(8,128)S(1)}) %tuple.22, (f32[12,8,128]{2,1,0:T(8,128)S(1)}, s32[3]{0:T(128)S(1)}, ...), branch_computations={%region_2.0_spmd, %region_3.0_spmd} | conditional | flops 20000000 | bytes 1393304 | solution.py:932
  28.2 0.7 %near_gradient.1 = f32[20,8,128]{2,1,0:T(8,128)S(1)} custom-call(s32[3]{0:T(128)S(1)} %get-tuple-element.43.where, f32[4,8,128]{2,1,0:T(8,128)S(1)} %get-tuple-element.44.drag, f32[12,8,128]{2,1,0:T(8,128)S(1)} %get-tuple-element.45.gradient, f32[4,8,128]{2,1,0:T(8,128)S(1)} %get-tuple-element.46.from_far, f32[4,8,128]{2,1,0:T(8,128)S(1)} %get-tuple-element.47.from_near), custom_call_target="tpu_custom_call" | custom-call | flops 20000000 | bytes 1000000 | tf_op jit(solution)/shard_map/cond/branch_0_fun/near_gradient/pallas_call | solution.py:743
  29.0 0.0 copy-start.1
  29.0 0.3 %copy-done = f32[19,20,8,128]{3,2,1,0:T(8,128)} copy-done((f32[19,20,8,128]{3,2,1,0:T(8,128)}, f32[19,20,8,128]{3,2,1,0:T(8,128)S(1)}, u32[]{:S(2)}) %copy-start) | copy-done | bytes 1556504
  29.3 0.3 %copy-done.1 = f32[20,8,128]{2,1,0:T(8,128)} copy-done((f32[20,8,128]{2,1,0:T(8,128)}, f32[20,8,128]{2,1,0:T(8,128)S(1)}, u32[]{:S(2)}) %copy-start.1) | copy-done | bytes 81944
  (6 shorter events, 0.0 us)
Async XLA Ops:
  2.0 8.8 %collective-permute-start.4 = (f32[23,2,8,128]{3,2,1,0:T(8,128)S(1)}, f32[23,2,8,128]{3,2,1,0:T(8,128)S(1)}, u32[]{:S(2)}, u32[]{:S(2)}) collective-permute-start(f32[23,2,8,128]{3,2,1,0:T(8,128)S(1)} %get-tuple-element.84), channel_id=1, source_target_pairs={{0,15},{1,2},{2,1},{3,4},{4,3},{5,6},{6,5},{7,8},{8,7},{9,10},{10,... | collective-permute-start | bytes 565256 | tf_op jit(solution)/shard_map/ppermute | solution.py:768
  7.5 3.3 %collective-permute-start.5 = (f32[23,2,8,128]{3,2,1,0:T(8,128)S(1)}, f32[23,2,8,128]{3,2,1,0:T(8,128)S(1)}, u32[]{:S(2)}, u32[]{:S(2)}) collective-permute-start(f32[23,2,8,128]{3,2,1,0:T(8,128)S(1)} %get-tuple-element.85), channel_id=1, source_target_pairs={{0,1},{1,0},{2,3},{3,2},{4,5},{5,4},{6,7},{7,6},{8,9},{9,8},{10,11... | collective-permute-start | bytes 565256 | tf_op jit(solution)/shard_map/ppermute | solution.py:767
  10.0 8.9 %collective-permute-start.6 = (f32[49,8,128]{2,1,0:T(8,128)S(1)}, f32[49,8,128]{2,1,0:T(8,128)S(1)}, u32[]{:S(2)}, u32[]{:S(2)}) collective-permute-start(f32[49,8,128]{2,1,0:T(8,128)S(1)} %get-tuple-element.100), channel_id=1, source_target_pairs={{0,15},{1,2},{2,1},{3,4},{4,3},{5,6},{6,5},{7,8},{8,7},{9,10},{10,... | collective-permute-start | bytes 602120 | tf_op jit(solution)/shard_map/ppermute | solution.py:806
  10.8 8.1 %collective-permute-start.7 = (f32[49,8,128]{2,1,0:T(8,128)S(1)}, f32[49,8,128]{2,1,0:T(8,128)S(1)}, u32[]{:S(2)}, u32[]{:S(2)}) collective-permute-start(f32[49,8,128]{2,1,0:T(8,128)S(1)} %get-tuple-element.101), channel_id=1, source_target_pairs={{0,1},{1,0},{2,3},{3,2},{4,5},{5,4},{6,7},{7,6},{8,9},{9,8},{10,11... | collective-permute-start | bytes 602120 | tf_op jit(solution)/shard_map/ppermute | solution.py:805
  11.9 1.4 %collective-permute-start.8 = (f32[4,8,128]{2,1,0:T(8,128)S(1)}, f32[4,8,128]{2,1,0:T(8,128)S(1)}, u32[]{:S(2)}, u32[]{:S(2)}) collective-permute-start(f32[4,8,128]{2,1,0:T(8,128)S(1)} %get-tuple-element.102), channel_id=1, source_target_pairs={{0,1},{1,0},{2,3},{3,2},{4,5},{5,4},{6,7},{7,6},{8,9},{9,8},{10,11... | collective-permute-start | bytes 49160 | tf_op jit(solution)/shard_map/ppermute | solution.py:841
  13.3 3.7 %collective-permute-start.9 = (f32[4,8,128]{2,1,0:T(8,128)S(1)}, f32[4,8,128]{2,1,0:T(8,128)S(1)}, u32[]{:S(2)}, u32[]{:S(2)}) collective-permute-start(f32[4,8,128]{2,1,0:T(8,128)S(1)} %add.12), channel_id=1, source_target_pairs={{0,4},{1,5},{2,6},{3,7},{4,0},{5,1},{6,2},{7,3},{8,12},{9,13},{10,... | collective-permute-start | bytes 49160 | tf_op jit(solution)/shard_map/ppermute | solution.py:841
  17.1 3.7 %collective-permute-start.10 = (f32[4,8,128]{2,1,0:T(8,128)S(1)}, f32[4,8,128]{2,1,0:T(8,128)S(1)}, u32[]{:S(2)}, u32[]{:S(2)}) collective-permute-start(f32[4,8,128]{2,1,0:T(8,128)S(1)} %add.13.summed), channel_id=1, source_target_pairs={{0,2},{1,3},{2,0},{3,1},{4,6},{5,7},{6,4},{7,5},{8,10},{9,11},{10,... | collective-permute-start | bytes 49160 | tf_op jit(solution)/shard_map/ppermute | solution.py:841
  20.8 7.4 %collective-permute-start.11 = (f32[4,8,128]{2,1,0:T(8,128)S(1)}, f32[4,8,128]{2,1,0:T(8,128)S(1)}, u32[]{:S(2)}, u32[]{:S(2)}) collective-permute-start(f32[4,8,128]{2,1,0:T(8,128)S(1)} %add.14.summed), channel_id=1, source_target_pairs={{0,8},{1,9},{2,10},{3,11},{4,12},{5,13},{6,14},{7,15},{8,0},{9,1},... | collective-permute-start | bytes 49160 | tf_op jit(solution)/shard_map/ppermute | solution.py:841
  23.3 4.9 %collective-permute-start.12 = (f32[4,8,128]{2,1,0:T(8,128)S(1)}, f32[4,8,128]{2,1,0:T(8,128)S(1)}, u32[]{:S(2)}, u32[]{:S(2)}) collective-permute-start(f32[4,8,128]{2,1,0:T(8,128)S(1)} %get-tuple-element.107), channel_id=1, source_target_pairs={{1,2},{2,1},{3,4},{4,3},{5,6},{6,5},{7,8},{8,7},{9,10},{10,9},{11,... | collective-permute-start | bytes 49160 | tf_op jit(solution)/shard_map/ppermute | solution.py:883
  23.9 4.3 %collective-permute-start.13 = (f32[4,8,128]{2,1,0:T(8,128)S(1)}, f32[4,8,128]{2,1,0:T(8,128)S(1)}, u32[]{:S(2)}, u32[]{:S(2)}) collective-permute-start(f32[4,8,128]{2,1,0:T(8,128)S(1)} %get-tuple-element.108), channel_id=1, source_target_pairs={{0,1},{1,0},{2,3},{3,2},{4,5},{5,4},{6,7},{7,6},{8,9},{9,8},{10,11... | collective-permute-start | bytes 49160 | tf_op jit(solution)/shard_map/ppermute | solution.py:882
  28.2 1.1 %copy-start = (f32[19,20,8,128]{3,2,1,0:T(8,128)}, f32[19,20,8,128]{3,2,1,0:T(8,128)S(1)}, u32[]{:S(2)}) copy-start(f32[19,20,8,128]{3,2,1,0:T(8,128)S(1)} %get-tuple-element.109) | copy-start | bytes 4669444
  29.0 0.6 %copy-start.1 = (f32[20,8,128]{2,1,0:T(8,128)}, f32[20,8,128]{2,1,0:T(8,128)S(1)}, u32[]{:S(2)}) copy-start(f32[20,8,128]{2,1,0:T(8,128)S(1)} %get-tuple-element.110) | copy-start | bytes 245764
